TPU v7x, 32 devices: a whole 2x2x4 slice. The times are simulated.
32 devices in a mesh: dir: 2 (over x), dp: 16 (over z, y, core).
Axes of the slice: x: 2, y: 2, z: 4, core: 2. Of those that a mesh axis runs over, the one named last changes fastest.
Arguments:
- hidden_in: bfloat16 [2, 16384, 768], P('dir', 'dp'), may hold values from -6 to 6
- lengths: int32 [16, 8], P('dp'), may hold values from 1 to 1024, 2048 in all within a row
- gain_in: float32 [768], replicated, may hold values from 0.5 to 1.5
- w_x: bfloat16 [768, 1536], replicated, may hold values from -0.21875 to 0.21875
- w_z: bfloat16 [768, 1536], replicated, may hold values from -0.21875 to 0.21875
- w_bcdt: bfloat16 [768, 304], replicated, may hold values from -0.21875 to 0.21875
- conv_w: float32 [4, 1792], replicated, may hold values from -3 to 3
- dt_bias: float32 [2, 24], replicated, may hold values from -6 to -2
- a_log: float32 [2, 24], replicated, may hold values from -4 to 0.5
- d_skip: float32 [24], replicated, may hold values from 0.5 to 2
- gain_mix: float32 [1536], replicated, may hold values from 0.5 to 1.5
- w_out: bfloat16 [1536, 768], replicated, may hold values from -0.15625 to 0.15625
- cotangent: bfloat16 [2, 16384, 768], P('dir', 'dp'), may hold values from -6 to 6
Outputs:
- hidden_out: bfloat16 [2, 16384, 768], P('dir', 'dp')
- grad_in: bfloat16 [2, 16384, 768], P('dir', 'dp')
- grad_w_x: float32 [768, 1536], P('dp')
- grad_w_z: float32 [768, 1536], P('dp')
- grad_w_bcdt: float32 [768, 304], P('dp')
- grad_w_out: float32 [1536, 768], P('dp')
- grad_gain_in: float32 [768], replicated
- grad_conv_w: float32 [4, 1792], replicated
- grad_dt_bias: float32 [2, 24], replicated
- grad_a_log: float32 [2, 24], replicated
- grad_d_skip: float32 [24], replicated
- grad_gain_mix: float32 [1536], replicated
Inputs may be any that keep to these rules, and one draw needn't show every extreme that they name: In each row the first 7 entries are sequence lengths and the last is padding; the row sums to 2048 and its largest entry is exactly 1024.
All inputs are finite; a program needn't handle non-finite values.
Results may differ from a plain program's by a relative error of at most 0.013.
Values may be sent and summed in bfloat16 or wider, within the bound.
No kernel may reach another device: no remote copies, remote signals or barrier semaphores. Data moves between devices by JAX's collectives and lax.ppermute only.
A program may use at most 320 MiB of HBM per device.

v0:
```python
import functools

import jax
import jax.numpy as jnp
import numpy as np
from jax import lax
from jax.experimental import pallas as pl
from jax.experimental.pallas import tpu as pltpu
from jax.sharding import PartitionSpec as P

F32 = jnp.float32
BF16 = jnp.bfloat16
CHUNK = 128
ROWS = 256
EPS = 1e-05
VMEM_BYTES = 56 * 1024 * 1024
NT = (((1,), (1,)), ((), ()))
TN = (((0,), (0,)), ((), ()))
EXACT = lax.Precision.HIGHEST


def mm(left, right):
    return jnp.dot(left, right, preferred_element_type=F32)


def mm_nt(left, right):
    return lax.dot_general(left, right, NT, preferred_element_type=F32)


def mm_tn(left, right):
    return lax.dot_general(left, right, TN, preferred_element_type=F32)


def exact_mm(left, right):
    return jnp.dot(left, right, precision=EXACT, preferred_element_type=F32)


def sequence_bounds(info_ref):
    count = info_ref.shape[0] - 1
    bounds, total = [], 0
    for position in range(count):
        total = total + info_ref[position]
        bounds.append(total)
    return bounds, info_ref[count]


def start_of(row, bounds):
    start = jnp.where(row < 0, -1, 0)
    for bound in bounds:
        start = jnp.where(row >= bound, bound, start)
    return start


def row_iota(count):
    return lax.broadcasted_iota(jnp.int32, (count, 1), 0)


def lane_iota(count):
    return lax.broadcasted_iota(jnp.int32, (1, count), 1)


def split_columns(rows):
    high = rows.astype(BF16).astype(F32)
    return jnp.concatenate([high, rows - high], axis=0).T.astype(BF16)


def head_sums(values, heads_ref, head_count):
    return mm_nt(heads_ref[0:head_count, :], values.astype(BF16))


def chunk_factors(dt, inc, rate, bounds, first):
    heads = dt.shape[0] // 2
    starts = start_of(first + lane_iota(CHUNK), bounds)
    before = start_of(first - 1, bounds)
    left = start_of(first, bounds)
    right = start_of(first + CHUNK - 1, bounds)
    after = start_of(first + CHUNK, bounds)
    inc0, inc1 = inc[:heads], inc[heads:]
    exc1 = inc1 - dt[heads:] * rate[heads:]
    total0, total1 = inc0[:, CHUNK - 1 : CHUNK], inc1[:, CHUNK - 1 : CHUNK]
    enter0 = jnp.where(starts == before, jnp.exp(-inc0), 0.0)
    enter1 = jnp.where(starts == after, jnp.exp(exc1 - total1), 0.0)
    leave0 = jnp.where(starts == right, dt[:heads] * jnp.exp(inc0 - total0), 0.0)
    leave1 = jnp.where(starts == left, dt[heads:] * jnp.exp(-exc1), 0.0)
    keep0 = jnp.where(before == right, jnp.exp(-total0), 0.0)
    keep1 = jnp.where(after == left, jnp.exp(-total1), 0.0)
    enter = jnp.concatenate([enter0, enter1], axis=0)
    leave = jnp.concatenate([leave0, leave1], axis=0)
    keep = jnp.concatenate([keep0, keep1], axis=0)
    return enter, leave, keep


def gates_kernel(x_ref, c_ref, gain_ref, wz_ref, wo_ref, normed_ref, z_ref, dnorm_ref):
    x = x_ref[...].astype(F32)
    inv = lax.rsqrt(jnp.mean(x * x, axis=1, keepdims=True) + EPS)
    normed = (x * inv * gain_ref[...]).astype(BF16)
    normed_ref[...] = normed
    z_ref[...] = mm(normed, wz_ref[...]).astype(BF16)
    dnorm_ref[...] = mm_nt(c_ref[...], wo_ref[...]).astype(BF16)


def proj_kernel(
    info_ref,
    normed_ref,
    halo_ref,
    gain_ref,
    wx_ref,
    wbc_ref,
    wdt_ref,
    taps_ref,
    bias_ref,
    alog_ref,
    e0_ref,
    e1_ref,
    pre_ref,
    act_ref,
    slope_ref,
    raw_ref,
    dt_ref,
    inc_ref,
    sf0_ref,
    sf1_ref,
    keep_ref,
    send_ref,
    buf,
    acc0,
    acc1,
    run1,
):
    step = pl.program_id(0)
    bounds, base = sequence_bounds(info_ref)
    inner = wx_ref.shape[1]
    channels = taps_ref.shape[1]
    heads = bias_ref.shape[0] // 2
    state = (channels - inner) // 4

    @pl.when(step == 0)
    def _():
        x = halo_ref[...].astype(F32)
        inv = lax.rsqrt(jnp.mean(x * x, axis=1, keepdims=True) + EPS)
        normed = (x * inv * gain_ref[...]).astype(BF16)
        px = mm(normed, wx_ref[...]).astype(BF16).astype(F32)
        pb = mm(normed, wbc_ref[...]).astype(BF16).astype(F32)
        buf[0:8, 0:inner] = px[8:16]
        buf[0:8, inner:channels] = pb[8:16]
        acc0[...] = jnp.zeros_like(acc0)
        acc1[...] = jnp.zeros_like(acc1)
        run1[...] = jnp.ones_like(run1)

    @pl.when(step > 0)
    def _():
        buf[0:8, :] = buf[ROWS : ROWS + 8, :]

    normed = normed_ref[...]
    px = mm(normed, wx_ref[...]).astype(BF16)
    pre_ref[:, 0:inner] = px
    buf[8 : ROWS + 8, 0:inner] = px.astype(F32)
    pb = mm(normed, wbc_ref[...]).astype(BF16)
    pre_ref[:, inner:channels] = pb
    buf[8 : ROWS + 8, inner:channels] = pb.astype(F32)

    first = base + step * ROWS
    rows = first + row_iota(ROWS)
    place = rows - start_of(rows, bounds)
    masks = [jnp.where(place >= lag, 1.0, 0.0) for lag in (1, 2, 3)]
    for tile in range(channels // 256):
        cols = slice(tile * 256, tile * 256 + 256)
        conv = buf[8 : ROWS + 8, cols] * taps_ref[3:4, cols]
        for lag in (1, 2, 3):
            conv = conv + buf[8 - lag : ROWS + 8 - lag, cols] * taps_ref[3 - lag : 4 - lag, cols] * (
                masks[lag - 1]
            )
        sig = jax.nn.sigmoid(conv)
        act_ref[:, cols] = (conv * sig).astype(BF16)
        slope_ref[:, cols] = (sig * (1.0 + conv * (1.0 - sig))).astype(BF16)

    raw = mm_nt(wdt_ref[...], normed).astype(BF16).astype(F32) + bias_ref[...]
    raw_ref[...] = raw
    dt = jnp.maximum(raw, 0.0) + jnp.log1p(jnp.exp(-jnp.abs(raw)))
    dt_ref[...] = dt
    rate = jnp.exp(alog_ref[...])
    upto = jnp.where(row_iota(CHUNK) <= lane_iota(CHUNK), 1.0, 0.0)
    for part in range(ROWS // CHUNK):
        span = slice(part * CHUNK, part * CHUNK + CHUNK)
        dt_c = dt[:, span]
        inc = exact_mm(dt_c * rate, upto)
        inc_ref[:, span] = inc
        _, leave, keep = chunk_factors(dt_c, inc, rate, bounds, first + part * CHUNK)
        leave_cols = split_columns(leave)
        keep_cols = split_columns(jnp.broadcast_to(keep, (2 * heads, CHUNK)))[0:16]
        keep0 = mm(keep_cols, e0_ref[...])[0:1]
        keep1 = mm(keep_cols, e1_ref[...])[0:1]
        keep_ref[part, 0:1, :] = keep0
        keep_ref[part, 1:2, :] = keep1
        x = act_ref[span, 0:inner].astype(F32)
        b0 = act_ref[span, inner : inner + state]
        b1 = act_ref[span, inner + 2 * state : inner + 3 * state]
        fresh0 = mm_tn(b0, (x * mm(leave_cols, e0_ref[...])).astype(BF16))
        sf0_ref[part] = fresh0.astype(BF16)
        acc0[...] = keep0 * acc0[...] + fresh0
        fresh1 = mm_tn(b1, (x * mm(leave_cols, e1_ref[...])).astype(BF16))
        sf1_ref[part] = fresh1.astype(BF16)
        acc1[...] = acc1[...] + run1[...] * fresh1
        run1[...] = run1[...] * keep1

    @pl.when(step == pl.num_programs(0) - 1)
    def _():
        send_ref[...] = jnp.where(base > 0, acc1[...], acc0[...]).astype(BF16)


def intra_kernel(info_ref, act_ref, dt_ref, inc_ref, alog_ref, y_ref, *, inner, state):
    bounds, base = sequence_bounds(info_ref)
    first = base + pl.program_id(0) * CHUNK
    heads = alog_ref.shape[0] // 2
    width = inner // heads
    t, s = row_iota(CHUNK), lane_iota(CHUNK)
    same = start_of(first + t, bounds) == start_of(first + s, bounds)
    lower = t > s
    b0 = act_ref[:, inner : inner + state]
    c0 = act_ref[:, inner + state : inner + 2 * state]
    b1 = act_ref[:, inner + 2 * state : inner + 3 * state]
    c1 = act_ref[:, inner + 3 * state : inner + 4 * state]
    scores = jnp.where(lower, mm_nt(c0, b0), mm_nt(c1, b1))
    scores = jnp.where(same & (t != s), scores, 0.0)
    dt = dt_ref[...]
    inc = inc_ref[...]
    log_dt = jnp.log(jnp.maximum(dt, 1e-37))
    exc1 = inc[heads:] - dt[heads:] * jnp.exp(alog_ref[heads:, :])
    out_cols = jnp.concatenate([-inc[:heads], exc1], axis=0).T
    in_rows = jnp.concatenate([inc[:heads] + log_dt[:heads], log_dt[heads:] - exc1], axis=0)
    lanes = lane_iota(2 * width)
    for pair in range(heads // 2):
        cols = slice(pair * 2 * width, (pair + 1) * 2 * width)
        weights = []
        for head in (2 * pair, 2 * pair + 1):
            spread = jnp.where(
                lower,
                out_cols[:, head : head + 1] + in_rows[head : head + 1, :],
                out_cols[:, heads + head : heads + head + 1]
                + in_rows[heads + head : heads + head + 1, :],
            )
            weights.append((jnp.exp(spread) * scores).astype(BF16))
        x = act_ref[:, cols]
        zero = jnp.zeros_like(x)
        x_cut = jnp.concatenate(
            [jnp.where(lanes < width, x, zero), jnp.where(lanes < width, zero, x)], axis=0
        )
        y_ref[:, cols] = mm(jnp.concatenate(weights, axis=1), x_cut).astype(BF16)


def mix_kernel(
    info_ref,
    x_ref,
    act_ref,
    dt_ref,
    inc_ref,
    alog_ref,
    sf0_ref,
    sf1_ref,
    keep_ref,
    recv_ref,
    yin_ref,
    z_ref,
    dnorm_ref,
    wo_ref,
    gain_ref,
    skip_ref,
    e0_ref,
    e1_ref,
    out_ref,
    mixed_ref,
    dz_ref,
    dy_ref,
    r_ref,
    df0_ref,
    df1_ref,
    s0_ref,
    s1_ref,
    send_ref,
    ggain_ref,
    gskip_ref,
    all0,
    all1,
    acc0,
    acc1,
    run0,
):
    step = pl.program_id(0)
    bounds, base = sequence_bounds(info_ref)
    first = base + step * CHUNK
    inner = gain_ref.shape[1]
    heads = alog_ref.shape[0] // 2
    state = recv_ref.shape[0]
    chunks = sf0_ref.shape[0]

    @pl.when(step == 0)
    def _():
        recv = recv_ref[...].astype(F32)
        zero = jnp.zeros_like(recv)
        carried = jnp.where(base > 0, recv, zero)
        for chunk in range(chunks):
            all0[chunk] = carried.astype(BF16)
            carried = keep_ref[chunk, 0:1, :] * carried + sf0_ref[chunk].astype(F32)
        carried = jnp.where(base > 0, zero, recv)
        for chunk in range(chunks - 1, -1, -1):
            all1[chunk] = carried.astype(BF16)
            carried = keep_ref[chunk, 1:2, :] * carried + sf1_ref[chunk].astype(F32)
        acc0[...] = jnp.zeros_like(acc0)
        acc1[...] = jnp.zeros_like(acc1)
        run0[...] = jnp.ones_like(run0)
        ggain_ref[...] = jnp.zeros_like(ggain_ref)
        gskip_ref[...] = jnp.zeros_like(gskip_ref)

    s0 = all0[step]
    s1 = all1[step]
    s0_ref[0] = s0
    s1_ref[0] = s1
    enter, _, _ = chunk_factors(dt_ref[...], inc_ref[...], jnp.exp(alog_ref[...]), bounds, first)
    enter_cols = split_columns(enter)
    enter0 = mm(enter_cols, e0_ref[...])
    enter1 = mm(enter_cols, e1_ref[...])
    c0 = act_ref[:, inner + state : inner + 2 * state]
    c1 = act_ref[:, inner + 3 * state : inner + 4 * state]
    y0 = enter0 * mm(c0, s0)
    y1 = enter1 * mm(c1, s1)
    conv = act_ref[:, 0:inner].astype(F32)
    live = jnp.where(first + row_iota(CHUNK) < bounds[len(bounds) - 2], 1.0, 0.0)
    mixer = live * (yin_ref[...].astype(F32) + y0 + y1 + skip_ref[...] * conv)
    z = z_ref[...].astype(F32)
    sig = jax.nn.sigmoid(z)
    gate = z * sig
    gated = mixer * gate
    scale = lax.rsqrt(jnp.mean(gated * gated, axis=1, keepdims=True) + EPS)
    unit = gated * scale
    mixed = (unit * gain_ref[...]).astype(BF16)
    mixed_ref[...] = mixed
    out_ref[...] = (x_ref[...].astype(F32) + mm(mixed, wo_ref[...])).astype(BF16)
    dnorm = dnorm_ref[...].astype(F32)
    ggain_ref[...] += jnp.sum(dnorm * unit, axis=0, keepdims=True)
    scaled = dnorm * gain_ref[...]
    dgated = scale * (scaled - unit * jnp.mean(scaled * unit, axis=1, keepdims=True))
    dz_ref[...] = (dgated * mixer * sig * (1.0 + z * (1.0 - sig))).astype(BF16)
    dmixer = live * dgated * gate
    dy = dmixer.astype(BF16)
    dy_ref[...] = dy
    gskip_ref[...] += jnp.sum(dmixer * conv, axis=0, keepdims=True)
    dy = dy.astype(F32)
    r_ref[0:heads, :] = head_sums(dy * y0, e0_ref, heads)
    r_ref[heads : 2 * heads, :] = head_sums(dy * y1, e0_ref, heads)
    df0 = mm_tn(c0, (dy * enter0).astype(BF16))
    df0_ref[0] = df0.astype(BF16)
    acc0[...] = acc0[...] + run0[...] * df0
    run0[...] = run0[...] * keep_ref[step, 0:1, :]
    df1 = mm_tn(c1, (dy * enter1).astype(BF16))
    df1_ref[0] = df1.astype(BF16)
    acc1[...] = keep_ref[step, 1:2, :] * acc1[...] + df1

    @pl.when(step == pl.num_programs(0) - 1)
    def _():
        send_ref[...] = jnp.where(base > 0, acc0[...], acc1[...]).astype(BF16)


def back_kernel(
    info_ref,
    act_ref,
    slope_ref,
    raw_ref,
    dt_ref,
    inc_ref,
    r_ref,
    alog_ref,
    dy_ref,
    s0_ref,
    s1_ref,
    df0_ref,
    df1_ref,
    keep_ref,
    recv_ref,
    skip_ref,
    e0_ref,
    e1_ref,
    dpre_ref,
    draw_ref,
    gbias_ref,
    galog_ref,
    all0,
    all1,
    cut0,
    cut1,
    own0,
    own1,
    dscore,
    dx,
):
    step = pl.program_id(0)
    bounds, base = sequence_bounds(info_ref)
    first = base + step * CHUNK
    inner = skip_ref.shape[1]
    heads = alog_ref.shape[0] // 2
    width = inner // heads
    state = recv_ref.shape[0]
    chunks = df0_ref.shape[0]

    @pl.when(step == 0)
    def _():
        recv = recv_ref[...].astype(F32)
        zero = jnp.zeros_like(recv)
        carried = jnp.where(base > 0, zero, recv)
        for chunk in range(chunks - 1, -1, -1):
            all0[chunk] = carried.astype(BF16)
            carried = keep_ref[chunk, 0:1, :] * carried + df0_ref[chunk].astype(F32)
        carried = jnp.where(base > 0, recv, zero)
        for chunk in range(chunks):
            all1[chunk] = carried.astype(BF16)
            carried = keep_ref[chunk, 1:2, :] * carried + df1_ref[chunk].astype(F32)
        gbias_ref[...] = jnp.zeros_like(gbias_ref)
        galog_ref[...] = jnp.zeros_like(galog_ref)

    s, t = row_iota(CHUNK), lane_iota(CHUNK)
    same = (start_of(first + s, bounds) == start_of(first + t, bounds)) & (s != t)
    early = s < t
    b0 = act_ref[:, inner : inner + state]
    c0 = act_ref[:, inner + state : inner + 2 * state]
    b1 = act_ref[:, inner + 2 * state : inner + 3 * state]
    c1 = act_ref[:, inner + 3 * state : inner + 4 * state]
    scores = jnp.where(early, mm_nt(b0, c0), mm_nt(b1, c1))
    scores = jnp.where(same, scores, 0.0)
    dt = dt_ref[...]
    inc = inc_ref[...]
    rate = jnp.exp(alog_ref[...])
    log_dt = jnp.log(jnp.maximum(dt, 1e-37))
    exc1 = inc[heads:] - dt[heads:] * rate[heads:]
    out_rows = jnp.concatenate([-inc[:heads], exc1], axis=0)
    in_cols = jnp.concatenate([inc[:heads] + log_dt[:heads], log_dt[heads:] - exc1], axis=0).T
    lanes = lane_iota(2 * width)
    beyond = jnp.where(s > t, 1.0, 0.0).astype(BF16)
    within = jnp.where(s < t, 1.0, 0.0).astype(BF16)
    tails = jnp.concatenate([beyond, within], axis=1)
    dscore[...] = jnp.zeros_like(dscore)
    for pair in range(heads // 2):
        cols = slice(pair * 2 * width, (pair + 1) * 2 * width)
        x = act_ref[:, cols]
        dy = dy_ref[:, cols]
        zero = jnp.zeros_like(x)
        x_cut = jnp.concatenate(
            [jnp.where(lanes < width, x, zero), jnp.where(lanes < width, zero, x)], axis=0
        )
        dweights = mm_nt(x_cut, dy)
        weights = []
        for part in (0, 1):
            head = 2 * pair + part
            spread = jnp.where(
                early,
                in_cols[:, head : head + 1] + out_rows[head : head + 1, :],
                in_cols[:, heads + head : heads + head + 1]
                + out_rows[heads + head : heads + head + 1, :],
            )
            decay = jnp.exp(spread)
            dweight = dweights[part * CHUNK : (part + 1) * CHUNK]
            weight = decay * scores
            weights.append(weight.astype(BF16))
            dscore[...] += dweight * decay
            sums = mm((dweight * weight).astype(BF16), tails)
            sums0, sums1 = sums[:, 0:CHUNK], sums[:, CHUNK : 2 * CHUNK]
            row = slice(head, head + 1)
            cut0[row, :] = jnp.sum(jnp.where(s <= t, sums0, 0.0), axis=0, keepdims=True)
            own0[row, :] = jnp.sum(jnp.where(s == t, sums0, 0.0), axis=0, keepdims=True)
            cut1[row, :] = jnp.sum(jnp.where(s >= t, sums1, 0.0), axis=0, keepdims=True)
            own1[row, :] = jnp.sum(jnp.where(s == t, sums1, 0.0), axis=0, keepdims=True)
        dy_cut = jnp.concatenate(
            [jnp.where(lanes < width, dy, zero), jnp.where(lanes < width, zero, dy)], axis=0
        )
        dx[:, cols] = mm(jnp.concatenate(weights, axis=1), dy_cut)
    dscores = jnp.where(same, dscore[...], 0.0)
    dscore0 = jnp.where(early, dscores, 0.0).astype(BF16)
    dscore1 = jnp.where(early, 0.0, dscores).astype(BF16)

    s0, s1 = s0_ref[0], s1_ref[0]
    ds0, ds1 = all0[step], all1[step]
    enter, leave, _ = chunk_factors(dt, inc, rate, bounds, first)
    enter_cols = split_columns(enter)
    leave_cols = split_columns(leave)
    xf = act_ref[:, 0:inner].astype(F32)
    dyf = dy_ref[...].astype(F32)
    from0 = mm(b0, ds0)
    leave0 = mm(leave_cols, e0_ref[...])
    out0 = xf * leave0
    k0 = head_sums(out0 * from0, e0_ref, heads)
    from1 = mm(b1, ds1)
    leave1 = mm(leave_cols, e1_ref[...])
    out1 = xf * leave1
    k1 = head_sums(out1 * from1, e0_ref, heads)
    dconv = dx[...] + leave0 * from0 + leave1 * from1 + skip_ref[...] * dyf
    dpre_ref[:, 0:inner] = (dconv * slope_ref[:, 0:inner].astype(F32)).astype(BF16)
    db0 = mm(dscore0, c0) + mm_nt(out0.astype(BF16), ds0)
    db1 = mm(dscore1, c1) + mm_nt(out1.astype(BF16), ds1)
    in0 = (dyf * mm(enter_cols, e0_ref[...])).astype(BF16)
    in1 = (dyf * mm(enter_cols, e1_ref[...])).astype(BF16)
    dc0 = mm_tn(dscore0, b0) + mm_nt(in0, s0)
    dc1 = mm_tn(dscore1, b1) + mm_nt(in1, s1)
    dbc = jnp.concatenate([db0, dc0, db1, dc1], axis=1)
    dpre_ref[:, inner:] = (dbc * slope_ref[:, inner:].astype(F32)).astype(BF16)

    kept0 = jnp.sum(ds0.astype(F32) * s0.astype(F32), axis=0, keepdims=True) * keep_ref[step, 0:1, :]
    kept1 = jnp.sum(ds1.astype(F32) * s1.astype(F32), axis=0, keepdims=True) * keep_ref[step, 1:2, :]
    kept = jnp.concatenate([kept0, kept1, jnp.zeros((6, inner), F32)], axis=0)
    kept_high = kept.astype(BF16)
    kept_low = (kept - kept_high.astype(F32)).astype(BF16)
    ones = e0_ref[0:heads, :]
    kept_sum = mm_nt(ones, kept_high) + mm_nt(ones, kept_low)
    r0, r1 = r_ref[0:heads, :], r_ref[heads : 2 * heads, :]
    after = jnp.where(s >= t, 1.0, 0.0)
    ahead = jnp.where(s < t, 1.0, 0.0)
    da0 = -(
        pltpu.roll(cut0[...], 1, 1)
        + exact_mm(r0, after)
        + exact_mm(k0, ahead)
        + kept_sum[:, 0:1]
    )
    da1 = -(
        pltpu.roll(cut1[...], CHUNK - 1, 1)
        + exact_mm(r1, 1.0 - ahead.T)
        + exact_mm(k1, 1.0 - after.T)
        + kept_sum[:, 1:2]
    )
    da = jnp.concatenate([da0, da1], axis=0)
    dlog = jnp.concatenate([own0[...] + k0, own1[...] + k1], axis=0)
    raw = raw_ref[...]
    sig = jax.nn.sigmoid(raw)
    ratio = jnp.where(raw < -20.0, 1.0, sig / jnp.maximum(dt, 1e-37))
    draw = dlog * ratio + da * rate * sig
    draw_ref[...] = draw.astype(BF16)
    gbias_ref[...] += jnp.sum(draw, axis=1, keepdims=True)
    galog_ref[...] += jnp.sum(da * dt * rate, axis=1, keepdims=True)


def weights_kernel(normed_ref, dz_ref, mixed_ref, c_ref, gz_ref, go_ref):
    gz_ref[...] = mm_tn(normed_ref[...], dz_ref[...]).astype(BF16)
    go_ref[...] = mm_tn(mixed_ref[...], c_ref[...]).astype(BF16)


def conv_back_kernel(
    info_ref, normed_ref, dpre_ref, halo_ref, pre_ref, taps_ref, dproj_ref, gw_ref, gtaps_ref, buf
):
    bounds, base = sequence_bounds(info_ref)
    count = dpre_ref.shape[0]
    buf[0:count, :] = dpre_ref[...].astype(F32)
    buf[count : count + 8, :] = halo_ref[0:8, :].astype(F32)
    rows = base + row_iota(count + 8)
    place = rows - start_of(rows, bounds)
    pre = pre_ref[...].astype(F32)
    shifted = buf[0:count, :]
    dproj = shifted * taps_ref[3:4, :]
    gtaps_ref[3:4, :] = jnp.sum(pre * shifted, axis=0, keepdims=True)
    for lag in (1, 2, 3):
        mask = jnp.where(place[lag : count + lag] >= lag, 1.0, 0.0)
        shifted = buf[lag : count + lag, :] * mask
        dproj = dproj + shifted * taps_ref[3 - lag : 4 - lag, :]
        gtaps_ref[3 - lag : 4 - lag, :] = jnp.sum(pre * shifted, axis=0, keepdims=True)
    dproj = dproj.astype(BF16)
    dproj_ref[...] = dproj
    gw_ref[...] = mm_tn(normed_ref[...], dproj).astype(BF16)


def inputs_kernel(
    x_ref,
    c_ref,
    gain_ref,
    dproj_ref,
    draw_ref,
    dz_ref,
    wx_ref,
    wbc_ref,
    wdt_ref,
    wz_ref,
    gin_ref,
    ggain_ref,
):
    inner = wx_ref.shape[1]

    @pl.when(pl.program_id(0) == 0)
    def _():
        ggain_ref[...] = jnp.zeros_like(ggain_ref)

    dn = mm_nt(dproj_ref[:, 0:inner], wx_ref[...])
    dn = dn + mm_nt(dproj_ref[:, inner:], wbc_ref[...])
    dn = dn + mm_nt(dz_ref[...], wz_ref[...])
    dn = dn + mm_tn(draw_ref[...], wdt_ref[...])
    x = x_ref[...].astype(F32)
    inv = lax.rsqrt(jnp.mean(x * x, axis=1, keepdims=True) + EPS)
    unit = x * inv
    ggain_ref[...] += jnp.sum(dn * unit, axis=0, keepdims=True)
    f = dn * gain_ref[...]
    back = inv * (f - unit * jnp.mean(f * unit, axis=1, keepdims=True))
    gin_ref[...] = (c_ref[...].astype(F32) + back).astype(BF16)


def smem():
    return pl.BlockSpec(memory_space=pltpu.SMEM)


def whole(shape):
    return pl.BlockSpec(shape, lambda i: (0,) * len(shape))


def rows_of(count, width):
    return pl.BlockSpec((count, width), lambda i: (i, 0))


def lanes_of(height, count):
    return pl.BlockSpec((height, count), lambda i: (0, i))


def parts_of(count, *rest):
    return pl.BlockSpec((count,) + rest, lambda i: (i,) + (0,) * len(rest))


def call(kernel, name, grid, in_specs, outs, scratch, flops, moved, args):
    return pl.pallas_call(
        kernel,
        name=name,
        grid=(grid,),
        in_specs=in_specs,
        out_specs=[spec for spec, _, _ in outs],
        out_shape=[jax.ShapeDtypeStruct(shape, dtype) for _, shape, dtype in outs],
        scratch_shapes=scratch,
        compiler_params=pltpu.CompilerParams(
            vmem_limit_bytes=VMEM_BYTES, dimension_semantics=("arbitrary",)
        ),
        cost_estimate=pl.CostEstimate(flops=flops, bytes_accessed=moved, transcendentals=0),
    )(*args)


def sum_shards(grad, dp_count):
    rows, width = grad.shape
    index = lax.axis_index("dp")
    held = grad.reshape(dp_count, rows // dp_count, width)
    bit = 1
    while bit < dp_count:
        paired = held.reshape(held.shape[0] // 2, 2, held.shape[1], width)
        mine = (index // bit) % 2
        kept = lax.dynamic_index_in_dim(paired, mine, 1, keepdims=False)
        sent = lax.dynamic_index_in_dim(paired, 1 - mine, 1, keepdims=False).astype(BF16)
        got = lax.ppermute(sent, "dp", [(i, i ^ bit) for i in range(dp_count)])
        held = kept.astype(F32) + got.astype(F32)
        bit *= 2
    held = held[0].astype(BF16)
    got = lax.ppermute(held, "dir", [(0, 1), (1, 0)])
    return held.astype(F32) + got.astype(F32)


def sum_all(values, dp_count):
    bit = 1
    while bit < dp_count:
        values = values + lax.ppermute(values, "dp", [(i, i ^ bit) for i in range(dp_count)])
        bit *= 2
    return values + lax.ppermute(values, "dir", [(0, 1), (1, 0)])


def local(
    dp_count,
    hidden_in,
    lengths,
    gain_in,
    w_x,
    w_z,
    w_bcdt,
    conv_w,
    dt_bias,
    a_log,
    d_skip,
    gain_mix,
    w_out,
    cotangent,
):
    x = hidden_in[0]
    cot = cotangent[0]
    count, model = x.shape
    inner = w_x.shape[1]
    channels = conv_w.shape[1]
    heads = d_skip.shape[0]
    width = inner // heads
    state = (channels - inner) // 4
    chunks = count // CHUNK
    steps = 2 * heads
    direction = lax.axis_index("dir")
    info = jnp.concatenate([lengths[0], (direction * count).astype(jnp.int32)[None]])
    swap = [(0, 1), (1, 0)]

    halo = lax.ppermute(x[count - 16 :], "dir", [(0, 1)])

    gain_row = gain_in[None, :]
    mix_row = gain_mix[None, :]
    skip_row = jnp.repeat(d_skip, width)[None, :]
    w_bc = w_bcdt[:, : 4 * state]
    w_dt = w_bcdt[:, 4 * state :].T
    bias = dt_bias.reshape(steps, 1)
    alog = a_log.reshape(steps, 1)
    spread = np.repeat(np.eye(heads, dtype=np.float32), width, axis=1)
    zeros = np.zeros_like(spread)
    e0 = jnp.asarray(np.concatenate([spread, zeros, spread, zeros]), BF16)
    e1 = jnp.asarray(np.concatenate([zeros, spread, zeros, spread]), BF16)

    def rows_out(size, columns, dtype):
        return (rows_of(size, columns), (count, columns), dtype)

    normed, gate_z, d_norm = call(
        gates_kernel,
        "gates",
        count // ROWS,
        [
            rows_of(ROWS, model),
            rows_of(ROWS, model),
            whole((1, model)),
            whole((model, inner)),
            whole((inner, model)),
        ],
        [
            rows_out(ROWS, model, BF16),
            rows_out(ROWS, inner, BF16),
            rows_out(ROWS, inner, BF16),
        ],
        [],
        4 * count * model * inner,
        4 * count * (model + inner) + 4 * model * inner,
        (x, cot, gain_row, w_z, w_out),
    )

    per = ROWS // CHUNK
    pre, act, slope, raw, dt, inc, sf0, sf1, keep, send = call(
        proj_kernel,
        "proj",
        count // ROWS,
        [
            smem(),
            rows_of(ROWS, model),
            whole((16, model)),
            whole((1, model)),
            whole((model, inner)),
            whole((model, 4 * state)),
            whole((steps, model)),
            whole(conv_w.shape),
            whole((steps, 1)),
            whole((steps, 1)),
            whole(e0.shape),
            whole(e1.shape),
        ],
        [
            rows_out(ROWS, channels, BF16),
            rows_out(ROWS, channels, BF16),
            rows_out(ROWS, channels, BF16),
            (lanes_of(steps, ROWS), (steps, count), F32),
            (lanes_of(steps, ROWS), (steps, count), F32),
            (lanes_of(steps, ROWS), (steps, count), F32),
            (parts_of(per, state, inner), (chunks, state, inner), BF16),
            (parts_of(per, state, inner), (chunks, state, inner), BF16),
            (parts_of(per, 2, inner), (chunks, 2, inner), F32),
            (whole((state, inner)), (state, inner), BF16),
        ],
        [
            pltpu.VMEM((ROWS + 8, channels), F32),
            pltpu.VMEM((state, inner), F32),
            pltpu.VMEM((state, inner), F32),
            pltpu.VMEM((1, inner), F32),
        ],
        3 * count * model * inner,
        8 * count * inner,
        (info, normed, halo, gain_row, w_x, w_bc, w_dt, conv_w, bias, alog, e0, e1),
    )
    received = lax.ppermute(send, "dir", swap)

    (y_in,) = call(
        functools.partial(intra_kernel, inner=inner, state=state),
        "intra",
        chunks,
        [
            smem(),
            rows_of(CHUNK, channels),
            lanes_of(steps, CHUNK),
            lanes_of(steps, CHUNK),
            whole((steps, 1)),
        ],
        [rows_out(CHUNK, inner, BF16)],
        [],
        8 * count * CHUNK * inner,
        6 * count * inner,
        (info, act, dt, inc, alog),
    )

    states = (parts_of(1, state, inner), (chunks, state, inner), BF16)
    all_states = whole((chunks, state, inner))
    out, mixed, dz, dy, r, df0, df1, s0, s1, d_send, g_gain_mix, g_skip = call(
        mix_kernel,
        "mix",
        chunks,
        [
            smem(),
            rows_of(CHUNK, model),
            rows_of(CHUNK, channels),
            lanes_of(steps, CHUNK),
            lanes_of(steps, CHUNK),
            whole((steps, 1)),
            all_states,
            all_states,
            whole((chunks, 2, inner)),
            whole((state, inner)),
            rows_of(CHUNK, inner),
            rows_of(CHUNK, inner),
            rows_of(CHUNK, inner),
            whole((inner, model)),
            whole((1, inner)),
            whole((1, inner)),
            whole(e0.shape),
            whole(e1.shape),
        ],
        [
            rows_out(CHUNK, model, BF16),
            rows_out(CHUNK, inner, BF16),
            rows_out(CHUNK, inner, BF16),
            rows_out(CHUNK, inner, BF16),
            (lanes_of(steps, CHUNK), (steps, count), F32),
            states,
            states,
            states,
            states,
            (whole((state, inner)), (state, inner), BF16),
            (whole((1, inner)), (1, inner), F32),
            (whole((1, inner)), (1, inner), F32),
        ],
        [
            pltpu.VMEM((chunks, state, inner), BF16),
            pltpu.VMEM((chunks, state, inner), BF16),
            pltpu.VMEM((state, inner), F32),
            pltpu.VMEM((state, inner), F32),
            pltpu.VMEM((1, inner), F32),
        ],
        3 * count * model * inner,
        16 * count * inner,
        (
            info,
            x,
            act,
            dt,
            inc,
            alog,
            sf0,
            sf1,
            keep,
            received,
            y_in,
            gate_z,
            d_norm,
            w_out,
            mix_row,
            skip_row,
            e0,
            e1,
        ),
    )
    d_received = lax.ppermute(d_send, "dir", swap)

    blocks = 4
    g_z, g_out = call(
        weights_kernel,
        "weights",
        blocks,
        [
            whole((count, model)),
            lanes_of(count, inner // blocks),
            lanes_of(count, inner // blocks),
            whole((count, model)),
        ],
        [
            (lanes_of(model, inner // blocks), (model, inner), BF16),
            (rows_of(inner // blocks, model), (inner, model), BF16),
        ],
        [],
        4 * count * model * inner,
        6 * count * inner,
        (normed, dz, mixed, cot),
    )

    dpre, draw, g_bias, g_alog = call(
        back_kernel,
        "back",
        chunks,
        [
            smem(),
            rows_of(CHUNK, channels),
            rows_of(CHUNK, channels),
            lanes_of(steps, CHUNK),
            lanes_of(steps, CHUNK),
            lanes_of(steps, CHUNK),
            lanes_of(steps, CHUNK),
            whole((steps, 1)),
            rows_of(CHUNK, inner),
            states[0],
            states[0],
            all_states,
            all_states,
            whole((chunks, 2, inner)),
            whole((state, inner)),
            whole((1, inner)),
            whole(e0.shape),
            whole(e1.shape),
        ],
        [
            rows_out(CHUNK, channels, BF16),
            (lanes_of(steps, CHUNK), (steps, count), BF16),
            (whole((steps, 1)), (steps, 1), F32),
            (whole((steps, 1)), (steps, 1), F32),
        ],
        [
            pltpu.VMEM((chunks, state, inner), BF16),
            pltpu.VMEM((chunks, state, inner), BF16),
            pltpu.VMEM((heads, CHUNK), F32),
            pltpu.VMEM((heads, CHUNK), F32),
            pltpu.VMEM((heads, CHUNK), F32),
            pltpu.VMEM((heads, CHUNK), F32),
            pltpu.VMEM((CHUNK, CHUNK), F32),
            pltpu.VMEM((CHUNK, inner), F32),
        ],
        24 * count * CHUNK * inner,
        16 * count * inner,
        (
            info,
            act,
            slope,
            raw,
            dt,
            inc,
            r,
            alog,
            dy,
            s0,
            s1,
            df0,
            df1,
            keep,
            d_received,
            skip_row,
            e0,
            e1,
        ),
    )
    d_halo = lax.ppermute(dpre[:16], "dir", [(1, 0)])

    tile = 256
    dproj, g_proj, g_taps = call(
        conv_back_kernel,
        "conv_back",
        channels // tile,
        [
            smem(),
            whole((count, model)),
            lanes_of(count, tile),
            lanes_of(16, tile),
            lanes_of(count, tile),
            lanes_of(conv_w.shape[0], tile),
        ],
        [
            (lanes_of(count, tile), (count, channels), BF16),
            (lanes_of(model, tile), (model, channels), BF16),
            (lanes_of(conv_w.shape[0], tile), conv_w.shape, F32),
        ],
        [pltpu.VMEM((count + 8, tile), F32)],
        2 * count * model * channels,
        6 * count * channels,
        (info, normed, dpre, d_halo, pre, conv_w),
    )
    g_dt = lax.dot_general(normed, draw, (((0,), (1,)), ((), ())), preferred_element_type=F32)
    g_bcdt = jnp.concatenate([g_proj[:, inner:], g_dt.astype(BF16)], axis=1)

    grad_in, g_gain_in = call(
        inputs_kernel,
        "inputs",
        count // ROWS,
        [
            rows_of(ROWS, model),
            rows_of(ROWS, model),
            whole((1, model)),
            rows_of(ROWS, channels),
            lanes_of(steps, ROWS),
            rows_of(ROWS, inner),
            whole((model, inner)),
            whole((model, 4 * state)),
            whole((steps, model)),
            whole((model, inner)),
        ],
        [
            rows_out(ROWS, model, BF16),
            (whole((1, model)), (1, model), F32),
        ],
        [],
        5 * count * model * inner,
        8 * count * inner,
        (x, cot, gain_row, dproj, draw, dz, w_x, w_bc, w_dt, w_z),
    )

    parts = [
        g_gain_in.reshape(-1),
        g_taps.reshape(-1),
        g_bias.reshape(-1),
        g_alog.reshape(-1),
        jnp.sum(g_skip.reshape(heads, width), axis=1),
        g_gain_mix.reshape(-1),
    ]
    sizes = [part.shape[0] for part in parts]
    small = sum_all(jnp.concatenate(parts), dp_count)
    ends = list(np.cumsum(sizes))
    small = [small[end - size : end] for end, size in zip(ends, sizes)]
    return (
        out[None],
        grad_in[None],
        sum_shards(g_proj[:, :inner], dp_count),
        sum_shards(g_z, dp_count),
        sum_shards(g_bcdt, dp_count),
        sum_shards(g_out, dp_count),
        small[0],
        small[1].reshape(conv_w.shape),
        small[2].reshape(dt_bias.shape),
        small[3].reshape(a_log.shape),
        small[4],
        small[5],
    )


def solution(mesh):
    return jax.shard_map(
        functools.partial(local, mesh.shape["dp"]),
        mesh=mesh,
        in_specs=(
            P("dir", "dp", None),
            P("dp", None),
            P(),
            P(),
            P(),
            P(),
            P(),
            P(),
            P(),
            P(),
            P(),
            P(),
            P("dir", "dp", None),
        ),
        out_specs=(
            P("dir", "dp", None),
            P("dir", "dp", None),
            P("dp", None),
            P("dp", None),
            P("dp", None),
            P("dp", None),
            P(),
            P(),
            P(),
            P(),
            P(),
            P(),
        ),
        check_vma=False,
    )
```

profile of v0, /device:TPU:0, one launch (start us, length us, event | category | flops | bytes accessed | tf_op | source)
XLA Modules:
  0.0 277.2 jit_solution(12612366472211697410)
XLA Ops:
  1.4 4.8 %collective-permute-start = (bf16[16,768]{1,0:T(8,128)(2,1)S(1)}, bf16[16,768]{1,0:T(8,128)(2,1)S(1)}, u32[]{:S(2)}, u32[]{:S(2)}) collective-permute-start(bf16[16,768]{1,0:T(8,128)(2,1)S(1)} %slice_bitcast_fusion.1), channel_id=1, source_target_pairs={{0,16},{1,17},{2,18},{3,19},{4,20},{5,21},{6,22},{7,23},{8,24},{9,... | collective-permute-start | bytes 73736 | tf_op jit(solution)/shard_map/ppermute | solution.py:690
  6.2 1.3 broadcast_in_dim.19.gain_ref
  7.5 1.5 slice_bitcast_fusion.wdt_ref
  9.0 9.7 %gates.1 = (bf16[1024,768]{1,0:T(8,128)(2,1)}, bf16[1024,1536]{1,0:T(8,128)(2,1)}, bf16[1024,1536]{1,0:T(8,128)(2,1)}) custom-call(bf16[1024,768]{1,0:T(8,128)(2,1)} %bitcast.114, bf16[1024,768]{1,0:T(8,128)(2,1)} %bitcast.119, f32[1,768]{1,0:T(1,128)} %broadcast_in_dim.19.gain_ref, bf16[768,1536]{1,0:T(8,128)(2,1)} %wz_ref.3, bf16[1536,768]{1,0:T(8,128)(2,1)} %wo_ref.3), custom_call_target="tpu_custom_call" | custom-call | flops 4831838208 | bytes 14155776 | tf_op jit(solution)/shard_map/gates/pallas_call | solution.py:619
  20.0 0.9 copy.63.wbc_ref
  22.2 18.8 %proj.1 = (bf16[1024,1792]{1,0:T(8,128)(2,1)}, bf16[1024,1792]{1,0:T(8,128)(2,1)}, bf16[1024,1792]{1,0:T(8,128)(2,1)}, f32[48,1024]{1,0:T(8,128)}, f32[48,1024]{...) custom-call(s32[9]{0:T(128)} %pad_add_fusion.info_ref, ...), custom_call_target="tpu_custom_call" | custom-call | flops 3623878656 | bytes 12582912 | tf_op jit(solution)/shard_map/proj/pallas_call | solution.py:619
  42.5 13.1 %intra.1.yin_ref = bf16[1024,1536]{1,0:T(8,128)(2,1)} custom-call(s32[9]{0:T(128)} %pad_add_fusion.info_ref, bf16[1024,1792]{1,0:T(8,128)(2,1)} %get-tuple-element.49.act_ref, f32[48,1024]{1,0:T(8,128)} %get-tuple-element.50.dt_ref, f32[48,1024]{1,0:T(8,128)} %get-tuple-element.51.inc_ref, f32[48,1]{1,0:T(8,128)} %reshape.154.alog_ref), custom_call_target="tpu_custom_call" | custom-call | flops 1610612736 | bytes 9437184 | tf_op jit(solution)/shard_map/intra/pallas_call | solution.py:619
  56.3 25.9 %mix.1 = (bf16[1024,768]{1,0:T(8,128)(2,1)}, bf16[1024,1536]{1,0:T(8,128)(2,1)}, bf16[1024,1536]{1,0:T(8,128)(2,1)}, bf16[1024,1536]{1,0:T(8,128)(2,1)}, f32[48,...) custom-call(s32[9]{0:T(128)} %pad_add_fusion.info_ref, ...), custom_call_target="tpu_custom_call" | custom-call | flops 3623878656 | bytes 25165824 | tf_op jit(solution)/shard_map/mix/pallas_call | solution.py:619
  82.2 2.1 collective-permute-start.2
  85.9 2.9 %collective-permute-done.2.recv_ref = bf16[64,1536]{1,0:T(8,128)(2,1)S(1)} collective-permute-done((bf16[64,1536]{1,0:T(8,128)(2,1)}, bf16[64,1536]{1,0:T(8,128)(2,1)S(1)}, u32[]{:S(2)}, u32[]{:S(2)}) %collective-permute-start.2) | collective-permute-done | bytes 196640 | tf_op jit(solution)/shard_map/ppermute | solution.py:860
  89.6 40.7 %back.1 = (bf16[1024,1792]{1,0:T(8,128)(2,1)}, bf16[48,1024]{1,0:T(8,128)(2,1)}, f32[48,1]{1,0:T(8,128)}, f32[48,1]{1,0:T(8,128)}) custom-call(s32[9]{0:T(128)} %pad_add_fusion.info_ref, bf16[1024,1792]{1,0:T(8,128)(2,1)} %get-tuple-element.49.act_ref, bf16[1024,1792]{1,0:T(8,128)(2,1)} %get-tuple-element.59.slope_ref, ...), custom_call_target="tpu_custom_call" | custom-call | flops 4831838208 | bytes 25165824 | tf_op jit(solution)/shard_map/back/pallas_call | solution.py:619
  130.2 0.8 slice.43
  131.1 1.3 collective-permute-start.3
  132.4 1.3 convolution_convert_fusion
  134.1 3.1 %collective-permute-done.3.halo_ref = bf16[16,1792]{1,0:T(8,128)(2,1)S(1)} collective-permute-done((bf16[16,1792]{1,0:T(8,128)(2,1)S(1)}, bf16[16,1792]{1,0:T(8,128)(2,1)S(1)}, u32[]{:S(2)}, u32[]{:S(2)}) %collective-permute-start.3) | collective-permute-done | bytes 57376 | tf_op jit(solution)/shard_map/ppermute | solution.py:946
  137.8 18.0 %conv_back.1 = (bf16[1024,1792]{1,0:T(8,128)(2,1)}, bf16[768,1792]{1,0:T(8,128)(2,1)}, f32[4,1792]{1,0:T(4,128)}) custom-call(s32[9]{0:T(128)} %pad_add_fusion.info_ref, bf16[1024,768]{1,0:T(8,128)(2,1)} %get-tuple-element.48.normed_ref, bf16[1024,1792]{1,0:T(8,128)(2,1)} %get-tuple-element.68.dpre_ref, bf16[16,1792]{1,0:T(8,128)(2,1)} %copy-done.13, ...), custom_call_target="tpu_custom_call" | custom-call | flops 2818572288 | bytes 11010048 | tf_op jit(solution)/shard_map/conv_back/pallas_call | solution.py:619
  155.8 11.7 %inputs.1 = (bf16[1024,768]{1,0:T(8,128)(2,1)}, f32[1,768]{1,0:T(1,128)}) custom-call(bf16[1024,768]{1,0:T(8,128)(2,1)} %bitcast.116, bf16[1024,768]{1,0:T(8,128)(2,1)} %bitcast.120, f32[1,768]{1,0:T(1,128)} %broadcast_in_dim.19.gain_ref, bf16[1024,1792]{1,0:T(8,128)(2,1)} %get-tuple-element.70.dproj_ref, bf16[48,1024]{1,0:T(8,128)(2,1)} %get-tuple-element.71.draw_ref, ...), custom_call_target="tpu_custom_call" | custom-call | flops 6039797760 | bytes 12582912 | tf_op jit(solution)/shard_map/inputs/pallas_call | solution.py:619
  168.3 1.0 slice.45
  170.0 1.6 collective-permute-start.25
  171.6 9.9 %weights.1 = (bf16[768,1536]{1,0:T(8,128)(2,1)}, bf16[1536,768]{1,0:T(8,128)(2,1)}) custom-call(bf16[1024,768]{1,0:T(8,128)(2,1)} %get-tuple-element.48.normed_ref, bf16[1024,1536]{1,0:T(8,128)(2,1)} %get-tuple-element.72.dz_ref, bf16[1024,1536]{1,0:T(8,128)(2,1)} %get-tuple-element.75.mixed_ref, bf16[1024,768]{1,0:T(8,128)(2,1)} %bitcast.121), custom_call_target="tpu_custom_call" | custom-call | flops 4831838208 | bytes 9437184 | tf_op jit(solution)/shard_map/weights/pallas_call | solution.py:619
  181.5 1.6 collective-permute-start.26
  183.8 2.6 dynamic-slice_bitcast_fusion
  186.4 2.6 collective-permute-start.27
  189.2 0.8 collective-permute-start.16
  190.0 1.1 dynamic-slice_bitcast_fusion.1
  191.2 0.9 collective-permute-done.27
  192.2 1.6 collective-permute-done.16
  193.8 1.9 collective-permute-start.17
  195.7 1.1 dynamic-slice_bitcast_fusion.2
  196.9 1.8 collective-permute-done.17
  202.6 1.4 reshape.146
  205.3 1.4 convert_add_fusion.7
  206.7 1.7 convert_add_fusion
  208.5 1.6 collective-permute-start.20
  210.1 1.6 convert_add_fusion.1
  212.3 1.6 convert_add_fusion.2
  214.0 1.6 collective-permute-start.5
  215.6 9.2 %collective-permute-done.20 = bf16[4,96,768]{2,1,0:T(8,128)(2,1)S(1)} collective-permute-done((bf16[4,96,768]{2,1,0:T(8,128)(2,1)S(1)}, bf16[4,96,768]{2,1,0:T(8,128)(2,1)S(1)}, u32[]{:S(2)}, u32[]{:S(2)}) %collective-permute-start.20) | collective-permute-done | bytes 589856 | tf_op jit(solution)/shard_map/ppermute | solution.py:644
  225.2 12.2 %collective-permute-done.10 = bf16[4,48,1536]{2,1,0:T(8,128)(2,1)S(1)} collective-permute-done((bf16[4,48,1536]{2,1,0:T(8,128)(2,1)S(1)}, bf16[4,48,1536]{2,1,0:T(8,128)(2,1)S(1)}, u32[]{:S(2)}, u32[]{:S(2)}) %collective-permute-start.10) | collective-permute-done | bytes 589856 | tf_op jit(solution)/shard_map/ppermute | solution.py:644
  237.9 9.6 %collective-permute-done.5 = bf16[4,48,1536]{2,1,0:T(8,128)(2,1)S(1)} collective-permute-done((bf16[4,48,1536]{2,1,0:T(8,128)(2,1)S(1)}, bf16[4,48,1536]{2,1,0:T(8,128)(2,1)S(1)}, u32[]{:S(2)}, u32[]{:S(2)}) %collective-permute-start.5) | collective-permute-done | bytes 589856 | tf_op jit(solution)/shard_map/ppermute | solution.py:644
  247.7 1.1 collective-permute-start.6
  248.8 1.9 collective-permute-start.22
  250.8 1.2 collective-permute-start.12
  252.0 9.6 %collective-permute-done.22 = bf16[1,96,768]{2,1,0:T(8,128)(2,1)S(1)} collective-permute-done((bf16[1,96,768]{2,1,0:T(8,128)(2,1)S(1)}, bf16[1,96,768]{2,1,0:T(8,128)(2,1)S(1)}, u32[]{:S(2)}, u32[]{:S(2)}) %collective-permute-start.22) | collective-permute-done | bytes 147488 | tf_op jit(solution)/shard_map/ppermute | solution.py:644
  261.7 3.0 %collective-permute-done.12 = bf16[1,48,1536]{2,1,0:T(8,128)(2,1)S(1)} collective-permute-done((bf16[1,48,1536]{2,1,0:T(8,128)(2,1)S(1)}, bf16[1,48,1536]{2,1,0:T(8,128)(2,1)S(1)}, u32[]{:S(2)}, u32[]{:S(2)}) %collective-permute-start.12) | collective-permute-done | bytes 147488 | tf_op jit(solution)/shard_map/ppermute | solution.py:644
  265.0 4.9 %collective-permute-done.13 = bf16[48,1536]{1,0:T(8,128)(2,1)S(1)} collective-permute-done((bf16[48,1536]{1,0:T(8,128)(2,1)S(1)}, bf16[48,1536]{1,0:T(8,128)(2,1)S(1)}, u32[]{:S(2)}, u32[]{:S(2)}) %collective-permute-start.13) | collective-permute-done | bytes 147488 | tf_op jit(solution)/shard_map/ppermute | solution.py:648
  271.2 1.9 collective-permute-start.8
  273.9 2.5 collective-permute-done.8
  (126 shorter events, 21.6 us)
Async XLA Ops:
  1.4 20.2 %collective-permute-start = (bf16[16,768]{1,0:T(8,128)(2,1)S(1)}, bf16[16,768]{1,0:T(8,128)(2,1)S(1)}, u32[]{:S(2)}, u32[]{:S(2)}) collective-permute-start(bf16[16,768]{1,0:T(8,128)(2,1)S(1)} %slice_bitcast_fusion.1), channel_id=1, source_target_pairs={{0,16},{1,17},{2,18},{3,19},{4,20},{5,21},{6,22},{7,23},{8,24},{9,... | collective-permute-start | bytes 73736 | tf_op jit(solution)/shard_map/ppermute | solution.py:690
  9.0 9.7 %copy-start.15 = (s32[1,8]{1,0:T(1,128)S(1)}, s32[1,8]{1,0:T(1,128)}, u32[]{:S(2)}) copy-start(s32[1,8]{1,0:T(1,128)} %param.16) | copy-start | bytes 100
  9.0 10.3 %copy-start.10 = (f32[2,24]{1,0:T(2,128)S(1)}, f32[2,24]{1,0:T(2,128)}, u32[]{:S(2)}) copy-start(f32[2,24]{1,0:T(2,128)} %param.23) | copy-start | bytes 580
  9.0 11.0 %slice-start = ((bf16[768,304]{0,1:T(8,128)(2,1)}), bf16[768,256]{0,1:T(8,128)(2,1)S(1)}, s32[]{:S(2)}) async-start(bf16[768,304]{0,1:T(8,128)(2,1)} %param.20), calls=%async_computation | async-start | bytes 786432 | tf_op jit(solution)/shard_map/slice | solution.py:695
  18.7 2.2 copy-start.11
  21.6 0.6 copy-start.14
  22.2 18.9 %copy-start.12 = (f32[24]{0:T(128)S(1)}, f32[24]{0:T(128)}, u32[]{:S(2)}) copy-start(f32[24]{0:T(128)} %param.24) | copy-start | bytes 292
  22.2 19.7 %copy-start.9 = (f32[1536]{0:T(1024)S(1)}, f32[1536]{0:T(1024)}, u32[]{:S(2)}) copy-start(f32[1536]{0:T(1024)} %param.25) | copy-start | bytes 18436
  41.1 14.6 %collective-permute-start.1 = (bf16[64,1536]{1,0:T(8,128)(2,1)}, bf16[64,1536]{1,0:T(8,128)(2,1)S(1)}, u32[]{:S(2)}, u32[]{:S(2)}) collective-permute-start(bf16[64,1536]{1,0:T(8,128)(2,1)} %get-tuple-element.55), channel_id=1, source_target_pairs={{0,16},{16,0},{1,17},{17,1},{2,18},{18,2},{3,19},{19,3},{4,20},{20... | collective-permute-start | bytes 589832 | tf_op jit(solution)/shard_map/ppermute | solution.py:770
  55.6 0.7 copy-start.5
  82.2 6.6 %collective-permute-start.2 = (bf16[64,1536]{1,0:T(8,128)(2,1)}, bf16[64,1536]{1,0:T(8,128)(2,1)S(1)}, u32[]{:S(2)}, u32[]{:S(2)}) collective-permute-start(bf16[64,1536]{1,0:T(8,128)(2,1)} %get-tuple-element.67), channel_id=1, source_target_pairs={{0,16},{16,0},{1,17},{17,1},{2,18},{18,2},{3,19},{19,3},{4,20},{20... | collective-permute-start | bytes 589832 | tf_op jit(solution)/shard_map/ppermute | solution.py:860
  88.9 0.7 copy-start.4
  89.5 42.8 %copy-start.3 = (bf16[1024,768]{1,0:T(8,128)(2,1)S(1)}, bf16[1024,768]{1,0:T(8,128)(2,1)}, u32[]{:S(2)}) copy-start(bf16[1024,768]{1,0:T(8,128)(2,1)} %get-tuple-element.48.normed_ref) | copy-start | bytes 4718596
  130.2 3.4 %copy-start.8 = (f32[48,1]{1,0:T(8,128)S(1)}, f32[48,1]{1,0:T(8,128)}, u32[]{:S(2)}) copy-start(f32[48,1]{1,0:T(8,128)} %get-tuple-element.80) | copy-start | bytes 580
  130.2 3.5 %copy-start.7 = (f32[48,1]{1,0:T(8,128)S(1)}, f32[48,1]{1,0:T(8,128)}, u32[]{:S(2)}) copy-start(f32[48,1]{1,0:T(8,128)} %get-tuple-element.81) | copy-start | bytes 580
  131.1 6.1 %collective-permute-start.3 = (bf16[16,1792]{1,0:T(8,128)(2,1)S(1)}, bf16[16,1792]{1,0:T(8,128)(2,1)S(1)}, u32[]{:S(2)}, u32[]{:S(2)}) collective-permute-start(bf16[16,1792]{1,0:T(8,128)(2,1)S(1)} %slice.43), channel_id=1, source_target_pairs={{16,0},{17,1},{18,2},{19,3},{20,4},{21,5},{22,6},{23,7},{24,8},{25... | collective-permute-start | bytes 172040 | tf_op jit(solution)/shard_map/ppermute | solution.py:946
  137.1 0.6 copy-start.13
  155.8 12.4 %copy-start.6 = (f32[4,1792]{1,0:T(4,128)S(1)}, f32[4,1792]{1,0:T(4,128)}, u32[]{:S(2)}) copy-start(f32[4,1792]{1,0:T(4,128)} %get-tuple-element.79) | copy-start | bytes 86020
  168.3 1.7 collective-permute-start.24
  169.5 13.7 %collective-permute-start.14 = (bf16[8,48,304]{2,1,0:T(8,128)(2,1)S(1)}, bf16[8,48,304]{2,1,0:T(8,128)(2,1)S(1)}, u32[]{:S(2)}, u32[]{:S(2)}) collective-permute-start(bf16[8,48,304]{2,1,0:T(8,128)(2,1)S(1)} %dynamic-slice_bitcast_fusion.3), channel_id=1, source_target_pairs={{0,1},{1,0},{2,3},{3,2},{4,5},{5,4},{6,7},{7,6},{8,9},{9,8},{10,11... | collective-permute-start | bytes 700424 | tf_op jit(solution)/shard_map/ppermute | solution.py:644
  170.0 11.5 %collective-permute-start.25 = (f32[9592]{0:T(1024)S(1)}, f32[9592]{0:T(1024)S(1)}, u32[]{:S(2)}, u32[]{:S(2)}) collective-permute-start(f32[9592]{0:T(1024)S(1)} %add.200), channel_id=1, source_target_pairs={{0,2},{1,3},{2,0},{3,1},{4,6},{5,7},{6,4},{7,5},{8,10},{9,11},{10,... | collective-permute-start | bytes 115112 | tf_op jit(solution)/shard_map/ppermute | solution.py:655
  181.5 4.9 %collective-permute-start.26 = (f32[9592]{0:T(1024)S(1)}, f32[9592]{0:T(1024)S(1)}, u32[]{:S(2)}, u32[]{:S(2)}) collective-permute-start(f32[9592]{0:T(1024)S(1)} %add.201), channel_id=1, source_target_pairs={{0,4},{1,5},{2,6},{3,7},{4,0},{5,1},{6,2},{7,3},{8,12},{9,13},{10,... | collective-permute-start | bytes 115112 | tf_op jit(solution)/shard_map/ppermute | solution.py:655
  183.3 5.8 %collective-permute-start.15 = (bf16[4,48,304]{2,1,0:T(8,128)(2,1)S(1)}, bf16[4,48,304]{2,1,0:T(8,128)(2,1)S(1)}, u32[]{:S(2)}, u32[]{:S(2)}) collective-permute-start(bf16[4,48,304]{2,1,0:T(8,128)(2,1)S(1)} %fusion.8), channel_id=1, source_target_pairs={{0,2},{1,3},{2,0},{3,1},{4,6},{5,7},{6,4},{7,5},{8,10},{9,11},{10,... | collective-permute-start | bytes 350216 | tf_op jit(solution)/shard_map/ppermute | solution.py:644
  183.8 6.1 %copy-start.1 = (bf16[768,1536]{1,0:T(8,128)(2,1)S(1)}, bf16[768,1536]{1,0:T(8,128)(2,1)}, u32[]{:S(2)}) copy-start(bf16[768,1536]{1,0:T(8,128)(2,1)} %get-tuple-element.76) | copy-start | bytes 7077892
  186.4 20.3 %collective-permute-start.19 = (bf16[8,96,768]{2,1,0:T(8,128)(2,1)}, bf16[8,96,768]{2,1,0:T(8,128)(2,1)S(1)}, u32[]{:S(2)}, u32[]{:S(2)}) collective-permute-start(bf16[8,96,768]{2,1,0:T(8,128)(2,1)} %dynamic-slice_bitcast_fusion), channel_id=1, source_target_pairs={{0,1},{1,0},{2,3},{3,2},{4,5},{5,4},{6,7},{7,6},{8,9},{9,8},{10,11... | collective-permute-start | bytes 3538952 | tf_op jit(solution)/shard_map/ppermute | solution.py:644
  186.4 4.6 %copy-start = (bf16[768,1792]{1,0:T(8,128)(2,1)S(1)}, bf16[768,1792]{1,0:T(8,128)(2,1)}, u32[]{:S(2)}) copy-start(bf16[768,1792]{1,0:T(8,128)(2,1)} %get-tuple-element.74) | copy-start | bytes 8257540
  186.4 5.7 %collective-permute-start.27 = (f32[9592]{0:T(1024)S(1)}, f32[9592]{0:T(1024)S(1)}, u32[]{:S(2)}, u32[]{:S(2)}) collective-permute-start(f32[9592]{0:T(1024)S(1)} %add.202), channel_id=1, source_target_pairs={{0,8},{1,9},{2,10},{3,11},{4,12},{5,13},{6,14},{7,15},{8,0},{9,1},... | collective-permute-start | bytes 115112 | tf_op jit(solution)/shard_map/ppermute | solution.py:655
  189.2 4.6 %collective-permute-start.16 = (bf16[2,48,304]{2,1,0:T(8,128)(2,1)S(1)}, bf16[2,48,304]{2,1,0:T(8,128)(2,1)S(1)}, u32[]{:S(2)}, u32[]{:S(2)}) collective-permute-start(bf16[2,48,304]{2,1,0:T(8,128)(2,1)S(1)} %fusion.10), channel_id=1, source_target_pairs={{0,4},{1,5},{2,6},{3,7},{4,0},{5,1},{6,2},{7,3},{8,12},{9,13},{10,... | collective-permute-start | bytes 175112 | tf_op jit(solution)/shard_map/ppermute | solution.py:644
  191.1 19.0 %collective-permute-start.9 = (bf16[8,48,1536]{2,1,0:T(8,128)(2,1)}, bf16[8,48,1536]{2,1,0:T(8,128)(2,1)}, u32[]{:S(2)}, u32[]{:S(2)}) collective-permute-start(bf16[8,48,1536]{2,1,0:T(8,128)(2,1)} %dynamic-slice_bitcast_fusion.1), channel_id=1, source_target_pairs={{0,1},{1,0},{2,3},{3,2},{4,5},{5,4},{6,7},{7,6},{8,9},{9,8},{10,11... | collective-permute-start | bytes 3538952 | tf_op jit(solution)/shard_map/ppermute | solution.py:644
  192.2 4.7 %collective-permute-start.28 = (f32[9592]{0:T(1024)S(1)}, f32[9592]{0:T(1024)S(1)}, u32[]{:S(2)}, u32[]{:S(2)}) collective-permute-start(f32[9592]{0:T(1024)S(1)} %add.203), channel_id=1, source_target_pairs={{0,16},{16,0},{1,17},{17,1},{2,18},{18,2},{3,19},{19,3},{4,20},{20... | collective-permute-start | bytes 115112 | tf_op jit(solution)/shard_map/ppermute | solution.py:657
  193.8 4.9 %collective-permute-start.17 = (bf16[1,48,304]{2,1,0:T(8,128)(2,1)S(1)}, bf16[1,48,304]{2,1,0:T(8,128)(2,1)S(1)}, u32[]{:S(2)}, u32[]{:S(2)}) collective-permute-start(bf16[1,48,304]{2,1,0:T(8,128)(2,1)S(1)} %dynamic-slice_convert_fusion.11), channel_id=1, source_target_pairs={{0,8},{1,9},{2,10},{3,11},{4,12},{5,13},{6,14},{7,15},{8,0},{9,1},... | collective-permute-start | bytes 87560 | tf_op jit(solution)/shard_map/ppermute | solution.py:644
  196.9 15.4 %collective-permute-start.4 = (bf16[8,48,1536]{2,1,0:T(8,128)(2,1)}, bf16[8,48,1536]{2,1,0:T(8,128)(2,1)}, u32[]{:S(2)}, u32[]{:S(2)}) collective-permute-start(bf16[8,48,1536]{2,1,0:T(8,128)(2,1)} %dynamic-slice_bitcast_fusion.2), channel_id=1, source_target_pairs={{0,1},{1,0},{2,3},{3,2},{4,5},{5,4},{6,7},{7,6},{8,9},{9,8},{10,11... | collective-permute-start | bytes 3538952 | tf_op jit(solution)/shard_map/ppermute | solution.py:644
  199.3 6.0 %collective-permute-start.18 = (bf16[48,304]{1,0:T(8,128)(2,1)}, bf16[48,304]{1,0:T(8,128)(2,1)}, u32[]{:S(2)}, u32[]{:S(2)}) collective-permute-start(bf16[48,304]{1,0:T(8,128)(2,1)} %fusion.11), channel_id=1, source_target_pairs={{0,16},{16,0},{1,17},{17,1},{2,18},{18,2},{3,19},{19,3},{4,20},{20... | collective-permute-start | bytes 87560 | tf_op jit(solution)/shard_map/ppermute | solution.py:648
  206.7 3.3 %copy-start.2 = (bf16[768,1536]{1,0:T(8,128)(2,1)S(1)}, bf16[768,1536]{1,0:T(8,128)(2,1)}, u32[]{:S(2)}) copy-start(bf16[768,1536]{1,0:T(8,128)(2,1)} %get-tuple-element.76) | copy-start | bytes 7077892
  208.5 16.3 %collective-permute-start.20 = (bf16[4,96,768]{2,1,0:T(8,128)(2,1)S(1)}, bf16[4,96,768]{2,1,0:T(8,128)(2,1)S(1)}, u32[]{:S(2)}, u32[]{:S(2)}) collective-permute-start(bf16[4,96,768]{2,1,0:T(8,128)(2,1)S(1)} %fusion.2), channel_id=1, source_target_pairs={{0,2},{1,3},{2,0},{3,1},{4,6},{5,7},{6,4},{7,5},{8,10},{9,11},{10,... | collective-permute-start | bytes 1769480 | tf_op jit(solution)/shard_map/ppermute | solution.py:644
  211.7 25.7 %collective-permute-start.10 = (bf16[4,48,1536]{2,1,0:T(8,128)(2,1)S(1)}, bf16[4,48,1536]{2,1,0:T(8,128)(2,1)S(1)}, u32[]{:S(2)}, u32[]{:S(2)}) collective-permute-start(bf16[4,48,1536]{2,1,0:T(8,128)(2,1)S(1)} %fusion.1), channel_id=1, source_target_pairs={{0,2},{1,3},{2,0},{3,1},{4,6},{5,7},{6,4},{7,5},{8,10},{9,11},{10,... | collective-permute-start | bytes 1769480 | tf_op jit(solution)/shard_map/ppermute | solution.py:644
  214.0 33.5 %collective-permute-start.5 = (bf16[4,48,1536]{2,1,0:T(8,128)(2,1)S(1)}, bf16[4,48,1536]{2,1,0:T(8,128)(2,1)S(1)}, u32[]{:S(2)}, u32[]{:S(2)}) collective-permute-start(bf16[4,48,1536]{2,1,0:T(8,128)(2,1)S(1)} %fusion), channel_id=1, source_target_pairs={{0,2},{1,3},{2,0},{3,1},{4,6},{5,7},{6,4},{7,5},{8,10},{9,11},{10,... | collective-permute-start | bytes 1769480 | tf_op jit(solution)/shard_map/ppermute | solution.py:644
  225.0 23.8 %collective-permute-start.21 = (bf16[2,96,768]{2,1,0:T(8,128)(2,1)S(1)}, bf16[2,96,768]{2,1,0:T(8,128)(2,1)S(1)}, u32[]{:S(2)}, u32[]{:S(2)}) collective-permute-start(bf16[2,96,768]{2,1,0:T(8,128)(2,1)S(1)} %fusion.5), channel_id=1, source_target_pairs={{0,4},{1,5},{2,6},{3,7},{4,0},{5,1},{6,2},{7,3},{8,12},{9,13},{10,... | collective-permute-start | bytes 884744 | tf_op jit(solution)/shard_map/ppermute | solution.py:644
  237.6 13.1 %collective-permute-start.11 = (bf16[2,48,1536]{2,1,0:T(8,128)(2,1)S(1)}, bf16[2,48,1536]{2,1,0:T(8,128)(2,1)S(1)}, u32[]{:S(2)}, u32[]{:S(2)}) collective-permute-start(bf16[2,48,1536]{2,1,0:T(8,128)(2,1)S(1)} %fusion.4), channel_id=1, source_target_pairs={{0,4},{1,5},{2,6},{3,7},{4,0},{5,1},{6,2},{7,3},{8,12},{9,13},{10,... | collective-permute-start | bytes 884744 | tf_op jit(solution)/shard_map/ppermute | solution.py:644
  247.7 17.2 %collective-permute-start.6 = (bf16[2,48,1536]{2,1,0:T(8,128)(2,1)S(1)}, bf16[2,48,1536]{2,1,0:T(8,128)(2,1)S(1)}, u32[]{:S(2)}, u32[]{:S(2)}) collective-permute-start(bf16[2,48,1536]{2,1,0:T(8,128)(2,1)S(1)} %fusion.3), channel_id=1, source_target_pairs={{0,4},{1,5},{2,6},{3,7},{4,0},{5,1},{6,2},{7,3},{8,12},{9,13},{10,... | collective-permute-start | bytes 884744 | tf_op jit(solution)/shard_map/ppermute | solution.py:644
  248.8 12.7 %collective-permute-start.22 = (bf16[1,96,768]{2,1,0:T(8,128)(2,1)S(1)}, bf16[1,96,768]{2,1,0:T(8,128)(2,1)S(1)}, u32[]{:S(2)}, u32[]{:S(2)}) collective-permute-start(bf16[1,96,768]{2,1,0:T(8,128)(2,1)S(1)} %dynamic-slice_convert_fusion.6), channel_id=1, source_target_pairs={{0,8},{1,9},{2,10},{3,11},{4,12},{5,13},{6,14},{7,15},{8,0},{9,1},... | collective-permute-start | bytes 442376 | tf_op jit(solution)/shard_map/ppermute | solution.py:644
  250.8 13.9 %collective-permute-start.12 = (bf16[1,48,1536]{2,1,0:T(8,128)(2,1)S(1)}, bf16[1,48,1536]{2,1,0:T(8,128)(2,1)S(1)}, u32[]{:S(2)}, u32[]{:S(2)}) collective-permute-start(bf16[1,48,1536]{2,1,0:T(8,128)(2,1)S(1)} %dynamic-slice_convert_fusion.8), channel_id=1, source_target_pairs={{0,8},{1,9},{2,10},{3,11},{4,12},{5,13},{6,14},{7,15},{8,0},{9,1},... | collective-permute-start | bytes 442376 | tf_op jit(solution)/shard_map/ppermute | solution.py:644
  261.6 11.6 %collective-permute-start.23 = (bf16[96,768]{1,0:T(8,128)(2,1)S(1)}, bf16[96,768]{1,0:T(8,128)(2,1)S(1)}, u32[]{:S(2)}, u32[]{:S(2)}) collective-permute-start(bf16[96,768]{1,0:T(8,128)(2,1)S(1)} %fusion.9), channel_id=1, source_target_pairs={{0,16},{16,0},{1,17},{17,1},{2,18},{18,2},{3,19},{19,3},{4,20},{20... | collective-permute-start | bytes 442376 | tf_op jit(solution)/shard_map/ppermute | solution.py:648
  264.8 5.2 %collective-permute-start.13 = (bf16[48,1536]{1,0:T(8,128)(2,1)S(1)}, bf16[48,1536]{1,0:T(8,128)(2,1)S(1)}, u32[]{:S(2)}, u32[]{:S(2)}) collective-permute-start(bf16[48,1536]{1,0:T(8,128)(2,1)S(1)} %fusion.7), channel_id=1, source_target_pairs={{0,16},{16,0},{1,17},{17,1},{2,18},{18,2},{3,19},{19,3},{4,20},{20... | collective-permute-start | bytes 442376 | tf_op jit(solution)/shard_map/ppermute | solution.py:648
  264.9 6.2 %collective-permute-start.7 = (bf16[1,48,1536]{2,1,0:T(8,128)(2,1)S(1)}, bf16[1,48,1536]{2,1,0:T(8,128)(2,1)S(1)}, u32[]{:S(2)}, u32[]{:S(2)}) collective-permute-start(bf16[1,48,1536]{2,1,0:T(8,128)(2,1)S(1)} %dynamic-slice_convert_fusion.9), channel_id=1, source_target_pairs={{0,8},{1,9},{2,10},{3,11},{4,12},{5,13},{6,14},{7,15},{8,0},{9,1},... | collective-permute-start | bytes 442376 | tf_op jit(solution)/shard_map/ppermute | solution.py:644
  271.2 5.2 %collective-permute-start.8 = (bf16[48,1536]{1,0:T(8,128)(2,1)S(1)}, bf16[48,1536]{1,0:T(8,128)(2,1)S(1)}, u32[]{:S(2)}, u32[]{:S(2)}) collective-permute-start(bf16[48,1536]{1,0:T(8,128)(2,1)S(1)} %fusion.6), channel_id=1, source_target_pairs={{0,16},{16,0},{1,17},{17,1},{2,18},{18,2},{3,19},{19,3},{4,20},{20... | collective-permute-start | bytes 442376 | tf_op jit(solution)/shard_map/ppermute | solution.py:648
where the time goes:
time: 278 us; the launch traced here: 277 us
  Pallas kernels  148 us (53%)
  waiting for transfers between devices  61.9 us (22%)
  starting transfers between devices  29.4 us (11%)
  local copies, waits for them, and re-layouts  22.7 us (8%)
  other arithmetic  13 us (5%)
    pallas_call x8, Pallas kernels, call(): pl.pallas_call(kernel, name=name, grid=(grid,), in_specs=in_specs, out_sp...  148 us
    ppermute x16, waiting for transfers between devices, sum_shards(): got = lax.ppermute(sent, 'dp', [(i, i ^ bit) for i in range(dp_count)])  47.5 us
    ppermute x16, starting transfers between devices, sum_shards(): got = lax.ppermute(sent, 'dp', [(i, i ^ bit) for i in range(dp_count)])  12.4 us
    ppermute x4, waiting for transfers between devices, sum_shards(): got = lax.ppermute(held, 'dir', [(0, 1), (1, 0)])  7.47 us
    ppermute x4, starting transfers between devices, sum_all(): lax.ppermute(values, 'dp', [(i, i ^ bit) for i in range(dp_count)])  5.89 us
  transfers between devices with their start and end apart: 29, of which 13 were waited for; matrix products, arithmetic and copies ran while one was open for 11% of the time, Pallas kernels for 12%

commit v1 on v0

v1 whole, which is shorter than its diff:
```python
import functools

import jax
import jax.numpy as jnp
import numpy as np
from jax import lax
from jax.experimental import pallas as pl
from jax.experimental.pallas import tpu as pltpu
from jax.sharding import PartitionSpec as P

F32 = jnp.float32
BF16 = jnp.bfloat16
CHUNK = 128
ROWS = 256
SUB = 64
EPS = 1e-05
LOG2E = 1.4426950408889634
SWAP = [(0, 1), (1, 0)]
MIB = 1024 * 1024
VMEM_GATES = 18
VMEM_PROJ = 20
VMEM_INTRA = 12
VMEM_MIX = 28
VMEM_WEIGHTS = 16
VMEM_BACK = 20
VMEM_CONV = 20
VMEM_INPUTS = 20
VMEM_SUMS = 8
NT = (((1,), (1,)), ((), ()))
TN = (((0,), (0,)), ((), ()))
EXACT = lax.Precision.HIGHEST


def mm(left, right):
    return jnp.dot(left, right, preferred_element_type=F32)


def mm_nt(left, right):
    return lax.dot_general(left, right, NT, preferred_element_type=F32)


def mm_tn(left, right):
    return lax.dot_general(left, right, TN, preferred_element_type=F32)


def exact_mm(left, right):
    return jnp.dot(left, right, precision=EXACT, preferred_element_type=F32)


def sequence_bounds(lengths_ref, half_rows):
    bounds, total = [], 0
    for position in range(lengths_ref.shape[1]):
        total = total + lengths_ref[0, position]
        bounds.append(total)
    return bounds, lax.axis_index("dir") * half_rows


def start_of(row, bounds):
    start = jnp.where(row < 0, -1, 0)
    for bound in bounds:
        start = jnp.where(row >= bound, bound, start)
    return start


def row_iota(count):
    return lax.broadcasted_iota(jnp.int32, (count, 1), 0)


def lane_iota(count):
    return lax.broadcasted_iota(jnp.int32, (1, count), 1)


def flag(condition):
    return jnp.where(condition, 1.0, 0.0)


def in_parts(values, parts):
    out = []
    for _ in range(parts):
        part = values.astype(BF16).astype(F32)
        out.append(part)
        values = values - part
    return jnp.concatenate(out, axis=0)


def fold(values):
    return jnp.sum(values.reshape(values.shape[0] // 8, 8, values.shape[1]), axis=0)


def row_of(ref):
    return ref[...].reshape(1, ref.shape[0])


def column_of(ref, steps):
    heads = steps // 2
    place = row_iota(steps)
    column = jnp.zeros((steps, 1), F32)
    for step in range(steps):
        column = jnp.where(place == step, ref[step // heads, step % heads], column)
    return column


def gates_kernel(
    lengths_ref,
    bias_ref,
    alog_ref,
    x_ref,
    c_ref,
    gain_ref,
    wz_ref,
    wo_ref,
    wbc_ref,
    e0_ref,
    e1_ref,
    normed_ref,
    turned_ref,
    z_ref,
    dnorm_ref,
    raw_ref,
    dt_ref,
    rate_ref,
    target_ref,
    source_ref,
    factors_ref,
    keeps_ref,
):
    step = pl.program_id(0)
    model = x_ref.shape[1]
    steps = raw_ref.shape[0]
    heads = steps // 2
    count = raw_ref.shape[1]
    x = x_ref[...].astype(F32)
    inv = lax.rsqrt(jnp.mean(x * x, axis=1, keepdims=True) + EPS)
    normed = (x * inv * row_of(gain_ref)).astype(BF16)
    normed_ref[...] = normed
    turned_ref[...] = normed.T
    z_ref[...] = mm(normed, wz_ref[...]).astype(BF16)
    dnorm_ref[...] = mm_nt(c_ref[...], wo_ref[...]).astype(BF16)
    raw = mm(normed, wbc_ref[:, wbc_ref.shape[1] - steps :]).astype(BF16).astype(F32).T
    raw_ref[:, pl.ds(pl.multiple_of(step * ROWS, ROWS), ROWS)] = raw

    @pl.when(step == pl.num_programs(0) - 1)
    def _():
        bounds, base = sequence_bounds(lengths_ref, count)
        rate = jnp.exp(column_of(alog_ref, steps))
        rate_ref[...] = jnp.broadcast_to(rate, (steps, 128))
        raw = raw_ref[...] + column_of(bias_ref, steps)
        raw_ref[...] = raw
        dt = jnp.maximum(raw, 0.0) + jnp.log1p(jnp.exp(-jnp.abs(raw)))
        dt_ref[...] = dt
        log_dt = jnp.log(jnp.maximum(dt, 1e-37))
        chunks = count // CHUNK
        upto = flag(row_iota(CHUNK) <= lane_iota(CHUNK))
        fall = dt * rate
        stacked = [fall[:, chunk * CHUNK : (chunk + 1) * CHUNK] for chunk in range(chunks)]
        summed = exact_mm(jnp.concatenate(stacked, axis=0), upto)
        lane = lane_iota(CHUNK)
        keeps = jnp.zeros((steps, CHUNK), F32)
        for chunk in range(chunks):
            span = slice(chunk * CHUNK, (chunk + 1) * CHUNK)
            first = base + chunk * CHUNK
            inc = summed[chunk * steps : (chunk + 1) * steps]
            dt_c, log_c = dt[:, span], log_dt[:, span]
            inc0 = inc[:heads]
            exc1 = inc[heads:] - fall[heads:, span]
            total0 = inc0[:, CHUNK - 1 :]
            total1 = inc[heads:, CHUNK - 1 :]
            target = jnp.concatenate([-inc0, exc1], axis=0) * LOG2E
            source = jnp.concatenate([inc0 + log_c[:heads], log_c[heads:] - exc1], axis=0) * LOG2E
            target_ref[:, span] = target
            source_ref[:, span] = source
            starts = start_of(first + lane, bounds)
            before = start_of(first - 1, bounds)
            left = start_of(first, bounds)
            right = start_of(first + CHUNK - 1, bounds)
            after = start_of(first + CHUNK, bounds)
            enter0 = jnp.where(starts == before, jnp.exp(-inc0), 0.0)
            enter1 = jnp.where(starts == after, jnp.exp(exc1 - total1), 0.0)
            leave0 = jnp.where(starts == right, dt_c[:heads] * jnp.exp(inc0 - total0), 0.0)
            leave1 = jnp.where(starts == left, dt_c[heads:] * jnp.exp(-exc1), 0.0)
            enter = jnp.concatenate([enter0, enter1], axis=0)
            leave = jnp.concatenate([leave0, leave1], axis=0)
            factors_ref[0, span, :] = in_parts(enter, 2).T.astype(BF16)
            factors_ref[1, span, :] = in_parts(leave, 2).T.astype(BF16)
            keep0 = jnp.where(before == right, jnp.exp(-total0), 0.0)
            keep1 = jnp.where(after == left, jnp.exp(-total1), 0.0)
            keeps = jnp.where(lane == chunk, jnp.concatenate([keep0, keep1], axis=0), keeps)
        ahead = jnp.zeros_like(keeps)
        behind = jnp.zeros_like(keeps)
        run_a = jnp.ones((steps, 1), F32)
        run_b = jnp.ones((steps, 1), F32)
        for chunk in range(chunks):
            ahead = jnp.where(lane == chunk, run_a, ahead)
            run_a = run_a * keeps[:, chunk : chunk + 1]
            last = chunks - 1 - chunk
            behind = jnp.where(lane == last, run_b, behind)
            run_b = run_b * keeps[:, last : last + 1]
        for place, values in enumerate((keeps, ahead, behind)):
            columns = in_parts(values, 2).T.astype(BF16)[0:16]
            keeps_ref[2 * place] = mm(columns, e0_ref[...])[0:chunks]
            keeps_ref[2 * place + 1] = mm(columns, e1_ref[...])[0:chunks]


def shifts(places, sign, height):
    row = lax.broadcasted_iota(jnp.int32, (height, 2 * CHUNK), 0)
    col = lax.broadcasted_iota(jnp.int32, (height, 2 * CHUNK), 1)
    parts = []
    for lag in (1, 2, 3):
        wanted = {-1: row + CHUNK - lag, 1: row + lag, 0: row - height + lag}[sign]
        parts.append(flag((col == wanted) & (places[lag - 1] >= lag)))
    return jnp.concatenate(parts, axis=0).astype(BF16)


def proj_kernel(
    lengths_ref,
    normed_ref,
    halo_ref,
    gain_ref,
    wx_ref,
    wbc_ref,
    taps_ref,
    factors_ref,
    keeps_ref,
    e0_ref,
    e1_ref,
    pre_ref,
    act_ref,
    slope_ref,
    s0_ref,
    sf1_ref,
    send_ref,
    prehalo_ref,
    turnhalo_ref,
    buf,
    acc0,
    acc1,
    left0,
    left1,
):
    step = pl.program_id(0)
    per = ROWS // CHUNK
    bounds, base = sequence_bounds(lengths_ref, pl.num_programs(0) * ROWS)
    inner = wx_ref.shape[1]
    channels = taps_ref.shape[1]
    state = (channels - inner) // 4

    @pl.when(step == 0)
    def _():
        x = halo_ref[...].astype(F32)
        inv = lax.rsqrt(jnp.mean(x * x, axis=1, keepdims=True) + EPS)
        normed = x * inv * row_of(gain_ref)
        turnhalo_ref[...] = normed.T.astype(BF16)
        normed = normed.astype(BF16)
        buf[0 : CHUNK - 16, :] = jnp.zeros((CHUNK - 16, channels), BF16)
        prehalo_ref[:, 0:inner] = mm(normed, wx_ref[...]).astype(BF16)
        prehalo_ref[:, inner:channels] = mm(normed, wbc_ref[:, 0 : channels - inner]).astype(BF16)
        buf[CHUNK - 16 : CHUNK, :] = prehalo_ref[...]
        acc0[...] = jnp.zeros_like(acc0)
        acc1[...] = jnp.zeros_like(acc1)

    @pl.when(step > 0)
    def _():
        buf[CHUNK - 16 : CHUNK, :] = buf[ROWS + CHUNK - 16 : ROWS + CHUNK, :]

    normed = normed_ref[...]
    for tile in range(inner // 256):
        cols = slice(tile * 256, tile * 256 + 256)
        px = mm(normed, wx_ref[:, cols]).astype(BF16)
        pre_ref[:, cols] = px
        buf[CHUNK : CHUNK + ROWS, cols] = px
    pb = mm(normed, wbc_ref[:, 0 : channels - inner]).astype(BF16)
    pre_ref[:, inner:channels] = pb
    buf[CHUNK : CHUNK + ROWS, inner:channels] = pb

    first = base + step * ROWS
    for part in range(per):
        offset = part * CHUNK
        rows = first + offset + row_iota(CHUNK)
        place = rows - start_of(rows, bounds)
        shift = shifts([place] * 3, -1, CHUNK)
        leave_cols = factors_ref[0, offset : offset + CHUNK, :]
        for tile in range(channels // 256):
            wide = slice(tile * 256, tile * 256 + 256)
            moved = mm(shift, buf[offset : offset + 2 * CHUNK, wide])
            if tile * 256 < inner:
                leave0 = mm(leave_cols, e0_ref[:, wide])
                leave1 = mm(leave_cols, e1_ref[:, wide])
            for column in (0, 128):
                cols = slice(tile * 256 + column, tile * 256 + column + 128)
                cut = slice(column, column + 128)
                for row in range(0, CHUNK, SUB):
                    here = buf[offset + CHUNK + row : offset + CHUNK + row + SUB, cols]
                    conv = here.astype(F32) * taps_ref[3:4, cols]
                    for lag in (1, 2, 3):
                        at = (lag - 1) * CHUNK + row
                        conv = conv + moved[at : at + SUB, cut] * taps_ref[3 - lag : 4 - lag, cols]
                    sig = jax.nn.sigmoid(conv)
                    act = conv * sig
                    span = slice(offset + row, offset + row + SUB)
                    act_ref[span, cols] = act.astype(BF16)
                    slope_ref[span, cols] = (sig + act - act * sig).astype(BF16)
                    if tile * 256 < inner:
                        held = slice(row, row + SUB)
                        left0[held, cols] = (act * leave0[held, cut]).astype(BF16)
                        left1[held, cols] = (act * leave1[held, cut]).astype(BF16)
        turned = act_ref[offset : offset + CHUNK, inner:channels].astype(F32).T.astype(BF16)
        s0_ref[part] = acc0[...].astype(BF16)
        chunk = pl.ds(step * per + part, 1)
        acc0[...] = keeps_ref[0, chunk, :] * acc0[...] + mm(turned[0:state], left0[...])
        fresh1 = mm(turned[2 * state : 3 * state], left1[...])
        sf1_ref[part] = fresh1.astype(BF16)
        acc1[...] = acc1[...] + keeps_ref[3, chunk, :] * fresh1

    @pl.when(step == pl.num_programs(0) - 1)
    def _():
        send_ref[...] = jnp.where(base > 0, acc1[...], acc0[...]).astype(BF16)


def bc_columns(act_ref, inner, state):
    return [act_ref[:, inner + part * state : inner + (part + 1) * state] for part in range(4)]


def cut_pair(values, width):
    zero = jnp.zeros_like(values)
    first = lane_iota(2 * width) < width
    return jnp.concatenate([jnp.where(first, values, zero), jnp.where(first, zero, values)], axis=0)


def intra_kernel(lengths_ref, act_ref, target_ref, source_ref, y_ref, *, heads, state):
    bounds, base = sequence_bounds(lengths_ref, pl.num_programs(0) * CHUNK)
    first = base + pl.program_id(0) * CHUNK
    inner = y_ref.shape[1]
    width = inner // heads
    t, s = row_iota(CHUNK), lane_iota(CHUNK)
    lower = t > s
    same = (start_of(first + t, bounds) == start_of(first + s, bounds)) & (t != s)
    b0, c0, b1, c1 = bc_columns(act_ref, inner, state)
    scores = jnp.where(lower, mm_nt(c0, b0), mm_nt(c1, b1))
    scores = jnp.where(same, scores, 0.0)
    columns = target_ref[...].T
    for pair in range(heads // 2):
        cols = slice(pair * 2 * width, (pair + 1) * 2 * width)
        weights = []
        for head in (2 * pair, 2 * pair + 1):
            power = jnp.where(
                lower,
                columns[:, head : head + 1] + source_ref[head : head + 1, :],
                columns[:, heads + head : heads + head + 1]
                + source_ref[heads + head : heads + head + 1, :],
            )
            weights.append((jnp.exp2(power) * scores).astype(BF16))
        x_cut = cut_pair(act_ref[:, cols], width)
        y_ref[:, cols] = mm(jnp.concatenate(weights, axis=1), x_cut).astype(BF16)


def mix_kernel(
    lengths_ref,
    skip_ref,
    x_ref,
    act_ref,
    factors_ref,
    sl0_ref,
    sf1_ref,
    keeps_ref,
    recv_ref,
    yin_ref,
    z_ref,
    dnorm_ref,
    wo_ref,
    gain_ref,
    e0_ref,
    e1_ref,
    out_ref,
    mixed_ref,
    dz_ref,
    dy_ref,
    r_ref,
    dcc_ref,
    dl0_ref,
    df1_ref,
    s0_ref,
    s1_ref,
    send_ref,
    sums_ref,
    carry1,
    acc0,
    acc1,
    enter0,
    enter1,
    from0,
    from1,
    gated_s,
    slope_s,
    gate_s,
    in0,
    in1,
    prod0,
    prod1,
    skip_s,
    gain_s,
):
    step = pl.program_id(0)
    chunk = pl.num_programs(0) - 1 - step
    bounds, base = sequence_bounds(lengths_ref, pl.num_programs(0) * CHUNK)
    first = base + chunk * CHUNK
    inner = gain_ref.shape[0]
    heads = r_ref.shape[0] // 2
    width = inner // heads
    state = recv_ref.shape[0]
    small = 32

    @pl.when(step == 0)
    def _():
        recv = recv_ref[...].astype(F32)
        carry1[...] = jnp.where(base > 0, jnp.zeros_like(recv), recv)
        acc0[...] = jnp.zeros_like(acc0)
        acc1[...] = jnp.zeros_like(acc1)
        sums_ref[...] = jnp.zeros_like(sums_ref)
        gain_s[...] = row_of(gain_ref)
        left = lane_iota(2 * width) < width
        for pair in range(heads // 2):
            skip_s[:, pair * 2 * width : (pair + 1) * 2 * width] = jnp.where(
                left, skip_ref[2 * pair], skip_ref[2 * pair + 1]
            )

    keep0 = keeps_ref[0, pl.ds(chunk, 1), :]
    keep1 = keeps_ref[1, pl.ds(chunk, 1), :]
    ahead0 = keeps_ref[2, pl.ds(chunk, 1), :] * jnp.where(base > 0, 1.0, 0.0)
    s0 = (sl0_ref[0].astype(F32) + ahead0 * recv_ref[...].astype(F32)).astype(BF16)
    s1 = carry1[...].astype(BF16)
    carry1[...] = keep1 * carry1[...] + sf1_ref[0].astype(F32)
    s0_ref[0] = s0
    s1_ref[0] = s1
    enter_cols = factors_ref[0]
    turned = act_ref[:, inner:].astype(F32).T.astype(BF16)
    _, c0, _, c1 = bc_columns(act_ref, inner, state)
    enter0[...] = mm(enter_cols, e0_ref[...])
    from0[...] = mm(c0, s0)
    enter1[...] = mm(enter_cols, e1_ref[...])
    from1[...] = mm(c1, s1)
    tiles = [slice(tile * 128, tile * 128 + 128) for tile in range(inner // 128)]
    for row in range(0, CHUNK, small):
        rows = slice(row, row + small)
        square = jnp.zeros((small, 128), F32)
        cross = jnp.zeros((small, 128), F32)
        for cols in tiles:
            mixer = yin_ref[rows, cols].astype(F32) + skip_s[:, cols] * act_ref[rows, cols].astype(F32)
            mixer = mixer + enter0[rows, cols] * from0[rows, cols]
            mixer = mixer + enter1[rows, cols] * from1[rows, cols]
            z = z_ref[rows, cols].astype(F32)
            sig = jax.nn.sigmoid(z)
            gate = z * sig
            gated = mixer * gate
            square = square + gated * gated
            cross = cross + dnorm_ref[rows, cols].astype(F32) * gain_s[:, cols] * gated
            gated_s[rows, cols] = gated
            gate_s[rows, cols] = gate
            slope_s[rows, cols] = mixer * (sig + gate - gate * sig)
        live = flag(first + row + row_iota(small) < bounds[len(bounds) - 2])
        scale = lax.rsqrt(jnp.sum(square, axis=1, keepdims=True) * (1.0 / inner) + EPS)
        back = scale * scale * (jnp.sum(cross, axis=1, keepdims=True) * (1.0 / inner))
        scale = jnp.broadcast_to(scale * live, (small, 128))
        back = jnp.broadcast_to(back, (small, 128))
        for cols in tiles:
            gated = gated_s[rows, cols]
            unit = gated * scale
            gain = gain_s[:, cols]
            mixed_ref[rows, cols] = (unit * gain).astype(BF16)
            dnorm = dnorm_ref[rows, cols].astype(F32)
            sums_ref[0:8, cols] += fold(dnorm * unit)
            dgated = scale * (dnorm * gain - gated * back)
            dz_ref[rows, cols] = (dgated * slope_s[rows, cols]).astype(BF16)
            dy = dgated * gate_s[rows, cols]
            dy_ref[rows, cols] = dy.astype(BF16)
            sums_ref[8:16, cols] += fold(dy * act_ref[rows, cols].astype(F32))
            entered0 = dy * enter0[rows, cols]
            entered1 = dy * enter1[rows, cols]
            in0[rows, cols] = entered0.astype(BF16)
            in1[rows, cols] = entered1.astype(BF16)
            prod0[rows, cols] = (entered0 * from0[rows, cols]).astype(BF16)
            prod1[rows, cols] = (entered1 * from1[rows, cols]).astype(BF16)
    out_ref[...] = (x_ref[...].astype(F32) + mm(mixed_ref[...], wo_ref[...])).astype(BF16)
    ones = e0_ref[0:heads, :]
    r_ref[0:heads, :] = mm_nt(ones, prod0[...])
    r_ref[heads : 2 * heads, :] = mm_nt(ones, prod1[...])
    dcc_ref[:, 0:state] = mm_nt(in0[...], s0)
    dcc_ref[:, state : 2 * state] = mm_nt(in1[...], s1)
    dl0_ref[0] = acc0[...].astype(BF16)
    acc0[...] = keep0 * acc0[...] + mm(turned[state : 2 * state], in0[...])
    df1 = mm(turned[3 * state : 4 * state], in1[...])
    df1_ref[0] = df1.astype(BF16)
    acc1[...] = acc1[...] + keeps_ref[5, pl.ds(chunk, 1), :] * df1

    @pl.when(step == pl.num_programs(0) - 1)
    def _():
        send_ref[...] = jnp.where(base > 0, acc0[...], acc1[...]).astype(BF16)


def back_kernel(
    lengths_ref,
    skip_ref,
    act_ref,
    slope_ref,
    target_ref,
    source_ref,
    factors_ref,
    dcc_ref,
    dy_ref,
    s0_ref,
    s1_ref,
    dl0_ref,
    df1_ref,
    keeps_ref,
    recv_ref,
    start_ref,
    e0_ref,
    e1_ref,
    spans_ref,
    dpre_ref,
    moves_ref,
    last_ref,
    carry1,
    dscore,
    low_s,
    all_s,
    out0,
    out1,
    prod0,
    prod1,
    ds0,
    ds1,
    *,
    skipped,
    chunks,
):
    step = pl.program_id(0)
    chunk = step + skipped
    bounds, base = sequence_bounds(lengths_ref, chunks * CHUNK)
    first = base + chunk * CHUNK
    heads = skip_ref.shape[0]
    inner = keeps_ref.shape[2]
    width = inner // heads
    state = recv_ref.shape[0]

    @pl.when(step == 0)
    def _():
        if skipped:
            carry1[...] = start_ref[...]
        else:
            recv = recv_ref[...].astype(F32)
            carry1[...] = jnp.where(base > 0, recv, jnp.zeros_like(recv))

    keep0 = keeps_ref[0, pl.ds(chunk, 1), :]
    keep1 = keeps_ref[1, pl.ds(chunk, 1), :]
    behind0 = keeps_ref[4, pl.ds(chunk, 1), :] * jnp.where(base > 0, 0.0, 1.0)
    d0 = dl0_ref[0].astype(F32) + behind0 * recv_ref[...].astype(F32)
    d1 = carry1[...]
    ds0[...] = d0.astype(BF16)
    ds1[...] = d1.astype(BF16)
    kept0 = jnp.sum(d0 * s0_ref[0].astype(F32), axis=0, keepdims=True) * keep0
    kept1 = jnp.sum(d1 * s1_ref[0].astype(F32), axis=0, keepdims=True) * keep1
    carry1[...] = keep1 * d1 + df1_ref[0].astype(F32)
    ones = e0_ref[0:heads, :]
    kept = jnp.concatenate([kept0, kept1, jnp.zeros((6, inner), F32)], axis=0)
    kept_high = kept.astype(BF16)
    kept_low = (kept - kept_high.astype(F32)).astype(BF16)
    kept_sum = mm_nt(ones, kept_high) + mm_nt(ones, kept_low)

    t = lane_iota(CHUNK)
    starts = start_of(first + t, bounds)
    b0, c0, b1, c1 = bc_columns(act_ref, inner, state)
    forward = mm_nt(b0, c0)
    backward = mm_nt(b1, c1)
    halves = []
    for row in range(0, CHUNK, SUB):
        s = row + row_iota(SUB)
        early = s < t
        same = (start_of(first + s, bounds) == starts) & (s != t)
        both = jnp.where(early, forward[row : row + SUB], backward[row : row + SUB])
        halves.append((slice(row, row + SUB), early, flag(early), jnp.where(same, both, 0.0)))
    in_cols = source_ref[...].T
    leave_cols = factors_ref[0]
    dscore[...] = jnp.zeros_like(dscore)
    left = lane_iota(2 * width) < width
    for pair in range(heads // 2):
        cols = slice(pair * 2 * width, (pair + 1) * 2 * width)
        dweights = mm_nt(cut_pair(act_ref[:, cols], width), dy_ref[:, cols])
        weights = []
        for part in (0, 1):
            head = 2 * pair + part
            held = slice(head * CHUNK, (head + 1) * CHUNK)
            parts = []
            sum0 = jnp.zeros((8, CHUNK), F32)
            sum1 = jnp.zeros((8, CHUNK), F32)
            for rows, early, early_f, scores in halves:
                power = jnp.where(
                    early,
                    in_cols[rows, head : head + 1] + target_ref[head : head + 1, :],
                    in_cols[rows, heads + head : heads + head + 1]
                    + target_ref[heads + head : heads + head + 1, :],
                )
                decay = jnp.exp2(power)
                parts.append((decay * scores).astype(BF16))
                at = part * CHUNK + rows.start
                dweight = dweights[at : at + SUB] * decay
                dscore[rows, :] += dweight
                change = dweight * scores
                low = change * early_f
                low_s[rows, held] = low.astype(BF16)
                all_s[rows, held] = change.astype(BF16)
                sum0 = sum0 + fold(low)
                sum1 = sum1 + fold(change)
            weights.append(jnp.concatenate(parts, axis=0))
            moves_ref[head : head + 1, :] = jnp.sum(sum0, axis=0, keepdims=True)
            moves_ref[heads + head : heads + head + 1, :] = jnp.sum(sum1, axis=0, keepdims=True)
        dx = mm(jnp.concatenate(weights, axis=1), cut_pair(dy_ref[:, cols], width))
        leave0 = mm(leave_cols, e0_ref[:, cols])
        leave1 = mm(leave_cols, e1_ref[:, cols])
        from0 = mm(b0, ds0[:, cols])
        from1 = mm(b1, ds1[:, cols])
        skip = jnp.where(left, skip_ref[2 * pair], skip_ref[2 * pair + 1])
        for rows, _, _, _ in halves:
            xf = act_ref[rows, cols].astype(F32)
            came0 = leave0[rows] * from0[rows]
            came1 = leave1[rows] * from1[rows]
            dconv = dx[rows] + skip * dy_ref[rows, cols].astype(F32) + came0 + came1
            dpre_ref[rows, cols] = (dconv * slope_ref[rows, cols].astype(F32)).astype(BF16)
            out0[rows, cols] = (xf * leave0[rows]).astype(BF16)
            out1[rows, cols] = (xf * leave1[rows]).astype(BF16)
            prod0[rows, cols] = (xf * came0).astype(BF16)
            prod1[rows, cols] = (xf * came1).astype(BF16)
    dscore0, dscore1 = [], []
    for rows, early, _, _ in halves:
        s = rows.start + row_iota(SUB)
        same = (start_of(first + s, bounds) == starts) & (s != t)
        both = jnp.where(same, dscore[rows, :], 0.0)
        dscore0.append(jnp.where(early, both, 0.0).astype(BF16))
        dscore1.append(jnp.where(early, 0.0, both).astype(BF16))
    dscore0 = jnp.concatenate(dscore0, axis=0)
    dscore1 = jnp.concatenate(dscore1, axis=0)
    moves_ref[2 * heads : 3 * heads, :] = mm_nt(spans_ref[...], low_s[...])
    moves_ref[3 * heads : 4 * heads, :] = mm_nt(spans_ref[...], all_s[...])
    moves_ref[4 * heads : 5 * heads, :] = mm_nt(ones, prod0[...])
    moves_ref[5 * heads : 6 * heads, :] = mm_nt(ones, prod1[...])
    moves_ref[6 * heads : 7 * heads, :] = jnp.broadcast_to(kept_sum[:, 0:1], (heads, CHUNK))
    moves_ref[7 * heads : 8 * heads, :] = jnp.broadcast_to(kept_sum[:, 1:2], (heads, CHUNK))
    db0 = mm(dscore0, c0) + mm_nt(out0[...], ds0[...])
    db1 = mm(dscore1, c1) + mm_nt(out1[...], ds1[...])
    dc0 = mm_tn(dscore0, b0) + dcc_ref[:, 0:state]
    dc1 = mm_tn(dscore1, b1) + dcc_ref[:, state : 2 * state]
    dbc = jnp.concatenate([db0, dc0, db1, dc1], axis=1)
    dpre_ref[:, inner:] = (dbc * slope_ref[:, inner:].astype(F32)).astype(BF16)

    @pl.when(step == pl.num_programs(0) - 1)
    def _():
        last_ref[...] = carry1[...]


def steps_back(raw, dt, rate, moves, r):
    steps = raw.shape[0]
    heads = steps // 2
    chunks = raw.shape[1] // CHUNK
    s, t = row_iota(CHUNK), lane_iota(CHUNK)

    def stack(values):
        parts = [values[:, chunk * CHUNK : (chunk + 1) * CHUNK] for chunk in range(chunks)]
        return jnp.concatenate(parts, axis=0)

    def unstack(values):
        parts = [values[chunk * heads : (chunk + 1) * heads] for chunk in range(chunks)]
        return jnp.concatenate(parts, axis=1)

    got0, got, own0, own, k0, k1, kept0, kept1 = [
        moves[part * heads : (part + 1) * heads] for part in range(8)
    ]
    own1, got1 = own - own0, got - got0
    da0 = exact_mm(stack(got0 + r[:heads] - own0), flag(s >= t)) + exact_mm(stack(k0), flag(s < t))
    da1 = exact_mm(stack(got1 + r[heads:] - own1), flag(s <= t)) + exact_mm(stack(k1), flag(s > t))
    da = -jnp.concatenate([unstack(da0) + kept0, unstack(da1) + kept1], axis=0)
    dlog = jnp.concatenate([own0 + k0, own1 + k1], axis=0)
    sig = jax.nn.sigmoid(raw)
    ratio = jnp.where(raw < -20.0, 1.0, sig / jnp.maximum(dt, 1e-37))
    return dlog * ratio + da * rate * sig, jnp.sum(da * dt, axis=1, keepdims=True) * rate


def weights_kernel(turned_ref, dz_ref, mixed_ref, c_ref, go_ref, gz_ref, *, half):
    gz_ref[...] = mm(turned_ref[...], dz_ref[...]).astype(BF16)
    product = mm_tn(mixed_ref[...], c_ref[...]).astype(BF16)
    if not half:
        go_ref[...] = product
        return
    model = c_ref.shape[1]
    for shard in range(product.shape[0] // (2 * half)):
        span = slice(shard * half, (shard + 1) * half)
        go_ref[span, 0:model] = product[2 * shard * half : (2 * shard + 1) * half]
        go_ref[span, model : 2 * model] = product[(2 * shard + 1) * half : (2 * shard + 2) * half]


def conv_back_kernel(
    lengths_ref,
    turned_ref,
    turnhalo_ref,
    dpre_ref,
    pre_ref,
    prehalo_ref,
    taps_ref,
    raw_ref,
    dt_ref,
    rate_ref,
    moves_ref,
    r_ref,
    dproj_ref,
    dhalo_ref,
    mine_ref,
    theirs_ref,
    draw_ref,
    sums_ref,
    shift,
    buf,
    *,
    shard,
):
    step = pl.program_id(0)
    count, wide = dpre_ref.shape
    chunks = count // CHUNK
    steps = raw_ref.shape[0]
    bounds, base = sequence_bounds(lengths_ref, count)

    @pl.when(step == 0)
    def _():
        for chunk in range(chunks):
            places = []
            for lag in (1, 2, 3):
                rows = base + chunk * CHUNK + lag + row_iota(CHUNK)
                places.append(rows - start_of(rows, bounds))
            shift[chunk * 3 * CHUNK : (chunk + 1) * 3 * CHUNK, :] = shifts(places, 1, CHUNK)
        places = []
        for lag in (1, 2, 3):
            rows = base + lag - 16 + row_iota(16)
            places.append(rows - start_of(rows, bounds))
        shift[chunks * 3 * CHUNK :, :] = shifts(places, 0, 16)
        buf[...] = jnp.zeros_like(buf)

    def hand_over(product):
        if not shard:
            mine_ref[...] = product
            return
        pieces = [product[place : place + shard] for place in range(0, product.shape[0], shard)]
        even = jnp.concatenate(pieces[0::2], axis=0)
        odd = jnp.concatenate(pieces[1::2], axis=0)
        core = lax.rem(lax.axis_index("dp"), 2)

        @pl.when(core == 0)
        def _():
            mine_ref[...] = even
            theirs_ref[...] = odd

        @pl.when(core == 1)
        def _():
            mine_ref[...] = odd
            theirs_ref[...] = even

    @pl.when(step < pl.num_programs(0) - 1)
    def _():
        buf[0:CHUNK, :] = dpre_ref[count - CHUNK :, :]
        moved = mm(shift[chunks * 3 * CHUNK :, :], dpre_ref[0 : 2 * CHUNK, :])
        halo_sums = [None] * 4
        dproj = jnp.zeros((16, wide), F32)
        pre = prehalo_ref[...].astype(F32)
        for lag in (1, 2, 3):
            part = moved[(lag - 1) * 16 : lag * 16]
            dproj = dproj + part * taps_ref[3 - lag : 4 - lag, :]
            halo_sums[3 - lag] = jnp.sum(pre * part, axis=0, keepdims=True)
        halo_sums[3] = jnp.zeros((1, wide), F32)
        dhalo_ref[...] = dproj.astype(BF16)
        sums = [[jnp.zeros((8, 128), F32) for _ in range(4)] for _ in range(wide // 128)]
        for chunk in range(chunks):
            if chunk < chunks - 1:
                pair = dpre_ref[chunk * CHUNK : chunk * CHUNK + 2 * CHUNK, :]
            else:
                pair = buf[...]
            moved = mm(shift[chunk * 3 * CHUNK : (chunk + 1) * 3 * CHUNK, :], pair)
            for place in range(wide // 128):
                cols = slice(place * 128, place * 128 + 128)
                for row in range(0, CHUNK, SUB):
                    span = slice(chunk * CHUNK + row, chunk * CHUNK + row + SUB)
                    pre = pre_ref[span, cols].astype(F32)
                    here = dpre_ref[span, cols].astype(F32)
                    dproj = here * taps_ref[3:4, cols]
                    sums[place][3] = sums[place][3] + fold(pre * here)
                    for lag in (1, 2, 3):
                        at = (lag - 1) * CHUNK + row
                        part = moved[at : at + SUB, cols]
                        dproj = dproj + part * taps_ref[3 - lag : 4 - lag, cols]
                        sums[place][3 - lag] = sums[place][3 - lag] + fold(pre * part)
                    dproj_ref[span, cols] = dproj.astype(BF16)
        sums_ref[...] = jnp.zeros_like(sums_ref)
        for place in range(wide // 128):
            cols = slice(place * 128, place * 128 + 128)
            for tap in range(4):
                sums_ref[tap : tap + 1, cols] = (
                    jnp.sum(sums[place][tap], axis=0, keepdims=True) + halo_sums[tap][:, cols]
                )
        product = mm(turned_ref[...], dproj_ref[...]) + mm(turnhalo_ref[...], dhalo_ref[...])
        hand_over(product.astype(BF16))

    @pl.when(step == pl.num_programs(0) - 1)
    def _():
        rate = rate_ref[:, 0:1]
        draw, drate = steps_back(raw_ref[...], dt_ref[...], rate, moves_ref[...], r_ref[...])
        low = draw.astype(BF16)
        draw_ref[...] = low
        product = mm_nt(turned_ref[...], low).astype(BF16)
        hand_over(
            jnp.concatenate([product, jnp.zeros((product.shape[0], wide - steps), BF16)], axis=1)
        )
        columns = [jnp.sum(draw, axis=1, keepdims=True), drate, jnp.zeros((steps, 6), F32)]
        sums_ref[...] = jnp.zeros_like(sums_ref)
        sums_ref[:, 0:steps] = jnp.concatenate(columns, axis=1).T


def quarters_kernel(mine_ref, got_ref, keep_ref, across_ref, along_ref, both_ref, *, shard):
    half = mine_ref.shape[1] // 2
    row_bit = lax.rem(lax.axis_index("dp") // 2, 2)
    side = lax.axis_index("dir")
    for place in range(keep_ref.shape[0] // shard):
        rows = slice(place * shard, (place + 1) * shard)
        for out_ref, row, column in (
            (keep_ref, row_bit, side),
            (across_ref, row_bit, 1 - side),
            (along_ref, 1 - row_bit, side),
            (both_ref, 1 - row_bit, 1 - side),
        ):
            here = pl.ds(pl.multiple_of((2 * place + row) * shard, shard), shard)
            cols = pl.ds(pl.multiple_of(column * half, half), half)
            total = mine_ref[here, cols].astype(F32) + got_ref[here, cols].astype(F32)
            out_ref[rows, :] = total.astype(out_ref.dtype)


def levels_kernel(keep_ref, a_ref, b_ref, c_ref, own_ref, s1_ref, s2_ref, s3_ref, *, shard):
    level = lax.axis_index("dp") // 4
    for bits, out_ref in enumerate((own_ref, s1_ref, s2_ref, s3_ref)):
        wanted = jnp.bitwise_xor(level, bits)
        rows = pl.ds(pl.multiple_of(wanted * shard, shard), shard)
        total = keep_ref[rows, :] + a_ref[rows, :].astype(F32)
        total = total + (b_ref[rows, :].astype(F32) + c_ref[rows, :].astype(F32))
        out_ref[...] = total.astype(out_ref.dtype)


def last_kernel(own_ref, a_ref, b_ref, c_ref, out_ref):
    total = own_ref[...] + a_ref[...].astype(F32)
    total = total + (b_ref[...].astype(F32) + c_ref[...].astype(F32))
    out_ref[...] = total.astype(BF16)


def finish_kernel(
    late_ref, lategot_ref, early_ref, earlygot_ref, small_ref, gx_ref, gz_ref, gbc_ref, go_ref,
    gtaps_ref, gmix_ref, gin_ref, gskip_ref, gbias_ref, galog_ref
):
    side = lax.axis_index("dir")
    half = late_ref.shape[1]
    inner = gx_ref.shape[1]
    model = go_ref.shape[1]
    shard = gx_ref.shape[0]
    first = jnp.where(side == 0, late_ref[...].astype(F32), lategot_ref[...].astype(F32))
    second = jnp.where(side == 0, lategot_ref[...].astype(F32), late_ref[...].astype(F32))
    gx_ref[:, 0:half] = first
    gx_ref[:, half:inner] = second[:, 0 : inner - half]
    gbc_ref[...] = second[:, inner - half : inner - half + gbc_ref.shape[1]]
    early = early_ref[...].astype(F32) + earlygot_ref[...].astype(F32)
    go_ref[0:shard, :] = early[:, 0:model]
    go_ref[shard : 2 * shard, :] = early[:, model : 2 * model]
    gz_ref[...] = early[:, 2 * model :]
    gtaps_ref[...] = small_ref[0:4, 0 : gtaps_ref.shape[1]]
    gmix_ref[...] = small_ref[4:5, 0:inner].reshape(inner)
    gin_ref[...] = small_ref[5:6, 0:model].reshape(model)
    heads = gskip_ref.shape[0]
    gskip_ref[...] = small_ref[6:7, 0:128].reshape(128)[0:heads]
    gbias_ref[0:1, :] = small_ref[6:7, 128 : 128 + heads]
    gbias_ref[1:2, :] = small_ref[6:7, 128 + heads : 128 + 2 * heads]
    galog_ref[0:1, :] = small_ref[6:7, 256 : 256 + heads]
    galog_ref[1:2, :] = small_ref[6:7, 256 + heads : 256 + 2 * heads]


def inputs_kernel(
    x_ref,
    c_ref,
    gain_ref,
    dproj_ref,
    dhalo_ref,
    draw_ref,
    dz_ref,
    wx_ref,
    wbc_ref,
    wz_ref,
    mix_sums_ref,
    tap_sums_ref,
    e0_ref,
    gin_ref,
    small_ref,
    total,
    dproj,
):
    step = pl.program_id(0)
    model, inner = wx_ref.shape
    steps = draw_ref.shape[0]
    heads = steps // 2
    narrow = wbc_ref.shape[1] - steps
    channels = inner + narrow

    @pl.when(step == 0)
    def _():
        total[...] = jnp.zeros_like(total)

    @pl.when(step == pl.num_programs(0) - 1)
    def _():
        tail = slice(dproj_ref.shape[0] - 16, dproj_ref.shape[0])
        both = dproj_ref[tail, :].astype(F32) + dhalo_ref[...].astype(F32)
        dproj[...] = dproj_ref[...]
        dproj[tail, :] = both.astype(BF16)

    @pl.when(step < pl.num_programs(0) - 1)
    def _():
        dproj[...] = dproj_ref[...]

    dn = mm_nt(dproj[:, 0:inner], wx_ref[...])
    dn = dn + mm_nt(dz_ref[...], wz_ref[...])
    dn = dn + mm_nt(dproj[:, inner:], wbc_ref[:, 0:narrow])
    dn = dn + mm_nt(draw_ref[...].astype(F32).T.astype(BF16), wbc_ref[:, narrow:])
    x = x_ref[...].astype(F32)
    inv = lax.rsqrt(jnp.mean(x * x, axis=1, keepdims=True) + EPS)
    unit = x * inv
    total[...] += fold(dn * unit)
    f = dn * row_of(gain_ref)
    back = inv * (f - unit * jnp.mean(f * unit, axis=1, keepdims=True))
    gin_ref[...] = (c_ref[...].astype(F32) + back).astype(BF16)

    @pl.when(step == pl.num_programs(0) - 1)
    def _():
        small_ref[...] = jnp.zeros_like(small_ref)
        small_ref[0:4, 0:channels] = tap_sums_ref[0:4, 0:channels]
        small_ref[4:5, 0:inner] = jnp.sum(mix_sums_ref[0:8, :], axis=0, keepdims=True)
        small_ref[5:6, 0:model] = jnp.sum(total[...], axis=0, keepdims=True)
        skips = in_parts(mix_sums_ref[8:16, :], 2).astype(BF16)
        skips = jnp.sum(mm_nt(e0_ref[0:heads, :], skips), axis=1, keepdims=True)
        skips = jnp.broadcast_to(skips, (heads, 128)).T
        small_ref[6:7, 0:heads] = skips[0:1]
        small_ref[6:7, 128:256] = tap_sums_ref[0:1, channels : channels + 128]
        small_ref[6:7, 256:384] = tap_sums_ref[1:2, channels : channels + 128]


def smem():
    return pl.BlockSpec(memory_space=pltpu.SMEM)


def resident():
    return pl.BlockSpec(memory_space=pltpu.VMEM)


def whole(shape):
    return pl.BlockSpec(shape, lambda i: (0,) * len(shape), pipeline_mode=pl.Buffered(1))


def rows_of(count, width):
    return pl.BlockSpec((count, width), lambda i: (i, 0))


def lanes_of(height, count):
    return pl.BlockSpec((height, count), lambda i: (0, i))


def parts_of(count, *rest):
    return pl.BlockSpec((count,) + rest, lambda i: (i,) + (0,) * len(rest))


def call(kernel, name, grid, in_specs, outs, scratch, flops, moved, args, vmem):
    return pl.pallas_call(
        kernel,
        name=name,
        grid=(grid,),
        in_specs=in_specs,
        out_specs=[spec for spec, _, _ in outs],
        out_shape=[jax.ShapeDtypeStruct(shape, dtype) for _, shape, dtype in outs],
        scratch_shapes=scratch,
        compiler_params=pltpu.CompilerParams(
            vmem_limit_bytes=vmem * MIB, dimension_semantics=("arbitrary",)
        ),
        cost_estimate=pl.CostEstimate(flops=flops, bytes_accessed=moved, transcendentals=0),
    )(*args)


def traded(values, axis, bit, size):
    return lax.ppermute(values, axis, [(i, i ^ bit) for i in range(size)])


def sum_shards(grad, dp_count):
    index = lax.axis_index("dp")
    held = grad.reshape(dp_count, grad.shape[0] // dp_count, grad.shape[1])
    bit = 1
    while bit < dp_count:
        paired = held.reshape(held.shape[0] // 2, 2, held.shape[1], held.shape[2])
        mine = (index // bit) % 2
        kept = lax.dynamic_index_in_dim(paired, mine, 1, keepdims=False)
        sent = lax.dynamic_index_in_dim(paired, 1 - mine, 1, keepdims=False).astype(BF16)
        held = kept.astype(F32) + traded(sent, "dp", bit, dp_count).astype(F32)
        bit *= 2
    held = held[0].astype(BF16)
    return held.astype(F32) + traded(held, "dir", 1, 2).astype(F32)


def sum_all(values, dp_count):
    bit = 1
    while bit < dp_count:
        values = values + traded(values, "dp", bit, dp_count)
        bit *= 2
    return values + traded(values, "dir", 1, 2)


def local(
    dp_count,
    hidden_in,
    lengths,
    gain_in,
    w_x,
    w_z,
    w_bcdt,
    conv_w,
    dt_bias,
    a_log,
    d_skip,
    gain_mix,
    w_out,
    cotangent,
):
    x = hidden_in[0]
    cot = cotangent[0]
    count, model = x.shape
    inner = w_x.shape[1]
    channels = conv_w.shape[1]
    heads = d_skip.shape[0]
    width = inner // heads
    state = (channels - inner) // 4
    chunks = count // CHUNK
    steps = 2 * heads

    halo = lax.ppermute(x[count - 16 :], "dir", [(0, 1)])

    spread = np.repeat(np.eye(heads, dtype=np.float32), width, axis=1)
    zeros = np.zeros_like(spread)
    e0 = jnp.asarray(np.concatenate([spread, zeros, spread, zeros]), BF16)
    e1 = jnp.asarray(np.concatenate([zeros, spread, zeros, spread]), BF16)
    spans = jnp.asarray(np.repeat(np.eye(heads, dtype=np.float32), CHUNK, axis=1), BF16)
    def rows_out(size, columns, dtype):
        return (rows_of(size, columns), (count, columns), dtype)

    def full(shape, dtype):
        return (pl.BlockSpec(shape, lambda i: (0,) * len(shape)), shape, dtype)

    normed, turned, gate_z, d_norm, raw, dt, rate, target, source, factors, keeps = call(
        gates_kernel,
        "gates",
        count // ROWS,
        [
            smem(),
            smem(),
            smem(),
            rows_of(ROWS, model),
            rows_of(ROWS, model),
            whole((model,)),
            whole((model, inner)),
            whole((inner, model)),
            whole(w_bcdt.shape),
            whole(e0.shape),
            whole(e1.shape),
        ],
        [
            rows_out(ROWS, model, BF16),
            (lanes_of(model, ROWS), (model, count), BF16),
            rows_out(ROWS, inner, BF16),
            rows_out(ROWS, inner, BF16),
            full((steps, count), F32),
            full((steps, count), F32),
            full((steps, 128), F32),
            full((steps, count), F32),
            full((steps, count), F32),
            full((2, count, 2 * steps), BF16),
            full((6, chunks, inner), F32),
        ],
        [],
        4 * count * model * inner,
        4 * count * (model + inner) + 4 * model * inner,
        (lengths, dt_bias, a_log, x, cot, gain_in, w_z, w_out, w_bcdt, e0, e1),
        VMEM_GATES,
    )

    per = ROWS // CHUNK
    state_f32 = pltpu.VMEM((state, inner), F32)
    state_bf16 = pltpu.VMEM((state, inner), BF16)
    row_f32 = pltpu.VMEM((1, inner), F32)
    chunk_f32 = pltpu.VMEM((CHUNK, inner), F32)
    chunk_bf16 = pltpu.VMEM((CHUNK, inner), BF16)
    pre, act, slope, sl0, sf1, send, pre_halo, turn_halo = call(
        proj_kernel,
        "proj",
        count // ROWS,
        [
            smem(),
            rows_of(ROWS, model),
            whole((16, model)),
            whole((model,)),
            whole((model, inner)),
            whole(w_bcdt.shape),
            whole(conv_w.shape),
            pl.BlockSpec((1, ROWS, 2 * steps), lambda i: (1, i, 0)),
            whole((6, chunks, inner)),
            whole(e0.shape),
            whole(e1.shape),
        ],
        [
            rows_out(ROWS, channels, BF16),
            rows_out(ROWS, channels, BF16),
            rows_out(ROWS, channels, BF16),
            (parts_of(per, state, inner), (chunks, state, inner), BF16),
            (parts_of(per, state, inner), (chunks, state, inner), BF16),
            full((state, inner), BF16),
            full((16, channels), BF16),
            full((model, 16), BF16),
        ],
        [
            pltpu.VMEM((CHUNK + ROWS, channels), BF16),
            state_f32,
            state_f32,
            chunk_bf16,
            chunk_bf16,
        ],
        3 * count * model * inner,
        8 * count * inner,
        (lengths, normed, halo, gain_in, w_x, w_bcdt, conv_w, factors, keeps, e0, e1),
        VMEM_PROJ,
    )
    received = lax.ppermute(send, "dir", SWAP)

    (y_in,) = call(
        functools.partial(intra_kernel, heads=heads, state=state),
        "intra",
        chunks,
        [
            smem(),
            rows_of(CHUNK, channels),
            lanes_of(steps, CHUNK),
            lanes_of(steps, CHUNK),
        ],
        [rows_out(CHUNK, inner, BF16)],
        [],
        8 * count * CHUNK * inner,
        6 * count * inner,
        (lengths, act, target, source),
        VMEM_INTRA,
    )

    def down_rows(width):
        return pl.BlockSpec((CHUNK, width), lambda i: (chunks - 1 - i, 0))

    def down_lanes(height):
        return pl.BlockSpec((height, CHUNK), lambda i: (0, chunks - 1 - i))

    def down_parts(*rest):
        return pl.BlockSpec((1,) + rest, lambda i: (chunks - 1 - i,) + (0,) * len(rest))

    states = (down_parts(state, inner), (chunks, state, inner), BF16)
    out, mixed, dz, dy, r, dcc, dl0, df1, s0, s1, d_send, mix_sums = call(
        mix_kernel,
        "mix",
        chunks,
        [
            smem(),
            smem(),
            down_rows(model),
            down_rows(channels),
            pl.BlockSpec((1, CHUNK, 2 * steps), lambda i: (0, chunks - 1 - i, 0)),
            down_parts(state, inner),
            down_parts(state, inner),
            whole((6, chunks, inner)),
            whole((state, inner)),
            down_rows(inner),
            down_rows(inner),
            down_rows(inner),
            whole((inner, model)),
            whole((inner,)),
            whole(e0.shape),
            whole(e1.shape),
        ],
        [
            (down_rows(model), (count, model), BF16),
            (down_rows(inner), (count, inner), BF16),
            (down_rows(inner), (count, inner), BF16),
            (down_rows(inner), (count, inner), BF16),
            (down_lanes(steps), (steps, count), F32),
            (down_rows(2 * state), (count, 2 * state), F32),
            states,
            states,
            states,
            states,
            full((state, inner), BF16),
            full((16, inner), F32),
        ],
        [state_f32] * 3 + [chunk_f32] * 7 + [chunk_bf16] * 4 + [row_f32] * 2,
        3 * count * model * inner,
        16 * count * inner,
        (
            lengths,
            d_skip,
            x,
            act,
            factors,
            sl0,
            sf1,
            keeps,
            received,
            y_in,
            gate_z,
            d_norm,
            w_out,
            gain_mix,
            e0,
            e1,
        ),
        VMEM_MIX,
    )
    d_received = lax.ppermute(d_send, "dir", SWAP)

    blocks = 4
    shard = model // dp_count
    half = shard if shard % 16 == 0 else 0
    out_spec = (
        (rows_of(model // blocks, inner), (model, inner), BF16)
        if half
        else (rows_of(inner // blocks, model), (inner, model), BF16)
    )
    g_out, g_z = call(
        functools.partial(weights_kernel, half=half),
        "weights",
        blocks,
        [
            whole((model, count)),
            lanes_of(count, inner // blocks),
            lanes_of(count, inner // blocks),
            whole((count, model)),
        ],
        [out_spec, (lanes_of(model, inner // blocks), (model, inner), BF16)],
        [],
        4 * count * model * inner,
        6 * count * inner,
        (turned, dz, mixed, cot),
        VMEM_WEIGHTS,
    )
    if not half:
        g_out = g_out.reshape(dp_count, 2, shard, model)
        g_out = g_out.transpose(0, 2, 1, 3).reshape(model, inner)
    g_early = jnp.concatenate([g_out, g_z], axis=1)
    early = lax.psum_scatter(g_early, "dp", scatter_dimension=0, tiled=True)

    def back(skipped, taken, start):
        def rows_from(width):
            return pl.BlockSpec((CHUNK, width), lambda i: (i + skipped, 0))

        def lanes_from(height):
            return pl.BlockSpec((height, CHUNK), lambda i: (0, i + skipped))

        def parts_from(*rest):
            return pl.BlockSpec((1,) + rest, lambda i: (i + skipped,) + (0,) * len(rest))

        return call(
            functools.partial(back_kernel, skipped=skipped, chunks=chunks),
            "back" + str(skipped),
            taken,
            [
                smem(),
                smem(),
                rows_from(channels),
                rows_from(channels),
                lanes_from(steps),
                lanes_from(steps),
                pl.BlockSpec((1, CHUNK, 2 * steps), lambda i: (1, i + skipped, 0)),
                rows_from(2 * state),
                rows_from(inner),
                parts_from(state, inner),
                parts_from(state, inner),
                parts_from(state, inner),
                parts_from(state, inner),
                whole((6, chunks, inner)),
                whole((state, inner)),
                whole(start.shape),
                whole(e0.shape),
                whole(e1.shape),
                whole(spans.shape),
            ],
            [
                (rows_of(CHUNK, channels), (taken * CHUNK, channels), BF16),
                (lanes_of(8 * heads, CHUNK), (8 * heads, taken * CHUNK), F32),
                full((state, inner), F32),
            ],
            [
                state_f32,
                pltpu.VMEM((CHUNK, CHUNK), F32),
                pltpu.VMEM((CHUNK, heads * CHUNK), BF16),
                pltpu.VMEM((CHUNK, heads * CHUNK), BF16),
            ]
            + [chunk_bf16] * 4
            + [state_bf16] * 2,
            24 * taken * CHUNK * CHUNK * inner,
            16 * taken * CHUNK * inner,
            (
                lengths,
                d_skip,
                act,
                slope,
                target,
                source,
                factors,
                dcc,
                dy,
                s0,
                s1,
                dl0,
                df1,
                keeps,
                d_received,
                start,
                e0,
                e1,
                spans,
            ),
            VMEM_BACK,
        )

    dpre, moves, _ = back(0, chunks, d_received)

    tile = 256
    tiles = channels // tile
    def tile_of(height):
        return pl.BlockSpec((height, tile), lambda i: (0, jnp.minimum(i, tiles - 1)))

    wide = (tiles + 1) * tile
    kept_rows = model // 2 if half else model
    dproj, dhalo, mine, theirs, draw, tap_sums = call(
        functools.partial(conv_back_kernel, shard=half),
        "conv_back",
        tiles + 1,
        [
            smem(),
            whole((model, count)),
            whole((model, 16)),
            tile_of(count),
            tile_of(count),
            tile_of(16),
            tile_of(conv_w.shape[0]),
            whole((steps, count)),
            whole((steps, count)),
            whole((steps, 128)),
            whole((8 * heads, count)),
            whole((steps, count)),
        ],
        [
            (tile_of(count), (count, channels), BF16),
            (tile_of(16), (16, channels), BF16),
            (lanes_of(kept_rows, tile), (kept_rows, wide), BF16),
            (lanes_of(kept_rows, tile), (kept_rows, wide), BF16),
            full((steps, count), BF16),
            (lanes_of(8, tile), (8, wide), F32),
        ],
        [
            pltpu.VMEM((3 * count + 48, 2 * CHUNK), BF16),
            pltpu.VMEM((2 * CHUNK, tile), BF16),
        ],
        2 * count * model * channels,
        6 * count * channels,
        (lengths, turned, turn_halo, dpre, pre, pre_halo, conv_w, raw, dt, rate, moves, r),
        VMEM_CONV,
    )
    d_halo = lax.ppermute(dhalo, "dir", [(1, 0)])

    grad_in, small = call(
        inputs_kernel,
        "inputs",
        count // ROWS,
        [
            rows_of(ROWS, model),
            rows_of(ROWS, model),
            whole((model,)),
            rows_of(ROWS, channels),
            whole((16, channels)),
            lanes_of(steps, ROWS),
            rows_of(ROWS, inner),
            whole((model, inner)),
            whole(w_bcdt.shape),
            whole((model, inner)),
            whole(mix_sums.shape),
            whole(tap_sums.shape),
            whole(e0.shape),
        ],
        [
            rows_out(ROWS, model, BF16),
            full((8, tap_sums.shape[1]), F32),
        ],
        [pltpu.VMEM((8, model), F32), pltpu.VMEM((ROWS, channels), BF16)],
        5 * count * model * inner,
        8 * count * inner,
        (x, cot, gain_in, dproj, d_halo, draw, dz, w_x, w_bcdt, w_z, mix_sums, tap_sums, e0),
        VMEM_INPUTS,
    )
    early_got = traded(early, "dir", 1, 2)
    small = sum_all(small, dp_count)
    if not half or dp_count != 16:
        late = sum_shards(mine, dp_count)
        early = early.astype(F32) + early_got.astype(F32)
        grad_out = jnp.concatenate([early[:, :model], early[:, model:inner]], axis=0)
        return (
            out[None],
            grad_in[None],
            late[:, :inner],
            early[:, inner:],
            late[:, inner : inner + 4 * state + steps],
            grad_out,
            small[5, :model],
            small[0:4, :channels],
            small[6, 128 : 128 + steps].reshape(dt_bias.shape),
            small[6, 256 : 256 + steps].reshape(a_log.shape),
            small[6, :heads],
            small[4, :inner],
        )

    def plain(kernel, name, args, outs):
        return pl.pallas_call(
            kernel,
            name=name,
            in_specs=[pl.BlockSpec(memory_space=pltpu.VMEM)] * len(args),
            out_specs=[pl.BlockSpec(memory_space=pltpu.VMEM)] * len(outs),
            out_shape=[jax.ShapeDtypeStruct(shape, dtype) for shape, dtype in outs],
            compiler_params=pltpu.CompilerParams(vmem_limit_bytes=VMEM_SUMS * MIB),
        )(*args)

    got = traded(theirs, "dp", 1, dp_count)
    quarter = (model // 4, wide // 2)
    kept, across, along, both = plain(
        functools.partial(quarters_kernel, shard=shard),
        "quarters",
        (mine, got),
        [(quarter, F32), (quarter, BF16), (quarter, BF16), (quarter, BF16)],
    )
    corners = [(a, b) for a in range(2) for b in range(dp_count)]
    across = traded(across, "dir", 1, 2)
    along = traded(along, "dp", 2, dp_count)
    both = lax.ppermute(
        both,
        ("dir", "dp"),
        [(a * dp_count + b, (1 - a) * dp_count + (b ^ 2)) for a, b in corners],
    )
    piece = (shard, wide // 2)
    own, *sends = plain(
        functools.partial(levels_kernel, shard=shard),
        "levels",
        (kept, across, along, both),
        [(piece, F32)] + [(piece, BF16)] * 3,
    )
    gots = [traded(sent, "dp", 4 * bits, dp_count) for bits, sent in zip((1, 2, 3), sends)]
    (late,) = plain(last_kernel, "last", (own, *gots), [(piece, BF16)])
    late_got = traded(late, "dir", 1, 2)
    g_x, g_zz, g_bc, g_o, g_taps, g_mix, g_in, g_skip, g_bias, g_alog = plain(
        finish_kernel,
        "finish",
        (late, late_got, early, early_got, small),
        [
            ((shard, inner), F32),
            ((shard, inner), F32),
            ((shard, w_bcdt.shape[1]), F32),
            ((2 * shard, model), F32),
            (conv_w.shape, F32),
            ((inner,), F32),
            ((model,), F32),
            ((heads,), F32),
            (dt_bias.shape, F32),
            (a_log.shape, F32),
        ],
    )
    return (
        out[None],
        grad_in[None],
        g_x,
        g_zz,
        g_bc,
        g_o,
        g_in,
        g_taps,
        g_bias,
        g_alog,
        g_skip,
        g_mix,
    )


def solution(mesh):
    return jax.shard_map(
        functools.partial(local, mesh.shape["dp"]),
        mesh=mesh,
        in_specs=(
            P("dir", "dp", None),
            P("dp", None),
            P(),
            P(),
            P(),
            P(),
            P(),
            P(),
            P(),
            P(),
            P(),
            P(),
            P("dir", "dp", None),
        ),
        out_specs=(
            P("dir", "dp", None),
            P("dir", "dp", None),
            P("dp", None),
            P("dp", None),
            P("dp", None),
            P("dp", None),
            P(),
            P(),
            P(),
            P(),
            P(),
            P(),
        ),
        check_vma=False,
    )
```

time: 278 us -> 228 us (0.82)
  waiting for transfers between devices: 61.9 us -> 24.1 us
  Pallas kernels: 148 us -> 118 us
  local copies, waits for them, and re-layouts: 22.7 us -> 41.8 us
  between operations: 1.11 us -> 14.7 us
  other arithmetic: 13 us -> 2.82 us
  starting transfers between devices: 29.4 us -> 25.8 us
    ppermute x28 -> x17, waiting for transfers between devices: 61.9 us -> 24.1 us  [the longest x13 19.5 us: traded(): return lax.ppermute(values, axis, [(i, i ^ bit) for i in range(size)])]
    unnamed x33 -> x149, local copies, waits for them, and re-layouts: 3.55 us -> 41.1 us
    pallas_call x8, Pallas kernels: 148 us -> 115 us  [call(): pl.pallas_call(kernel, name=name, grid=(grid,), in_specs=in_specs, out_sp...]
    add x21 -> x5, other arithmetic: 9.18 us -> 0.04 us  [the longest x4 0.04 us: sum_all(): values = values + traded(values, 'dp', bit, dp_count)]
    squeeze x4 -> x0, local copies, waits for them, and re-layouts: 4.88 us -> none  [sum_shards(): lax.dynamic_index_in_dim(paired, 1 - mine, 1, keepdims=False).astype(BF16)]
    slice x10 -> x0, local copies, waits for them, and re-layouts: 4.56 us -> none  [the longest x5 2.53 us: local(): small = [small[end - size:end] for end, size in zip(ends, sizes)]]
    reshape x7 -> x0, local copies, waits for them, and re-layouts: 4.13 us -> none  [the longest x1 1.37 us: local(): small[1].reshape(conv_w.shape)]
    ppermute x28 -> x17, starting transfers between devices: 24.5 us -> 21 us  [the longest x13 17.2 us: traded(): return lax.ppermute(values, axis, [(i, i ^ bit) for i in range(size)])]
  transfers between devices with their start and end apart: 29 -> 19, of which waited for: 13 -> 8; matrix products, arithmetic and copies ran while one was open for 11% -> 1% of each run, Pallas kernels for 12% -> 32%
where the time goes in v1:
time: 228 us; the launch traced here: 227 us
  Pallas kernels  118 us (52%)
  local copies, waits for them, and re-layouts  41.8 us (18%)
  starting transfers between devices  25.8 us (11%)
  waiting for transfers between devices  24.1 us (11%)
  between operations  14.7 us (6%)
  other arithmetic  2.82 us (1%)
    pallas_call x8, Pallas kernels, call(): pl.pallas_call(kernel, name=name, grid=(grid,), in_specs=in_specs, out_sp...  115 us
    unnamed x149, local copies, waits for them, and re-layouts  41.1 us
    ppermute x13, waiting for transfers between devices, traded(): return lax.ppermute(values, axis, [(i, i ^ bit) for i in range(size)])  19.5 us
    ppermute x13, starting transfers between devices, traded(): return lax.ppermute(values, axis, [(i, i ^ bit) for i in range(size)])  17.2 us
    ppermute x1, starting transfers between devices, local(): halo = lax.ppermute(x[count - 16:], 'dir', [(0, 1)])  4.83 us
    ppermute x1, waiting for transfers between devices, local(): d_received = lax.ppermute(d_send, 'dir', SWAP)  4.57 us
  transfers between devices with their start and end apart: 19, of which 8 were waited for; matrix products, arithmetic and copies ran while one was open for 1% of the time, Pallas kernels for 32%

profile of v1, /device:TPU:0, one launch (start us, length us, event | category | flops | bytes accessed | tf_op | source)
XLA Modules:
  0.0 226.8 jit_solution(6179178931186571371)
XLA Ops:
  8.0 4.8 %collective-permute-start = (bf16[16,768]{1,0:T(8,128)(2,1)S(1)}, bf16[16,768]{1,0:T(8,128)(2,1)S(1)}, u32[]{:S(2)}, u32[]{:S(2)}) collective-permute-start(bf16[16,768]{1,0:T(8,128)(2,1)S(1)} %slice_bitcast_fusion), channel_id=1, source_target_pairs={{0,16},{1,17},{2,18},{3,19},{4,20},{5,21},{6,22},{7,23},{8,24},{9,... | collective-permute-start | bytes 73736 | tf_op jit(solution)/shard_map/ppermute | solution.py:1046
  12.8 1.3 copy.28.wbc_ref
  14.2 1.9 copy-done.9
  16.0 1.4 copy-done.13
  20.0 1.7 copy-done.59
  21.7 1.4 copy-done.63
  25.2 9.0 %gates.1 = (bf16[1024,768]{1,0:T(8,128)(2,1)S(1)}, bf16[768,1024]{1,0:T(8,128)(2,1)S(1)}, bf16[1024,1536]{1,0:T(8,128)(2,1)S(1)}, bf16[1024,1536]{1,0:T(8,128)(2...) custom-call(s32[1,8]{1,0:T(1,128)S(1)} %copy-done.52, ...), custom_call_target="tpu_custom_call" | custom-call | flops 4831838208 | bytes 14155776 | tf_op jit(solution)/shard_map/gates/pallas_call | solution.py:977
  34.2 1.6 copy-done.7
  35.8 1.6 copy-done.8
  38.2 13.3 %proj.1 = (bf16[1024,1792]{1,0:T(8,128)(2,1)S(1)}, bf16[1024,1792]{1,0:T(8,128)(2,1)S(1)}, bf16[1024,1792]{1,0:T(8,128)(2,1)S(1)}, bf16[8,64,1536]{2,1,0:T(8,128...) custom-call(s32[1,8]{1,0:T(1,128)S(1)} %copy-done.52, ...), custom_call_target="tpu_custom_call" | custom-call | flops 3623878656 | bytes 12582912 | tf_op jit(solution)/shard_map/proj/pallas_call | solution.py:977
  51.6 1.9 copy-done.3
  53.5 1.9 copy-done.5
  55.4 11.0 %intra.1.yin_ref = bf16[1024,1536]{1,0:T(8,128)(2,1)S(1)} custom-call(s32[1,8]{1,0:T(1,128)S(1)} %copy-done.52, bf16[1024,1792]{1,0:T(8,128)(2,1)S(1)} %get-tuple-element.76.act_ref, f32[48,1024]{1,0:T(8,128)S(1)} %get-tuple-element.80.target_ref, f32[48,1024]{1,0:T(8,128)S(1)} %get-tuple-element.81.source_ref), custom_call_target="tpu_custom_call" | custom-call | flops 1610612736 | bytes 9437184 | tf_op jit(solution)/shard_map/intra/pallas_call | solution.py:977
  66.5 1.7 copy-done.2
  68.2 23.8 %mix.1 = (bf16[1024,768]{1,0:T(8,128)(2,1)}, bf16[1024,1536]{1,0:T(8,128)(2,1)S(1)}, bf16[1024,1536]{1,0:T(8,128)(2,1)S(1)}, bf16[1024,1536]{1,0:T(8,128)(2,1)S(...) custom-call(s32[1,8]{1,0:T(1,128)S(1)} %copy-done.53, ...), custom_call_target="tpu_custom_call" | custom-call | flops 3623878656 | bytes 25165824 | tf_op jit(solution)/shard_map/mix/pallas_call | solution.py:977
  93.5 7.5 %weights.1 = (bf16[768,1536]{1,0:T(8,128)(2,1)S(1)}, bf16[768,1536]{1,0:T(8,128)(2,1)S(1)}) custom-call(bf16[768,1024]{1,0:T(8,128)(2,1)S(1)} %get-tuple-element.85.turned_ref, bf16[1024,1536]{1,0:T(8,128)(2,1)S(1)} %get-tuple-element.106.dz_ref, bf16[1024,1536]{1,0:T(8,128)(2,1)S(1)} %get-tuple-element.120.mixed_ref, bf16[1024,768]{1,0:T(8,128)(2,1)S(1)} %bitcast.10), custom_call_target="tpu_custom_call" | custom-call | flops 4831838208 | bytes 9437184 | tf_op jit(solution)/shard_map/weights/pallas_call | solution.py:977
  101.1 2.8 %pad_maximum_fusion = bf16[768,3072]{1,0:T(8,128)(2,1)} fusion(bf16[768,1536]{1,0:T(8,128)(2,1)S(1)} %get-tuple-element.122, bf16[768,1536]{1,0:T(8,128)(2,1)S(1)} %get-tuple-element.121), kind=kLoop, calls=%fused_computation | loop fusion | flops 9437184 | bytes 9437184 | tf_op jit(solution)/shard_map/concatenate | solution.py:1260
  103.9 2.1 collective-permute-start.2
  105.9 4.6 %collective-permute-done.2.recv_ref.start_ref = bf16[64,1536]{1,0:T(8,128)(2,1)S(1)} collective-permute-done((bf16[64,1536]{1,0:T(8,128)(2,1)}, bf16[64,1536]{1,0:T(8,128)(2,1)S(1)}, u32[]{:S(2)}, u32[]{:S(2)}) %collective-permute-start.2) | collective-permute-done | bytes 196640 | tf_op jit(solution)/shard_map/ppermute | solution.py:1230
  110.5 2.1 copy-done.1
  112.6 2.3 %copy-done.6 = bf16[1024,1792]{1,0:T(8,128)(2,1)S(1)} copy-done((bf16[1024,1792]{1,0:T(8,128)(2,1)S(1)}, bf16[1024,1792]{1,0:T(8,128)(2,1)}, u32[]{:S(2)}) %copy-start.6) | copy-done | bytes 3670040
  114.9 1.1 copy-done.12
  116.0 1.5 copy-done.17
  117.5 1.5 copy-done.19
  119.0 1.5 copy-done.21
  120.5 1.5 copy-done.23
  125.8 1.0 copy-done.40
  128.4 26.9 %back0.1 = (bf16[1024,1792]{1,0:T(8,128)(2,1)S(1)}, f32[192,1024]{1,0:T(8,128)S(1)}, f32[64,1536]{1,0:T(8,128)}) custom-call(s32[1,8]{1,0:T(1,128)S(1)} %copy-done.53, f32[24]{0:T(128)S(1)} %copy-done.56, bf16[1024,1792]{1,0:T(8,128)(2,1)S(1)} %copy-done.1, bf16[1024,1792]{1,0:T(8,128)(2,1)S(1)} %copy-done.6, f32[48,1024]{1,0:T(8,128)S(1)} %copy-done.34, ...), custom_call_target="tpu_custom_call" | custom-call | flops 4831838208 | bytes 25165824 | tf_op jit(solution)/shard_map/back0/pallas_call | solution.py:977
  155.4 14.7 %conv_back.1 = (bf16[1024,1792]{1,0:T(8,128)(2,1)S(1)}, bf16[16,1792]{1,0:T(8,128)(2,1)S(1)}, bf16[384,2048]{1,0:T(8,128)(2,1)S(1)}, bf16[384,2048]{1,0:T(8,128)...) custom-call(s32[1,8]{1,0:T(1,128)S(1)} %copy-done.53, bf16[768,1024]{1,0:T(8,128)(2,1)S(1)} %copy-done.25, ...), custom_call_target="tpu_custom_call" | custom-call | flops 2818572288 | bytes 11010048 | tf_op jit(solution)/shard_map/conv_back/pallas_call | solution.py:977
  170.2 1.4 collective-permute-start.3
  171.7 2.0 collective-permute-done.4.got_ref
  173.6 1.2 quarters.1
  174.9 1.8 collective-permute-start.5
  176.7 1.5 collective-permute-start.6
  178.4 8.8 %inputs.1 = (bf16[1024,768]{1,0:T(8,128)(2,1)}, f32[8,2048]{1,0:T(8,128)S(1)}) custom-call(bf16[1024,768]{1,0:T(8,128)(2,1)S(1)} %bitcast.8, bf16[1024,768]{1,0:T(8,128)(2,1)S(1)} %bitcast.11, f32[768]{0:T(1024)S(1)} %copy-done.71, bf16[1024,1792]{1,0:T(8,128)(2,1)S(1)} %get-tuple-element.103.dproj_ref, ...), custom_call_target="tpu_custom_call" | custom-call | flops 6039797760 | bytes 12582912 | tf_op jit(solution)/shard_map/inputs/pallas_call | solution.py:977
  187.2 1.8 collective-permute-start.12
  189.1 1.6 collective-permute-start.14
  190.6 6.9 %collective-permute-done.14 = f32[8,2048]{1,0:T(8,128)S(1)} collective-permute-done((f32[8,2048]{1,0:T(8,128)S(1)}, f32[8,2048]{1,0:T(8,128)S(1)}, u32[]{:S(2)}, u32[]{:S(2)}) %collective-permute-start.14) | collective-permute-done | bytes 65568 | tf_op jit(solution)/shard_map/ppermute | solution.py:993
  197.6 1.6 collective-permute-start.15
  199.9 2.5 %collective-permute-start.9 = (bf16[48,1024]{1,0:T(8,128)(2,1)S(1)}, bf16[48,1024]{1,0:T(8,128)(2,1)S(1)}, u32[]{:S(2)}, u32[]{:S(2)}) collective-permute-start(bf16[48,1024]{1,0:T(8,128)(2,1)S(1)} %get-tuple-element.118), channel_id=1, source_target_pairs={{0,8},{1,9},{2,10},{3,11},{4,12},{5,13},{6,14},{7,15},{8,0},{9,1},... | collective-permute-start | bytes 294920 | tf_op jit(solution)/shard_map/ppermute | solution.py:993
  202.4 1.4 collective-permute-start.10
  203.9 1.8 collective-permute-start.16
  205.7 1.5 collective-permute-done.9.b_ref
  207.3 3.7 %collective-permute-done.10.c_ref = bf16[48,1024]{1,0:T(8,128)(2,1)S(1)} collective-permute-done((bf16[48,1024]{1,0:T(8,128)(2,1)S(1)}, bf16[48,1024]{1,0:T(8,128)(2,1)S(1)}, u32[]{:S(2)}, u32[]{:S(2)}) %collective-permute-start.10) | collective-permute-done | bytes 98336 | tf_op jit(solution)/shard_map/ppermute | solution.py:993
  211.0 1.3 collective-permute-start.11
  212.3 2.3 %collective-permute-done.16 = f32[8,2048]{1,0:T(8,128)S(1)} collective-permute-done((f32[8,2048]{1,0:T(8,128)S(1)}, f32[8,2048]{1,0:T(8,128)S(1)}, u32[]{:S(2)}, u32[]{:S(2)}) %collective-permute-start.16) | collective-permute-done | bytes 65568 | tf_op jit(solution)/shard_map/ppermute | solution.py:993
  214.6 1.3 collective-permute-start.17
  215.9 3.1 %collective-permute-done.17 = f32[8,2048]{1,0:T(8,128)S(1)} collective-permute-done((f32[8,2048]{1,0:T(8,128)S(1)}, f32[8,2048]{1,0:T(8,128)S(1)}, u32[]{:S(2)}, u32[]{:S(2)}) %collective-permute-start.17) | collective-permute-done | bytes 65568 | tf_op jit(solution)/shard_map/ppermute | solution.py:993
  (159 shorter events, 15.2 us)
Async XLA Ops:
  7.2 180.0 %reduce-scatter.2.cloned.1.call-start = ((), (), s32[]{:S(2)}) async-start(), calls=%async_computation.1 | async-start | bytes 5013504 | tf_op jit(solution)/shard_map/reduce_scatter | solution.py:1261
  8.0 30.2 %collective-permute-start = (bf16[16,768]{1,0:T(8,128)(2,1)S(1)}, bf16[16,768]{1,0:T(8,128)(2,1)S(1)}, u32[]{:S(2)}, u32[]{:S(2)}) collective-permute-start(bf16[16,768]{1,0:T(8,128)(2,1)S(1)} %slice_bitcast_fusion), channel_id=1, source_target_pairs={{0,16},{1,17},{2,18},{3,19},{4,20},{5,21},{6,22},{7,23},{8,24},{9,... | collective-permute-start | bytes 73736 | tf_op jit(solution)/shard_map/ppermute | solution.py:1046
  14.1 24.0 %copy-start.37 = (bf16[768,304]{1,0:T(8,128)(2,1)}, bf16[768,304]{1,0:T(8,128)(2,1)S(1)}, u32[]{:S(2)}) copy-start(bf16[768,304]{1,0:T(8,128)(2,1)S(1)} %copy.28.wbc_ref) | copy-start | bytes 1400836
  25.1 13.0 %copy-start.27 = (bf16[96,1536]{1,0:T(8,128)(2,1)S(1)}, bf16[96,1536]{1,0:T(8,128)(2,1)}, u32[]{:S(2)}) copy-start(bf16[96,1536]{1,0:T(8,128)(2,1)} %constant.6.clone.e0_ref) | copy-start | bytes 884740
  25.2 13.1 %copy-start.29 = (bf16[96,1536]{1,0:T(8,128)(2,1)S(1)}, bf16[96,1536]{1,0:T(8,128)(2,1)}, u32[]{:S(2)}) copy-start(bf16[96,1536]{1,0:T(8,128)(2,1)} %constant.7.clone.e1_ref) | copy-start | bytes 884740
  25.2 13.1 %copy-start.51 = (f32[4,1792]{1,0:T(4,128)S(1)}, f32[4,1792]{1,0:T(4,128)}, u32[]{:S(2)}) copy-start(f32[4,1792]{1,0:T(4,128)} %taps_ref.3) | copy-start | bytes 86020
  25.2 13.1 %copy-start.61 = (bf16[768,1536]{1,0:T(8,128)(2,1)S(1)}, bf16[768,1536]{1,0:T(8,128)(2,1)}, u32[]{:S(2)}) copy-start(bf16[768,1536]{1,0:T(8,128)(2,1)} %wx_ref.3) | copy-start | bytes 7077892
  25.2 13.1 %copy-start.70 = (f32[768]{0:T(1024)S(1)}, f32[768]{0:T(1024)}, u32[]{:S(2)}) copy-start(f32[768]{0:T(1024)} %gain_ref.7) | copy-start | bytes 9220
  38.1 13.5 %copy-start.42 = (f32[48,1024]{1,0:T(8,128)}, f32[48,1024]{1,0:T(8,128)S(1)}, u32[]{:S(2)}) copy-start(f32[48,1024]{1,0:T(8,128)S(1)} %get-tuple-element.98.raw_ref) | copy-start | bytes 589828
  38.1 17.2 %copy-start.33 = (f32[48,1024]{1,0:T(8,128)}, f32[48,1024]{1,0:T(8,128)S(1)}, u32[]{:S(2)}) copy-start(f32[48,1024]{1,0:T(8,128)S(1)} %get-tuple-element.80.target_ref) | copy-start | bytes 589828
  38.1 17.2 %copy-start.35 = (f32[48,1024]{1,0:T(8,128)}, f32[48,1024]{1,0:T(8,128)S(1)}, u32[]{:S(2)}) copy-start(f32[48,1024]{1,0:T(8,128)S(1)} %get-tuple-element.81.source_ref) | copy-start | bytes 589828
  38.1 30.0 %copy-start.11 = (bf16[2,1024,96]{2,1,0:T(8,128)(2,1)}, bf16[2,1024,96]{2,1,0:T(8,128)(2,1)S(1)}, u32[]{:S(2)}) copy-start(bf16[2,1024,96]{2,1,0:T(8,128)(2,1)S(1)} %get-tuple-element.74.factors_ref) | copy-start | bytes 1179652
  38.1 30.0 %copy-start.31 = (f32[6,8,1536]{2,1,0:T(8,128)}, f32[6,8,1536]{2,1,0:T(8,128)S(1)}, u32[]{:S(2)}) copy-start(f32[6,8,1536]{2,1,0:T(8,128)S(1)} %get-tuple-element.75.keeps_ref) | copy-start | bytes 884740
  38.2 55.3 %copy-start.24 = (bf16[768,1024]{1,0:T(8,128)(2,1)}, bf16[768,1024]{1,0:T(8,128)(2,1)S(1)}, u32[]{:S(2)}) copy-start(bf16[768,1024]{1,0:T(8,128)(2,1)S(1)} %get-tuple-element.85.turned_ref) | copy-start | bytes 4718596
  55.4 12.8 %collective-permute-start.1 = (bf16[64,1536]{1,0:T(8,128)(2,1)S(1)}, bf16[64,1536]{1,0:T(8,128)(2,1)S(1)}, u32[]{:S(2)}, u32[]{:S(2)}) collective-permute-start(bf16[64,1536]{1,0:T(8,128)(2,1)S(1)} %get-tuple-element.79), channel_id=1, source_target_pairs={{0,16},{16,0},{1,17},{17,1},{2,18},{18,2},{3,19},{19,3},{4,20},{20... | collective-permute-start | bytes 589832 | tf_op jit(solution)/shard_map/ppermute | solution.py:1141
  55.4 12.8 %copy-start.10 = (bf16[1536,768]{1,0:T(8,128)(2,1)S(1)}, bf16[1536,768]{1,0:T(8,128)(2,1)}, u32[]{:S(2)}) copy-start(bf16[1536,768]{1,0:T(8,128)(2,1)} %wo_ref.3) | copy-start | bytes 7077892
  55.4 12.8 %copy-start.14 = (bf16[1,1024,768]{2,1,0:T(8,128)(2,1)S(1)}, bf16[1,1024,768]{2,1,0:T(8,128)(2,1)}, u32[]{:S(2)}) copy-start(bf16[1,1024,768]{2,1,0:T(8,128)(2,1)} %param.16) | copy-start | bytes 4718596
  55.4 12.8 %copy-start.53 = (s32[1,8]{1,0:T(1,128)S(1)}, s32[1,8]{1,0:T(1,128)}, u32[]{:S(2)}) copy-start(s32[1,8]{1,0:T(1,128)} %lengths_ref.11) | copy-start | bytes 100
  55.4 12.8 %copy-start.54 = (f32[1536]{0:T(1024)S(1)}, f32[1536]{0:T(1024)}, u32[]{:S(2)}) copy-start(f32[1536]{0:T(1024)} %gain_ref.6) | copy-start | bytes 18436
  55.4 12.8 %copy-start.55 = (f32[24]{0:T(128)S(1)}, f32[24]{0:T(128)}, u32[]{:S(2)}) copy-start(f32[24]{0:T(128)} %skip_ref.3) | copy-start | bytes 292
  68.2 25.2 %copy-start.64 = (bf16[1,1024,768]{2,1,0:T(8,128)(2,1)S(1)}, bf16[1,1024,768]{2,1,0:T(8,128)(2,1)}, u32[]{:S(2)}) copy-start(bf16[1,1024,768]{2,1,0:T(8,128)(2,1)} %param.28) | copy-start | bytes 4718596
  103.9 6.7 %collective-permute-start.2 = (bf16[64,1536]{1,0:T(8,128)(2,1)}, bf16[64,1536]{1,0:T(8,128)(2,1)S(1)}, u32[]{:S(2)}, u32[]{:S(2)}) collective-permute-start(bf16[64,1536]{1,0:T(8,128)(2,1)} %copy-done.66), channel_id=1, source_target_pairs={{0,16},{16,0},{1,17},{17,1},{2,18},{18,2},{3,19},{19,3},{4,20},{20... | collective-permute-start | bytes 589832 | tf_op jit(solution)/shard_map/ppermute | solution.py:1230
  128.4 26.9 %copy-start.4 = (bf16[1024,1792]{1,0:T(8,128)(2,1)S(1)}, bf16[1024,1792]{1,0:T(8,128)(2,1)}, u32[]{:S(2)}) copy-start(bf16[1024,1792]{1,0:T(8,128)(2,1)} %copy-done.3) | copy-start | bytes 11010052
  128.4 26.9 %copy-start.25 = (bf16[768,1024]{1,0:T(8,128)(2,1)S(1)}, bf16[768,1024]{1,0:T(8,128)(2,1)}, u32[]{:S(2)}) copy-start(bf16[768,1024]{1,0:T(8,128)(2,1)} %copy-done.24) | copy-start | bytes 4718596
  128.4 26.9 %copy-start.43 = (f32[48,1024]{1,0:T(8,128)S(1)}, f32[48,1024]{1,0:T(8,128)}, u32[]{:S(2)}) copy-start(f32[48,1024]{1,0:T(8,128)} %copy-done.42) | copy-start | bytes 589828
  128.4 26.9 %copy-start.45 = (f32[48,1024]{1,0:T(8,128)S(1)}, f32[48,1024]{1,0:T(8,128)}, u32[]{:S(2)}) copy-start(f32[48,1024]{1,0:T(8,128)} %copy-done.44) | copy-start | bytes 589828
  128.4 26.9 %copy-start.47 = (bf16[768,16]{1,0:T(8,128)(2,1)S(1)}, bf16[768,16]{1,0:T(8,128)(2,1)}, u32[]{:S(2)}) copy-start(bf16[768,16]{1,0:T(8,128)(2,1)} %copy-done.46) | copy-start | bytes 73732
  128.4 26.9 %copy-start.49 = (f32[48,1024]{1,0:T(8,128)S(1)}, f32[48,1024]{1,0:T(8,128)}, u32[]{:S(2)}) copy-start(f32[48,1024]{1,0:T(8,128)} %copy-done.48) | copy-start | bytes 589828
  155.3 23.0 %copy-start.58 = (bf16[1024,1536]{1,0:T(8,128)(2,1)S(1)}, bf16[1024,1536]{1,0:T(8,128)(2,1)}, u32[]{:S(2)}) copy-start(bf16[1024,1536]{1,0:T(8,128)(2,1)} %copy-done.57) | copy-start | bytes 9437188
  155.3 23.0 %copy-start.60 = (bf16[768,1536]{1,0:T(8,128)(2,1)S(1)}, bf16[768,1536]{1,0:T(8,128)(2,1)}, u32[]{:S(2)}) copy-start(bf16[768,1536]{1,0:T(8,128)(2,1)} %wz_ref.3) | copy-start | bytes 7077892
  155.4 23.0 %copy-start.62 = (bf16[768,1536]{1,0:T(8,128)(2,1)S(1)}, bf16[768,1536]{1,0:T(8,128)(2,1)}, u32[]{:S(2)}) copy-start(bf16[768,1536]{1,0:T(8,128)(2,1)} %wx_ref.3) | copy-start | bytes 7077892
  155.4 23.0 %copy-start.65 = (bf16[1,1024,768]{2,1,0:T(8,128)(2,1)S(1)}, bf16[1,1024,768]{2,1,0:T(8,128)(2,1)}, u32[]{:S(2)}) copy-start(bf16[1,1024,768]{2,1,0:T(8,128)(2,1)} %param.28) | copy-start | bytes 4718596
  170.2 3.5 %collective-permute-start.4 = (bf16[384,2048]{1,0:T(8,128)(2,1)S(1)}, bf16[384,2048]{1,0:T(8,128)(2,1)S(1)}, u32[]{:S(2)}, u32[]{:S(2)}) collective-permute-start(bf16[384,2048]{1,0:T(8,128)(2,1)S(1)} %get-tuple-element.111), channel_id=1, source_target_pairs={{0,1},{1,0},{2,3},{3,2},{4,5},{5,4},{6,7},{7,6},{8,9},{9,8},{10,11... | collective-permute-start | bytes 4718600 | tf_op jit(solution)/shard_map/ppermute | solution.py:993
  170.2 8.1 %collective-permute-start.3 = (bf16[16,1792]{1,0:T(8,128)(2,1)S(1)}, bf16[16,1792]{1,0:T(8,128)(2,1)S(1)}, u32[]{:S(2)}, u32[]{:S(2)}) collective-permute-start(bf16[16,1792]{1,0:T(8,128)(2,1)S(1)} %get-tuple-element.104), channel_id=1, source_target_pairs={{16,0},{17,1},{18,2},{19,3},{20,4},{21,5},{22,6},{23,7},{24,8},{25... | collective-permute-start | bytes 172040 | tf_op jit(solution)/shard_map/ppermute | solution.py:1381
  174.9 24.3 %collective-permute-start.5 = (bf16[192,1024]{1,0:T(8,128)(2,1)}, bf16[192,1024]{1,0:T(8,128)(2,1)S(1)}, u32[]{:S(2)}, u32[]{:S(2)}) collective-permute-start(bf16[192,1024]{1,0:T(8,128)(2,1)} %get-tuple-element.113), channel_id=1, source_target_pairs={{0,16},{16,0},{1,17},{17,1},{2,18},{18,2},{3,19},{19,3},{4,20},{20... | collective-permute-start | bytes 1179656 | tf_op jit(solution)/shard_map/ppermute | solution.py:993
  176.7 22.6 %collective-permute-start.6 = (bf16[192,1024]{1,0:T(8,128)(2,1)}, bf16[192,1024]{1,0:T(8,128)(2,1)S(1)}, u32[]{:S(2)}, u32[]{:S(2)}) collective-permute-start(bf16[192,1024]{1,0:T(8,128)(2,1)} %get-tuple-element.114), channel_id=1, source_target_pairs={{0,2},{1,3},{2,0},{3,1},{4,6},{5,7},{6,4},{7,5},{8,10},{9,11},{10,... | collective-permute-start | bytes 1179656 | tf_op jit(solution)/shard_map/ppermute | solution.py:993
  178.1 21.1 %collective-permute-start.7 = (bf16[192,1024]{1,0:T(8,128)(2,1)}, bf16[192,1024]{1,0:T(8,128)(2,1)S(1)}, u32[]{:S(2)}, u32[]{:S(2)}) collective-permute-start(bf16[192,1024]{1,0:T(8,128)(2,1)} %get-tuple-element.115), channel_id=1, source_target_pairs={{0,18},{1,19},{2,16},{3,17},{4,22},{5,23},{6,20},{7,21},{8,26},{9,... | collective-permute-start | bytes 1179656 | tf_op jit(solution)/shard_map/ppermute | solution.py:1454
  187.2 1.9 collective-permute-start.13
  187.2 31.8 %copy-start.41 = (bf16[48,3072]{1,0:T(8,128)(2,1)S(1)}, bf16[48,3072]{1,0:T(8,128)(2,1)}, u32[]{:S(2)}) copy-start(bf16[48,3072]{1,0:T(8,128)(2,1)} %reduce-scatter.2.cloned.1.call-done.early_ref) | copy-start | bytes 884740
  187.2 31.8 %collective-permute-start.12 = (bf16[48,3072]{1,0:T(8,128)(2,1)}, bf16[48,3072]{1,0:T(8,128)(2,1)S(1)}, u32[]{:S(2)}, u32[]{:S(2)}) collective-permute-start(bf16[48,3072]{1,0:T(8,128)(2,1)} %reduce-scatter.2.cloned.1.call-done.early_ref), channel_id=1, source_target_pairs={{0,16},{16,0},{1,17},{17,1},{2,18},{18,2},{3,19},{19,3},{4,20},{20... | collective-permute-start | bytes 884744 | tf_op jit(solution)/shard_map/ppermute | solution.py:993
  189.1 8.5 %collective-permute-start.14 = (f32[8,2048]{1,0:T(8,128)S(1)}, f32[8,2048]{1,0:T(8,128)S(1)}, u32[]{:S(2)}, u32[]{:S(2)}) collective-permute-start(f32[8,2048]{1,0:T(8,128)S(1)} %add.17), channel_id=1, source_target_pairs={{0,2},{1,3},{2,0},{3,1},{4,6},{5,7},{6,4},{7,5},{8,10},{9,11},{10,... | collective-permute-start | bytes 196616 | tf_op jit(solution)/shard_map/ppermute | solution.py:993
  197.6 6.3 %collective-permute-start.15 = (f32[8,2048]{1,0:T(8,128)S(1)}, f32[8,2048]{1,0:T(8,128)S(1)}, u32[]{:S(2)}, u32[]{:S(2)}) collective-permute-start(f32[8,2048]{1,0:T(8,128)S(1)} %add.18), channel_id=1, source_target_pairs={{0,4},{1,5},{2,6},{3,7},{4,0},{5,1},{6,2},{7,3},{8,12},{9,13},{10,... | collective-permute-start | bytes 196616 | tf_op jit(solution)/shard_map/ppermute | solution.py:993
  199.4 6.3 %collective-permute-start.8 = (bf16[48,1024]{1,0:T(8,128)(2,1)S(1)}, bf16[48,1024]{1,0:T(8,128)(2,1)S(1)}, u32[]{:S(2)}, u32[]{:S(2)}) collective-permute-start(bf16[48,1024]{1,0:T(8,128)(2,1)S(1)} %get-tuple-element.117), channel_id=1, source_target_pairs={{0,4},{1,5},{2,6},{3,7},{4,0},{5,1},{6,2},{7,3},{8,12},{9,13},{10,... | collective-permute-start | bytes 294920 | tf_op jit(solution)/shard_map/ppermute | solution.py:993
  199.9 7.3 %collective-permute-start.9 = (bf16[48,1024]{1,0:T(8,128)(2,1)S(1)}, bf16[48,1024]{1,0:T(8,128)(2,1)S(1)}, u32[]{:S(2)}, u32[]{:S(2)}) collective-permute-start(bf16[48,1024]{1,0:T(8,128)(2,1)S(1)} %get-tuple-element.118), channel_id=1, source_target_pairs={{0,8},{1,9},{2,10},{3,11},{4,12},{5,13},{6,14},{7,15},{8,0},{9,1},... | collective-permute-start | bytes 294920 | tf_op jit(solution)/shard_map/ppermute | solution.py:993
  202.4 8.5 %collective-permute-start.10 = (bf16[48,1024]{1,0:T(8,128)(2,1)S(1)}, bf16[48,1024]{1,0:T(8,128)(2,1)S(1)}, u32[]{:S(2)}, u32[]{:S(2)}) collective-permute-start(bf16[48,1024]{1,0:T(8,128)(2,1)S(1)} %get-tuple-element.119), channel_id=1, source_target_pairs={{0,12},{1,13},{2,14},{3,15},{4,8},{5,9},{6,10},{7,11},{8,4},{9,5},... | collective-permute-start | bytes 294920 | tf_op jit(solution)/shard_map/ppermute | solution.py:993
  203.9 10.7 %collective-permute-start.16 = (f32[8,2048]{1,0:T(8,128)S(1)}, f32[8,2048]{1,0:T(8,128)S(1)}, u32[]{:S(2)}, u32[]{:S(2)}) collective-permute-start(f32[8,2048]{1,0:T(8,128)S(1)} %add.19), channel_id=1, source_target_pairs={{0,8},{1,9},{2,10},{3,11},{4,12},{5,13},{6,14},{7,15},{8,0},{9,1},... | collective-permute-start | bytes 196616 | tf_op jit(solution)/shard_map/ppermute | solution.py:993
  211.0 8.0 %collective-permute-start.11 = (bf16[48,1024]{1,0:T(8,128)(2,1)S(1)}, bf16[48,1024]{1,0:T(8,128)(2,1)S(1)}, u32[]{:S(2)}, u32[]{:S(2)}) collective-permute-start(bf16[48,1024]{1,0:T(8,128)(2,1)S(1)} %last.1.late_ref), channel_id=1, source_target_pairs={{0,16},{16,0},{1,17},{17,1},{2,18},{18,2},{3,19},{19,3},{4,20},{20... | collective-permute-start | bytes 294920 | tf_op jit(solution)/shard_map/ppermute | solution.py:993
  214.6 4.3 %collective-permute-start.17 = (f32[8,2048]{1,0:T(8,128)S(1)}, f32[8,2048]{1,0:T(8,128)S(1)}, u32[]{:S(2)}, u32[]{:S(2)}) collective-permute-start(f32[8,2048]{1,0:T(8,128)S(1)} %add.20), channel_id=1, source_target_pairs={{0,16},{16,0},{1,17},{17,1},{2,18},{18,2},{3,19},{19,3},{4,20},{20... | collective-permute-start | bytes 196616 | tf_op jit(solution)/shard_map/ppermute | solution.py:993
  (45 other events, 148.0 us)
Sparse Core Ops, SparseCore 0:
  104.0 77.3 reduce-scatter.1

commit v2 on v1

--- a/solution.py
+++ b/solution.py
@@ -17,15 +17,24 @@
 LOG2E = 1.4426950408889634
 SWAP = [(0, 1), (1, 0)]
 MIB = 1024 * 1024
-VMEM_GATES = 18
-VMEM_PROJ = 20
+VMEM_GATES = 56
+VMEM_PROJ = 56
 VMEM_INTRA = 12
-VMEM_MIX = 28
-VMEM_WEIGHTS = 16
-VMEM_BACK = 20
-VMEM_CONV = 20
-VMEM_INPUTS = 20
+VMEM_MIX = 56
+VMEM_WEIGHTS = 56
+VMEM_BACK = 56
+VMEM_CONV = 56
+VMEM_INPUTS = 56
 VMEM_SUMS = 8
+US_GATES = 10
+US_PROJ = 20
+US_INTRA = 12
+US_MIX = 35
+US_WEIGHTS = 10
+US_BACK = 30
+US_CONV = 17
+US_INPUTS = 12
+US_SUMS = 2
 NT = (((1,), (1,)), ((), ()))
 TN = (((0,), (0,)), ((), ()))
 EXACT = lax.Precision.HIGHEST
@@ -60,6 +69,12 @@
     for bound in bounds:
         start = jnp.where(row >= bound, bound, start)
     return start
+
+
+def same_sequence(first, bounds):
+    starts = start_of(first + lane_iota(CHUNK), bounds)
+    turned = jnp.broadcast_to(starts.astype(F32), (8, CHUNK)).T[:, 0:1]
+    return (turned == starts.astype(F32)) & (row_iota(CHUNK) != lane_iota(CHUNK))
 
 
 def row_iota(count):
@@ -100,22 +115,18 @@
     return column
 
 
-def gates_kernel(
+def gates_kernel(normed_ref, c_ref, wz_ref, wo_ref, z_ref, dnorm_ref, turned_ref):
+    turned_ref[...] = normed_ref[...].T
+    z_ref[...] = mm(normed_ref[...], wz_ref[...]).astype(BF16)
+    dnorm_ref[...] = mm_nt(c_ref[...], wo_ref[...]).astype(BF16)
+
+
+def step_factors(
     lengths_ref,
     bias_ref,
     alog_ref,
-    x_ref,
-    c_ref,
-    gain_ref,
-    wz_ref,
-    wo_ref,
-    wbc_ref,
     e0_ref,
     e1_ref,
-    normed_ref,
-    turned_ref,
-    z_ref,
-    dnorm_ref,
     raw_ref,
     dt_ref,
     rate_ref,
@@ -124,105 +135,101 @@
     factors_ref,
     keeps_ref,
 ):
-    step = pl.program_id(0)
-    model = x_ref.shape[1]
-    steps = raw_ref.shape[0]
+    steps, count = raw_ref.shape
     heads = steps // 2
-    count = raw_ref.shape[1]
-    x = x_ref[...].astype(F32)
-    inv = lax.rsqrt(jnp.mean(x * x, axis=1, keepdims=True) + EPS)
-    normed = (x * inv * row_of(gain_ref)).astype(BF16)
-    normed_ref[...] = normed
-    turned_ref[...] = normed.T
-    z_ref[...] = mm(normed, wz_ref[...]).astype(BF16)
-    dnorm_ref[...] = mm_nt(c_ref[...], wo_ref[...]).astype(BF16)
-    raw = mm(normed, wbc_ref[:, wbc_ref.shape[1] - steps :]).astype(BF16).astype(F32).T
-    raw_ref[:, pl.ds(pl.multiple_of(step * ROWS, ROWS), ROWS)] = raw
-
-    @pl.when(step == pl.num_programs(0) - 1)
-    def _():
-        bounds, base = sequence_bounds(lengths_ref, count)
-        rate = jnp.exp(column_of(alog_ref, steps))
-        rate_ref[...] = jnp.broadcast_to(rate, (steps, 128))
-        raw = raw_ref[...] + column_of(bias_ref, steps)
-        raw_ref[...] = raw
-        dt = jnp.maximum(raw, 0.0) + jnp.log1p(jnp.exp(-jnp.abs(raw)))
-        dt_ref[...] = dt
-        log_dt = jnp.log(jnp.maximum(dt, 1e-37))
-        chunks = count // CHUNK
-        upto = flag(row_iota(CHUNK) <= lane_iota(CHUNK))
-        fall = dt * rate
-        stacked = [fall[:, chunk * CHUNK : (chunk + 1) * CHUNK] for chunk in range(chunks)]
-        summed = exact_mm(jnp.concatenate(stacked, axis=0), upto)
-        lane = lane_iota(CHUNK)
-        keeps = jnp.zeros((steps, CHUNK), F32)
-        for chunk in range(chunks):
-            span = slice(chunk * CHUNK, (chunk + 1) * CHUNK)
-            first = base + chunk * CHUNK
-            inc = summed[chunk * steps : (chunk + 1) * steps]
-            dt_c, log_c = dt[:, span], log_dt[:, span]
-            inc0 = inc[:heads]
-            exc1 = inc[heads:] - fall[heads:, span]
-            total0 = inc0[:, CHUNK - 1 :]
-            total1 = inc[heads:, CHUNK - 1 :]
-            target = jnp.concatenate([-inc0, exc1], axis=0) * LOG2E
-            source = jnp.concatenate([inc0 + log_c[:heads], log_c[heads:] - exc1], axis=0) * LOG2E
-            target_ref[:, span] = target
-            source_ref[:, span] = source
-            starts = start_of(first + lane, bounds)
-            before = start_of(first - 1, bounds)
-            left = start_of(first, bounds)
-            right = start_of(first + CHUNK - 1, bounds)
-            after = start_of(first + CHUNK, bounds)
-            enter0 = jnp.where(starts == before, jnp.exp(-inc0), 0.0)
-            enter1 = jnp.where(starts == after, jnp.exp(exc1 - total1), 0.0)
-            leave0 = jnp.where(starts == right, dt_c[:heads] * jnp.exp(inc0 - total0), 0.0)
-            leave1 = jnp.where(starts == left, dt_c[heads:] * jnp.exp(-exc1), 0.0)
-            enter = jnp.concatenate([enter0, enter1], axis=0)
-            leave = jnp.concatenate([leave0, leave1], axis=0)
-            factors_ref[0, span, :] = in_parts(enter, 2).T.astype(BF16)
-            factors_ref[1, span, :] = in_parts(leave, 2).T.astype(BF16)
-            keep0 = jnp.where(before == right, jnp.exp(-total0), 0.0)
-            keep1 = jnp.where(after == left, jnp.exp(-total1), 0.0)
-            keeps = jnp.where(lane == chunk, jnp.concatenate([keep0, keep1], axis=0), keeps)
-        ahead = jnp.zeros_like(keeps)
-        behind = jnp.zeros_like(keeps)
-        run_a = jnp.ones((steps, 1), F32)
-        run_b = jnp.ones((steps, 1), F32)
-        for chunk in range(chunks):
-            ahead = jnp.where(lane == chunk, run_a, ahead)
-            run_a = run_a * keeps[:, chunk : chunk + 1]
-            last = chunks - 1 - chunk
-            behind = jnp.where(lane == last, run_b, behind)
-            run_b = run_b * keeps[:, last : last + 1]
-        for place, values in enumerate((keeps, ahead, behind)):
-            columns = in_parts(values, 2).T.astype(BF16)[0:16]
-            keeps_ref[2 * place] = mm(columns, e0_ref[...])[0:chunks]
-            keeps_ref[2 * place + 1] = mm(columns, e1_ref[...])[0:chunks]
-
-
-def shifts(places, sign, height):
-    row = lax.broadcasted_iota(jnp.int32, (height, 2 * CHUNK), 0)
-    col = lax.broadcasted_iota(jnp.int32, (height, 2 * CHUNK), 1)
+    bounds, base = sequence_bounds(lengths_ref, count)
+    rate = jnp.exp(column_of(alog_ref, steps))
+    rate_ref[...] = jnp.broadcast_to(rate, (steps, 128))
+    raw = raw_ref[...] + column_of(bias_ref, steps)
+    raw_ref[...] = raw
+    dt = jnp.maximum(raw, 0.0) + jnp.log1p(jnp.exp(-jnp.abs(raw)))
+    dt_ref[...] = dt
+    log_dt = jnp.log(jnp.maximum(dt, 1e-37))
+    chunks = count // CHUNK
+    upto = flag(row_iota(CHUNK) <= lane_iota(CHUNK))
+    fall = dt * rate
+    stacked = [fall[:, chunk * CHUNK : (chunk + 1) * CHUNK] for chunk in range(chunks)]
+    summed = exact_mm(jnp.concatenate(stacked, axis=0), upto)
+    lane = lane_iota(CHUNK)
+    keeps = jnp.zeros((steps, CHUNK), F32)
+    for chunk in range(chunks):
+        span = slice(chunk * CHUNK, (chunk + 1) * CHUNK)
+        first = base + chunk * CHUNK
+        inc = summed[chunk * steps : (chunk + 1) * steps]
+        dt_c, log_c = dt[:, span], log_dt[:, span]
+        inc0 = inc[:heads]
+        exc1 = inc[heads:] - fall[heads:, span]
+        total0 = inc0[:, CHUNK - 1 :]
+        total1 = inc[heads:, CHUNK - 1 :]
+        target = jnp.concatenate([-inc0, exc1], axis=0) * LOG2E
+        source = jnp.concatenate([inc0 + log_c[:heads], log_c[heads:] - exc1], axis=0) * LOG2E
+        target_ref[:, span] = target
+        source_ref[:, span] = source
+        starts = start_of(first + lane, bounds)
+        before = start_of(first - 1, bounds)
+        left = start_of(first, bounds)
+        right = start_of(first + CHUNK - 1, bounds)
+        after = start_of(first + CHUNK, bounds)
+        enter0 = jnp.where(starts == before, jnp.exp(-inc0), 0.0)
+        enter1 = jnp.where(starts == after, jnp.exp(exc1 - total1), 0.0)
+        leave0 = jnp.where(starts == right, dt_c[:heads] * jnp.exp(inc0 - total0), 0.0)
+        leave1 = jnp.where(starts == left, dt_c[heads:] * jnp.exp(-exc1), 0.0)
+        enter = jnp.concatenate([enter0, enter1], axis=0)
+        leave = jnp.concatenate([leave0, leave1], axis=0)
+        factors_ref[0, span, :] = in_parts(enter, 2).T.astype(BF16)
+        factors_ref[1, span, :] = in_parts(leave, 2).T.astype(BF16)
+        keep0 = jnp.where(before == right, jnp.exp(-total0), 0.0)
+        keep1 = jnp.where(after == left, jnp.exp(-total1), 0.0)
+        keeps = jnp.where(lane == chunk, jnp.concatenate([keep0, keep1], axis=0), keeps)
+    ahead = jnp.zeros_like(keeps)
+    behind = jnp.zeros_like(keeps)
+    run_a = jnp.ones((steps, 1), F32)
+    run_b = jnp.ones((steps, 1), F32)
+    for chunk in range(chunks):
+        ahead = jnp.where(lane == chunk, run_a, ahead)
+        run_a = run_a * keeps[:, chunk : chunk + 1]
+        last = chunks - 1 - chunk
+        behind = jnp.where(lane == last, run_b, behind)
+        run_b = run_b * keeps[:, last : last + 1]
+    for place, values in enumerate((keeps, ahead, behind)):
+        columns = in_parts(values, 2).T.astype(BF16)[0:16]
+        keeps_ref[2 * place] = mm(columns, e0_ref[...])[0:chunks]
+        keeps_ref[2 * place + 1] = mm(columns, e1_ref[...])[0:chunks]
+
+
+def shifts(first, bounds, sign, height):
+    row = lax.broadcasted_iota(jnp.int32, (height, CHUNK + 16), 0)
+    col = lane_iota(CHUNK + 16)
     parts = []
     for lag in (1, 2, 3):
-        wanted = {-1: row + CHUNK - lag, 1: row + lag, 0: row - height + lag}[sign]
-        parts.append(flag((col == wanted) & (places[lag - 1] >= lag)))
+        later = first + col + (lag - 16 if sign < 0 else 0)
+        near = later - start_of(later, bounds) < lag
+        place = jnp.where(near, -CHUNK, col)
+        offset = {-1: 16 - lag, 1: lag, 0: lag - height}[sign]
+        parts.append(flag(place == row + offset))
     return jnp.concatenate(parts, axis=0).astype(BF16)
 
 
 def proj_kernel(
     lengths_ref,
-    normed_ref,
+    bias_ref,
+    alog_ref,
+    x_ref,
     halo_ref,
     gain_ref,
     wx_ref,
     wbc_ref,
     taps_ref,
+    e0_ref,
+    e1_ref,
+    normed_ref,
+    raw_ref,
+    dt_ref,
+    rate_ref,
+    target_ref,
+    source_ref,
     factors_ref,
     keeps_ref,
-    e0_ref,
-    e1_ref,
     pre_ref,
     act_ref,
     slope_ref,
@@ -246,42 +253,67 @@
 
     @pl.when(step == 0)
     def _():
+        count = x_ref.shape[0]
+        gain = row_of(gain_ref)
+
+        @pl.loop(0, count // CHUNK, unroll=4)
+        def _(chunk):
+            rows = pl.ds(pl.multiple_of(chunk * CHUNK, CHUNK), CHUNK)
+            x = x_ref[rows, :].astype(F32)
+            inv = lax.rsqrt(jnp.mean(x * x, axis=1, keepdims=True) + EPS)
+            normed = (x * inv * gain).astype(BF16)
+            normed_ref[rows, :] = normed
+            raw = mm_nt(wbc_ref[channels - inner :, :], normed)
+            raw_ref[:, rows] = raw.astype(BF16).astype(F32)
+
+        step_factors(
+            lengths_ref,
+            bias_ref,
+            alog_ref,
+            e0_ref,
+            e1_ref,
+            raw_ref,
+            dt_ref,
+            rate_ref,
+            target_ref,
+            source_ref,
+            factors_ref,
+            keeps_ref,
+        )
         x = halo_ref[...].astype(F32)
         inv = lax.rsqrt(jnp.mean(x * x, axis=1, keepdims=True) + EPS)
-        normed = x * inv * row_of(gain_ref)
+        normed = x * inv * gain
         turnhalo_ref[...] = normed.T.astype(BF16)
         normed = normed.astype(BF16)
-        buf[0 : CHUNK - 16, :] = jnp.zeros((CHUNK - 16, channels), BF16)
         prehalo_ref[:, 0:inner] = mm(normed, wx_ref[...]).astype(BF16)
-        prehalo_ref[:, inner:channels] = mm(normed, wbc_ref[:, 0 : channels - inner]).astype(BF16)
-        buf[CHUNK - 16 : CHUNK, :] = prehalo_ref[...]
+        prehalo_ref[:, inner:channels] = mm_nt(normed, wbc_ref[0 : channels - inner, :]).astype(BF16)
+        buf[0:16, :] = prehalo_ref[...]
         acc0[...] = jnp.zeros_like(acc0)
         acc1[...] = jnp.zeros_like(acc1)
 
     @pl.when(step > 0)
     def _():
-        buf[CHUNK - 16 : CHUNK, :] = buf[ROWS + CHUNK - 16 : ROWS + CHUNK, :]
-
-    normed = normed_ref[...]
+        buf[0:16, :] = buf[ROWS : ROWS + 16, :]
+
+    normed = normed_ref[pl.ds(pl.multiple_of(step * ROWS, ROWS), ROWS), :]
     for tile in range(inner // 256):
         cols = slice(tile * 256, tile * 256 + 256)
         px = mm(normed, wx_ref[:, cols]).astype(BF16)
         pre_ref[:, cols] = px
-        buf[CHUNK : CHUNK + ROWS, cols] = px
-    pb = mm(normed, wbc_ref[:, 0 : channels - inner]).astype(BF16)
+        buf[16 : 16 + ROWS, cols] = px
+    pb = mm_nt(normed, wbc_ref[0 : channels - inner, :]).astype(BF16)
     pre_ref[:, inner:channels] = pb
-    buf[CHUNK : CHUNK + ROWS, inner:channels] = pb
+    buf[16 : 16 + ROWS, inner:channels] = pb
 
     first = base + step * ROWS
     for part in range(per):
         offset = part * CHUNK
-        rows = first + offset + row_iota(CHUNK)
-        place = rows - start_of(rows, bounds)
-        shift = shifts([place] * 3, -1, CHUNK)
-        leave_cols = factors_ref[0, offset : offset + CHUNK, :]
+        shift = shifts(first + offset, bounds, -1, CHUNK)
+        here = pl.ds(pl.multiple_of(step * ROWS + offset, CHUNK), CHUNK)
+        leave_cols = factors_ref[1, here, :]
         for tile in range(channels // 256):
             wide = slice(tile * 256, tile * 256 + 256)
-            moved = mm(shift, buf[offset : offset + 2 * CHUNK, wide])
+            moved = mm(shift, buf[offset : offset + CHUNK + 16, wide])
             if tile * 256 < inner:
                 leave0 = mm(leave_cols, e0_ref[:, wide])
                 leave1 = mm(leave_cols, e1_ref[:, wide])
@@ -289,7 +321,7 @@
                 cols = slice(tile * 256 + column, tile * 256 + column + 128)
                 cut = slice(column, column + 128)
                 for row in range(0, CHUNK, SUB):
-                    here = buf[offset + CHUNK + row : offset + CHUNK + row + SUB, cols]
+                    here = buf[offset + 16 + row : offset + 16 + row + SUB, cols]
                     conv = here.astype(F32) * taps_ref[3:4, cols]
                     for lag in (1, 2, 3):
                         at = (lag - 1) * CHUNK + row
@@ -326,44 +358,18 @@
     return jnp.concatenate([jnp.where(first, values, zero), jnp.where(first, zero, values)], axis=0)
 
 
-def intra_kernel(lengths_ref, act_ref, target_ref, source_ref, y_ref, *, heads, state):
-    bounds, base = sequence_bounds(lengths_ref, pl.num_programs(0) * CHUNK)
-    first = base + pl.program_id(0) * CHUNK
-    inner = y_ref.shape[1]
-    width = inner // heads
-    t, s = row_iota(CHUNK), lane_iota(CHUNK)
-    lower = t > s
-    same = (start_of(first + t, bounds) == start_of(first + s, bounds)) & (t != s)
-    b0, c0, b1, c1 = bc_columns(act_ref, inner, state)
-    scores = jnp.where(lower, mm_nt(c0, b0), mm_nt(c1, b1))
-    scores = jnp.where(same, scores, 0.0)
-    columns = target_ref[...].T
-    for pair in range(heads // 2):
-        cols = slice(pair * 2 * width, (pair + 1) * 2 * width)
-        weights = []
-        for head in (2 * pair, 2 * pair + 1):
-            power = jnp.where(
-                lower,
-                columns[:, head : head + 1] + source_ref[head : head + 1, :],
-                columns[:, heads + head : heads + head + 1]
-                + source_ref[heads + head : heads + head + 1, :],
-            )
-            weights.append((jnp.exp2(power) * scores).astype(BF16))
-        x_cut = cut_pair(act_ref[:, cols], width)
-        y_ref[:, cols] = mm(jnp.concatenate(weights, axis=1), x_cut).astype(BF16)
-
-
 def mix_kernel(
     lengths_ref,
     skip_ref,
     x_ref,
     act_ref,
+    target_ref,
+    source_ref,
     factors_ref,
     sl0_ref,
     sf1_ref,
     keeps_ref,
     recv_ref,
-    yin_ref,
     z_ref,
     dnorm_ref,
     wo_ref,
@@ -389,6 +395,7 @@
     enter1,
     from0,
     from1,
+    within,
     gated_s,
     slope_s,
     gate_s,
@@ -433,18 +440,36 @@
     s1_ref[0] = s1
     enter_cols = factors_ref[0]
     turned = act_ref[:, inner:].astype(F32).T.astype(BF16)
-    _, c0, _, c1 = bc_columns(act_ref, inner, state)
+    b0, c0, b1, c1 = bc_columns(act_ref, inner, state)
     enter0[...] = mm(enter_cols, e0_ref[...])
     from0[...] = mm(c0, s0)
     enter1[...] = mm(enter_cols, e1_ref[...])
     from1[...] = mm(c1, s1)
+    t, s = row_iota(CHUNK), lane_iota(CHUNK)
+    lower = t > s
+    scores = jnp.where(lower, mm_nt(c0, b0), mm_nt(c1, b1))
+    scores = jnp.where(same_sequence(first, bounds), scores, 0.0)
+    columns = target_ref[...].T
+    for pair in range(heads // 2):
+        cols = slice(pair * 2 * width, (pair + 1) * 2 * width)
+        weights = []
+        for head in (2 * pair, 2 * pair + 1):
+            power = jnp.where(
+                lower,
+                columns[:, head : head + 1] + source_ref[head : head + 1, :],
+                columns[:, heads + head : heads + head + 1]
+                + source_ref[heads + head : heads + head + 1, :],
+            )
+            weights.append((jnp.exp2(power) * scores).astype(BF16))
+        x_cut = cut_pair(act_ref[:, cols], width)
+        within[:, cols] = mm(jnp.concatenate(weights, axis=1), x_cut)
     tiles = [slice(tile * 128, tile * 128 + 128) for tile in range(inner // 128)]
     for row in range(0, CHUNK, small):
         rows = slice(row, row + small)
         square = jnp.zeros((small, 128), F32)
         cross = jnp.zeros((small, 128), F32)
         for cols in tiles:
-            mixer = yin_ref[rows, cols].astype(F32) + skip_s[:, cols] * act_ref[rows, cols].astype(F32)
+            mixer = within[rows, cols] + skip_s[:, cols] * act_ref[rows, cols].astype(F32)
             mixer = mixer + enter0[rows, cols] * from0[rows, cols]
             mixer = mixer + enter1[rows, cols] * from1[rows, cols]
             z = z_ref[rows, cols].astype(F32)
@@ -567,17 +592,14 @@
     kept_sum = mm_nt(ones, kept_high) + mm_nt(ones, kept_low)
 
     t = lane_iota(CHUNK)
-    starts = start_of(first + t, bounds)
     b0, c0, b1, c1 = bc_columns(act_ref, inner, state)
-    forward = mm_nt(b0, c0)
-    backward = mm_nt(b1, c1)
+    same = same_sequence(first, bounds)
+    both = jnp.where(row_iota(CHUNK) < t, mm_nt(b0, c0), mm_nt(b1, c1))
+    both = jnp.where(same, both, 0.0)
     halves = []
     for row in range(0, CHUNK, SUB):
-        s = row + row_iota(SUB)
-        early = s < t
-        same = (start_of(first + s, bounds) == starts) & (s != t)
-        both = jnp.where(early, forward[row : row + SUB], backward[row : row + SUB])
-        halves.append((slice(row, row + SUB), early, flag(early), jnp.where(same, both, 0.0)))
+        early = row + row_iota(SUB) < t
+        halves.append((slice(row, row + SUB), early, flag(early), both[row : row + SUB]))
     in_cols = source_ref[...].T
     leave_cols = factors_ref[0]
     dscore[...] = jnp.zeros_like(dscore)
@@ -629,15 +651,9 @@
             out1[rows, cols] = (xf * leave1[rows]).astype(BF16)
             prod0[rows, cols] = (xf * came0).astype(BF16)
             prod1[rows, cols] = (xf * came1).astype(BF16)
-    dscore0, dscore1 = [], []
-    for rows, early, _, _ in halves:
-        s = rows.start + row_iota(SUB)
-        same = (start_of(first + s, bounds) == starts) & (s != t)
-        both = jnp.where(same, dscore[rows, :], 0.0)
-        dscore0.append(jnp.where(early, both, 0.0).astype(BF16))
-        dscore1.append(jnp.where(early, 0.0, both).astype(BF16))
-    dscore0 = jnp.concatenate(dscore0, axis=0)
-    dscore1 = jnp.concatenate(dscore1, axis=0)
+    dscores = jnp.where(same, dscore[...], 0.0)
+    dscore0 = jnp.where(row_iota(CHUNK) < t, dscores, 0.0).astype(BF16)
+    dscore1 = jnp.where(row_iota(CHUNK) < t, 0.0, dscores).astype(BF16)
     moves_ref[2 * heads : 3 * heads, :] = mm_nt(spans_ref[...], low_s[...])
     moves_ref[3 * heads : 4 * heads, :] = mm_nt(spans_ref[...], all_s[...])
     moves_ref[4 * heads : 5 * heads, :] = mm_nt(ones, prod0[...])
@@ -683,17 +699,14 @@
     return dlog * ratio + da * rate * sig, jnp.sum(da * dt, axis=1, keepdims=True) * rate
 
 
-def weights_kernel(turned_ref, dz_ref, mixed_ref, c_ref, go_ref, gz_ref, *, half):
-    gz_ref[...] = mm(turned_ref[...], dz_ref[...]).astype(BF16)
+def weights_kernel(turned_ref, dz_ref, mixed_ref, c_ref, both_ref, *, half):
+    model = c_ref.shape[1]
     product = mm_tn(mixed_ref[...], c_ref[...]).astype(BF16)
-    if not half:
-        go_ref[...] = product
-        return
-    model = c_ref.shape[1]
     for shard in range(product.shape[0] // (2 * half)):
         span = slice(shard * half, (shard + 1) * half)
-        go_ref[span, 0:model] = product[2 * shard * half : (2 * shard + 1) * half]
-        go_ref[span, model : 2 * model] = product[(2 * shard + 1) * half : (2 * shard + 2) * half]
+        both_ref[span, 0:model] = product[2 * shard * half : (2 * shard + 1) * half]
+        both_ref[span, model : 2 * model] = product[(2 * shard + 1) * half : (2 * shard + 2) * half]
+    both_ref[:, 2 * model :] = mm(turned_ref[...], dz_ref[...]).astype(BF16)
 
 
 def conv_back_kernel(
@@ -729,16 +742,10 @@
     @pl.when(step == 0)
     def _():
         for chunk in range(chunks):
-            places = []
-            for lag in (1, 2, 3):
-                rows = base + chunk * CHUNK + lag + row_iota(CHUNK)
-                places.append(rows - start_of(rows, bounds))
-            shift[chunk * 3 * CHUNK : (chunk + 1) * 3 * CHUNK, :] = shifts(places, 1, CHUNK)
-        places = []
-        for lag in (1, 2, 3):
-            rows = base + lag - 16 + row_iota(16)
-            places.append(rows - start_of(rows, bounds))
-        shift[chunks * 3 * CHUNK :, :] = shifts(places, 0, 16)
+            shift[chunk * 3 * CHUNK : (chunk + 1) * 3 * CHUNK, :] = shifts(
+                base + chunk * CHUNK, bounds, 1, CHUNK
+            )
+        shift[chunks * 3 * CHUNK :, :] = shifts(base, bounds, 0, 16)
         buf[...] = jnp.zeros_like(buf)
 
     def hand_over(product):
@@ -763,7 +770,7 @@
     @pl.when(step < pl.num_programs(0) - 1)
     def _():
         buf[0:CHUNK, :] = dpre_ref[count - CHUNK :, :]
-        moved = mm(shift[chunks * 3 * CHUNK :, :], dpre_ref[0 : 2 * CHUNK, :])
+        moved = mm(shift[chunks * 3 * CHUNK :, :], dpre_ref[0 : CHUNK + 16, :])
         halo_sums = [None] * 4
         dproj = jnp.zeros((16, wide), F32)
         pre = prehalo_ref[...].astype(F32)
@@ -776,7 +783,7 @@
         sums = [[jnp.zeros((8, 128), F32) for _ in range(4)] for _ in range(wide // 128)]
         for chunk in range(chunks):
             if chunk < chunks - 1:
-                pair = dpre_ref[chunk * CHUNK : chunk * CHUNK + 2 * CHUNK, :]
+                pair = dpre_ref[chunk * CHUNK : chunk * CHUNK + CHUNK + 16, :]
             else:
                 pair = buf[...]
             moved = mm(shift[chunk * 3 * CHUNK : (chunk + 1) * 3 * CHUNK, :], pair)
@@ -837,33 +844,66 @@
             out_ref[rows, :] = total.astype(out_ref.dtype)
 
 
-def levels_kernel(keep_ref, a_ref, b_ref, c_ref, own_ref, s1_ref, s2_ref, s3_ref, *, shard):
+def two_halves(small):
+    half = small.shape[1] // 2
+    return jnp.concatenate([small[:, 0:half], small[:, half:]], axis=0)
+
+
+def levels_kernel(
+    keep_ref, a_ref, b_ref, c_ref, small_ref, own_ref, s1_ref, s2_ref, s3_ref, *, shard
+):
     level = lax.axis_index("dp") // 4
+    parts = in_parts(two_halves(small_ref[...]), 2)
+    few = parts.shape[0] // 2
+    own_ref[shard : shard + few, :] = parts[0:few] + parts[few:]
     for bits, out_ref in enumerate((own_ref, s1_ref, s2_ref, s3_ref)):
         wanted = jnp.bitwise_xor(level, bits)
         rows = pl.ds(pl.multiple_of(wanted * shard, shard), shard)
         total = keep_ref[rows, :] + a_ref[rows, :].astype(F32)
         total = total + (b_ref[rows, :].astype(F32) + c_ref[rows, :].astype(F32))
-        out_ref[...] = total.astype(out_ref.dtype)
-
-
-def last_kernel(own_ref, a_ref, b_ref, c_ref, out_ref):
-    total = own_ref[...] + a_ref[...].astype(F32)
-    total = total + (b_ref[...].astype(F32) + c_ref[...].astype(F32))
-    out_ref[...] = total.astype(BF16)
+        out_ref[0:shard, :] = total.astype(out_ref.dtype)
+        if bits:
+            out_ref[shard : shard + 2 * few, :] = parts.astype(BF16)
+
+
+def joined(ref, shard):
+    few = (ref.shape[0] - shard) // 2
+    small = ref[shard : shard + few, :].astype(F32) + ref[shard + few :, :].astype(F32)
+    return ref[0:shard, :].astype(F32), small
+
+
+def last_kernel(own_ref, a_ref, b_ref, c_ref, out_ref, *, shard):
+    a, b, c = (joined(ref, shard) for ref in (a_ref, b_ref, c_ref))
+    out_ref[0:shard, :] = (own_ref[0:shard, :] + a[0] + (b[0] + c[0])).astype(BF16)
+    small = in_parts(own_ref[shard:, :] + a[1] + (b[1] + c[1]), 2)
+    out_ref[shard:, :] = small.astype(BF16)
 
 
 def finish_kernel(
-    late_ref, lategot_ref, early_ref, earlygot_ref, small_ref, gx_ref, gz_ref, gbc_ref, go_ref,
-    gtaps_ref, gmix_ref, gin_ref, gskip_ref, gbias_ref, galog_ref
+    late_ref,
+    lategot_ref,
+    early_ref,
+    earlygot_ref,
+    gx_ref,
+    gz_ref,
+    gbc_ref,
+    go_ref,
+    gtaps_ref,
+    gmix_ref,
+    gin_ref,
+    gskip_ref,
+    gbias_ref,
+    galog_ref,
 ):
     side = lax.axis_index("dir")
     half = late_ref.shape[1]
     inner = gx_ref.shape[1]
     model = go_ref.shape[1]
     shard = gx_ref.shape[0]
-    first = jnp.where(side == 0, late_ref[...].astype(F32), lategot_ref[...].astype(F32))
-    second = jnp.where(side == 0, lategot_ref[...].astype(F32), late_ref[...].astype(F32))
+    mine, small = joined(late_ref, shard)
+    other, small_other = joined(lategot_ref, shard)
+    first = jnp.where(side == 0, mine, other)
+    second = jnp.where(side == 0, other, mine)
     gx_ref[:, 0:half] = first
     gx_ref[:, half:inner] = second[:, 0 : inner - half]
     gbc_ref[...] = second[:, inner - half : inner - half + gbc_ref.shape[1]]
@@ -871,15 +911,17 @@
     go_ref[0:shard, :] = early[:, 0:model]
     go_ref[shard : 2 * shard, :] = early[:, model : 2 * model]
     gz_ref[...] = early[:, 2 * model :]
-    gtaps_ref[...] = small_ref[0:4, 0 : gtaps_ref.shape[1]]
-    gmix_ref[...] = small_ref[4:5, 0:inner].reshape(inner)
-    gin_ref[...] = small_ref[5:6, 0:model].reshape(model)
+    small = small + small_other
+    small = jnp.concatenate([small[0:8], small[8:16]], axis=1)
+    gtaps_ref[...] = small[0:4, 0 : gtaps_ref.shape[1]]
+    gmix_ref[...] = small[4:5, 0:inner].reshape(inner)
+    gin_ref[...] = small[5:6, 0:model].reshape(model)
     heads = gskip_ref.shape[0]
-    gskip_ref[...] = small_ref[6:7, 0:128].reshape(128)[0:heads]
-    gbias_ref[0:1, :] = small_ref[6:7, 128 : 128 + heads]
-    gbias_ref[1:2, :] = small_ref[6:7, 128 + heads : 128 + 2 * heads]
-    galog_ref[0:1, :] = small_ref[6:7, 256 : 256 + heads]
-    galog_ref[1:2, :] = small_ref[6:7, 256 + heads : 256 + 2 * heads]
+    gskip_ref[...] = small[6:7, 0:128].reshape(128)[0:heads]
+    gbias_ref[0:1, :] = small[6:7, 128 : 128 + heads]
+    gbias_ref[1:2, :] = small[6:7, 128 + heads : 128 + 2 * heads]
+    galog_ref[0:1, :] = small[6:7, 256 : 256 + heads]
+    galog_ref[1:2, :] = small[6:7, 256 + heads : 256 + 2 * heads]
 
 
 def inputs_kernel(
@@ -905,7 +947,7 @@
     model, inner = wx_ref.shape
     steps = draw_ref.shape[0]
     heads = steps // 2
-    narrow = wbc_ref.shape[1] - steps
+    narrow = wbc_ref.shape[0] - steps
     channels = inner + narrow
 
     @pl.when(step == 0)
@@ -925,8 +967,8 @@
 
     dn = mm_nt(dproj[:, 0:inner], wx_ref[...])
     dn = dn + mm_nt(dz_ref[...], wz_ref[...])
-    dn = dn + mm_nt(dproj[:, inner:], wbc_ref[:, 0:narrow])
-    dn = dn + mm_nt(draw_ref[...].astype(F32).T.astype(BF16), wbc_ref[:, narrow:])
+    dn = dn + mm(dproj[:, inner:], wbc_ref[0:narrow, :])
+    dn = dn + mm_tn(draw_ref[...], wbc_ref[narrow:, :])
     x = x_ref[...].astype(F32)
     inv = lax.rsqrt(jnp.mean(x * x, axis=1, keepdims=True) + EPS)
     unit = x * inv
@@ -973,7 +1015,12 @@
     return pl.BlockSpec((count,) + rest, lambda i: (i,) + (0,) * len(rest))
 
 
-def call(kernel, name, grid, in_specs, outs, scratch, flops, moved, args, vmem):
+def cost(microseconds):
+    flops = int(microseconds * 1.15e9)
+    return pl.CostEstimate(flops=flops, bytes_accessed=0, transcendentals=0)
+
+
+def call(kernel, name, grid, in_specs, outs, scratch, cost_us, args, vmem):
     return pl.pallas_call(
         kernel,
         name=name,
@@ -985,12 +1032,16 @@
         compiler_params=pltpu.CompilerParams(
             vmem_limit_bytes=vmem * MIB, dimension_semantics=("arbitrary",)
         ),
-        cost_estimate=pl.CostEstimate(flops=flops, bytes_accessed=moved, transcendentals=0),
+        cost_estimate=cost(cost_us),
     )(*args)
 
 
 def traded(values, axis, bit, size):
     return lax.ppermute(values, axis, [(i, i ^ bit) for i in range(size)])
+
+
+def ordered(first, second):
+    return lax.optimization_barrier((first, second))
 
 
 def sum_shards(grad, dp_count):
@@ -1043,6 +1094,7 @@
     chunks = count // CHUNK
     steps = 2 * heads
 
+    w_narrow = w_bcdt.T
     halo = lax.ppermute(x[count - 16 :], "dir", [(0, 1)])
 
     spread = np.repeat(np.eye(heads, dtype=np.float32), width, axis=1)
@@ -1056,28 +1108,48 @@
     def full(shape, dtype):
         return (pl.BlockSpec(shape, lambda i: (0,) * len(shape)), shape, dtype)
 
-    normed, turned, gate_z, d_norm, raw, dt, rate, target, source, factors, keeps = call(
-        gates_kernel,
-        "gates",
+    per = ROWS // CHUNK
+    state_f32 = pltpu.VMEM((state, inner), F32)
+    state_bf16 = pltpu.VMEM((state, inner), BF16)
+    row_f32 = pltpu.VMEM((1, inner), F32)
+    chunk_f32 = pltpu.VMEM((CHUNK, inner), F32)
+    chunk_bf16 = pltpu.VMEM((CHUNK, inner), BF16)
+    (
+        normed,
+        raw,
+        dt,
+        rate,
+        target,
+        source,
+        factors,
+        keeps,
+        pre,
+        act,
+        slope,
+        sl0,
+        sf1,
+        send,
+        pre_halo,
+        turn_halo,
+    ) = call(
+        proj_kernel,
+        "proj",
         count // ROWS,
         [
             smem(),
             smem(),
             smem(),
-            rows_of(ROWS, model),
-            rows_of(ROWS, model),
+            whole((count, model)),
+            whole((16, model)),
             whole((model,)),
             whole((model, inner)),
-            whole((inner, model)),
-            whole(w_bcdt.shape),
+            whole(w_narrow.shape),
+            whole(conv_w.shape),
             whole(e0.shape),
             whole(e1.shape),
         ],
         [
-            rows_out(ROWS, model, BF16),
-            (lanes_of(model, ROWS), (model, count), BF16),
-            rows_out(ROWS, inner, BF16),
-            rows_out(ROWS, inner, BF16),
+            full((count, model), BF16),
             full((steps, count), F32),
             full((steps, count), F32),
             full((steps, 128), F32),
@@ -1085,38 +1157,6 @@
             full((steps, count), F32),
             full((2, count, 2 * steps), BF16),
             full((6, chunks, inner), F32),
-        ],
-        [],
-        4 * count * model * inner,
-        4 * count * (model + inner) + 4 * model * inner,
-        (lengths, dt_bias, a_log, x, cot, gain_in, w_z, w_out, w_bcdt, e0, e1),
-        VMEM_GATES,
-    )
-
-    per = ROWS // CHUNK
-    state_f32 = pltpu.VMEM((state, inner), F32)
-    state_bf16 = pltpu.VMEM((state, inner), BF16)
-    row_f32 = pltpu.VMEM((1, inner), F32)
-    chunk_f32 = pltpu.VMEM((CHUNK, inner), F32)
-    chunk_bf16 = pltpu.VMEM((CHUNK, inner), BF16)
-    pre, act, slope, sl0, sf1, send, pre_halo, turn_halo = call(
-        proj_kernel,
-        "proj",
-        count // ROWS,
-        [
-            smem(),
-            rows_of(ROWS, model),
-            whole((16, model)),
-            whole((model,)),
-            whole((model, inner)),
-            whole(w_bcdt.shape),
-            whole(conv_w.shape),
-            pl.BlockSpec((1, ROWS, 2 * steps), lambda i: (1, i, 0)),
-            whole((6, chunks, inner)),
-            whole(e0.shape),
-            whole(e1.shape),
-        ],
-        [
             rows_out(ROWS, channels, BF16),
             rows_out(ROWS, channels, BF16),
             rows_out(ROWS, channels, BF16),
@@ -1127,35 +1167,37 @@
             full((model, 16), BF16),
         ],
         [
-            pltpu.VMEM((CHUNK + ROWS, channels), BF16),
+            pltpu.VMEM((16 + ROWS, channels), BF16),
             state_f32,
             state_f32,
             chunk_bf16,
             chunk_bf16,
         ],
-        3 * count * model * inner,
-        8 * count * inner,
-        (lengths, normed, halo, gain_in, w_x, w_bcdt, conv_w, factors, keeps, e0, e1),
+        US_PROJ,
+        (lengths, dt_bias, a_log, x, halo, gain_in, w_x, w_narrow, conv_w, e0, e1),
         VMEM_PROJ,
     )
     received = lax.ppermute(send, "dir", SWAP)
 
-    (y_in,) = call(
-        functools.partial(intra_kernel, heads=heads, state=state),
-        "intra",
-        chunks,
+    gate_z, d_norm, turned = call(
+        gates_kernel,
+        "gates",
+        count // ROWS,
         [
-            smem(),
-            rows_of(CHUNK, channels),
-            lanes_of(steps, CHUNK),
-            lanes_of(steps, CHUNK),
+            rows_of(ROWS, model),
+            rows_of(ROWS, model),
+            whole((model, inner)),
+            whole((inner, model)),
         ],
-        [rows_out(CHUNK, inner, BF16)],
+        [
+            rows_out(ROWS, inner, BF16),
+            rows_out(ROWS, inner, BF16),
+            (lanes_of(model, ROWS), (model, count), BF16),
+        ],
         [],
-        8 * count * CHUNK * inner,
-        6 * count * inner,
-        (lengths, act, target, source),
-        VMEM_INTRA,
+        US_GATES,
+        (normed, cot, w_z, w_out),
+        VMEM_GATES,
     )
 
     def down_rows(width):
@@ -1177,12 +1219,13 @@
             smem(),
             down_rows(model),
             down_rows(channels),
+            down_lanes(steps),
+            down_lanes(steps),
             pl.BlockSpec((1, CHUNK, 2 * steps), lambda i: (0, chunks - 1 - i, 0)),
             down_parts(state, inner),
             down_parts(state, inner),
             whole((6, chunks, inner)),
             whole((state, inner)),
-            down_rows(inner),
             down_rows(inner),
             down_rows(inner),
             whole((inner, model)),
@@ -1204,20 +1247,20 @@
             full((state, inner), BF16),
             full((16, inner), F32),
         ],
-        [state_f32] * 3 + [chunk_f32] * 7 + [chunk_bf16] * 4 + [row_f32] * 2,
-        3 * count * model * inner,
-        16 * count * inner,
+        [state_f32] * 3 + [chunk_f32] * 8 + [chunk_bf16] * 4 + [row_f32] * 2,
+        US_MIX,
         (
             lengths,
             d_skip,
             x,
             act,
+            target,
+            source,
             factors,
             sl0,
             sf1,
             keeps,
             received,
-            y_in,
             gate_z,
             d_norm,
             w_out,
@@ -1232,32 +1275,27 @@
     blocks = 4
     shard = model // dp_count
     half = shard if shard % 16 == 0 else 0
-    out_spec = (
-        (rows_of(model // blocks, inner), (model, inner), BF16)
-        if half
-        else (rows_of(inner // blocks, model), (inner, model), BF16)
-    )
-    g_out, g_z = call(
-        functools.partial(weights_kernel, half=half),
+    (g_early,) = call(
+        functools.partial(weights_kernel, half=half or model // 16),
         "weights",
         blocks,
         [
-            whole((model, count)),
-            lanes_of(count, inner // blocks),
+            rows_of(model // blocks, count),
+            whole((count, inner)),
             lanes_of(count, inner // blocks),
             whole((count, model)),
         ],
-        [out_spec, (lanes_of(model, inner // blocks), (model, inner), BF16)],
+        [(rows_of(model // blocks, 2 * inner), (model, 2 * inner), BF16)],
         [],
-        4 * count * model * inner,
-        6 * count * inner,
+        US_WEIGHTS,
         (turned, dz, mixed, cot),
         VMEM_WEIGHTS,
     )
     if not half:
-        g_out = g_out.reshape(dp_count, 2, shard, model)
-        g_out = g_out.transpose(0, 2, 1, 3).reshape(model, inner)
-    g_early = jnp.concatenate([g_out, g_z], axis=1)
+        g_out = g_early[:, :inner].reshape(16, model // 16, 2, model).transpose(0, 2, 1, 3)
+        g_out = g_out.reshape(dp_count, 2, shard, model).transpose(0, 2, 1, 3)
+        g_early = jnp.concatenate([g_out.reshape(model, inner), g_early[:, inner:]], axis=1)
+    g_early, d_received = ordered(g_early, d_received)
     early = lax.psum_scatter(g_early, "dp", scatter_dimension=0, tiled=True)
 
     def back(skipped, taken, start):
@@ -1308,8 +1346,7 @@
             ]
             + [chunk_bf16] * 4
             + [state_bf16] * 2,
-            24 * taken * CHUNK * CHUNK * inner,
-            16 * taken * CHUNK * inner,
+            US_BACK,
             (
                 lengths,
                 d_skip,
@@ -1370,11 +1407,10 @@
             (lanes_of(8, tile), (8, wide), F32),
         ],
         [
-            pltpu.VMEM((3 * count + 48, 2 * CHUNK), BF16),
-            pltpu.VMEM((2 * CHUNK, tile), BF16),
+            pltpu.VMEM((3 * count + 48, CHUNK + 16), BF16),
+            pltpu.VMEM((CHUNK + 16, tile), BF16),
         ],
-        2 * count * model * channels,
-        6 * count * channels,
+        US_CONV,
         (lengths, turned, turn_halo, dpre, pre, pre_halo, conv_w, raw, dt, rate, moves, r),
         VMEM_CONV,
     )
@@ -1393,7 +1429,7 @@
             lanes_of(steps, ROWS),
             rows_of(ROWS, inner),
             whole((model, inner)),
-            whole(w_bcdt.shape),
+            whole(w_narrow.shape),
             whole((model, inner)),
             whole(mix_sums.shape),
             whole(tap_sums.shape),
@@ -1404,15 +1440,14 @@
             full((8, tap_sums.shape[1]), F32),
         ],
         [pltpu.VMEM((8, model), F32), pltpu.VMEM((ROWS, channels), BF16)],
-        5 * count * model * inner,
-        8 * count * inner,
-        (x, cot, gain_in, dproj, d_halo, draw, dz, w_x, w_bcdt, w_z, mix_sums, tap_sums, e0),
+        US_INPUTS,
+        (x, cot, gain_in, dproj, d_halo, draw, dz, w_x, w_narrow, w_z, mix_sums, tap_sums, e0),
         VMEM_INPUTS,
     )
-    early_got = traded(early, "dir", 1, 2)
-    small = sum_all(small, dp_count)
     if not half or dp_count != 16:
+        small = sum_all(small, dp_count)
         late = sum_shards(mine, dp_count)
+        early_got = traded(early, "dir", 1, 2)
         early = early.astype(F32) + early_got.astype(F32)
         grad_out = jnp.concatenate([early[:, :model], early[:, model:inner]], axis=0)
         return (
@@ -1438,6 +1473,7 @@
             out_specs=[pl.BlockSpec(memory_space=pltpu.VMEM)] * len(outs),
             out_shape=[jax.ShapeDtypeStruct(shape, dtype) for shape, dtype in outs],
             compiler_params=pltpu.CompilerParams(vmem_limit_bytes=VMEM_SUMS * MIB),
+            cost_estimate=cost(US_SUMS),
         )(*args)
 
     got = traded(theirs, "dp", 1, dp_count)
@@ -1456,20 +1492,27 @@
         ("dir", "dp"),
         [(a * dp_count + b, (1 - a) * dp_count + (b ^ 2)) for a, b in corners],
     )
-    piece = (shard, wide // 2)
+    _, both = ordered(small, both)
+    for bit in (1, 2):
+        small = small + traded(small, "dp", bit, dp_count)
+    piece = (shard + 4 * small.shape[0], wide // 2)
     own, *sends = plain(
         functools.partial(levels_kernel, shard=shard),
         "levels",
-        (kept, across, along, both),
-        [(piece, F32)] + [(piece, BF16)] * 3,
+        (kept, across, along, both, small),
+        [((shard + 2 * small.shape[0], wide // 2), F32)] + [(piece, BF16)] * 3,
     )
     gots = [traded(sent, "dp", 4 * bits, dp_count) for bits, sent in zip((1, 2, 3), sends)]
-    (late,) = plain(last_kernel, "last", (own, *gots), [(piece, BF16)])
+    (late,) = plain(
+        functools.partial(last_kernel, shard=shard), "last", (own, *gots), [(piece, BF16)]
+    )
+    early, _ = ordered(early, late)
+    early_got = traded(early, "dir", 1, 2)
     late_got = traded(late, "dir", 1, 2)
     g_x, g_zz, g_bc, g_o, g_taps, g_mix, g_in, g_skip, g_bias, g_alog = plain(
         finish_kernel,
         "finish",
-        (late, late_got, early, early_got, small),
+        (late, late_got, early, early_got),
         [
             ((shard, inner), F32),
             ((shard, inner), F32),

time: 228 us -> 211 us (0.925)
  local copies, waits for them, and re-layouts: 41.8 us -> 5.66 us
  Pallas kernels: 118 us -> 133 us
  waiting for transfers between devices: 24.1 us -> 34.5 us
  starting transfers between devices: 25.8 us -> 20.5 us
    unnamed x149 -> x12, local copies, waits for them, and re-layouts: 41.1 us -> 4.91 us
    pallas_call x8 -> x7, Pallas kernels: 115 us -> 132 us  [call(): pl.pallas_call(kernel, name=name, grid=(grid,), in_specs=in_specs, out_sp...]
    ppermute x13 -> x10, waiting for transfers between devices: 19.5 us -> 33 us  [traded(): return lax.ppermute(values, axis, [(i, i ^ bit) for i in range(size)])]
    ppermute x13 -> x10, starting transfers between devices: 17.2 us -> 11.7 us  [traded(): return lax.ppermute(values, axis, [(i, i ^ bit) for i in range(size)])]
    ppermute x1, waiting for transfers between devices: 4.57 us -> 0.01 us  [local(): d_received = lax.ppermute(d_send, 'dir', SWAP)]
    concatenate x1 -> x0, other arithmetic: 2.78 us -> none  [local(): g_early = jnp.concatenate([g_out, g_z], axis=1)]
    ppermute x1, starting transfers between devices: 0.01 us -> 2.37 us  [local(): received = lax.ppermute(send, 'dir', SWAP)]
  transfers between devices with their start and end apart: 19 -> 16, of which waited for: 8 -> 7; matrix products, arithmetic and copies ran while one was open for 1% -> 0% of each run, Pallas kernels for 32% -> 38%
where the time goes in v2:
time: 211 us; the launch traced here: 209 us
  Pallas kernels  133 us (63%)
  waiting for transfers between devices  34.5 us (16%)
  starting transfers between devices  20.5 us (10%)
  between operations  14.2 us (7%)
  local copies, waits for them, and re-layouts  5.66 us (3%)
    pallas_call x7, Pallas kernels, call(): pl.pallas_call(kernel, name=name, grid=(grid,), in_specs=in_specs, out_sp...  132 us
    ppermute x10, waiting for transfers between devices, traded(): return lax.ppermute(values, axis, [(i, i ^ bit) for i in range(size)])  33 us
    ppermute x10, starting transfers between devices, traded(): return lax.ppermute(values, axis, [(i, i ^ bit) for i in range(size)])  11.7 us
    unnamed x12, local copies, waits for them, and re-layouts  4.91 us
    ppermute x1, starting transfers between devices, local(): halo = lax.ppermute(x[count - 16:], 'dir', [(0, 1)])  4.83 us
  transfers between devices with their start and end apart: 16, of which 7 were waited for; matrix products, arithmetic and copies ran while one was open for 0% of the time, Pallas kernels for 38%

profile of v2, /device:TPU:0, one launch (start us, length us, event | category | flops | bytes accessed | tf_op | source)
XLA Modules:
  0.0 209.0 jit_solution(7745984394375014072)
XLA Ops:
  7.2 0.0 reduce-scatter.2.cloned.1.call-start
  7.2 0.7 slice_bitcast_fusion
  8.0 4.8 %collective-permute-start = (bf16[16,768]{1,0:T(8,128)(2,1)S(1)}, bf16[16,768]{1,0:T(8,128)(2,1)S(1)}, u32[]{:S(2)}, u32[]{:S(2)}) collective-permute-start(bf16[16,768]{1,0:T(8,128)(2,1)S(1)} %slice_bitcast_fusion), channel_id=1, source_target_pairs={{0,16},{1,17},{2,18},{3,19},{4,20},{5,21},{6,22},{7,23},{8,24},{9,... | collective-permute-start | bytes 73736 | tf_op jit(solution)/shard_map/ppermute | solution.py:1098
  12.8 1.5 collective-permute-done.halo_ref
  14.3 0.6 copy-done.5
  14.9 20.8 %proj.1 = (bf16[1024,768]{1,0:T(8,128)(2,1)}, f32[48,1024]{1,0:T(8,128)}, f32[48,1024]{1,0:T(8,128)}, f32[48,128]{1,0:T(8,128)}, f32[48,1024]{1,0:T(8,128)}, /*i...) custom-call(s32[1,8]{1,0:T(1,128)} %lengths_ref.7, ...), custom_call_target="tpu_custom_call" | custom-call | flops 23000000512 | tf_op jit(solution)/shard_map/proj/pallas_call | solution.py:1024
  35.7 2.4 %collective-permute-start.1 = (bf16[64,1536]{1,0:T(8,128)(2,1)}, bf16[64,1536]{1,0:T(8,128)(2,1)S(1)}, u32[]{:S(2)}, u32[]{:S(2)}) collective-permute-start(bf16[64,1536]{1,0:T(8,128)(2,1)} %get-tuple-element.82), channel_id=1, source_target_pairs={{0,16},{16,0},{1,17},{17,1},{2,18},{18,2},{3,19},{19,3},{4,20},{20... | collective-permute-start | bytes 589832 | tf_op jit(solution)/shard_map/ppermute | solution.py:1180
  38.1 9.5 %gates.1 = (bf16[1024,1536]{1,0:T(8,128)(2,1)}, bf16[1024,1536]{1,0:T(8,128)(2,1)}, bf16[768,1024]{1,0:T(8,128)(2,1)}) custom-call(bf16[1024,768]{1,0:T(8,128)(2,1)} %get-tuple-element.83.normed_ref, bf16[1024,768]{1,0:T(8,128)(2,1)} %bitcast.10, bf16[768,1536]{1,0:T(8,128)(2,1)} %wz_ref.3, bf16[1536,768]{1,0:T(8,128)(2,1)} %wo_ref.3), custom_call_target="tpu_custom_call" | custom-call | flops 11500000256 | tf_op jit(solution)/shard_map/gates/pallas_call | solution.py:1024
  47.6 0.0 collective-permute-done.1.recv_ref
  47.6 0.7 copy-done.3
  48.2 33.1 %mix.1 = (bf16[1024,768]{1,0:T(8,128)(2,1)}, bf16[1024,1536]{1,0:T(8,128)(2,1)}, bf16[1024,1536]{1,0:T(8,128)(2,1)}, bf16[1024,1536]{1,0:T(8,128)(2,1)}, f32[48,...) custom-call(s32[1,8]{1,0:T(1,128)} %lengths_ref.7, ...), custom_call_target="tpu_custom_call" | custom-call | flops 40249999360 | tf_op jit(solution)/shard_map/mix/pallas_call | solution.py:1024
  81.4 0.1 collective-permute-start.2
  81.5 9.8 %weights.1 = bf16[768,3072]{1,0:T(8,128)(2,1)} custom-call(bf16[768,1024]{1,0:T(8,128)(2,1)} %get-tuple-element.87.turned_ref, bf16[1024,1536]{1,0:T(8,128)(2,1)} %get-tuple-element.96.dz_ref, bf16[1024,1536]{1,0:T(8,128)(2,1)} %get-tuple-element.97.mixed_ref, bf16[1024,768]{1,0:T(8,128)(2,1)} %bitcast.11), custom_call_target="tpu_custom_call" | custom-call | flops 11500000256 | tf_op jit(solution)/shard_map/weights/pallas_call | solution.py:1024
  91.3 0.0 collective-permute-done.2.recv_ref.start_ref
  91.3 0.0 reduce-scatter.2.cloned.1.call-update
  91.3 0.6 copy-done.2
  91.9 30.0 %back0.1 = (bf16[1024,1792]{1,0:T(8,128)(2,1)}, f32[192,1024]{1,0:T(8,128)}, f32[64,1536]{1,0:T(8,128)}) custom-call(s32[1,8]{1,0:T(1,128)} %lengths_ref.7, f32[24]{0:T(128)} %skip_ref.3, bf16[1024,1792]{1,0:T(8,128)(2,1)} %get-tuple-element.75.act_ref, bf16[1024,1792]{1,0:T(8,128)(2,1)} %get-tuple-element.89.slope_ref, ...), custom_call_target="tpu_custom_call" | custom-call | flops 34500001792 | tf_op jit(solution)/shard_map/back0/pallas_call | solution.py:1024
  122.0 16.1 %conv_back.1 = (bf16[1024,1792]{1,0:T(8,128)(2,1)}, bf16[16,1792]{1,0:T(8,128)(2,1)}, bf16[384,2048]{1,0:T(8,128)(2,1)}, bf16[384,2048]{1,0:T(8,128)(2,1)}, bf16[48,1024]{1,0:T(8,128)(2,1)}, /*index=5*/f32[8,2048]{1,0:T(8,128)}) custom-call(s32[1,8]{1,0:T(1,128)} %lengths_ref.7, bf16[768,1024]{1,0:T(8,128)(2,1)} %get-tuple-element.87.turned_ref, ...), custom_call_target="tpu_custom_call" | custom-call | flops 19549999104 | tf_op jit(solution)/shard_map/conv_back/pallas_call | solution.py:1024
  138.1 0.1 collective-permute-start.4
  138.2 1.3 collective-permute-start.3
  139.5 2.3 %collective-permute-done.4.got_ref = bf16[384,2048]{1,0:T(8,128)(2,1)S(1)} collective-permute-done((bf16[384,2048]{1,0:T(8,128)(2,1)}, bf16[384,2048]{1,0:T(8,128)(2,1)S(1)}, u32[]{:S(2)}, u32[]{:S(2)}) %collective-permute-start.4) | collective-permute-done | bytes 1572896 | tf_op jit(solution)/shard_map/ppermute | solution.py:1040
  141.8 1.4 copy-done.1
  143.2 0.3 quarters.1
  143.5 2.0 collective-permute-start.5
  145.5 1.5 collective-permute-start.6
  147.0 0.1 collective-permute-start.7
  147.1 0.0 collective-permute-done.3.dhalo_ref
  147.1 0.6 copy-done.4
  147.7 12.4 %inputs.1 = (bf16[1024,768]{1,0:T(8,128)(2,1)}, f32[8,2048]{1,0:T(8,128)}) custom-call(bf16[1024,768]{1,0:T(8,128)(2,1)} %bitcast.9, bf16[1024,768]{1,0:T(8,128)(2,1)} %bitcast.12, f32[768]{0:T(1024)} %gain_ref.5, bf16[1024,1792]{1,0:T(8,128)(2,1)} %get-tuple-element.108.dproj_ref, bf16[16,1792]{1,0:T(8,128)(2,1)} %copy-done.4, ...), custom_call_target="tpu_custom_call" | custom-call | flops 13799999488 | tf_op jit(solution)/shard_map/inputs/pallas_call | solution.py:1024
  160.1 0.1 collective-permute-start.8
  160.2 1.5 collective-permute-done.8
  161.7 0.9 add.8
  162.5 1.6 collective-permute-start.9
  164.1 5.2 %collective-permute-done.9 = f32[8,2048]{1,0:T(8,128)S(1)} collective-permute-done((f32[8,2048]{1,0:T(8,128)S(1)}, f32[8,2048]{1,0:T(8,128)S(1)}, u32[]{:S(2)}, u32[]{:S(2)}) %collective-permute-start.9) | collective-permute-done | bytes 65568 | tf_op jit(solution)/shard_map/ppermute | solution.py:1040
  169.4 0.0 collective-permute-done.5.a_ref
  169.4 0.2 levels.1
  169.6 1.6 collective-permute-start.10
  171.2 2.5 %collective-permute-start.11 = (bf16[80,1024]{1,0:T(8,128)(2,1)S(1)}, bf16[80,1024]{1,0:T(8,128)(2,1)S(1)}, u32[]{:S(2)}, u32[]{:S(2)}) collective-permute-start(bf16[80,1024]{1,0:T(8,128)(2,1)S(1)} %get-tuple-element.124), channel_id=1, source_target_pairs={{0,8},{1,9},{2,10},{3,11},{4,12},{5,13},{6,14},{7,15},{8,0},{9,1},... | collective-permute-start | bytes 491528 | tf_op jit(solution)/shard_map/ppermute | solution.py:1040
  173.7 0.3 collective-permute-start.12
  174.0 8.7 %collective-permute-done.10.a_ref = bf16[80,1024]{1,0:T(8,128)(2,1)S(1)} collective-permute-done((bf16[80,1024]{1,0:T(8,128)(2,1)S(1)}, bf16[80,1024]{1,0:T(8,128)(2,1)S(1)}, u32[]{:S(2)}, u32[]{:S(2)}) %collective-permute-start.10) | collective-permute-done | bytes 163872 | tf_op jit(solution)/shard_map/ppermute | solution.py:1040
  182.7 5.8 %collective-permute-done.11.b_ref = bf16[80,1024]{1,0:T(8,128)(2,1)S(1)} collective-permute-done((bf16[80,1024]{1,0:T(8,128)(2,1)S(1)}, bf16[80,1024]{1,0:T(8,128)(2,1)S(1)}, u32[]{:S(2)}, u32[]{:S(2)}) %collective-permute-start.11) | collective-permute-done | bytes 163872 | tf_op jit(solution)/shard_map/ppermute | solution.py:1040
  188.5 0.1 last.1.late_ref
  188.6 0.0 reduce-scatter.2.cloned.1.call-done.early_ref
  188.7 0.5 collective-permute-start.14
  189.1 1.6 collective-permute-start.13
  190.7 9.5 %collective-permute-done.13.lategot_ref = bf16[80,1024]{1,0:T(8,128)(2,1)S(1)} collective-permute-done((bf16[80,1024]{1,0:T(8,128)(2,1)S(1)}, bf16[80,1024]{1,0:T(8,128)(2,1)S(1)}, u32[]{:S(2)}, u32[]{:S(2)}) %collective-permute-start.13) | collective-permute-done | bytes 163872 | tf_op jit(solution)/shard_map/ppermute | solution.py:1040
  200.2 1.0 copy-done
  201.2 1.0 finish.1
  (11 shorter events, 0.0 us)
Async XLA Ops:
  7.2 181.5 %reduce-scatter.2.cloned.1.call-start = ((), (), s32[]{:S(2)}) async-start(), calls=%async_computation.1 | async-start | bytes 5013504 | tf_op jit(solution)/shard_map/reduce_scatter | solution.py:1299
  8.0 6.3 %collective-permute-start = (bf16[16,768]{1,0:T(8,128)(2,1)S(1)}, bf16[16,768]{1,0:T(8,128)(2,1)S(1)}, u32[]{:S(2)}, u32[]{:S(2)}) collective-permute-start(bf16[16,768]{1,0:T(8,128)(2,1)S(1)} %slice_bitcast_fusion), channel_id=1, source_target_pairs={{0,16},{1,17},{2,18},{3,19},{4,20},{5,21},{6,22},{7,23},{8,24},{9,... | collective-permute-start | bytes 73736 | tf_op jit(solution)/shard_map/ppermute | solution.py:1098
  14.3 0.6 copy-start.5
  35.7 11.8 %collective-permute-start.1 = (bf16[64,1536]{1,0:T(8,128)(2,1)}, bf16[64,1536]{1,0:T(8,128)(2,1)S(1)}, u32[]{:S(2)}, u32[]{:S(2)}) collective-permute-start(bf16[64,1536]{1,0:T(8,128)(2,1)} %get-tuple-element.82), channel_id=1, source_target_pairs={{0,16},{16,0},{1,17},{17,1},{2,18},{18,2},{3,19},{19,3},{4,20},{20... | collective-permute-start | bytes 589832 | tf_op jit(solution)/shard_map/ppermute | solution.py:1180
  47.6 0.7 copy-start.3
  81.4 9.9 %collective-permute-start.2 = (bf16[64,1536]{1,0:T(8,128)(2,1)}, bf16[64,1536]{1,0:T(8,128)(2,1)S(1)}, u32[]{:S(2)}, u32[]{:S(2)}) collective-permute-start(bf16[64,1536]{1,0:T(8,128)(2,1)} %get-tuple-element.98), channel_id=1, source_target_pairs={{0,16},{16,0},{1,17},{17,1},{2,18},{18,2},{3,19},{19,3},{4,20},{20... | collective-permute-start | bytes 589832 | tf_op jit(solution)/shard_map/ppermute | solution.py:1273
  91.3 0.7 copy-start.2
  138.1 3.7 %collective-permute-start.4 = (bf16[384,2048]{1,0:T(8,128)(2,1)}, bf16[384,2048]{1,0:T(8,128)(2,1)S(1)}, u32[]{:S(2)}, u32[]{:S(2)}) collective-permute-start(bf16[384,2048]{1,0:T(8,128)(2,1)} %get-tuple-element.115), channel_id=1, source_target_pairs={{0,1},{1,0},{2,3},{3,2},{4,5},{5,4},{6,7},{7,6},{8,9},{9,8},{10,11... | collective-permute-start | bytes 4718600 | tf_op jit(solution)/shard_map/ppermute | solution.py:1040
  138.2 8.9 %collective-permute-start.3 = (bf16[16,1792]{1,0:T(8,128)(2,1)}, bf16[16,1792]{1,0:T(8,128)(2,1)S(1)}, u32[]{:S(2)}, u32[]{:S(2)}) collective-permute-start(bf16[16,1792]{1,0:T(8,128)(2,1)} %get-tuple-element.109), channel_id=1, source_target_pairs={{16,0},{17,1},{18,2},{19,3},{20,4},{21,5},{22,6},{23,7},{24,8},{25... | collective-permute-start | bytes 172040 | tf_op jit(solution)/shard_map/ppermute | solution.py:1417
  141.8 1.4 copy-start.1
  143.5 25.8 %collective-permute-start.5 = (bf16[192,1024]{1,0:T(8,128)(2,1)S(1)}, bf16[192,1024]{1,0:T(8,128)(2,1)S(1)}, u32[]{:S(2)}, u32[]{:S(2)}) collective-permute-start(bf16[192,1024]{1,0:T(8,128)(2,1)S(1)} %get-tuple-element.117), channel_id=1, source_target_pairs={{0,16},{16,0},{1,17},{17,1},{2,18},{18,2},{3,19},{19,3},{4,20},{20... | collective-permute-start | bytes 1179656 | tf_op jit(solution)/shard_map/ppermute | solution.py:1040
  145.5 23.9 %collective-permute-start.6 = (bf16[192,1024]{1,0:T(8,128)(2,1)S(1)}, bf16[192,1024]{1,0:T(8,128)(2,1)S(1)}, u32[]{:S(2)}, u32[]{:S(2)}) collective-permute-start(bf16[192,1024]{1,0:T(8,128)(2,1)S(1)} %get-tuple-element.118), channel_id=1, source_target_pairs={{0,2},{1,3},{2,0},{3,1},{4,6},{5,7},{6,4},{7,5},{8,10},{9,11},{10,... | collective-permute-start | bytes 1179656 | tf_op jit(solution)/shard_map/ppermute | solution.py:1040
  147.0 22.3 %collective-permute-start.7 = (bf16[192,1024]{1,0:T(8,128)(2,1)S(1)}, bf16[192,1024]{1,0:T(8,128)(2,1)S(1)}, u32[]{:S(2)}, u32[]{:S(2)}) collective-permute-start(bf16[192,1024]{1,0:T(8,128)(2,1)S(1)} %get-tuple-element.120), channel_id=1, source_target_pairs={{0,18},{1,19},{2,16},{3,17},{4,22},{5,23},{6,20},{7,21},{8,26},{9,... | collective-permute-start | bytes 1179656 | tf_op jit(solution)/shard_map/ppermute | solution.py:1490
  147.1 0.6 copy-start.4
  160.1 1.5 collective-permute-start.8
  162.5 6.8 %collective-permute-start.9 = (f32[8,2048]{1,0:T(8,128)S(1)}, f32[8,2048]{1,0:T(8,128)S(1)}, u32[]{:S(2)}, u32[]{:S(2)}) collective-permute-start(f32[8,2048]{1,0:T(8,128)S(1)} %add.8), channel_id=1, source_target_pairs={{0,2},{1,3},{2,0},{3,1},{4,6},{5,7},{6,4},{7,5},{8,10},{9,11},{10,... | collective-permute-start | bytes 196616 | tf_op jit(solution)/shard_map/ppermute | solution.py:1040
  169.6 13.1 %collective-permute-start.10 = (bf16[80,1024]{1,0:T(8,128)(2,1)S(1)}, bf16[80,1024]{1,0:T(8,128)(2,1)S(1)}, u32[]{:S(2)}, u32[]{:S(2)}) collective-permute-start(bf16[80,1024]{1,0:T(8,128)(2,1)S(1)} %get-tuple-element.123), channel_id=1, source_target_pairs={{0,4},{1,5},{2,6},{3,7},{4,0},{5,1},{6,2},{7,3},{8,12},{9,13},{10,... | collective-permute-start | bytes 491528 | tf_op jit(solution)/shard_map/ppermute | solution.py:1040
  171.2 17.3 %collective-permute-start.11 = (bf16[80,1024]{1,0:T(8,128)(2,1)S(1)}, bf16[80,1024]{1,0:T(8,128)(2,1)S(1)}, u32[]{:S(2)}, u32[]{:S(2)}) collective-permute-start(bf16[80,1024]{1,0:T(8,128)(2,1)S(1)} %get-tuple-element.124), channel_id=1, source_target_pairs={{0,8},{1,9},{2,10},{3,11},{4,12},{5,13},{6,14},{7,15},{8,0},{9,1},... | collective-permute-start | bytes 491528 | tf_op jit(solution)/shard_map/ppermute | solution.py:1040
  173.7 14.9 %collective-permute-start.12 = (bf16[80,1024]{1,0:T(8,128)(2,1)S(1)}, bf16[80,1024]{1,0:T(8,128)(2,1)S(1)}, u32[]{:S(2)}, u32[]{:S(2)}) collective-permute-start(bf16[80,1024]{1,0:T(8,128)(2,1)S(1)} %get-tuple-element.125), channel_id=1, source_target_pairs={{0,12},{1,13},{2,14},{3,15},{4,8},{5,9},{6,10},{7,11},{8,4},{9,5},... | collective-permute-start | bytes 491528 | tf_op jit(solution)/shard_map/ppermute | solution.py:1040
  188.7 11.6 %collective-permute-start.14 = (bf16[48,3072]{1,0:T(8,128)(2,1)}, bf16[48,3072]{1,0:T(8,128)(2,1)S(1)}, u32[]{:S(2)}, u32[]{:S(2)}) collective-permute-start(bf16[48,3072]{1,0:T(8,128)(2,1)} %reduce-scatter.2.cloned.1.call-done.early_ref), channel_id=1, source_target_pairs={{0,16},{16,0},{1,17},{17,1},{2,18},{18,2},{3,19},{19,3},{4,20},{20... | collective-permute-start | bytes 884744 | tf_op jit(solution)/shard_map/ppermute | solution.py:1040
  189.1 11.1 %collective-permute-start.13 = (bf16[80,1024]{1,0:T(8,128)(2,1)S(1)}, bf16[80,1024]{1,0:T(8,128)(2,1)S(1)}, u32[]{:S(2)}, u32[]{:S(2)}) collective-permute-start(bf16[80,1024]{1,0:T(8,128)(2,1)S(1)} %last.1.late_ref), channel_id=1, source_target_pairs={{0,16},{16,0},{1,17},{17,1},{2,18},{18,2},{3,19},{19,3},{4,20},{20... | collective-permute-start | bytes 491528 | tf_op jit(solution)/shard_map/ppermute | solution.py:1040
  200.2 1.0 copy-start
Sparse Core Ops, SparseCore 0:
  91.4 91.2 reduce-scatter.1

commit v3 on v2

--- a/solution.py
+++ b/solution.py
@@ -541,6 +541,8 @@
     e0_ref,
     e1_ref,
     spans_ref,
+    _dpre_ref,
+    _moves_ref,
     dpre_ref,
     moves_ref,
     last_ref,
@@ -699,14 +701,39 @@
     return dlog * ratio + da * rate * sig, jnp.sum(da * dt, axis=1, keepdims=True) * rate
 
 
-def weights_kernel(turned_ref, dz_ref, mixed_ref, c_ref, both_ref, *, half):
-    model = c_ref.shape[1]
+def by_core(product, shard, mine_ref, theirs_ref):
+    pieces = [product[place : place + shard] for place in range(0, product.shape[0], shard)]
+    even = jnp.concatenate(pieces[0::2], axis=0)
+    odd = jnp.concatenate(pieces[1::2], axis=0)
+    core = lax.rem(lax.axis_index("dp"), 2)
+
+    @pl.when(core == 0)
+    def _():
+        mine_ref[...] = even
+        theirs_ref[...] = odd
+
+    @pl.when(core == 1)
+    def _():
+        mine_ref[...] = odd
+        theirs_ref[...] = even
+
+
+def weights_kernel(
+    turned_ref, dz_ref, mixed_ref, c_ref, wz_ref, mine_ref, theirs_ref, gain_ref, *, shard
+):
     product = mm_tn(mixed_ref[...], c_ref[...]).astype(BF16)
-    for shard in range(product.shape[0] // (2 * half)):
-        span = slice(shard * half, (shard + 1) * half)
-        both_ref[span, 0:model] = product[2 * shard * half : (2 * shard + 1) * half]
-        both_ref[span, model : 2 * model] = product[(2 * shard + 1) * half : (2 * shard + 2) * half]
-    both_ref[:, 2 * model :] = mm(turned_ref[...], dz_ref[...]).astype(BF16)
+    pieces = []
+    for place in range(0, product.shape[0], 2 * shard):
+        pieces.append(
+            jnp.concatenate(
+                [product[place : place + shard], product[place + shard : place + 2 * shard]], axis=1
+            )
+        )
+    gate = mm(turned_ref[...], dz_ref[...])
+    both = jnp.concatenate([jnp.concatenate(pieces, axis=0), gate.astype(BF16)], axis=1)
+    by_core(both, shard, mine_ref, theirs_ref)
+    share = (gate * wz_ref[...].astype(F32)).astype(BF16)
+    gain_ref[0] = mm_nt(jnp.ones((8, share.shape[1]), BF16), share)[0:1]
 
 
 def conv_back_kernel(
@@ -722,14 +749,22 @@
     rate_ref,
     moves_ref,
     r_ref,
+    w_ref,
+    narrow_ref,
+    gain_ref,
+    share_ref,
+    mix_sums_ref,
+    e0_ref,
     dproj_ref,
     dhalo_ref,
     mine_ref,
     theirs_ref,
     draw_ref,
-    sums_ref,
+    small_ref,
     shift,
     buf,
+    gains,
+    sums_ref,
     *,
     shard,
 ):
@@ -747,25 +782,17 @@
             )
         shift[chunks * 3 * CHUNK :, :] = shifts(base, bounds, 0, 16)
         buf[...] = jnp.zeros_like(buf)
-
-    def hand_over(product):
-        if not shard:
-            mine_ref[...] = product
-            return
-        pieces = [product[place : place + shard] for place in range(0, product.shape[0], shard)]
-        even = jnp.concatenate(pieces[0::2], axis=0)
-        odd = jnp.concatenate(pieces[1::2], axis=0)
-        core = lax.rem(lax.axis_index("dp"), 2)
-
-        @pl.when(core == 0)
-        def _():
-            mine_ref[...] = even
-            theirs_ref[...] = odd
-
-        @pl.when(core == 1)
-        def _():
-            mine_ref[...] = odd
-            theirs_ref[...] = even
+        gains[...] = jnp.zeros_like(gains)
+        sums_ref[...] = jnp.zeros_like(sums_ref)
+
+    last = pl.num_programs(0) - 1
+    inner = w_ref.shape[1]
+    tile_here = pl.ds(pl.multiple_of(step * wide, wide), wide)
+
+    def hand_over(product, weights):
+        share = (product * weights.astype(F32)).astype(BF16)
+        gains[...] += mm_nt(jnp.ones((8, share.shape[1]), BF16), share)
+        by_core(product.astype(BF16), shard, mine_ref, theirs_ref)
 
     @pl.when(step < pl.num_programs(0) - 1)
     def _():
@@ -801,15 +828,22 @@
                         dproj = dproj + part * taps_ref[3 - lag : 4 - lag, cols]
                         sums[place][3 - lag] = sums[place][3 - lag] + fold(pre * part)
                     dproj_ref[span, cols] = dproj.astype(BF16)
-        sums_ref[...] = jnp.zeros_like(sums_ref)
         for place in range(wide // 128):
             cols = slice(place * 128, place * 128 + 128)
+            at = pl.ds(pl.multiple_of(step * wide + place * 128, 128), 128)
             for tap in range(4):
-                sums_ref[tap : tap + 1, cols] = (
+                sums_ref[tap : tap + 1, at] = (
                     jnp.sum(sums[place][tap], axis=0, keepdims=True) + halo_sums[tap][:, cols]
                 )
         product = mm(turned_ref[...], dproj_ref[...]) + mm(turnhalo_ref[...], dhalo_ref[...])
-        hand_over(product.astype(BF16))
+
+        @pl.when(step < last - 1)
+        def _():
+            hand_over(product, w_ref[:, tile_here])
+
+        @pl.when(step == last - 1)
+        def _():
+            hand_over(product, narrow_ref[0:wide, :].astype(F32).T)
 
     @pl.when(step == pl.num_programs(0) - 1)
     def _():
@@ -817,43 +851,91 @@
         draw, drate = steps_back(raw_ref[...], dt_ref[...], rate, moves_ref[...], r_ref[...])
         low = draw.astype(BF16)
         draw_ref[...] = low
-        product = mm_nt(turned_ref[...], low).astype(BF16)
+        product = mm_nt(turned_ref[...], low)
+        fill = jnp.zeros((product.shape[0], wide - steps), F32)
+        steps_weights = narrow_ref[narrow_ref.shape[0] - steps :, :].astype(F32).T
         hand_over(
-            jnp.concatenate([product, jnp.zeros((product.shape[0], wide - steps), BF16)], axis=1)
+            jnp.concatenate([product, fill], axis=1),
+            jnp.concatenate([steps_weights, fill], axis=1),
         )
-        columns = [jnp.sum(draw, axis=1, keepdims=True), drate, jnp.zeros((steps, 6), F32)]
-        sums_ref[...] = jnp.zeros_like(sums_ref)
-        sums_ref[:, 0:steps] = jnp.concatenate(columns, axis=1).T
-
-
-def quarters_kernel(mine_ref, got_ref, keep_ref, across_ref, along_ref, both_ref, *, shard):
+        heads = steps // 2
+        model = w_ref.shape[0]
+        sums_ref[4:5, 0:inner] = jnp.sum(mix_sums_ref[0:8, :], axis=0, keepdims=True)
+        share = jnp.concatenate([share_ref[part] for part in range(share_ref.shape[0])], axis=1)
+        sums_ref[5:6, 0:model] = (gains[0:1, :] + share) / row_of(gain_ref)
+        skips = in_parts(mix_sums_ref[8:16, :], 2).astype(BF16)
+        skips = jnp.sum(mm_nt(e0_ref[0:heads, :], skips), axis=1, keepdims=True)
+        columns = [jnp.concatenate([skips, skips], axis=0), jnp.sum(draw, axis=1, keepdims=True)]
+        columns = jnp.concatenate(columns + [drate, jnp.zeros((steps, 5), F32)], axis=1).T
+        for place in range(3):
+            sums_ref[6:7, 128 * place : 128 * place + steps] = columns[place : place + 1]
+        small_ref[...] = in_parts(sums_ref[...], 2).astype(BF16)
+
+
+def halve_kernel(kept_ref, got_ref, keep_ref, send_ref, *, bit):
+    shard = keep_ref.shape[0]
+    mine = lax.rem(lax.axis_index("dp") // bit, 2)
+    for place, out_ref in ((mine, keep_ref), (1 - mine, send_ref)):
+        rows = pl.ds(pl.multiple_of(place * shard, shard), shard)
+        total = kept_ref[rows, :].astype(F32) + got_ref[rows, :].astype(F32)
+        out_ref[...] = total.astype(out_ref.dtype)
+
+
+def sum_kernel(kept_ref, got_ref, out_ref):
+    out_ref[...] = (kept_ref[...].astype(F32) + got_ref[...].astype(F32)).astype(BF16)
+
+
+def two_halves(small):
+    half = small.shape[1] // 2
+    return jnp.concatenate([small[:, 0:half], small[:, half:]], axis=0)
+
+
+def parts_sum(parts):
+    half = parts.shape[0] // 2
+    return parts[0:half].astype(F32) + parts[half:].astype(F32)
+
+
+def quarters_kernel(
+    mine_ref,
+    got_ref,
+    small_ref,
+    smallgot_ref,
+    keep_ref,
+    across_ref,
+    along_ref,
+    both_ref,
+    *,
+    shard,
+):
     half = mine_ref.shape[1] // 2
     row_bit = lax.rem(lax.axis_index("dp") // 2, 2)
     side = lax.axis_index("dir")
-    for place in range(keep_ref.shape[0] // shard):
-        rows = slice(place * shard, (place + 1) * shard)
-        for out_ref, row, column in (
-            (keep_ref, row_bit, side),
-            (across_ref, row_bit, 1 - side),
-            (along_ref, 1 - row_bit, side),
-            (both_ref, 1 - row_bit, 1 - side),
-        ):
+    count = mine_ref.shape[0] // 2
+    small = two_halves(parts_sum(small_ref[...]) + parts_sum(smallgot_ref[...]))
+    few = small.shape[0]
+    parts = in_parts(small, 2)
+    keep_ref[count:, :] = parts[0:few] + parts[few:]
+    for out_ref, row, column in (
+        (keep_ref, row_bit, side),
+        (across_ref, row_bit, 1 - side),
+        (along_ref, 1 - row_bit, side),
+        (both_ref, 1 - row_bit, 1 - side),
+    ):
+        if out_ref is not keep_ref:
+            out_ref[count:, :] = parts.astype(BF16)
+        for place in range(count // shard):
+            rows = slice(place * shard, (place + 1) * shard)
             here = pl.ds(pl.multiple_of((2 * place + row) * shard, shard), shard)
             cols = pl.ds(pl.multiple_of(column * half, half), half)
             total = mine_ref[here, cols].astype(F32) + got_ref[here, cols].astype(F32)
             out_ref[rows, :] = total.astype(out_ref.dtype)
 
 
-def two_halves(small):
-    half = small.shape[1] // 2
-    return jnp.concatenate([small[:, 0:half], small[:, half:]], axis=0)
-
-
-def levels_kernel(
-    keep_ref, a_ref, b_ref, c_ref, small_ref, own_ref, s1_ref, s2_ref, s3_ref, *, shard
-):
+def levels_kernel(keep_ref, a_ref, b_ref, c_ref, own_ref, s1_ref, s2_ref, s3_ref, *, shard):
     level = lax.axis_index("dp") // 4
-    parts = in_parts(two_halves(small_ref[...]), 2)
+    count = 4 * shard
+    small = [parts_sum(ref[count:, :]) for ref in (a_ref, b_ref, c_ref)]
+    parts = in_parts(keep_ref[count:, :] + small[0] + (small[1] + small[2]), 2)
     few = parts.shape[0] // 2
     own_ref[shard : shard + few, :] = parts[0:few] + parts[few:]
     for bits, out_ref in enumerate((own_ref, s1_ref, s2_ref, s3_ref)):
@@ -867,16 +949,13 @@
 
 
 def joined(ref, shard):
-    few = (ref.shape[0] - shard) // 2
-    small = ref[shard : shard + few, :].astype(F32) + ref[shard + few :, :].astype(F32)
-    return ref[0:shard, :].astype(F32), small
-
-
-def last_kernel(own_ref, a_ref, b_ref, c_ref, out_ref, *, shard):
+    return ref[0:shard, :].astype(F32), parts_sum(ref[shard:, :])
+
+
+def last_kernel(own_ref, a_ref, b_ref, c_ref, out_ref, small_ref, *, shard):
     a, b, c = (joined(ref, shard) for ref in (a_ref, b_ref, c_ref))
-    out_ref[0:shard, :] = (own_ref[0:shard, :] + a[0] + (b[0] + c[0])).astype(BF16)
-    small = in_parts(own_ref[shard:, :] + a[1] + (b[1] + c[1]), 2)
-    out_ref[shard:, :] = small.astype(BF16)
+    out_ref[...] = (own_ref[0:shard, :] + a[0] + (b[0] + c[0])).astype(BF16)
+    small_ref[...] = own_ref[shard:, :] + a[1] + (b[1] + c[1])
 
 
 def finish_kernel(
@@ -884,6 +963,7 @@
     lategot_ref,
     early_ref,
     earlygot_ref,
+    small_ref,
     gx_ref,
     gz_ref,
     gbc_ref,
@@ -900,8 +980,8 @@
     inner = gx_ref.shape[1]
     model = go_ref.shape[1]
     shard = gx_ref.shape[0]
-    mine, small = joined(late_ref, shard)
-    other, small_other = joined(lategot_ref, shard)
+    mine = late_ref[...].astype(F32)
+    other = lategot_ref[...].astype(F32)
     first = jnp.where(side == 0, mine, other)
     second = jnp.where(side == 0, other, mine)
     gx_ref[:, 0:half] = first
@@ -911,8 +991,7 @@
     go_ref[0:shard, :] = early[:, 0:model]
     go_ref[shard : 2 * shard, :] = early[:, model : 2 * model]
     gz_ref[...] = early[:, 2 * model :]
-    small = small + small_other
-    small = jnp.concatenate([small[0:8], small[8:16]], axis=1)
+    small = jnp.concatenate([small_ref[0:8, :], small_ref[8:16, :]], axis=1)
     gtaps_ref[...] = small[0:4, 0 : gtaps_ref.shape[1]]
     gmix_ref[...] = small[4:5, 0:inner].reshape(inner)
     gin_ref[...] = small[5:6, 0:model].reshape(model)
@@ -935,24 +1014,13 @@
     wx_ref,
     wbc_ref,
     wz_ref,
-    mix_sums_ref,
-    tap_sums_ref,
-    e0_ref,
     gin_ref,
-    small_ref,
-    total,
     dproj,
 ):
     step = pl.program_id(0)
-    model, inner = wx_ref.shape
+    inner = wx_ref.shape[1]
     steps = draw_ref.shape[0]
-    heads = steps // 2
     narrow = wbc_ref.shape[0] - steps
-    channels = inner + narrow
-
-    @pl.when(step == 0)
-    def _():
-        total[...] = jnp.zeros_like(total)
 
     @pl.when(step == pl.num_programs(0) - 1)
     def _():
@@ -972,24 +1040,10 @@
     x = x_ref[...].astype(F32)
     inv = lax.rsqrt(jnp.mean(x * x, axis=1, keepdims=True) + EPS)
     unit = x * inv
-    total[...] += fold(dn * unit)
     f = dn * row_of(gain_ref)
     back = inv * (f - unit * jnp.mean(f * unit, axis=1, keepdims=True))
     gin_ref[...] = (c_ref[...].astype(F32) + back).astype(BF16)
 
-    @pl.when(step == pl.num_programs(0) - 1)
-    def _():
-        small_ref[...] = jnp.zeros_like(small_ref)
-        small_ref[0:4, 0:channels] = tap_sums_ref[0:4, 0:channels]
-        small_ref[4:5, 0:inner] = jnp.sum(mix_sums_ref[0:8, :], axis=0, keepdims=True)
-        small_ref[5:6, 0:model] = jnp.sum(total[...], axis=0, keepdims=True)
-        skips = in_parts(mix_sums_ref[8:16, :], 2).astype(BF16)
-        skips = jnp.sum(mm_nt(e0_ref[0:heads, :], skips), axis=1, keepdims=True)
-        skips = jnp.broadcast_to(skips, (heads, 128)).T
-        small_ref[6:7, 0:heads] = skips[0:1]
-        small_ref[6:7, 128:256] = tap_sums_ref[0:1, channels : channels + 128]
-        small_ref[6:7, 256:384] = tap_sums_ref[1:2, channels : channels + 128]
-
 
 def smem():
     return pl.BlockSpec(memory_space=pltpu.SMEM)
@@ -997,6 +1051,10 @@
 
 def resident():
     return pl.BlockSpec(memory_space=pltpu.VMEM)
+
+
+def anywhere():
+    return pl.BlockSpec(memory_space=pl.ANY)
 
 
 def whole(shape):
@@ -1020,7 +1078,7 @@
     return pl.CostEstimate(flops=flops, bytes_accessed=0, transcendentals=0)
 
 
-def call(kernel, name, grid, in_specs, outs, scratch, cost_us, args, vmem):
+def call(kernel, name, grid, in_specs, outs, scratch, cost_us, args, vmem, aliases=()):
     return pl.pallas_call(
         kernel,
         name=name,
@@ -1029,6 +1087,7 @@
         out_specs=[spec for spec, _, _ in outs],
         out_shape=[jax.ShapeDtypeStruct(shape, dtype) for _, shape, dtype in outs],
         scratch_shapes=scratch,
+        input_output_aliases=dict(aliases),
         compiler_params=pltpu.CompilerParams(
             vmem_limit_bytes=vmem * MIB, dimension_semantics=("arbitrary",)
         ),
@@ -1272,11 +1331,39 @@
     )
     d_received = lax.ppermute(d_send, "dir", SWAP)
 
+    def plain(kernel, name, args, outs, specs=None, out_specs=None, grid=()):
+        resident = [pl.BlockSpec(memory_space=pltpu.VMEM)]
+        return pl.pallas_call(
+            kernel,
+            name=name,
+            grid=grid,
+            in_specs=specs or resident * len(args),
+            out_specs=out_specs or resident * len(outs),
+            out_shape=[jax.ShapeDtypeStruct(shape, dtype) for shape, dtype in outs],
+            compiler_params=pltpu.CompilerParams(vmem_limit_bytes=VMEM_SUMS * MIB),
+            cost_estimate=cost(US_SUMS),
+        )(*args)
+
+    def halve(name, kept, got, bit):
+        rows, wide = got.shape
+        outs = [((rows // 2, wide), F32), ((rows // 2, wide), BF16)]
+        return plain(
+            functools.partial(halve_kernel, bit=bit),
+            name,
+            (kept, got),
+            outs,
+            [rows_of(2 * piece, wide)] * 2,
+            [rows_of(piece, wide)] * 2,
+            (rows // (2 * piece),),
+        )
+
     blocks = 4
     shard = model // dp_count
-    half = shard if shard % 16 == 0 else 0
-    (g_early,) = call(
-        functools.partial(weights_kernel, half=half or model // 16),
+    direct = dp_count == 16 and shard % 16 == 0
+    piece = model // 16
+    early_rows = (rows_of(model // 2 // blocks, 2 * inner), (model // 2, 2 * inner), BF16)
+    early_mine, early_theirs, z_share = call(
+        functools.partial(weights_kernel, shard=piece),
         "weights",
         blocks,
         [
@@ -1284,21 +1371,21 @@
             whole((count, inner)),
             lanes_of(count, inner // blocks),
             whole((count, model)),
+            rows_of(model // blocks, inner),
         ],
-        [(rows_of(model // blocks, 2 * inner), (model, 2 * inner), BF16)],
+        [
+            early_rows,
+            early_rows,
+            (pl.BlockSpec((1, 1, model // blocks), lambda i: (i, 0, 0)), (blocks, 1, model // blocks), F32),
+        ],
         [],
         US_WEIGHTS,
-        (turned, dz, mixed, cot),
+        (turned, dz, mixed, cot, w_z),
         VMEM_WEIGHTS,
     )
-    if not half:
-        g_out = g_early[:, :inner].reshape(16, model // 16, 2, model).transpose(0, 2, 1, 3)
-        g_out = g_out.reshape(dp_count, 2, shard, model).transpose(0, 2, 1, 3)
-        g_early = jnp.concatenate([g_out.reshape(model, inner), g_early[:, inner:]], axis=1)
-    g_early, d_received = ordered(g_early, d_received)
-    early = lax.psum_scatter(g_early, "dp", scatter_dimension=0, tiled=True)
-
-    def back(skipped, taken, start):
+    (early_mine, early_theirs), d_received = ordered((early_mine, early_theirs), d_received)
+
+    def back(skipped, taken, start, dpre, moves):
         def rows_from(width):
             return pl.BlockSpec((CHUNK, width), lambda i: (i + skipped, 0))
 
@@ -1332,10 +1419,12 @@
                 whole(e0.shape),
                 whole(e1.shape),
                 whole(spans.shape),
+                anywhere(),
+                anywhere(),
             ],
             [
-                (rows_of(CHUNK, channels), (taken * CHUNK, channels), BF16),
-                (lanes_of(8 * heads, CHUNK), (8 * heads, taken * CHUNK), F32),
+                (rows_from(channels), (count, channels), BF16),
+                (lanes_from(8 * heads), (8 * heads, count), F32),
                 full((state, inner), F32),
             ],
             [
@@ -1346,7 +1435,7 @@
             ]
             + [chunk_bf16] * 4
             + [state_bf16] * 2,
-            US_BACK,
+            US_BACK * taken // chunks,
             (
                 lengths,
                 d_skip,
@@ -1367,11 +1456,25 @@
                 e0,
                 e1,
                 spans,
+                dpre,
+                moves,
             ),
             VMEM_BACK,
+            {19: 0, 20: 1} if skipped else {},
         )
 
-    dpre, moves, _ = back(0, chunks, d_received)
+    first = 1
+    dpre, moves, carry = back(0, first, d_received, received, received)
+    if direct:
+        early_got = traded(early_theirs, "dp", 1, dp_count)
+        early_keep, early_send = halve("halve_y", early_mine, early_got, 2)
+        early_send, carry = ordered(early_send, carry)
+        early_got = traded(early_send, "dp", 2, dp_count)
+    dpre, moves, _ = back(first, chunks - first, carry, dpre, moves)
+    if direct:
+        early_keep, early_send = halve("halve_z", early_keep, early_got, 4)
+        early_send, dpre = ordered(early_send, dpre)
+        early_got = traded(early_send, "dp", 4, dp_count)
 
     tile = 256
     tiles = channels // tile
@@ -1379,9 +1482,9 @@
         return pl.BlockSpec((height, tile), lambda i: (0, jnp.minimum(i, tiles - 1)))
 
     wide = (tiles + 1) * tile
-    kept_rows = model // 2 if half else model
-    dproj, dhalo, mine, theirs, draw, tap_sums = call(
-        functools.partial(conv_back_kernel, shard=half),
+    late_out = (lanes_of(model // 2, tile), (model // 2, wide), BF16)
+    dproj, dhalo, late_mine, late_theirs, draw, small = call(
+        functools.partial(conv_back_kernel, shard=piece),
         "conv_back",
         tiles + 1,
         [
@@ -1397,26 +1500,53 @@
             whole((steps, 128)),
             whole((8 * heads, count)),
             whole((steps, count)),
+            whole((model, inner)),
+            whole(w_narrow.shape),
+            whole((model,)),
+            whole(z_share.shape),
+            whole(mix_sums.shape),
+            whole(e0.shape),
         ],
         [
             (tile_of(count), (count, channels), BF16),
             (tile_of(16), (16, channels), BF16),
-            (lanes_of(kept_rows, tile), (kept_rows, wide), BF16),
-            (lanes_of(kept_rows, tile), (kept_rows, wide), BF16),
+            late_out,
+            late_out,
             full((steps, count), BF16),
-            (lanes_of(8, tile), (8, wide), F32),
+            full((16, wide), BF16),
         ],
         [
             pltpu.VMEM((3 * count + 48, CHUNK + 16), BF16),
             pltpu.VMEM((CHUNK + 16, tile), BF16),
+            pltpu.VMEM((8, model), F32),
+            pltpu.VMEM((8, wide), F32),
         ],
         US_CONV,
-        (lengths, turned, turn_halo, dpre, pre, pre_halo, conv_w, raw, dt, rate, moves, r),
+        (
+            lengths,
+            turned,
+            turn_halo,
+            dpre,
+            pre,
+            pre_halo,
+            conv_w,
+            raw,
+            dt,
+            rate,
+            moves,
+            r,
+            w_x,
+            w_narrow,
+            gain_in,
+            z_share,
+            mix_sums,
+            e0,
+        ),
         VMEM_CONV,
     )
     d_halo = lax.ppermute(dhalo, "dir", [(1, 0)])
 
-    grad_in, small = call(
+    (grad_in,) = call(
         inputs_kernel,
         "inputs",
         count // ROWS,
@@ -1431,32 +1561,32 @@
             whole((model, inner)),
             whole(w_narrow.shape),
             whole((model, inner)),
-            whole(mix_sums.shape),
-            whole(tap_sums.shape),
-            whole(e0.shape),
         ],
-        [
-            rows_out(ROWS, model, BF16),
-            full((8, tap_sums.shape[1]), F32),
-        ],
-        [pltpu.VMEM((8, model), F32), pltpu.VMEM((ROWS, channels), BF16)],
+        [rows_out(ROWS, model, BF16)],
+        [pltpu.VMEM((ROWS, channels), BF16)],
         US_INPUTS,
-        (x, cot, gain_in, dproj, d_halo, draw, dz, w_x, w_narrow, w_z, mix_sums, tap_sums, e0),
+        (x, cot, gain_in, dproj, d_halo, draw, dz, w_x, w_narrow, w_z),
         VMEM_INPUTS,
     )
-    if not half or dp_count != 16:
-        small = sum_all(small, dp_count)
-        late = sum_shards(mine, dp_count)
-        early_got = traded(early, "dir", 1, 2)
-        early = early.astype(F32) + early_got.astype(F32)
-        grad_out = jnp.concatenate([early[:, :model], early[:, model:inner]], axis=0)
+
+    if not direct:
+        def undivided(mine, theirs):
+            even = lax.axis_index("dp") % 2 == 0
+            both = [jnp.where(even, mine, theirs), jnp.where(even, theirs, mine)]
+            both = [part.reshape(8, 1, piece, part.shape[1]) for part in both]
+            return jnp.concatenate(both, axis=1).reshape(model, mine.shape[1])
+
+        early = undivided(early_mine, early_theirs)
+        g_out = early[:, :inner].reshape(16, piece, 2, model).transpose(0, 2, 1, 3)
+        late = sum_shards(undivided(late_mine, late_theirs), dp_count)
+        small = sum_all(small[0:8].astype(F32) + small[8:16].astype(F32), dp_count)
         return (
             out[None],
             grad_in[None],
             late[:, :inner],
-            early[:, inner:],
+            sum_shards(early[:, inner:], dp_count),
             late[:, inner : inner + 4 * state + steps],
-            grad_out,
+            sum_shards(g_out.reshape(inner, model), dp_count),
             small[5, :model],
             small[0:4, :channels],
             small[6, 128 : 128 + steps].reshape(dt_bias.shape),
@@ -1465,24 +1595,18 @@
             small[4, :inner],
         )
 
-    def plain(kernel, name, args, outs):
-        return pl.pallas_call(
-            kernel,
-            name=name,
-            in_specs=[pl.BlockSpec(memory_space=pltpu.VMEM)] * len(args),
-            out_specs=[pl.BlockSpec(memory_space=pltpu.VMEM)] * len(outs),
-            out_shape=[jax.ShapeDtypeStruct(shape, dtype) for shape, dtype in outs],
-            compiler_params=pltpu.CompilerParams(vmem_limit_bytes=VMEM_SUMS * MIB),
-            cost_estimate=cost(US_SUMS),
-        )(*args)
-
-    got = traded(theirs, "dp", 1, dp_count)
-    quarter = (model // 4, wide // 2)
+    early_got, late_theirs = ordered(early_got, late_theirs)
+    late_got = traded(late_theirs, "dp", 1, dp_count)
+    small_got = traded(small, "dp", 1, dp_count)
+    early_keep, early_send = halve("halve_z2", early_keep, early_got, 8)
+    early_send, late_got = ordered(early_send, late_got)
+    early_got = traded(early_send, "dp", 8, dp_count)
+    quarter = (model // 4 + 32, wide // 2)
     kept, across, along, both = plain(
-        functools.partial(quarters_kernel, shard=shard),
+        functools.partial(quarters_kernel, shard=piece),
         "quarters",
-        (mine, got),
-        [(quarter, F32), (quarter, BF16), (quarter, BF16), (quarter, BF16)],
+        (late_mine, late_got, small, small_got),
+        [((model // 4 + 16, wide // 2), F32), (quarter, BF16), (quarter, BF16), (quarter, BF16)],
     )
     corners = [(a, b) for a in range(2) for b in range(dp_count)]
     across = traded(across, "dir", 1, 2)
@@ -1492,32 +1616,33 @@
         ("dir", "dp"),
         [(a * dp_count + b, (1 - a) * dp_count + (b ^ 2)) for a, b in corners],
     )
-    _, both = ordered(small, both)
-    for bit in (1, 2):
-        small = small + traded(small, "dp", bit, dp_count)
-    piece = (shard + 4 * small.shape[0], wide // 2)
+    (early,) = plain(sum_kernel, "early_sum", (early_keep, early_got), [((piece, 2 * inner), BF16)])
+    grad_in, early, both = lax.optimization_barrier((grad_in, early, both))
+    early_got = traded(early, "dir", 1, 2)
+    message = (piece + 32, wide // 2)
     own, *sends = plain(
-        functools.partial(levels_kernel, shard=shard),
+        functools.partial(levels_kernel, shard=piece),
         "levels",
-        (kept, across, along, both, small),
-        [((shard + 2 * small.shape[0], wide // 2), F32)] + [(piece, BF16)] * 3,
+        (kept, across, along, both),
+        [((piece + 16, wide // 2), F32)] + [(message, BF16)] * 3,
     )
     gots = [traded(sent, "dp", 4 * bits, dp_count) for bits, sent in zip((1, 2, 3), sends)]
-    (late,) = plain(
-        functools.partial(last_kernel, shard=shard), "last", (own, *gots), [(piece, BF16)]
+    late, small = plain(
+        functools.partial(last_kernel, shard=piece),
+        "last",
+        (own, *gots),
+        [((piece, wide // 2), BF16), ((16, wide // 2), F32)],
     )
-    early, _ = ordered(early, late)
-    early_got = traded(early, "dir", 1, 2)
     late_got = traded(late, "dir", 1, 2)
     g_x, g_zz, g_bc, g_o, g_taps, g_mix, g_in, g_skip, g_bias, g_alog = plain(
         finish_kernel,
         "finish",
-        (late, late_got, early, early_got),
+        (late, late_got, early, early_got, small),
         [
-            ((shard, inner), F32),
-            ((shard, inner), F32),
-            ((shard, w_bcdt.shape[1]), F32),
-            ((2 * shard, model), F32),
+            ((piece, inner), F32),
+            ((piece, inner), F32),
+            ((piece, w_bcdt.shape[1]), F32),
+            ((2 * piece, model), F32),
             (conv_w.shape, F32),
             ((inner,), F32),
             ((model,), F32),

time: 211 us -> 195 us (0.924)
  between operations: 14.2 us -> 0.81 us
  waiting for transfers between devices: 34.5 us -> 22.5 us
  Pallas kernels: 133 us -> 141 us
  starting transfers between devices: 20.5 us -> 26.8 us
  local copies, waits for them, and re-layouts: 5.66 us -> 3.25 us
    ppermute x10 -> x13, waiting for transfers between devices: 33 us -> 21 us  [traded(): return lax.ppermute(values, axis, [(i, i ^ bit) for i in range(size)])]
    pallas_call x7 -> x8, Pallas kernels: 132 us -> 138 us  [call(): pl.pallas_call(kernel, name=name, grid=(grid,), in_specs=in_specs, out_sp...]
    ppermute x10 -> x13, starting transfers between devices: 11.7 us -> 15.2 us  [traded(): return lax.ppermute(values, axis, [(i, i ^ bit) for i in range(size)])]
    ppermute x1, starting transfers between devices: 0.08 us -> 3 us  [local(): lax.ppermute(both, ('dir', 'dp'), [(a * dp_count + b, (1 - a) * dp_count...]
    unnamed x12 -> x14, local copies, waits for them, and re-layouts: 4.91 us -> 2.51 us
  transfers between devices with their start and end apart: 16 -> 18, of which waited for: 7 -> 7; matrix products, arithmetic and copies ran while one was open for 0% -> 0% of each run, Pallas kernels for 38% -> 44%
where the time goes in v3:
time: 195 us; the launch traced here: 194 us
  Pallas kernels  141 us (72%)
  starting transfers between devices  26.8 us (14%)
  waiting for transfers between devices  22.5 us (12%)
  local copies, waits for them, and re-layouts  3.25 us (2%)
    pallas_call x8, Pallas kernels, call(): pl.pallas_call(kernel, name=name, grid=(grid,), in_specs=in_specs, out_sp...  138 us
    ppermute x13, waiting for transfers between devices, traded(): return lax.ppermute(values, axis, [(i, i ^ bit) for i in range(size)])  21 us
    ppermute x13, starting transfers between devices, traded(): return lax.ppermute(values, axis, [(i, i ^ bit) for i in range(size)])  15.2 us
    ppermute x1, starting transfers between devices, local(): halo = lax.ppermute(x[count - 16:], 'dir', [(0, 1)])  4.83 us
  transfers between devices with their start and end apart: 18, of which 7 were waited for; matrix products, arithmetic and copies ran while one was open for 0% of the time, Pallas kernels for 44%

profile of v3, /device:TPU:0, one launch (start us, length us, event | category | flops | bytes accessed | tf_op | source)
XLA Modules:
  0.0 194.4 jit_solution(15740986237205256895)
XLA Ops:
  0.6 0.7 slice_bitcast_fusion
  1.4 4.8 %collective-permute-start = (bf16[16,768]{1,0:T(8,128)(2,1)S(1)}, bf16[16,768]{1,0:T(8,128)(2,1)S(1)}, u32[]{:S(2)}, u32[]{:S(2)}) collective-permute-start(bf16[16,768]{1,0:T(8,128)(2,1)S(1)} %slice_bitcast_fusion), channel_id=1, source_target_pairs={{0,16},{1,17},{2,18},{3,19},{4,20},{5,21},{6,22},{7,23},{8,24},{9,... | collective-permute-start | bytes 73736 | tf_op jit(solution)/shard_map/ppermute | solution.py:1157
  6.2 1.5 collective-permute-done.halo_ref
  7.7 0.6 copy-done.6
  8.3 20.8 %proj.1 = (bf16[1024,768]{1,0:T(8,128)(2,1)}, f32[48,1024]{1,0:T(8,128)}, f32[48,1024]{1,0:T(8,128)}, f32[48,128]{1,0:T(8,128)}, f32[48,1024]{1,0:T(8,128)}, /*i...) custom-call(s32[1,8]{1,0:T(1,128)} %lengths_ref.9, ...), custom_call_target="tpu_custom_call" | custom-call | flops 23000000512 | tf_op jit(solution)/shard_map/proj/pallas_call | solution.py:1082
  29.1 2.4 %collective-permute-start.1 = (bf16[64,1536]{1,0:T(8,128)(2,1)}, bf16[64,1536]{1,0:T(8,128)(2,1)S(1)}, u32[]{:S(2)}, u32[]{:S(2)}) collective-permute-start(bf16[64,1536]{1,0:T(8,128)(2,1)} %get-tuple-element.104), channel_id=1, source_target_pairs={{0,16},{16,0},{1,17},{17,1},{2,18},{18,2},{3,19},{19,3},{4,20},{20... | collective-permute-start | bytes 589832 | tf_op jit(solution)/shard_map/ppermute | solution.py:1239
  31.5 9.5 %gates.1 = (bf16[1024,1536]{1,0:T(8,128)(2,1)}, bf16[1024,1536]{1,0:T(8,128)(2,1)}, bf16[768,1024]{1,0:T(8,128)(2,1)}) custom-call(bf16[1024,768]{1,0:T(8,128)(2,1)} %get-tuple-element.105.normed_ref, bf16[1024,768]{1,0:T(8,128)(2,1)} %bitcast.10, bf16[768,1536]{1,0:T(8,128)(2,1)} %wz_ref.5, bf16[1536,768]{1,0:T(8,128)(2,1)} %wo_ref.3), custom_call_target="tpu_custom_call" | custom-call | flops 11500000256 | tf_op jit(solution)/shard_map/gates/pallas_call | solution.py:1082
  41.0 0.0 collective-permute-done.1.recv_ref._dpre_ref._moves_ref
  41.0 0.7 copy-done.4
  41.7 33.1 %mix.1 = (bf16[1024,768]{1,0:T(8,128)(2,1)}, bf16[1024,1536]{1,0:T(8,128)(2,1)}, bf16[1024,1536]{1,0:T(8,128)(2,1)}, bf16[1024,1536]{1,0:T(8,128)(2,1)}, f32[48,...) custom-call(s32[1,8]{1,0:T(1,128)} %lengths_ref.9, ...), custom_call_target="tpu_custom_call" | custom-call | flops 40249999360 | tf_op jit(solution)/shard_map/mix/pallas_call | solution.py:1082
  74.9 0.1 collective-permute-start.2
  75.0 11.8 %weights.1 = (bf16[384,3072]{1,0:T(8,128)(2,1)}, bf16[384,3072]{1,0:T(8,128)(2,1)}, f32[4,1,192]{2,1,0:T(1,128)}) custom-call(bf16[768,1024]{1,0:T(8,128)(2,1)} %get-tuple-element.109.turned_ref, bf16[1024,1536]{1,0:T(8,128)(2,1)} %get-tuple-element.111.dz_ref, bf16[1024,1536]{1,0:T(8,128)(2,1)} %get-tuple-element.112.mixed_ref, bf16[1024,768]{1,0:T(8,128)(2,1)} %bitcast.11, ...), custom_call_target="tpu_custom_call" | custom-call | flops 11500000256 | tf_op jit(solution)/shard_map/weights/pallas_call | solution.py:1082
  86.8 0.1 collective-permute-start.3
  86.9 0.6 copy-done.3
  87.5 6.1 %back0.1 = (bf16[1024,1792]{1,0:T(8,128)(2,1)}, f32[192,1024]{1,0:T(8,128)}, f32[64,1536]{1,0:T(8,128)}) custom-call(s32[1,8]{1,0:T(1,128)} %lengths_ref.9, f32[24]{0:T(128)} %skip_ref.5, bf16[1024,1792]{1,0:T(8,128)(2,1)} %get-tuple-element.97.act_ref, bf16[1024,1792]{1,0:T(8,128)(2,1)} %get-tuple-element.120.slope_ref, ...), custom_call_target="tpu_custom_call" | custom-call | flops 3449999872 | tf_op jit(solution)/shard_map/back0/pallas_call | solution.py:1082
  93.6 0.6 halve_y.1
  94.2 1.6 collective-permute-start.4
  95.8 26.2 %back1.1 = (bf16[1024,1792]{1,0:T(8,128)(2,1)}, f32[192,1024]{1,0:T(8,128)}, f32[64,1536]{1,0:T(8,128)}) custom-call(s32[1,8]{1,0:T(1,128)} %lengths_ref.9, f32[24]{0:T(128)} %skip_ref.5, bf16[1024,1792]{1,0:T(8,128)(2,1)} %get-tuple-element.97.act_ref, ...), custom_call_target="tpu_custom_call", output_to_operand_aliasing={{0}: (19, {}), {1}: (20, {})} | custom-call | flops 29899999232 | tf_op jit(solution)/shard_map/back1/pallas_call | solution.py:1082
  122.1 0.0 collective-permute-done.4.got_ref
  122.1 0.3 halve_z.1
  122.4 1.6 collective-permute-start.6
  124.0 18.8 %conv_back.1 = (bf16[1024,1792]{1,0:T(8,128)(2,1)}, bf16[16,1792]{1,0:T(8,128)(2,1)}, bf16[384,2048]{1,0:T(8,128)(2,1)}, bf16[384,2048]{1,0:T(8,128)(2,1)}, bf16...) custom-call(s32[1,8]{1,0:T(1,128)} %lengths_ref.9, bf16[768,1024]{1,0:T(8,128)(2,1)} %get-tuple-element.109.turned_ref, ...), custom_call_target="tpu_custom_call" | custom-call | flops 19549999104 | tf_op jit(solution)/shard_map/conv_back/pallas_call | solution.py:1082
  142.9 0.1 collective-permute-start.7
  142.9 1.3 collective-permute-start.5
  144.2 0.6 collective-permute-start.9
  144.8 0.1 halve_z2.1
  144.9 1.7 collective-permute-done.7.got_ref
  146.5 2.6 %collective-permute-start.8 = (bf16[48,3072]{1,0:T(8,128)(2,1)S(1)}, bf16[48,3072]{1,0:T(8,128)(2,1)S(1)}, u32[]{:S(2)}, u32[]{:S(2)}) collective-permute-start(bf16[48,3072]{1,0:T(8,128)(2,1)S(1)} %get-tuple-element.155), channel_id=1, source_target_pairs={{0,8},{1,9},{2,10},{3,11},{4,12},{5,13},{6,14},{7,15},{8,0},{9,1},... | collective-permute-start | bytes 884744 | tf_op jit(solution)/shard_map/ppermute | solution.py:1099
  149.1 0.4 quarters.1
  149.5 3.0 %collective-permute-start.10 = (bf16[224,1024]{1,0:T(8,128)(2,1)S(1)}, bf16[224,1024]{1,0:T(8,128)(2,1)S(1)}, u32[]{:S(2)}, u32[]{:S(2)}) collective-permute-start(bf16[224,1024]{1,0:T(8,128)(2,1)S(1)} %get-tuple-element.159), channel_id=1, source_target_pairs={{0,18},{1,19},{2,16},{3,17},{4,22},{5,23},{6,20},{7,21},{8,26},{9,... | collective-permute-start | bytes 1376264 | tf_op jit(solution)/shard_map/ppermute | solution.py:1614
  152.5 0.0 collective-permute-start.11
  152.5 0.6 collective-permute-start.12
  153.2 0.6 copy-done.5
  153.8 11.9 %inputs.1 = bf16[1024,768]{1,0:T(8,128)(2,1)} custom-call(bf16[1024,768]{1,0:T(8,128)(2,1)} %bitcast.9, bf16[1024,768]{1,0:T(8,128)(2,1)} %bitcast.12, f32[768]{0:T(1024)} %gain_ref.7, bf16[1024,1792]{1,0:T(8,128)(2,1)} %get-tuple-element.145.dproj_ref, bf16[16,1792]{1,0:T(8,128)(2,1)} %copy-done.5, bf16[48,1024]{1,0:T(8,128)(2,1)} %get-tuple-element.147.draw_ref, ...), custom_call_target="tpu_custom_call" | custom-call | flops 13799999488 | tf_op jit(solution)/shard_map/inputs/pallas_call | solution.py:1082
  165.7 0.1 early_sum.1.early_ref
  165.7 6.9 %collective-permute-done.11.a_ref = bf16[224,1024]{1,0:T(8,128)(2,1)S(1)} collective-permute-done((bf16[224,1024]{1,0:T(8,128)(2,1)S(1)}, bf16[224,1024]{1,0:T(8,128)(2,1)S(1)}, u32[]{:S(2)}, u32[]{:S(2)}) %collective-permute-start.11) | collective-permute-done | bytes 458784 | tf_op jit(solution)/shard_map/ppermute | solution.py:1099
  172.7 0.2 collective-permute-done.12.b_ref
  172.9 0.2 levels.1
  173.1 0.5 collective-permute-start.13
  173.6 0.5 collective-permute-start.14
  174.1 3.4 %collective-permute-start.15 = (bf16[80,1024]{1,0:T(8,128)(2,1)S(1)}, bf16[80,1024]{1,0:T(8,128)(2,1)S(1)}, u32[]{:S(2)}, u32[]{:S(2)}) collective-permute-start(bf16[80,1024]{1,0:T(8,128)(2,1)S(1)} %get-tuple-element.168), channel_id=1, source_target_pairs={{0,12},{1,13},{2,14},{3,15},{4,8},{5,9},{6,10},{7,11},{8,4},{9,5},... | collective-permute-start | bytes 491528 | tf_op jit(solution)/shard_map/ppermute | solution.py:1099
  177.5 1.8 collective-permute-start.17
  179.3 2.3 %collective-permute-done.13.a_ref = bf16[80,1024]{1,0:T(8,128)(2,1)S(1)} collective-permute-done((bf16[80,1024]{1,0:T(8,128)(2,1)S(1)}, bf16[80,1024]{1,0:T(8,128)(2,1)S(1)}, u32[]{:S(2)}, u32[]{:S(2)}) %collective-permute-start.13) | collective-permute-done | bytes 163872 | tf_op jit(solution)/shard_map/ppermute | solution.py:1099
  181.6 7.0 %collective-permute-done.14.b_ref = bf16[80,1024]{1,0:T(8,128)(2,1)S(1)} collective-permute-done((bf16[80,1024]{1,0:T(8,128)(2,1)S(1)}, bf16[80,1024]{1,0:T(8,128)(2,1)S(1)}, u32[]{:S(2)}, u32[]{:S(2)}) %collective-permute-start.14) | collective-permute-done | bytes 163872 | tf_op jit(solution)/shard_map/ppermute | solution.py:1099
  188.7 0.1 last.1
  188.7 1.9 collective-permute-start.16
  190.6 2.8 %collective-permute-done.16.lategot_ref = bf16[48,1024]{1,0:T(8,128)(2,1)S(1)} collective-permute-done((bf16[48,1024]{1,0:T(8,128)(2,1)S(1)}, bf16[48,1024]{1,0:T(8,128)(2,1)S(1)}, u32[]{:S(2)}, u32[]{:S(2)}) %collective-permute-start.16) | collective-permute-done | bytes 98336 | tf_op jit(solution)/shard_map/ppermute | solution.py:1099
  193.4 1.0 finish.1
  (19 shorter events, 0.0 us)
Async XLA Ops:
  1.4 6.3 %collective-permute-start = (bf16[16,768]{1,0:T(8,128)(2,1)S(1)}, bf16[16,768]{1,0:T(8,128)(2,1)S(1)}, u32[]{:S(2)}, u32[]{:S(2)}) collective-permute-start(bf16[16,768]{1,0:T(8,128)(2,1)S(1)} %slice_bitcast_fusion), channel_id=1, source_target_pairs={{0,16},{1,17},{2,18},{3,19},{4,20},{5,21},{6,22},{7,23},{8,24},{9,... | collective-permute-start | bytes 73736 | tf_op jit(solution)/shard_map/ppermute | solution.py:1157
  7.7 0.6 copy-start.6
  29.1 11.9 %collective-permute-start.1 = (bf16[64,1536]{1,0:T(8,128)(2,1)}, bf16[64,1536]{1,0:T(8,128)(2,1)S(1)}, u32[]{:S(2)}, u32[]{:S(2)}) collective-permute-start(bf16[64,1536]{1,0:T(8,128)(2,1)} %get-tuple-element.104), channel_id=1, source_target_pairs={{0,16},{16,0},{1,17},{17,1},{2,18},{18,2},{3,19},{19,3},{4,20},{20... | collective-permute-start | bytes 589832 | tf_op jit(solution)/shard_map/ppermute | solution.py:1239
  41.0 0.7 copy-start.4
  74.9 11.9 %collective-permute-start.2 = (bf16[64,1536]{1,0:T(8,128)(2,1)}, bf16[64,1536]{1,0:T(8,128)(2,1)S(1)}, u32[]{:S(2)}, u32[]{:S(2)}) collective-permute-start(bf16[64,1536]{1,0:T(8,128)(2,1)} %get-tuple-element.115), channel_id=1, source_target_pairs={{0,16},{16,0},{1,17},{17,1},{2,18},{18,2},{3,19},{19,3},{4,20},{20... | collective-permute-start | bytes 589832 | tf_op jit(solution)/shard_map/ppermute | solution.py:1332
  86.8 0.7 copy-start.3
  86.8 6.8 %collective-permute-start.3 = (bf16[384,3072]{1,0:T(8,128)(2,1)}, bf16[384,3072]{1,0:T(8,128)(2,1)S(1)}, u32[]{:S(2)}, u32[]{:S(2)}) collective-permute-start(bf16[384,3072]{1,0:T(8,128)(2,1)} %get-tuple-element.117), channel_id=1, source_target_pairs={{0,1},{1,0},{2,3},{3,2},{4,5},{5,4},{6,7},{7,6},{8,9},{9,8},{10,11... | collective-permute-start | bytes 7077896 | tf_op jit(solution)/shard_map/ppermute | solution.py:1099
  87.5 6.1 %copy-start.1 = (bf16[384,3072]{1,0:T(8,128)(2,1)S(1)}, bf16[384,3072]{1,0:T(8,128)(2,1)}, u32[]{:S(2)}) copy-start(bf16[384,3072]{1,0:T(8,128)(2,1)} %get-tuple-element.116.kept_ref) | copy-start | bytes 7077892
  94.2 27.8 %collective-permute-start.4 = (bf16[192,3072]{1,0:T(8,128)(2,1)S(1)}, bf16[192,3072]{1,0:T(8,128)(2,1)S(1)}, u32[]{:S(2)}, u32[]{:S(2)}) collective-permute-start(bf16[192,3072]{1,0:T(8,128)(2,1)S(1)} %get-tuple-element.129), channel_id=1, source_target_pairs={{0,2},{1,3},{2,0},{3,1},{4,6},{5,7},{6,4},{7,5},{8,10},{9,11},{10,... | collective-permute-start | bytes 3538952 | tf_op jit(solution)/shard_map/ppermute | solution.py:1099
  122.4 20.5 %collective-permute-start.6 = (bf16[96,3072]{1,0:T(8,128)(2,1)S(1)}, bf16[96,3072]{1,0:T(8,128)(2,1)S(1)}, u32[]{:S(2)}, u32[]{:S(2)}) collective-permute-start(bf16[96,3072]{1,0:T(8,128)(2,1)S(1)} %get-tuple-element.149), channel_id=1, source_target_pairs={{0,4},{1,5},{2,6},{3,7},{4,0},{5,1},{6,2},{7,3},{8,12},{9,13},{10,... | collective-permute-start | bytes 1769480 | tf_op jit(solution)/shard_map/ppermute | solution.py:1099
  142.9 3.7 %collective-permute-start.7 = (bf16[384,2048]{1,0:T(8,128)(2,1)}, bf16[384,2048]{1,0:T(8,128)(2,1)S(1)}, u32[]{:S(2)}, u32[]{:S(2)}) collective-permute-start(bf16[384,2048]{1,0:T(8,128)(2,1)} %get-tuple-element.154), channel_id=1, source_target_pairs={{0,1},{1,0},{2,3},{3,2},{4,5},{5,4},{6,7},{7,6},{8,9},{9,8},{10,11... | collective-permute-start | bytes 4718600 | tf_op jit(solution)/shard_map/ppermute | solution.py:1099
  142.9 10.2 %collective-permute-start.5 = (bf16[16,1792]{1,0:T(8,128)(2,1)}, bf16[16,1792]{1,0:T(8,128)(2,1)S(1)}, u32[]{:S(2)}, u32[]{:S(2)}) collective-permute-start(bf16[16,1792]{1,0:T(8,128)(2,1)} %get-tuple-element.146), channel_id=1, source_target_pairs={{16,0},{17,1},{18,2},{19,3},{20,4},{21,5},{22,6},{23,7},{24,8},{25... | collective-permute-start | bytes 172040 | tf_op jit(solution)/shard_map/ppermute | solution.py:1547
  144.2 4.9 %collective-permute-start.9 = (bf16[16,2048]{1,0:T(8,128)(2,1)}, bf16[16,2048]{1,0:T(8,128)(2,1)S(1)}, u32[]{:S(2)}, u32[]{:S(2)}) collective-permute-start(bf16[16,2048]{1,0:T(8,128)(2,1)} %get-tuple-element.158.small_ref), channel_id=1, source_target_pairs={{0,1},{1,0},{2,3},{3,2},{4,5},{5,4},{6,7},{7,6},{8,9},{9,8},{10,11... | collective-permute-start | bytes 196616 | tf_op jit(solution)/shard_map/ppermute | solution.py:1099
  144.8 4.3 %copy-start = (bf16[16,2048]{1,0:T(8,128)(2,1)S(1)}, bf16[16,2048]{1,0:T(8,128)(2,1)}, u32[]{:S(2)}) copy-start(bf16[16,2048]{1,0:T(8,128)(2,1)} %get-tuple-element.158.small_ref) | copy-start | bytes 196612
  144.8 4.3 %copy-start.2 = (bf16[384,2048]{1,0:T(8,128)(2,1)S(1)}, bf16[384,2048]{1,0:T(8,128)(2,1)}, u32[]{:S(2)}) copy-start(bf16[384,2048]{1,0:T(8,128)(2,1)} %get-tuple-element.156.mine_ref) | copy-start | bytes 4718596
  146.5 19.1 %collective-permute-start.8 = (bf16[48,3072]{1,0:T(8,128)(2,1)S(1)}, bf16[48,3072]{1,0:T(8,128)(2,1)S(1)}, u32[]{:S(2)}, u32[]{:S(2)}) collective-permute-start(bf16[48,3072]{1,0:T(8,128)(2,1)S(1)} %get-tuple-element.155), channel_id=1, source_target_pairs={{0,8},{1,9},{2,10},{3,11},{4,12},{5,13},{6,14},{7,15},{8,0},{9,1},... | collective-permute-start | bytes 884744 | tf_op jit(solution)/shard_map/ppermute | solution.py:1099
  149.5 16.2 %collective-permute-start.10 = (bf16[224,1024]{1,0:T(8,128)(2,1)S(1)}, bf16[224,1024]{1,0:T(8,128)(2,1)S(1)}, u32[]{:S(2)}, u32[]{:S(2)}) collective-permute-start(bf16[224,1024]{1,0:T(8,128)(2,1)S(1)} %get-tuple-element.159), channel_id=1, source_target_pairs={{0,18},{1,19},{2,16},{3,17},{4,22},{5,23},{6,20},{7,21},{8,26},{9,... | collective-permute-start | bytes 1376264 | tf_op jit(solution)/shard_map/ppermute | solution.py:1614
  152.5 20.2 %collective-permute-start.11 = (bf16[224,1024]{1,0:T(8,128)(2,1)S(1)}, bf16[224,1024]{1,0:T(8,128)(2,1)S(1)}, u32[]{:S(2)}, u32[]{:S(2)}) collective-permute-start(bf16[224,1024]{1,0:T(8,128)(2,1)S(1)} %get-tuple-element.162), channel_id=1, source_target_pairs={{0,16},{16,0},{1,17},{17,1},{2,18},{18,2},{3,19},{19,3},{4,20},{20... | collective-permute-start | bytes 1376264 | tf_op jit(solution)/shard_map/ppermute | solution.py:1099
  152.5 20.3 %collective-permute-start.12 = (bf16[224,1024]{1,0:T(8,128)(2,1)S(1)}, bf16[224,1024]{1,0:T(8,128)(2,1)S(1)}, u32[]{:S(2)}, u32[]{:S(2)}) collective-permute-start(bf16[224,1024]{1,0:T(8,128)(2,1)S(1)} %get-tuple-element.163), channel_id=1, source_target_pairs={{0,2},{1,3},{2,0},{3,1},{4,6},{5,7},{6,4},{7,5},{8,10},{9,11},{10,... | collective-permute-start | bytes 1376264 | tf_op jit(solution)/shard_map/ppermute | solution.py:1099
  153.2 0.6 copy-start.5
  173.1 8.5 %collective-permute-start.13 = (bf16[80,1024]{1,0:T(8,128)(2,1)S(1)}, bf16[80,1024]{1,0:T(8,128)(2,1)S(1)}, u32[]{:S(2)}, u32[]{:S(2)}) collective-permute-start(bf16[80,1024]{1,0:T(8,128)(2,1)S(1)} %get-tuple-element.166), channel_id=1, source_target_pairs={{0,4},{1,5},{2,6},{3,7},{4,0},{5,1},{6,2},{7,3},{8,12},{9,13},{10,... | collective-permute-start | bytes 491528 | tf_op jit(solution)/shard_map/ppermute | solution.py:1099
  173.6 15.0 %collective-permute-start.14 = (bf16[80,1024]{1,0:T(8,128)(2,1)S(1)}, bf16[80,1024]{1,0:T(8,128)(2,1)S(1)}, u32[]{:S(2)}, u32[]{:S(2)}) collective-permute-start(bf16[80,1024]{1,0:T(8,128)(2,1)S(1)} %get-tuple-element.167), channel_id=1, source_target_pairs={{0,8},{1,9},{2,10},{3,11},{4,12},{5,13},{6,14},{7,15},{8,0},{9,1},... | collective-permute-start | bytes 491528 | tf_op jit(solution)/shard_map/ppermute | solution.py:1099
  174.1 14.5 %collective-permute-start.15 = (bf16[80,1024]{1,0:T(8,128)(2,1)S(1)}, bf16[80,1024]{1,0:T(8,128)(2,1)S(1)}, u32[]{:S(2)}, u32[]{:S(2)}) collective-permute-start(bf16[80,1024]{1,0:T(8,128)(2,1)S(1)} %get-tuple-element.168), channel_id=1, source_target_pairs={{0,12},{1,13},{2,14},{3,15},{4,8},{5,9},{6,10},{7,11},{8,4},{9,5},... | collective-permute-start | bytes 491528 | tf_op jit(solution)/shard_map/ppermute | solution.py:1099
  177.5 15.9 %collective-permute-start.17 = (bf16[48,3072]{1,0:T(8,128)(2,1)S(1)}, bf16[48,3072]{1,0:T(8,128)(2,1)S(1)}, u32[]{:S(2)}, u32[]{:S(2)}) collective-permute-start(bf16[48,3072]{1,0:T(8,128)(2,1)S(1)} %early_sum.1.early_ref), channel_id=1, source_target_pairs={{0,16},{16,0},{1,17},{17,1},{2,18},{18,2},{3,19},{19,3},{4,20},{20... | collective-permute-start | bytes 884744 | tf_op jit(solution)/shard_map/ppermute | solution.py:1099
  188.7 4.7 %collective-permute-start.16 = (bf16[48,1024]{1,0:T(8,128)(2,1)S(1)}, bf16[48,1024]{1,0:T(8,128)(2,1)S(1)}, u32[]{:S(2)}, u32[]{:S(2)}) collective-permute-start(bf16[48,1024]{1,0:T(8,128)(2,1)S(1)} %get-tuple-element.169.late_ref), channel_id=1, source_target_pairs={{0,16},{16,0},{1,17},{17,1},{2,18},{18,2},{3,19},{19,3},{4,20},{20... | collective-permute-start | bytes 294920 | tf_op jit(solution)/shard_map/ppermute | solution.py:1099

commit v4 on v3

--- a/solution.py
+++ b/solution.py
@@ -29,11 +29,11 @@
 US_GATES = 10
 US_PROJ = 20
 US_INTRA = 12
-US_MIX = 35
+US_MIX = 30
 US_WEIGHTS = 10
 US_BACK = 30
 US_CONV = 17
-US_INPUTS = 12
+US_INPUTS = 16
 US_SUMS = 2
 NT = (((1,), (1,)), ((), ()))
 TN = (((0,), (0,)), ((), ()))
@@ -361,7 +361,6 @@
 def mix_kernel(
     lengths_ref,
     skip_ref,
-    x_ref,
     act_ref,
     target_ref,
     source_ref,
@@ -372,11 +371,9 @@
     recv_ref,
     z_ref,
     dnorm_ref,
-    wo_ref,
     gain_ref,
     e0_ref,
     e1_ref,
-    out_ref,
     mixed_ref,
     dz_ref,
     dy_ref,
@@ -504,7 +501,6 @@
             in1[rows, cols] = entered1.astype(BF16)
             prod0[rows, cols] = (entered0 * from0[rows, cols]).astype(BF16)
             prod1[rows, cols] = (entered1 * from1[rows, cols]).astype(BF16)
-    out_ref[...] = (x_ref[...].astype(F32) + mm(mixed_ref[...], wo_ref[...])).astype(BF16)
     ones = e0_ref[0:heads, :]
     r_ref[0:heads, :] = mm_nt(ones, prod0[...])
     r_ref[heads : 2 * heads, :] = mm_nt(ones, prod1[...])
@@ -548,14 +544,11 @@
     last_ref,
     carry1,
     dscore,
-    low_s,
-    all_s,
     out0,
     out1,
-    prod0,
-    prod1,
     ds0,
     ds1,
+    kept,
     *,
     skipped,
     chunks,
@@ -587,11 +580,6 @@
     kept0 = jnp.sum(d0 * s0_ref[0].astype(F32), axis=0, keepdims=True) * keep0
     kept1 = jnp.sum(d1 * s1_ref[0].astype(F32), axis=0, keepdims=True) * keep1
     carry1[...] = keep1 * d1 + df1_ref[0].astype(F32)
-    ones = e0_ref[0:heads, :]
-    kept = jnp.concatenate([kept0, kept1, jnp.zeros((6, inner), F32)], axis=0)
-    kept_high = kept.astype(BF16)
-    kept_low = (kept - kept_high.astype(F32)).astype(BF16)
-    kept_sum = mm_nt(ones, kept_high) + mm_nt(ones, kept_low)
 
     t = lane_iota(CHUNK)
     b0, c0, b1, c1 = bc_columns(act_ref, inner, state)
@@ -606,17 +594,29 @@
     leave_cols = factors_ref[0]
     dscore[...] = jnp.zeros_like(dscore)
     left = lane_iota(2 * width) < width
-    for pair in range(heads // 2):
-        cols = slice(pair * 2 * width, (pair + 1) * 2 * width)
+
+    def columns_of(pair):
+        return slice(pair * 2 * width, (pair + 1) * 2 * width)
+
+    def products(pair):
+        cols = columns_of(pair)
         dweights = mm_nt(cut_pair(act_ref[:, cols], width), dy_ref[:, cols])
-        weights = []
+        return dweights
+
+    def carried(pair):
+        cols = columns_of(pair)
+        leave0 = mm(leave_cols, e0_ref[:, cols])
+        leave1 = mm(leave_cols, e1_ref[:, cols])
+        return leave0, leave1, mm(b0, ds0[:, cols]), mm(b1, ds1[:, cols])
+
+    def within(pair, dweights):
+        weights, lows, alls, scored = [], [], [], [0.0] * len(halves)
         for part in (0, 1):
             head = 2 * pair + part
-            held = slice(head * CHUNK, (head + 1) * CHUNK)
-            parts = []
+            parts, low_parts, all_parts = [], [], []
             sum0 = jnp.zeros((8, CHUNK), F32)
             sum1 = jnp.zeros((8, CHUNK), F32)
-            for rows, early, early_f, scores in halves:
+            for place, (rows, early, early_f, scores) in enumerate(halves):
                 power = jnp.where(
                     early,
                     in_cols[rows, head : head + 1] + target_ref[head : head + 1, :],
@@ -627,22 +627,30 @@
                 parts.append((decay * scores).astype(BF16))
                 at = part * CHUNK + rows.start
                 dweight = dweights[at : at + SUB] * decay
-                dscore[rows, :] += dweight
+                scored[place] = scored[place] + dweight
                 change = dweight * scores
                 low = change * early_f
-                low_s[rows, held] = low.astype(BF16)
-                all_s[rows, held] = change.astype(BF16)
+                low_parts.append(low.astype(BF16))
+                all_parts.append(change.astype(BF16))
                 sum0 = sum0 + fold(low)
                 sum1 = sum1 + fold(change)
             weights.append(jnp.concatenate(parts, axis=0))
+            lows.append(jnp.concatenate(low_parts, axis=0))
+            alls.append(jnp.concatenate(all_parts, axis=0))
             moves_ref[head : head + 1, :] = jnp.sum(sum0, axis=0, keepdims=True)
             moves_ref[heads + head : heads + head + 1, :] = jnp.sum(sum1, axis=0, keepdims=True)
-        dx = mm(jnp.concatenate(weights, axis=1), cut_pair(dy_ref[:, cols], width))
-        leave0 = mm(leave_cols, e0_ref[:, cols])
-        leave1 = mm(leave_cols, e1_ref[:, cols])
-        from0 = mm(b0, ds0[:, cols])
-        from1 = mm(b1, ds1[:, cols])
+        for place, (rows, _, _, _) in enumerate(halves):
+            dscore[rows, :] += scored[place]
+        return jnp.concatenate(weights, axis=1), lows + alls
+
+    def gathered(pair, weights, lows, states):
+        cols = columns_of(pair)
+        leave0, leave1, from0, from1 = states
+        dx = mm(weights, cut_pair(dy_ref[:, cols], width))
         skip = jnp.where(left, skip_ref[2 * pair], skip_ref[2 * pair + 1])
+        firsts, totals = [], []
+        sum0 = jnp.zeros((8, 2 * width), F32)
+        sum1 = jnp.zeros((8, 2 * width), F32)
         for rows, _, _, _ in halves:
             xf = act_ref[rows, cols].astype(F32)
             came0 = leave0[rows] * from0[rows]
@@ -651,17 +659,48 @@
             dpre_ref[rows, cols] = (dconv * slope_ref[rows, cols].astype(F32)).astype(BF16)
             out0[rows, cols] = (xf * leave0[rows]).astype(BF16)
             out1[rows, cols] = (xf * leave1[rows]).astype(BF16)
-            prod0[rows, cols] = (xf * came0).astype(BF16)
-            prod1[rows, cols] = (xf * came1).astype(BF16)
+            came0 = xf * came0
+            came1 = xf * came1
+            sum0 = sum0 + fold(came0)
+            sum1 = sum1 + fold(came1)
+            firsts.append(came0.astype(BF16))
+            totals.append(came1.astype(BF16))
+        kept[0:8, cols] = sum0
+        kept[8:16, cols] = sum1
+        return lows + [jnp.concatenate(firsts, axis=0), jnp.concatenate(totals, axis=0)]
+
+    def summed(pair, lows):
+        sums = mm_nt(spans_ref[...], jnp.concatenate(lows, axis=1))
+        moves_ref[2 * heads + 2 * pair : 2 * heads + 2 * pair + 2, :] = sums[0:2]
+        moves_ref[3 * heads + 2 * pair : 3 * heads + 2 * pair + 2, :] = sums[2:4]
+
+
+    pairs = heads // 2
+    ahead = {0: products(0)}
+    held, done = {}, {}
+    for pair in range(pairs + 2):
+        if pair + 1 < pairs:
+            ahead[pair + 1] = products(pair + 1)
+        if 0 < pair <= pairs:
+            weights, lows = held.pop(pair - 1)
+            states = carried(pair - 1)
+            done[pair - 1] = gathered(pair - 1, weights, lows, states)
+        if pair < pairs:
+            held[pair] = within(pair, ahead.pop(pair))
+        if pair > 1:
+            summed(pair - 2, done.pop(pair - 2))
     dscores = jnp.where(same, dscore[...], 0.0)
     dscore0 = jnp.where(row_iota(CHUNK) < t, dscores, 0.0).astype(BF16)
     dscore1 = jnp.where(row_iota(CHUNK) < t, 0.0, dscores).astype(BF16)
-    moves_ref[2 * heads : 3 * heads, :] = mm_nt(spans_ref[...], low_s[...])
-    moves_ref[3 * heads : 4 * heads, :] = mm_nt(spans_ref[...], all_s[...])
-    moves_ref[4 * heads : 5 * heads, :] = mm_nt(ones, prod0[...])
-    moves_ref[5 * heads : 6 * heads, :] = mm_nt(ones, prod1[...])
-    moves_ref[6 * heads : 7 * heads, :] = jnp.broadcast_to(kept_sum[:, 0:1], (heads, CHUNK))
-    moves_ref[7 * heads : 8 * heads, :] = jnp.broadcast_to(kept_sum[:, 1:2], (heads, CHUNK))
+    kept[0:1, :] += kept0
+    kept[8:9, :] += kept1
+    kept_sum = mm_nt(e0_ref[0:heads, :], in_parts(kept[...], 2).astype(BF16))
+    kept_sum = kept_sum[:, 0:16] + kept_sum[:, 16:32]
+    for direction in (0, 1):
+        column = jnp.sum(kept_sum[:, 8 * direction : 8 * direction + 8], axis=1, keepdims=True)
+        moves_ref[(4 + direction) * heads : (5 + direction) * heads, :] = jnp.broadcast_to(
+            column, (heads, CHUNK)
+        )
     db0 = mm(dscore0, c0) + mm_nt(out0[...], ds0[...])
     db1 = mm(dscore1, c1) + mm_nt(out1[...], ds1[...])
     dc0 = mm_tn(dscore0, b0) + dcc_ref[:, 0:state]
@@ -688,14 +727,14 @@
         parts = [values[chunk * heads : (chunk + 1) * heads] for chunk in range(chunks)]
         return jnp.concatenate(parts, axis=1)
 
-    got0, got, own0, own, k0, k1, kept0, kept1 = [
-        moves[part * heads : (part + 1) * heads] for part in range(8)
+    got0, got, own0, own, kept0, kept1 = [
+        moves[part * heads : (part + 1) * heads] for part in range(6)
     ]
     own1, got1 = own - own0, got - got0
-    da0 = exact_mm(stack(got0 + r[:heads] - own0), flag(s >= t)) + exact_mm(stack(k0), flag(s < t))
-    da1 = exact_mm(stack(got1 + r[heads:] - own1), flag(s <= t)) + exact_mm(stack(k1), flag(s > t))
+    da0 = exact_mm(stack(got0 + r[:heads] - own0), flag(s >= t))
+    da1 = exact_mm(stack(got1 + r[heads:] - own1), flag(s <= t))
     da = -jnp.concatenate([unstack(da0) + kept0, unstack(da1) + kept1], axis=0)
-    dlog = jnp.concatenate([own0 + k0, own1 + k1], axis=0)
+    dlog = jnp.concatenate([own0, own1], axis=0)
     sig = jax.nn.sigmoid(raw)
     ratio = jnp.where(raw < -20.0, 1.0, sig / jnp.maximum(dt, 1e-37))
     return dlog * ratio + da * rate * sig, jnp.sum(da * dt, axis=1, keepdims=True) * rate
@@ -869,7 +908,7 @@
         columns = jnp.concatenate(columns + [drate, jnp.zeros((steps, 5), F32)], axis=1).T
         for place in range(3):
             sums_ref[6:7, 128 * place : 128 * place + steps] = columns[place : place + 1]
-        small_ref[...] = in_parts(sums_ref[...], 2).astype(BF16)
+        small_ref[...] = narrowed(two_halves(sums_ref[...]))
 
 
 def halve_kernel(kept_ref, got_ref, keep_ref, send_ref, *, bit):
@@ -885,14 +924,15 @@
     out_ref[...] = (kept_ref[...].astype(F32) + got_ref[...].astype(F32)).astype(BF16)
 
 
+def narrowed(small):
+    few = small[6:7] + small[7:8]
+    high = few.astype(BF16).astype(F32)
+    return jnp.concatenate([small[0:6], high, few - high, small[8:16]], axis=0).astype(BF16)
+
+
 def two_halves(small):
     half = small.shape[1] // 2
     return jnp.concatenate([small[:, 0:half], small[:, half:]], axis=0)
-
-
-def parts_sum(parts):
-    half = parts.shape[0] // 2
-    return parts[0:half].astype(F32) + parts[half:].astype(F32)
 
 
 def quarters_kernel(
@@ -911,10 +951,8 @@
     row_bit = lax.rem(lax.axis_index("dp") // 2, 2)
     side = lax.axis_index("dir")
     count = mine_ref.shape[0] // 2
-    small = two_halves(parts_sum(small_ref[...]) + parts_sum(smallgot_ref[...]))
-    few = small.shape[0]
-    parts = in_parts(small, 2)
-    keep_ref[count:, :] = parts[0:few] + parts[few:]
+    small = narrowed(small_ref[...].astype(F32) + smallgot_ref[...].astype(F32))
+    keep_ref[count:, :] = small.astype(F32)
     for out_ref, row, column in (
         (keep_ref, row_bit, side),
         (across_ref, row_bit, 1 - side),
@@ -922,7 +960,7 @@
         (both_ref, 1 - row_bit, 1 - side),
     ):
         if out_ref is not keep_ref:
-            out_ref[count:, :] = parts.astype(BF16)
+            out_ref[count:, :] = small
         for place in range(count // shard):
             rows = slice(place * shard, (place + 1) * shard)
             here = pl.ds(pl.multiple_of((2 * place + row) * shard, shard), shard)
@@ -934,10 +972,9 @@
 def levels_kernel(keep_ref, a_ref, b_ref, c_ref, own_ref, s1_ref, s2_ref, s3_ref, *, shard):
     level = lax.axis_index("dp") // 4
     count = 4 * shard
-    small = [parts_sum(ref[count:, :]) for ref in (a_ref, b_ref, c_ref)]
-    parts = in_parts(keep_ref[count:, :] + small[0] + (small[1] + small[2]), 2)
-    few = parts.shape[0] // 2
-    own_ref[shard : shard + few, :] = parts[0:few] + parts[few:]
+    small = [ref[count:, :].astype(F32) for ref in (a_ref, b_ref, c_ref)]
+    small = narrowed(keep_ref[count:, :] + small[0] + (small[1] + small[2]))
+    own_ref[shard:, :] = small.astype(F32)
     for bits, out_ref in enumerate((own_ref, s1_ref, s2_ref, s3_ref)):
         wanted = jnp.bitwise_xor(level, bits)
         rows = pl.ds(pl.multiple_of(wanted * shard, shard), shard)
@@ -945,17 +982,14 @@
         total = total + (b_ref[rows, :].astype(F32) + c_ref[rows, :].astype(F32))
         out_ref[0:shard, :] = total.astype(out_ref.dtype)
         if bits:
-            out_ref[shard : shard + 2 * few, :] = parts.astype(BF16)
-
-
-def joined(ref, shard):
-    return ref[0:shard, :].astype(F32), parts_sum(ref[shard:, :])
+            out_ref[shard:, :] = small
 
 
 def last_kernel(own_ref, a_ref, b_ref, c_ref, out_ref, small_ref, *, shard):
-    a, b, c = (joined(ref, shard) for ref in (a_ref, b_ref, c_ref))
-    out_ref[...] = (own_ref[0:shard, :] + a[0] + (b[0] + c[0])).astype(BF16)
-    small_ref[...] = own_ref[shard:, :] + a[1] + (b[1] + c[1])
+    total = own_ref[...] + a_ref[...].astype(F32)
+    total = total + (b_ref[...].astype(F32) + c_ref[...].astype(F32))
+    out_ref[...] = total[0:shard].astype(BF16)
+    small_ref[...] = total[shard:]
 
 
 def finish_kernel(
@@ -995,12 +1029,13 @@
     gtaps_ref[...] = small[0:4, 0 : gtaps_ref.shape[1]]
     gmix_ref[...] = small[4:5, 0:inner].reshape(inner)
     gin_ref[...] = small[5:6, 0:model].reshape(model)
+    few = small[6:7] + small[7:8]
     heads = gskip_ref.shape[0]
-    gskip_ref[...] = small[6:7, 0:128].reshape(128)[0:heads]
-    gbias_ref[0:1, :] = small[6:7, 128 : 128 + heads]
-    gbias_ref[1:2, :] = small[6:7, 128 + heads : 128 + 2 * heads]
-    galog_ref[0:1, :] = small[6:7, 256 : 256 + heads]
-    galog_ref[1:2, :] = small[6:7, 256 + heads : 256 + 2 * heads]
+    gskip_ref[...] = few[:, 0:128].reshape(128)[0:heads]
+    gbias_ref[0:1, :] = few[:, 128 : 128 + heads]
+    gbias_ref[1:2, :] = few[:, 128 + heads : 128 + 2 * heads]
+    galog_ref[0:1, :] = few[:, 256 : 256 + heads]
+    galog_ref[1:2, :] = few[:, 256 + heads : 256 + 2 * heads]
 
 
 def inputs_kernel(
@@ -1014,7 +1049,10 @@
     wx_ref,
     wbc_ref,
     wz_ref,
+    mixed_ref,
+    wo_ref,
     gin_ref,
+    out_ref,
     dproj,
 ):
     step = pl.program_id(0)
@@ -1040,6 +1078,7 @@
     x = x_ref[...].astype(F32)
     inv = lax.rsqrt(jnp.mean(x * x, axis=1, keepdims=True) + EPS)
     unit = x * inv
+    out_ref[...] = (x + mm(mixed_ref[...], wo_ref[...])).astype(BF16)
     f = dn * row_of(gain_ref)
     back = inv * (f - unit * jnp.mean(f * unit, axis=1, keepdims=True))
     gin_ref[...] = (c_ref[...].astype(F32) + back).astype(BF16)
@@ -1160,7 +1199,16 @@
     zeros = np.zeros_like(spread)
     e0 = jnp.asarray(np.concatenate([spread, zeros, spread, zeros]), BF16)
     e1 = jnp.asarray(np.concatenate([zeros, spread, zeros, spread]), BF16)
-    spans = jnp.asarray(np.repeat(np.eye(heads, dtype=np.float32), CHUNK, axis=1), BF16)
+    spans = np.zeros((8, 6 * CHUNK), np.float32)
+    for head in range(2):
+        columns = slice(head * width, (head + 1) * width)
+        spans[head, head * CHUNK : (head + 1) * CHUNK] = 1.0
+        spans[head, 4 * CHUNK : 5 * CHUNK][columns] = 1.0
+        spans[2 + head, (2 + head) * CHUNK : (3 + head) * CHUNK] = 1.0
+        spans[2 + head, 4 * CHUNK : 5 * CHUNK][columns] = 1.0
+        spans[2 + head, 5 * CHUNK : 6 * CHUNK][columns] = 1.0
+    spans = jnp.asarray(spans, BF16)
+
     def rows_out(size, columns, dtype):
         return (rows_of(size, columns), (count, columns), dtype)
 
@@ -1269,14 +1317,13 @@
         return pl.BlockSpec((1,) + rest, lambda i: (chunks - 1 - i,) + (0,) * len(rest))
 
     states = (down_parts(state, inner), (chunks, state, inner), BF16)
-    out, mixed, dz, dy, r, dcc, dl0, df1, s0, s1, d_send, mix_sums = call(
+    mixed, dz, dy, r, dcc, dl0, df1, s0, s1, d_send, mix_sums = call(
         mix_kernel,
         "mix",
         chunks,
         [
             smem(),
             smem(),
-            down_rows(model),
             down_rows(channels),
             down_lanes(steps),
             down_lanes(steps),
@@ -1287,13 +1334,11 @@
             whole((state, inner)),
             down_rows(inner),
             down_rows(inner),
-            whole((inner, model)),
             whole((inner,)),
             whole(e0.shape),
             whole(e1.shape),
         ],
         [
-            (down_rows(model), (count, model), BF16),
             (down_rows(inner), (count, inner), BF16),
             (down_rows(inner), (count, inner), BF16),
             (down_rows(inner), (count, inner), BF16),
@@ -1311,7 +1356,6 @@
         (
             lengths,
             d_skip,
-            x,
             act,
             target,
             source,
@@ -1322,7 +1366,6 @@
             received,
             gate_z,
             d_norm,
-            w_out,
             gain_mix,
             e0,
             e1,
@@ -1424,17 +1467,16 @@
             ],
             [
                 (rows_from(channels), (count, channels), BF16),
-                (lanes_from(8 * heads), (8 * heads, count), F32),
+                (lanes_from(6 * heads), (6 * heads, count), F32),
                 full((state, inner), F32),
             ],
             [
                 state_f32,
                 pltpu.VMEM((CHUNK, CHUNK), F32),
-                pltpu.VMEM((CHUNK, heads * CHUNK), BF16),
-                pltpu.VMEM((CHUNK, heads * CHUNK), BF16),
             ]
-            + [chunk_bf16] * 4
-            + [state_bf16] * 2,
+            + [chunk_bf16] * 2
+            + [state_bf16] * 2
+            + [pltpu.VMEM((16, inner), F32)],
             US_BACK * taken // chunks,
             (
                 lengths,
@@ -1498,7 +1540,7 @@
             whole((steps, count)),
             whole((steps, count)),
             whole((steps, 128)),
-            whole((8 * heads, count)),
+            whole((6 * heads, count)),
             whole((steps, count)),
             whole((model, inner)),
             whole(w_narrow.shape),
@@ -1513,7 +1555,7 @@
             late_out,
             late_out,
             full((steps, count), BF16),
-            full((16, wide), BF16),
+            full((16, wide // 2), BF16),
         ],
         [
             pltpu.VMEM((3 * count + 48, CHUNK + 16), BF16),
@@ -1546,7 +1588,7 @@
     )
     d_halo = lax.ppermute(dhalo, "dir", [(1, 0)])
 
-    (grad_in,) = call(
+    grad_in, out = call(
         inputs_kernel,
         "inputs",
         count // ROWS,
@@ -1561,11 +1603,13 @@
             whole((model, inner)),
             whole(w_narrow.shape),
             whole((model, inner)),
+            rows_of(ROWS, inner),
+            whole((inner, model)),
         ],
-        [rows_out(ROWS, model, BF16)],
+        [rows_out(ROWS, model, BF16), rows_out(ROWS, model, BF16)],
         [pltpu.VMEM((ROWS, channels), BF16)],
         US_INPUTS,
-        (x, cot, gain_in, dproj, d_halo, draw, dz, w_x, w_narrow, w_z),
+        (x, cot, gain_in, dproj, d_halo, draw, dz, w_x, w_narrow, w_z, mixed, w_out),
         VMEM_INPUTS,
     )
 
@@ -1579,7 +1623,8 @@
         early = undivided(early_mine, early_theirs)
         g_out = early[:, :inner].reshape(16, piece, 2, model).transpose(0, 2, 1, 3)
         late = sum_shards(undivided(late_mine, late_theirs), dp_count)
-        small = sum_all(small[0:8].astype(F32) + small[8:16].astype(F32), dp_count)
+        small = jnp.concatenate([small[0:8], small[8:16]], axis=1).astype(F32)
+        small = sum_all(small, dp_count)
         return (
             out[None],
             grad_in[None],
@@ -1598,16 +1643,15 @@
     early_got, late_theirs = ordered(early_got, late_theirs)
     late_got = traded(late_theirs, "dp", 1, dp_count)
     small_got = traded(small, "dp", 1, dp_count)
-    early_keep, early_send = halve("halve_z2", early_keep, early_got, 8)
-    early_send, late_got = ordered(early_send, late_got)
-    early_got = traded(early_send, "dp", 8, dp_count)
-    quarter = (model // 4 + 32, wide // 2)
+    quarter = (model // 4 + 16, wide // 2)
     kept, across, along, both = plain(
         functools.partial(quarters_kernel, shard=piece),
         "quarters",
         (late_mine, late_got, small, small_got),
         [((model // 4 + 16, wide // 2), F32), (quarter, BF16), (quarter, BF16), (quarter, BF16)],
     )
+    early_got, both = ordered(early_got, both)
+    early_keep, early_send = halve("halve_z2", early_keep, early_got, 8)
     corners = [(a, b) for a in range(2) for b in range(dp_count)]
     across = traded(across, "dir", 1, 2)
     along = traded(along, "dp", 2, dp_count)
@@ -1616,10 +1660,11 @@
         ("dir", "dp"),
         [(a * dp_count + b, (1 - a) * dp_count + (b ^ 2)) for a, b in corners],
     )
+    early_got = traded(early_send, "dp", 8, dp_count)
     (early,) = plain(sum_kernel, "early_sum", (early_keep, early_got), [((piece, 2 * inner), BF16)])
     grad_in, early, both = lax.optimization_barrier((grad_in, early, both))
     early_got = traded(early, "dir", 1, 2)
-    message = (piece + 32, wide // 2)
+    message = (piece + 16, wide // 2)
     own, *sends = plain(
         functools.partial(levels_kernel, shard=piece),
         "levels",

time: 195 us -> 188 us (0.964)
  Pallas kernels: 141 us -> 136 us
  waiting for transfers between devices: 22.5 us -> 18.9 us
  local copies, waits for them, and re-layouts: 3.25 us -> 5.38 us
    pallas_call x8, Pallas kernels: 138 us -> 134 us  [call(): pl.pallas_call(kernel, name=name, grid=(grid,), in_specs=in_specs, out_sp...]
    ppermute x13, waiting for transfers between devices: 21 us -> 17.3 us  [traded(): return lax.ppermute(values, axis, [(i, i ^ bit) for i in range(size)])]
    unnamed x14, local copies, waits for them, and re-layouts: 2.51 us -> 4.64 us
  transfers between devices with their start and end apart: 18 -> 18, of which waited for: 7 -> 8; matrix products, arithmetic and copies ran while one was open for 0% -> 0% of each run, Pallas kernels for 44% -> 45%
where the time goes in v4:
time: 188 us
  Pallas kernels  136 us (72%)
  starting transfers between devices  26.6 us (14%)
  waiting for transfers between devices  18.9 us (10%)
  local copies, waits for them, and re-layouts  5.38 us (3%)
    pallas_call x8, Pallas kernels, call(): pl.pallas_call(kernel, name=name, grid=(grid,), in_specs=in_specs, out_sp...  134 us
    ppermute x13, waiting for transfers between devices, traded(): return lax.ppermute(values, axis, [(i, i ^ bit) for i in range(size)])  17.3 us
    ppermute x13, starting transfers between devices, traded(): return lax.ppermute(values, axis, [(i, i ^ bit) for i in range(size)])  15.1 us
    ppermute x1, starting transfers between devices, local(): halo = lax.ppermute(x[count - 16:], 'dir', [(0, 1)])  4.83 us
    unnamed x14, local copies, waits for them, and re-layouts  4.64 us
  transfers between devices with their start and end apart: 18, of which 8 were waited for; matrix products, arithmetic and copies ran while one was open for 0% of the time, Pallas kernels for 45%

profile of v4, /device:TPU:0, one launch (start us, length us, event | category | flops | bytes accessed | tf_op | source)
XLA Modules:
  0.0 188.0 jit_solution(17012249415187859489)
XLA Ops:
  0.6 0.7 slice_bitcast_fusion
  1.4 4.8 %collective-permute-start = (bf16[16,768]{1,0:T(8,128)(2,1)S(1)}, bf16[16,768]{1,0:T(8,128)(2,1)S(1)}, u32[]{:S(2)}, u32[]{:S(2)}) collective-permute-start(bf16[16,768]{1,0:T(8,128)(2,1)S(1)} %slice_bitcast_fusion), channel_id=1, source_target_pairs={{0,16},{1,17},{2,18},{3,19},{4,20},{5,21},{6,22},{7,23},{8,24},{9,... | collective-permute-start | bytes 73736 | tf_op jit(solution)/shard_map/ppermute | solution.py:1196
  6.2 1.5 collective-permute-done.halo_ref
  7.7 0.6 copy-done.6
  8.3 20.8 %proj.1 = (bf16[1024,768]{1,0:T(8,128)(2,1)}, f32[48,1024]{1,0:T(8,128)}, f32[48,1024]{1,0:T(8,128)}, f32[48,128]{1,0:T(8,128)}, f32[48,1024]{1,0:T(8,128)}, /*i...) custom-call(s32[1,8]{1,0:T(1,128)} %lengths_ref.9, ...), custom_call_target="tpu_custom_call" | custom-call | flops 23000000512 | tf_op jit(solution)/shard_map/proj/pallas_call | solution.py:1121
  29.2 2.4 %collective-permute-start.1 = (bf16[64,1536]{1,0:T(8,128)(2,1)}, bf16[64,1536]{1,0:T(8,128)(2,1)S(1)}, u32[]{:S(2)}, u32[]{:S(2)}) collective-permute-start(bf16[64,1536]{1,0:T(8,128)(2,1)} %get-tuple-element.108), channel_id=1, source_target_pairs={{0,16},{16,0},{1,17},{17,1},{2,18},{18,2},{3,19},{19,3},{4,20},{20... | collective-permute-start | bytes 589832 | tf_op jit(solution)/shard_map/ppermute | solution.py:1287
  31.5 9.5 %gates.1 = (bf16[1024,1536]{1,0:T(8,128)(2,1)}, bf16[1024,1536]{1,0:T(8,128)(2,1)}, bf16[768,1024]{1,0:T(8,128)(2,1)}) custom-call(bf16[1024,768]{1,0:T(8,128)(2,1)} %get-tuple-element.98.normed_ref, bf16[1024,768]{1,0:T(8,128)(2,1)} %bitcast.9, bf16[768,1536]{1,0:T(8,128)(2,1)} %wz_ref.5, bf16[1536,768]{1,0:T(8,128)(2,1)} %wo_ref.3), custom_call_target="tpu_custom_call" | custom-call | flops 11500000256 | tf_op jit(solution)/shard_map/gates/pallas_call | solution.py:1121
  41.1 0.7 copy-done.4
  41.7 28.8 %mix.1 = (bf16[1024,1536]{1,0:T(8,128)(2,1)}, bf16[1024,1536]{1,0:T(8,128)(2,1)}, bf16[1024,1536]{1,0:T(8,128)(2,1)}, f32[48,1024]{1,0:T(8,128)}, f32[1024,128]{...) custom-call(s32[1,8]{1,0:T(1,128)} %lengths_ref.9, ...), custom_call_target="tpu_custom_call" | custom-call | flops 34500001792 | tf_op jit(solution)/shard_map/mix/pallas_call | solution.py:1121
  70.5 0.1 collective-permute-start.2
  70.6 11.8 %weights.1 = (bf16[384,3072]{1,0:T(8,128)(2,1)}, bf16[384,3072]{1,0:T(8,128)(2,1)}, f32[4,1,192]{2,1,0:T(1,128)}) custom-call(bf16[768,1024]{1,0:T(8,128)(2,1)} %get-tuple-element.99.turned_ref, bf16[1024,1536]{1,0:T(8,128)(2,1)} %get-tuple-element.111.dz_ref, bf16[1024,1536]{1,0:T(8,128)(2,1)} %get-tuple-element.112.mixed_ref, bf16[1024,768]{1,0:T(8,128)(2,1)} %bitcast.10, ...), custom_call_target="tpu_custom_call" | custom-call | flops 11500000256 | tf_op jit(solution)/shard_map/weights/pallas_call | solution.py:1121
  82.4 0.1 collective-permute-start.3
  82.5 0.6 copy-done.3
  83.1 5.7 %back0.1 = (bf16[1024,1792]{1,0:T(8,128)(2,1)}, f32[144,1024]{1,0:T(8,128)}, f32[64,1536]{1,0:T(8,128)}) custom-call(s32[1,8]{1,0:T(1,128)} %lengths_ref.9, f32[24]{0:T(128)} %skip_ref.5, bf16[1024,1792]{1,0:T(8,128)(2,1)} %get-tuple-element.101.act_ref, bf16[1024,1792]{1,0:T(8,128)(2,1)} %get-tuple-element.120.slope_ref, ...), custom_call_target="tpu_custom_call" | custom-call | flops 3449999872 | tf_op jit(solution)/shard_map/back0/pallas_call | solution.py:1121
  88.8 0.6 halve_y.1
  89.4 1.6 collective-permute-start.4
  91.0 22.9 %back1.1 = (bf16[1024,1792]{1,0:T(8,128)(2,1)}, f32[144,1024]{1,0:T(8,128)}, f32[64,1536]{1,0:T(8,128)}) custom-call(s32[1,8]{1,0:T(1,128)} %lengths_ref.9, f32[24]{0:T(128)} %skip_ref.5, bf16[1024,1792]{1,0:T(8,128)(2,1)} %get-tuple-element.101.act_ref, ...), custom_call_target="tpu_custom_call", output_to_operand_aliasing={{0}: (19, {}), {1}: (20, {})} | custom-call | flops 29899999232 | tf_op jit(solution)/shard_map/back1/pallas_call | solution.py:1121
  113.9 3.3 %collective-permute-done.4.got_ref = bf16[192,3072]{1,0:T(8,128)(2,1)S(1)} collective-permute-done((bf16[192,3072]{1,0:T(8,128)(2,1)S(1)}, bf16[192,3072]{1,0:T(8,128)(2,1)S(1)}, u32[]{:S(2)}, u32[]{:S(2)}) %collective-permute-start.4) | collective-permute-done | bytes 1179680 | tf_op jit(solution)/shard_map/ppermute | solution.py:1138
  117.3 0.2 halve_z.1
  117.5 1.6 collective-permute-start.6
  119.1 18.6 %conv_back.1 = (bf16[1024,1792]{1,0:T(8,128)(2,1)}, bf16[16,1792]{1,0:T(8,128)(2,1)}, bf16[384,2048]{1,0:T(8,128)(2,1)}, bf16[384,2048]{1,0:T(8,128)(2,1)}, bf16...) custom-call(s32[1,8]{1,0:T(1,128)} %lengths_ref.9, bf16[768,1024]{1,0:T(8,128)(2,1)} %get-tuple-element.99.turned_ref, ...), custom_call_target="tpu_custom_call" | custom-call | flops 19549999104 | tf_op jit(solution)/shard_map/conv_back/pallas_call | solution.py:1121
  137.8 0.1 collective-permute-start.7
  137.9 0.5 collective-permute-start.8
  138.4 1.3 collective-permute-start.5
  139.6 1.9 collective-permute-done.8.smallgot_ref
  141.5 0.8 copy-done
  142.3 1.4 copy-done.2
  143.7 0.4 quarters.1
  144.1 0.1 halve_z2.1
  144.2 2.6 %collective-permute-start.9 = (bf16[48,3072]{1,0:T(8,128)(2,1)S(1)}, bf16[48,3072]{1,0:T(8,128)(2,1)S(1)}, u32[]{:S(2)}, u32[]{:S(2)}) collective-permute-start(bf16[48,3072]{1,0:T(8,128)(2,1)S(1)} %get-tuple-element.160), channel_id=1, source_target_pairs={{0,8},{1,9},{2,10},{3,11},{4,12},{5,13},{6,14},{7,15},{8,0},{9,1},... | collective-permute-start | bytes 884744 | tf_op jit(solution)/shard_map/ppermute | solution.py:1138
  146.8 2.9 %collective-permute-start.10 = (bf16[208,1024]{1,0:T(8,128)(2,1)S(1)}, bf16[208,1024]{1,0:T(8,128)(2,1)S(1)}, u32[]{:S(2)}, u32[]{:S(2)}) collective-permute-start(bf16[208,1024]{1,0:T(8,128)(2,1)S(1)} %get-tuple-element.161), channel_id=1, source_target_pairs={{0,18},{1,19},{2,16},{3,17},{4,22},{5,23},{6,20},{7,21},{8,26},{9,... | collective-permute-start | bytes 1277960 | tf_op jit(solution)/shard_map/ppermute | solution.py:1658
  149.8 0.5 collective-permute-start.12
  150.3 0.6 copy-done.5
  151.0 15.5 %inputs.1 = (bf16[1024,768]{1,0:T(8,128)(2,1)}, bf16[1024,768]{1,0:T(8,128)(2,1)}) custom-call(bf16[1024,768]{1,0:T(8,128)(2,1)} %bitcast.8, bf16[1024,768]{1,0:T(8,128)(2,1)} %bitcast.11, f32[768]{0:T(1024)} %gain_ref.7, bf16[1024,1792]{1,0:T(8,128)(2,1)} %get-tuple-element.145.dproj_ref, bf16[16,1792]{1,0:T(8,128)(2,1)} %copy-done.5, ...), custom_call_target="tpu_custom_call" | custom-call | flops 18400000000 | tf_op jit(solution)/shard_map/inputs/pallas_call | solution.py:1121
  166.5 0.1 early_sum.1.early_ref
  166.6 2.0 %collective-permute-done.11.a_ref = bf16[208,1024]{1,0:T(8,128)(2,1)S(1)} collective-permute-done((bf16[208,1024]{1,0:T(8,128)(2,1)S(1)}, bf16[208,1024]{1,0:T(8,128)(2,1)S(1)}, u32[]{:S(2)}, u32[]{:S(2)}) %collective-permute-start.11) | collective-permute-done | bytes 426016 | tf_op jit(solution)/shard_map/ppermute | solution.py:1138
  168.5 0.2 collective-permute-done.12.b_ref
  168.7 0.2 levels.1
  168.9 0.5 collective-permute-start.13
  169.4 0.4 collective-permute-start.14
  169.8 3.6 %collective-permute-start.15 = (bf16[64,1024]{1,0:T(8,128)(2,1)S(1)}, bf16[64,1024]{1,0:T(8,128)(2,1)S(1)}, u32[]{:S(2)}, u32[]{:S(2)}) collective-permute-start(bf16[64,1024]{1,0:T(8,128)(2,1)S(1)} %get-tuple-element.170), channel_id=1, source_target_pairs={{0,12},{1,13},{2,14},{3,15},{4,8},{5,9},{6,10},{7,11},{8,4},{9,5},... | collective-permute-start | bytes 393224 | tf_op jit(solution)/shard_map/ppermute | solution.py:1138
  173.4 1.8 collective-permute-start.17
  175.2 0.8 collective-permute-done.13.a_ref
  176.0 6.3 %collective-permute-done.14.b_ref = bf16[64,1024]{1,0:T(8,128)(2,1)S(1)} collective-permute-done((bf16[64,1024]{1,0:T(8,128)(2,1)S(1)}, bf16[64,1024]{1,0:T(8,128)(2,1)S(1)}, u32[]{:S(2)}, u32[]{:S(2)}) %collective-permute-start.14) | collective-permute-done | bytes 131104 | tf_op jit(solution)/shard_map/ppermute | solution.py:1138
  182.3 0.1 last.1
  182.3 1.8 collective-permute-start.16
  184.1 2.9 %collective-permute-done.16.lategot_ref = bf16[48,1024]{1,0:T(8,128)(2,1)S(1)} collective-permute-done((bf16[48,1024]{1,0:T(8,128)(2,1)S(1)}, bf16[48,1024]{1,0:T(8,128)(2,1)S(1)}, u32[]{:S(2)}, u32[]{:S(2)}) %collective-permute-start.16) | collective-permute-done | bytes 98336 | tf_op jit(solution)/shard_map/ppermute | solution.py:1138
  187.0 1.0 finish.1
  (19 shorter events, 0.1 us)
Async XLA Ops:
  1.4 6.3 %collective-permute-start = (bf16[16,768]{1,0:T(8,128)(2,1)S(1)}, bf16[16,768]{1,0:T(8,128)(2,1)S(1)}, u32[]{:S(2)}, u32[]{:S(2)}) collective-permute-start(bf16[16,768]{1,0:T(8,128)(2,1)S(1)} %slice_bitcast_fusion), channel_id=1, source_target_pairs={{0,16},{1,17},{2,18},{3,19},{4,20},{5,21},{6,22},{7,23},{8,24},{9,... | collective-permute-start | bytes 73736 | tf_op jit(solution)/shard_map/ppermute | solution.py:1196
  7.7 0.6 copy-start.6
  29.2 11.9 %collective-permute-start.1 = (bf16[64,1536]{1,0:T(8,128)(2,1)}, bf16[64,1536]{1,0:T(8,128)(2,1)S(1)}, u32[]{:S(2)}, u32[]{:S(2)}) collective-permute-start(bf16[64,1536]{1,0:T(8,128)(2,1)} %get-tuple-element.108), channel_id=1, source_target_pairs={{0,16},{16,0},{1,17},{17,1},{2,18},{18,2},{3,19},{19,3},{4,20},{20... | collective-permute-start | bytes 589832 | tf_op jit(solution)/shard_map/ppermute | solution.py:1287
  41.0 0.7 copy-start.4
  70.5 11.9 %collective-permute-start.2 = (bf16[64,1536]{1,0:T(8,128)(2,1)}, bf16[64,1536]{1,0:T(8,128)(2,1)S(1)}, u32[]{:S(2)}, u32[]{:S(2)}) collective-permute-start(bf16[64,1536]{1,0:T(8,128)(2,1)} %get-tuple-element.115), channel_id=1, source_target_pairs={{0,16},{16,0},{1,17},{17,1},{2,18},{18,2},{3,19},{19,3},{4,20},{20... | collective-permute-start | bytes 589832 | tf_op jit(solution)/shard_map/ppermute | solution.py:1375
  82.4 0.7 copy-start.3
  82.4 6.4 %collective-permute-start.3 = (bf16[384,3072]{1,0:T(8,128)(2,1)}, bf16[384,3072]{1,0:T(8,128)(2,1)S(1)}, u32[]{:S(2)}, u32[]{:S(2)}) collective-permute-start(bf16[384,3072]{1,0:T(8,128)(2,1)} %get-tuple-element.117), channel_id=1, source_target_pairs={{0,1},{1,0},{2,3},{3,2},{4,5},{5,4},{6,7},{7,6},{8,9},{9,8},{10,11... | collective-permute-start | bytes 7077896 | tf_op jit(solution)/shard_map/ppermute | solution.py:1138
  83.1 5.7 %copy-start.1 = (bf16[384,3072]{1,0:T(8,128)(2,1)S(1)}, bf16[384,3072]{1,0:T(8,128)(2,1)}, u32[]{:S(2)}) copy-start(bf16[384,3072]{1,0:T(8,128)(2,1)} %get-tuple-element.116.kept_ref) | copy-start | bytes 7077892
  89.4 27.9 %collective-permute-start.4 = (bf16[192,3072]{1,0:T(8,128)(2,1)S(1)}, bf16[192,3072]{1,0:T(8,128)(2,1)S(1)}, u32[]{:S(2)}, u32[]{:S(2)}) collective-permute-start(bf16[192,3072]{1,0:T(8,128)(2,1)S(1)} %get-tuple-element.129), channel_id=1, source_target_pairs={{0,2},{1,3},{2,0},{3,1},{4,6},{5,7},{6,4},{7,5},{8,10},{9,11},{10,... | collective-permute-start | bytes 3538952 | tf_op jit(solution)/shard_map/ppermute | solution.py:1138
  117.5 20.3 %collective-permute-start.6 = (bf16[96,3072]{1,0:T(8,128)(2,1)S(1)}, bf16[96,3072]{1,0:T(8,128)(2,1)S(1)}, u32[]{:S(2)}, u32[]{:S(2)}) collective-permute-start(bf16[96,3072]{1,0:T(8,128)(2,1)S(1)} %get-tuple-element.151), channel_id=1, source_target_pairs={{0,4},{1,5},{2,6},{3,7},{4,0},{5,1},{6,2},{7,3},{8,12},{9,13},{10,... | collective-permute-start | bytes 1769480 | tf_op jit(solution)/shard_map/ppermute | solution.py:1138
  137.8 3.7 %collective-permute-start.7 = (bf16[384,2048]{1,0:T(8,128)(2,1)}, bf16[384,2048]{1,0:T(8,128)(2,1)S(1)}, u32[]{:S(2)}, u32[]{:S(2)}) collective-permute-start(bf16[384,2048]{1,0:T(8,128)(2,1)} %get-tuple-element.155), channel_id=1, source_target_pairs={{0,1},{1,0},{2,3},{3,2},{4,5},{5,4},{6,7},{7,6},{8,9},{9,8},{10,11... | collective-permute-start | bytes 4718600 | tf_op jit(solution)/shard_map/ppermute | solution.py:1138
  137.9 3.7 %collective-permute-start.8 = (bf16[16,1024]{1,0:T(8,128)(2,1)}, bf16[16,1024]{1,0:T(8,128)(2,1)S(1)}, u32[]{:S(2)}, u32[]{:S(2)}) collective-permute-start(bf16[16,1024]{1,0:T(8,128)(2,1)} %get-tuple-element.156.small_ref), channel_id=1, source_target_pairs={{0,1},{1,0},{2,3},{3,2},{4,5},{5,4},{6,7},{7,6},{8,9},{9,8},{10,11... | collective-permute-start | bytes 98312 | tf_op jit(solution)/shard_map/ppermute | solution.py:1138
  138.4 12.0 %collective-permute-start.5 = (bf16[16,1792]{1,0:T(8,128)(2,1)}, bf16[16,1792]{1,0:T(8,128)(2,1)S(1)}, u32[]{:S(2)}, u32[]{:S(2)}) collective-permute-start(bf16[16,1792]{1,0:T(8,128)(2,1)} %get-tuple-element.146), channel_id=1, source_target_pairs={{16,0},{17,1},{18,2},{19,3},{20,4},{21,5},{22,6},{23,7},{24,8},{25... | collective-permute-start | bytes 172040 | tf_op jit(solution)/shard_map/ppermute | solution.py:1589
  141.5 0.8 copy-start
  142.3 1.4 copy-start.2
  144.2 22.3 %collective-permute-start.9 = (bf16[48,3072]{1,0:T(8,128)(2,1)S(1)}, bf16[48,3072]{1,0:T(8,128)(2,1)S(1)}, u32[]{:S(2)}, u32[]{:S(2)}) collective-permute-start(bf16[48,3072]{1,0:T(8,128)(2,1)S(1)} %get-tuple-element.160), channel_id=1, source_target_pairs={{0,8},{1,9},{2,10},{3,11},{4,12},{5,13},{6,14},{7,15},{8,0},{9,1},... | collective-permute-start | bytes 884744 | tf_op jit(solution)/shard_map/ppermute | solution.py:1138
  146.8 19.7 %collective-permute-start.10 = (bf16[208,1024]{1,0:T(8,128)(2,1)S(1)}, bf16[208,1024]{1,0:T(8,128)(2,1)S(1)}, u32[]{:S(2)}, u32[]{:S(2)}) collective-permute-start(bf16[208,1024]{1,0:T(8,128)(2,1)S(1)} %get-tuple-element.161), channel_id=1, source_target_pairs={{0,18},{1,19},{2,16},{3,17},{4,22},{5,23},{6,20},{7,21},{8,26},{9,... | collective-permute-start | bytes 1277960 | tf_op jit(solution)/shard_map/ppermute | solution.py:1658
  149.8 18.8 %collective-permute-start.11 = (bf16[208,1024]{1,0:T(8,128)(2,1)S(1)}, bf16[208,1024]{1,0:T(8,128)(2,1)S(1)}, u32[]{:S(2)}, u32[]{:S(2)}) collective-permute-start(bf16[208,1024]{1,0:T(8,128)(2,1)S(1)} %get-tuple-element.164), channel_id=1, source_target_pairs={{0,16},{16,0},{1,17},{17,1},{2,18},{18,2},{3,19},{19,3},{4,20},{20... | collective-permute-start | bytes 1277960 | tf_op jit(solution)/shard_map/ppermute | solution.py:1138
  149.8 18.9 %collective-permute-start.12 = (bf16[208,1024]{1,0:T(8,128)(2,1)S(1)}, bf16[208,1024]{1,0:T(8,128)(2,1)S(1)}, u32[]{:S(2)}, u32[]{:S(2)}) collective-permute-start(bf16[208,1024]{1,0:T(8,128)(2,1)S(1)} %get-tuple-element.165), channel_id=1, source_target_pairs={{0,2},{1,3},{2,0},{3,1},{4,6},{5,7},{6,4},{7,5},{8,10},{9,11},{10,... | collective-permute-start | bytes 1277960 | tf_op jit(solution)/shard_map/ppermute | solution.py:1138
  150.3 0.6 copy-start.5
  168.9 7.1 %collective-permute-start.13 = (bf16[64,1024]{1,0:T(8,128)(2,1)S(1)}, bf16[64,1024]{1,0:T(8,128)(2,1)S(1)}, u32[]{:S(2)}, u32[]{:S(2)}) collective-permute-start(bf16[64,1024]{1,0:T(8,128)(2,1)S(1)} %get-tuple-element.168), channel_id=1, source_target_pairs={{0,4},{1,5},{2,6},{3,7},{4,0},{5,1},{6,2},{7,3},{8,12},{9,13},{10,... | collective-permute-start | bytes 393224 | tf_op jit(solution)/shard_map/ppermute | solution.py:1138
  169.4 12.8 %collective-permute-start.14 = (bf16[64,1024]{1,0:T(8,128)(2,1)S(1)}, bf16[64,1024]{1,0:T(8,128)(2,1)S(1)}, u32[]{:S(2)}, u32[]{:S(2)}) collective-permute-start(bf16[64,1024]{1,0:T(8,128)(2,1)S(1)} %get-tuple-element.169), channel_id=1, source_target_pairs={{0,8},{1,9},{2,10},{3,11},{4,12},{5,13},{6,14},{7,15},{8,0},{9,1},... | collective-permute-start | bytes 393224 | tf_op jit(solution)/shard_map/ppermute | solution.py:1138
  169.8 12.5 %collective-permute-start.15 = (bf16[64,1024]{1,0:T(8,128)(2,1)S(1)}, bf16[64,1024]{1,0:T(8,128)(2,1)S(1)}, u32[]{:S(2)}, u32[]{:S(2)}) collective-permute-start(bf16[64,1024]{1,0:T(8,128)(2,1)S(1)} %get-tuple-element.170), channel_id=1, source_target_pairs={{0,12},{1,13},{2,14},{3,15},{4,8},{5,9},{6,10},{7,11},{8,4},{9,5},... | collective-permute-start | bytes 393224 | tf_op jit(solution)/shard_map/ppermute | solution.py:1138
  173.4 13.6 %collective-permute-start.17 = (bf16[48,3072]{1,0:T(8,128)(2,1)S(1)}, bf16[48,3072]{1,0:T(8,128)(2,1)S(1)}, u32[]{:S(2)}, u32[]{:S(2)}) collective-permute-start(bf16[48,3072]{1,0:T(8,128)(2,1)S(1)} %early_sum.1.early_ref), channel_id=1, source_target_pairs={{0,16},{16,0},{1,17},{17,1},{2,18},{18,2},{3,19},{19,3},{4,20},{20... | collective-permute-start | bytes 884744 | tf_op jit(solution)/shard_map/ppermute | solution.py:1138
  182.3 4.7 %collective-permute-start.16 = (bf16[48,1024]{1,0:T(8,128)(2,1)S(1)}, bf16[48,1024]{1,0:T(8,128)(2,1)S(1)}, u32[]{:S(2)}, u32[]{:S(2)}) collective-permute-start(bf16[48,1024]{1,0:T(8,128)(2,1)S(1)} %get-tuple-element.171.late_ref), channel_id=1, source_target_pairs={{0,16},{16,0},{1,17},{17,1},{2,18},{18,2},{3,19},{19,3},{4,20},{20... | collective-permute-start | bytes 294920 | tf_op jit(solution)/shard_map/ppermute | solution.py:1138

commit v5 on v4

--- a/solution.py
+++ b/solution.py
@@ -17,11 +17,11 @@
 LOG2E = 1.4426950408889634
 SWAP = [(0, 1), (1, 0)]
 MIB = 1024 * 1024
-VMEM_GATES = 56
+VMEM_GATES = 52
 VMEM_PROJ = 56
 VMEM_INTRA = 12
-VMEM_MIX = 56
-VMEM_WEIGHTS = 56
+VMEM_MIX = 52
+VMEM_WEIGHTS = 52
 VMEM_BACK = 56
 VMEM_CONV = 56
 VMEM_INPUTS = 56
@@ -828,9 +828,12 @@
     inner = w_ref.shape[1]
     tile_here = pl.ds(pl.multiple_of(step * wide, wide), wide)
 
-    def hand_over(product, weights):
+    def share_of(product, weights):
         share = (product * weights.astype(F32)).astype(BF16)
         gains[...] += mm_nt(jnp.ones((8, share.shape[1]), BF16), share)
+
+    def hand_over(product, weights):
+        share_of(product, weights)
         by_core(product.astype(BF16), shard, mine_ref, theirs_ref)
 
     @pl.when(step < pl.num_programs(0) - 1)
@@ -875,14 +878,15 @@
                     jnp.sum(sums[place][tap], axis=0, keepdims=True) + halo_sums[tap][:, cols]
                 )
         product = mm(turned_ref[...], dproj_ref[...]) + mm(turnhalo_ref[...], dhalo_ref[...])
+        by_core(product.astype(BF16), shard, mine_ref, theirs_ref)
 
         @pl.when(step < last - 1)
         def _():
-            hand_over(product, w_ref[:, tile_here])
+            share_of(product, w_ref[:, tile_here])
 
         @pl.when(step == last - 1)
         def _():
-            hand_over(product, narrow_ref[0:wide, :].astype(F32).T)
+            share_of(product, narrow_ref[0:wide, :].astype(F32).T)
 
     @pl.when(step == pl.num_programs(0) - 1)
     def _():
@@ -1650,7 +1654,6 @@
         (late_mine, late_got, small, small_got),
         [((model // 4 + 16, wide // 2), F32), (quarter, BF16), (quarter, BF16), (quarter, BF16)],
     )
-    early_got, both = ordered(early_got, both)
     early_keep, early_send = halve("halve_z2", early_keep, early_got, 8)
     corners = [(a, b) for a in range(2) for b in range(dp_count)]
     across = traded(across, "dir", 1, 2)

time: 188 us -> 184 us (0.979)
  local copies, waits for them, and re-layouts: 5.38 us -> 2.63 us
    unnamed x14 -> x38, local copies, waits for them, and re-layouts: 4.64 us -> 1.88 us
  transfers between devices with their start and end apart: 18 -> 18, of which waited for: 8 -> 7; matrix products, arithmetic and copies ran while one was open for 0% -> 0% of each run, Pallas kernels for 45% -> 46%
where the time goes in v5:
time: 184 us; the launch traced here: 183 us
  Pallas kernels  135 us (73%)
  starting transfers between devices  27.3 us (15%)
  waiting for transfers between devices  17.1 us (9%)
  local copies, waits for them, and re-layouts  2.63 us (1%)
    pallas_call x8, Pallas kernels, call(): pl.pallas_call(kernel, name=name, grid=(grid,), in_specs=in_specs, out_sp...  133 us
    ppermute x13, waiting for transfers between devices, traded(): return lax.ppermute(values, axis, [(i, i ^ bit) for i in range(size)])  15.6 us
    ppermute x13, starting transfers between devices, traded(): return lax.ppermute(values, axis, [(i, i ^ bit) for i in range(size)])  15.3 us
    ppermute x1, starting transfers between devices, local(): halo = lax.ppermute(x[count - 16:], 'dir', [(0, 1)])  4.83 us
  transfers between devices with their start and end apart: 18, of which 7 were waited for; matrix products, arithmetic and copies ran while one was open for 0% of the time, Pallas kernels for 46%

profile of v5, /device:TPU:0, one launch (start us, length us, event | category | flops | bytes accessed | tf_op | source)
XLA Modules:
  0.0 183.4 jit_solution(17542751190611353540)
XLA Ops:
  0.6 0.7 slice_bitcast_fusion
  1.4 4.8 %collective-permute-start = (bf16[16,768]{1,0:T(8,128)(2,1)S(1)}, bf16[16,768]{1,0:T(8,128)(2,1)S(1)}, u32[]{:S(2)}, u32[]{:S(2)}) collective-permute-start(bf16[16,768]{1,0:T(8,128)(2,1)S(1)} %slice_bitcast_fusion), channel_id=1, source_target_pairs={{0,16},{1,17},{2,18},{3,19},{4,20},{5,21},{6,22},{7,23},{8,24},{9,... | collective-permute-start | bytes 73736 | tf_op jit(solution)/shard_map/ppermute | solution.py:1200
  6.2 1.5 collective-permute-done.halo_ref
  7.7 0.6 copy-done.18
  8.3 20.8 %proj.1 = (bf16[1024,768]{1,0:T(8,128)(2,1)}, f32[48,1024]{1,0:T(8,128)}, f32[48,1024]{1,0:T(8,128)}, f32[48,128]{1,0:T(8,128)}, f32[48,1024]{1,0:T(8,128)}, /*i...) custom-call(s32[1,8]{1,0:T(1,128)} %lengths_ref.9, ...), custom_call_target="tpu_custom_call" | custom-call | flops 23000000512 | tf_op jit(solution)/shard_map/proj/pallas_call | solution.py:1125
  29.2 2.4 %collective-permute-start.1 = (bf16[64,1536]{1,0:T(8,128)(2,1)}, bf16[64,1536]{1,0:T(8,128)(2,1)S(1)}, u32[]{:S(2)}, u32[]{:S(2)}) collective-permute-start(bf16[64,1536]{1,0:T(8,128)(2,1)} %get-tuple-element.106), channel_id=1, source_target_pairs={{0,16},{16,0},{1,17},{17,1},{2,18},{18,2},{3,19},{19,3},{4,20},{20... | collective-permute-start | bytes 589832 | tf_op jit(solution)/shard_map/ppermute | solution.py:1291
  31.6 0.0 copy-start.6
  31.6 0.0 copy-start.7
  31.6 0.0 copy-start.9
  31.6 9.4 %gates.1 = (bf16[1024,1536]{1,0:T(8,128)(2,1)}, bf16[1024,1536]{1,0:T(8,128)(2,1)}, bf16[768,1024]{1,0:T(8,128)(2,1)S(1)}) custom-call(bf16[1024,768]{1,0:T(8,128)(2,1)} %get-tuple-element.96.normed_ref, bf16[1024,768]{1,0:T(8,128)(2,1)} %bitcast.9, bf16[768,1536]{1,0:T(8,128)(2,1)} %wz_ref.5, bf16[1536,768]{1,0:T(8,128)(2,1)} %wo_ref.3), custom_call_target="tpu_custom_call" | custom-call | flops 11500000256 | tf_op jit(solution)/shard_map/gates/pallas_call | solution.py:1125
  41.0 28.5 %mix.1 = (bf16[1024,1536]{1,0:T(8,128)(2,1)}, bf16[1024,1536]{1,0:T(8,128)(2,1)}, bf16[1024,1536]{1,0:T(8,128)(2,1)}, f32[48,1024]{1,0:T(8,128)S(1)}, f32[1024,1...) custom-call(s32[1,8]{1,0:T(1,128)S(1)} %copy-done.7, ...), custom_call_target="tpu_custom_call" | custom-call | flops 34500001792 | tf_op jit(solution)/shard_map/mix/pallas_call | solution.py:1125
  69.6 0.1 collective-permute-start.2
  69.7 11.6 %weights.1 = (bf16[384,3072]{1,0:T(8,128)(2,1)}, bf16[384,3072]{1,0:T(8,128)(2,1)}, f32[4,1,192]{2,1,0:T(1,128)S(1)}) custom-call(bf16[768,1024]{1,0:T(8,128)(2,1)S(1)} %get-tuple-element.97.turned_ref, bf16[1024,1536]{1,0:T(8,128)(2,1)} %get-tuple-element.109.dz_ref, bf16[1024,1536]{1,0:T(8,128)(2,1)} %get-tuple-element.110.mixed_ref, ...), custom_call_target="tpu_custom_call" | custom-call | flops 11500000256 | tf_op jit(solution)/shard_map/weights/pallas_call | solution.py:1125
  81.4 0.1 collective-permute-start.3
  81.5 0.5 copy-done.15
  82.0 0.1 copy-done.16
  82.1 5.7 %back0.1 = (bf16[1024,1792]{1,0:T(8,128)(2,1)}, f32[144,1024]{1,0:T(8,128)}, f32[64,1536]{1,0:T(8,128)}) custom-call(s32[1,8]{1,0:T(1,128)} %lengths_ref.9, f32[24]{0:T(128)} %skip_ref.5, bf16[1024,1792]{1,0:T(8,128)(2,1)} %get-tuple-element.99.act_ref, bf16[1024,1792]{1,0:T(8,128)(2,1)} %get-tuple-element.118.slope_ref, ...), custom_call_target="tpu_custom_call" | custom-call | flops 3449999872 | tf_op jit(solution)/shard_map/back0/pallas_call | solution.py:1125
  87.8 0.6 halve_y.1
  88.4 1.6 collective-permute-start.4
  90.0 23.0 %back1.1 = (bf16[1024,1792]{1,0:T(8,128)(2,1)}, f32[144,1024]{1,0:T(8,128)}, f32[64,1536]{1,0:T(8,128)}) custom-call(s32[1,8]{1,0:T(1,128)} %lengths_ref.9, f32[24]{0:T(128)} %skip_ref.5, bf16[1024,1792]{1,0:T(8,128)(2,1)} %get-tuple-element.99.act_ref, ...), custom_call_target="tpu_custom_call", output_to_operand_aliasing={{0}: (19, {}), {1}: (20, {})} | custom-call | flops 29899999232 | tf_op jit(solution)/shard_map/back1/pallas_call | solution.py:1125
  113.0 3.3 %collective-permute-done.4.got_ref = bf16[192,3072]{1,0:T(8,128)(2,1)S(1)} collective-permute-done((bf16[192,3072]{1,0:T(8,128)(2,1)S(1)}, bf16[192,3072]{1,0:T(8,128)(2,1)S(1)}, u32[]{:S(2)}, u32[]{:S(2)}) %collective-permute-start.4) | collective-permute-done | bytes 1179680 | tf_op jit(solution)/shard_map/ppermute | solution.py:1142
  116.3 0.2 halve_z.1
  116.5 1.6 collective-permute-start.6
  118.2 18.2 %conv_back.1 = (bf16[1024,1792]{1,0:T(8,128)(2,1)}, bf16[16,1792]{1,0:T(8,128)(2,1)}, bf16[384,2048]{1,0:T(8,128)(2,1)}, bf16[384,2048]{1,0:T(8,128)(2,1)}, bf16...) custom-call(s32[1,8]{1,0:T(1,128)} %lengths_ref.9, bf16[768,1024]{1,0:T(8,128)(2,1)} %copy-done.12, ...), custom_call_target="tpu_custom_call" | custom-call | flops 19549999104 | tf_op jit(solution)/shard_map/conv_back/pallas_call | solution.py:1125
  136.4 0.1 collective-permute-start.8
  136.5 1.3 collective-permute-start.5
  137.8 0.6 collective-permute-start.9
  138.3 0.1 halve_z2.1
  138.4 2.6 %collective-permute-start.7 = (bf16[48,3072]{1,0:T(8,128)(2,1)S(1)}, bf16[48,3072]{1,0:T(8,128)(2,1)S(1)}, u32[]{:S(2)}, u32[]{:S(2)}) collective-permute-start(bf16[48,3072]{1,0:T(8,128)(2,1)S(1)} %get-tuple-element.153), channel_id=1, source_target_pairs={{0,8},{1,9},{2,10},{3,11},{4,12},{5,13},{6,14},{7,15},{8,0},{9,1},... | collective-permute-start | bytes 884744 | tf_op jit(solution)/shard_map/ppermute | solution.py:1142
  141.1 0.4 quarters.1
  141.5 3.4 %collective-permute-start.10 = (bf16[208,1024]{1,0:T(8,128)(2,1)S(1)}, bf16[208,1024]{1,0:T(8,128)(2,1)S(1)}, u32[]{:S(2)}, u32[]{:S(2)}) collective-permute-start(bf16[208,1024]{1,0:T(8,128)(2,1)S(1)} %get-tuple-element.157), channel_id=1, source_target_pairs={{0,18},{1,19},{2,16},{3,17},{4,22},{5,23},{6,20},{7,21},{8,26},{9,... | collective-permute-start | bytes 1277960 | tf_op jit(solution)/shard_map/ppermute | solution.py:1661
  144.9 0.6 collective-permute-start.12
  145.5 0.6 copy-done.17
  146.1 15.5 %inputs.1 = (bf16[1024,768]{1,0:T(8,128)(2,1)}, bf16[1024,768]{1,0:T(8,128)(2,1)}) custom-call(bf16[1024,768]{1,0:T(8,128)(2,1)} %bitcast.8, bf16[1024,768]{1,0:T(8,128)(2,1)} %bitcast.11, f32[768]{0:T(1024)} %gain_ref.7, bf16[1024,1792]{1,0:T(8,128)(2,1)} %get-tuple-element.143.dproj_ref, bf16[16,1792]{1,0:T(8,128)(2,1)} %copy-done.17, ...), custom_call_target="tpu_custom_call" | custom-call | flops 18400000000 | tf_op jit(solution)/shard_map/inputs/pallas_call | solution.py:1125
  161.7 0.1 early_sum.1.early_ref
  161.8 1.5 collective-permute-done.11.a_ref
  163.3 0.7 collective-permute-done.12.b_ref
  164.0 0.2 levels.1
  164.2 0.5 collective-permute-start.13
  164.7 1.5 collective-permute-start.14
  166.2 2.4 %collective-permute-start.15 = (bf16[64,1024]{1,0:T(8,128)(2,1)S(1)}, bf16[64,1024]{1,0:T(8,128)(2,1)S(1)}, u32[]{:S(2)}, u32[]{:S(2)}) collective-permute-start(bf16[64,1024]{1,0:T(8,128)(2,1)S(1)} %get-tuple-element.166), channel_id=1, source_target_pairs={{0,12},{1,13},{2,14},{3,15},{4,8},{5,9},{6,10},{7,11},{8,4},{9,5},... | collective-permute-start | bytes 393224 | tf_op jit(solution)/shard_map/ppermute | solution.py:1142
  168.7 1.8 collective-permute-start.17
  170.4 1.4 collective-permute-done.13.a_ref
  171.8 5.8 %collective-permute-done.14.b_ref = bf16[64,1024]{1,0:T(8,128)(2,1)S(1)} collective-permute-done((bf16[64,1024]{1,0:T(8,128)(2,1)S(1)}, bf16[64,1024]{1,0:T(8,128)(2,1)S(1)}, u32[]{:S(2)}, u32[]{:S(2)}) %collective-permute-start.14) | collective-permute-done | bytes 131104 | tf_op jit(solution)/shard_map/ppermute | solution.py:1142
  177.6 0.1 last.1
  177.7 1.9 %collective-permute-start.16 = (bf16[48,1024]{1,0:T(8,128)(2,1)S(1)}, bf16[48,1024]{1,0:T(8,128)(2,1)S(1)}, u32[]{:S(2)}, u32[]{:S(2)}) collective-permute-start(bf16[48,1024]{1,0:T(8,128)(2,1)S(1)} %get-tuple-element.167.late_ref), channel_id=1, source_target_pairs={{0,16},{16,0},{1,17},{17,1},{2,18},{18,2},{3,19},{19,3},{4,20},{20... | collective-permute-start | bytes 294920 | tf_op jit(solution)/shard_map/ppermute | solution.py:1142
  179.6 2.8 %collective-permute-done.16.lategot_ref = bf16[48,1024]{1,0:T(8,128)(2,1)S(1)} collective-permute-done((bf16[48,1024]{1,0:T(8,128)(2,1)S(1)}, bf16[48,1024]{1,0:T(8,128)(2,1)S(1)}, u32[]{:S(2)}, u32[]{:S(2)}) %collective-permute-start.16) | collective-permute-done | bytes 98336 | tf_op jit(solution)/shard_map/ppermute | solution.py:1142
  182.4 1.0 finish.1
  (43 shorter events, 0.1 us)
Async XLA Ops:
  1.4 6.3 %collective-permute-start = (bf16[16,768]{1,0:T(8,128)(2,1)S(1)}, bf16[16,768]{1,0:T(8,128)(2,1)S(1)}, u32[]{:S(2)}, u32[]{:S(2)}) collective-permute-start(bf16[16,768]{1,0:T(8,128)(2,1)S(1)} %slice_bitcast_fusion), channel_id=1, source_target_pairs={{0,16},{1,17},{2,18},{3,19},{4,20},{5,21},{6,22},{7,23},{8,24},{9,... | collective-permute-start | bytes 73736 | tf_op jit(solution)/shard_map/ppermute | solution.py:1200
  7.7 0.6 copy-start.18
  29.2 11.8 %collective-permute-start.1 = (bf16[64,1536]{1,0:T(8,128)(2,1)}, bf16[64,1536]{1,0:T(8,128)(2,1)S(1)}, u32[]{:S(2)}, u32[]{:S(2)}) collective-permute-start(bf16[64,1536]{1,0:T(8,128)(2,1)} %get-tuple-element.106), channel_id=1, source_target_pairs={{0,16},{16,0},{1,17},{17,1},{2,18},{18,2},{3,19},{19,3},{4,20},{20... | collective-permute-start | bytes 589832 | tf_op jit(solution)/shard_map/ppermute | solution.py:1291
  31.5 9.4 %copy-start.1 = (bf16[96,1536]{1,0:T(8,128)(2,1)S(1)}, bf16[96,1536]{1,0:T(8,128)(2,1)}, u32[]{:S(2)}) copy-start(bf16[96,1536]{1,0:T(8,128)(2,1)} %constant.6.clone.e0_ref) | copy-start | bytes 884740
  31.5 9.4 %copy-start.2 = (bf16[96,1536]{1,0:T(8,128)(2,1)S(1)}, bf16[96,1536]{1,0:T(8,128)(2,1)}, u32[]{:S(2)}) copy-start(bf16[96,1536]{1,0:T(8,128)(2,1)} %constant.7.clone.e1_ref) | copy-start | bytes 884740
  31.5 9.4 %copy-start.3 = (f32[6,8,1536]{2,1,0:T(8,128)S(1)}, f32[6,8,1536]{2,1,0:T(8,128)}, u32[]{:S(2)}) copy-start(f32[6,8,1536]{2,1,0:T(8,128)} %get-tuple-element.105.keeps_ref) | copy-start | bytes 884740
  31.5 9.5 %copy-start.4 = (f32[48,1024]{1,0:T(8,128)S(1)}, f32[48,1024]{1,0:T(8,128)}, u32[]{:S(2)}) copy-start(f32[48,1024]{1,0:T(8,128)} %get-tuple-element.100.target_ref) | copy-start | bytes 589828
  31.6 9.5 %copy-start.5 = (f32[48,1024]{1,0:T(8,128)S(1)}, f32[48,1024]{1,0:T(8,128)}, u32[]{:S(2)}) copy-start(f32[48,1024]{1,0:T(8,128)} %get-tuple-element.101.source_ref) | copy-start | bytes 589828
  31.6 9.5 %copy-start.6 = (f32[24]{0:T(128)S(1)}, f32[24]{0:T(128)}, u32[]{:S(2)}) copy-start(f32[24]{0:T(128)} %skip_ref.5) | copy-start | bytes 292
  31.6 9.5 %copy-start.7 = (s32[1,8]{1,0:T(1,128)S(1)}, s32[1,8]{1,0:T(1,128)}, u32[]{:S(2)}) copy-start(s32[1,8]{1,0:T(1,128)} %lengths_ref.9) | copy-start | bytes 100
  31.6 9.5 %copy-start.9 = (f32[1536]{0:T(1024)S(1)}, f32[1536]{0:T(1024)}, u32[]{:S(2)}) copy-start(f32[1536]{0:T(1024)} %gain_ref.5) | copy-start | bytes 18436
  41.0 28.8 %copy-start.12 = (bf16[768,1024]{1,0:T(8,128)(2,1)}, bf16[768,1024]{1,0:T(8,128)(2,1)S(1)}, u32[]{:S(2)}) copy-start(bf16[768,1024]{1,0:T(8,128)(2,1)S(1)} %get-tuple-element.97.turned_ref) | copy-start | bytes 4718596
  41.0 28.6 %copy-start = (bf16[64,1536]{1,0:T(8,128)(2,1)}, bf16[64,1536]{1,0:T(8,128)(2,1)S(1)}, u32[]{:S(2)}) copy-start(bf16[64,1536]{1,0:T(8,128)(2,1)S(1)} %collective-permute-done.1.recv_ref._dpre_ref._moves_ref) | copy-start | bytes 589828
  69.6 11.8 %copy-start.13 = (f32[48,1024]{1,0:T(8,128)}, f32[48,1024]{1,0:T(8,128)S(1)}, u32[]{:S(2)}) copy-start(f32[48,1024]{1,0:T(8,128)S(1)} %get-tuple-element.140.r_ref) | copy-start | bytes 589828
  69.6 11.8 %copy-start.14 = (f32[16,1536]{1,0:T(8,128)}, f32[16,1536]{1,0:T(8,128)S(1)}, u32[]{:S(2)}) copy-start(f32[16,1536]{1,0:T(8,128)S(1)} %get-tuple-element.142.mix_sums_ref) | copy-start | bytes 294916
  69.6 11.8 %collective-permute-start.2 = (bf16[64,1536]{1,0:T(8,128)(2,1)S(1)}, bf16[64,1536]{1,0:T(8,128)(2,1)S(1)}, u32[]{:S(2)}, u32[]{:S(2)}) collective-permute-start(bf16[64,1536]{1,0:T(8,128)(2,1)S(1)} %get-tuple-element.113), channel_id=1, source_target_pairs={{0,16},{16,0},{1,17},{17,1},{2,18},{18,2},{3,19},{19,3},{4,20},{20... | collective-permute-start | bytes 589832 | tf_op jit(solution)/shard_map/ppermute | solution.py:1379
  81.4 0.6 copy-start.15
  81.4 0.7 copy-start.16
  81.4 6.4 %collective-permute-start.3 = (bf16[384,3072]{1,0:T(8,128)(2,1)}, bf16[384,3072]{1,0:T(8,128)(2,1)S(1)}, u32[]{:S(2)}, u32[]{:S(2)}) collective-permute-start(bf16[384,3072]{1,0:T(8,128)(2,1)} %get-tuple-element.115), channel_id=1, source_target_pairs={{0,1},{1,0},{2,3},{3,2},{4,5},{5,4},{6,7},{7,6},{8,9},{9,8},{10,11... | collective-permute-start | bytes 7077896 | tf_op jit(solution)/shard_map/ppermute | solution.py:1142
  82.0 5.7 %copy-start.10 = (bf16[384,3072]{1,0:T(8,128)(2,1)S(1)}, bf16[384,3072]{1,0:T(8,128)(2,1)}, u32[]{:S(2)}) copy-start(bf16[384,3072]{1,0:T(8,128)(2,1)} %get-tuple-element.114.kept_ref) | copy-start | bytes 7077892
  88.4 27.9 %collective-permute-start.4 = (bf16[192,3072]{1,0:T(8,128)(2,1)S(1)}, bf16[192,3072]{1,0:T(8,128)(2,1)S(1)}, u32[]{:S(2)}, u32[]{:S(2)}) collective-permute-start(bf16[192,3072]{1,0:T(8,128)(2,1)S(1)} %get-tuple-element.127), channel_id=1, source_target_pairs={{0,2},{1,3},{2,0},{3,1},{4,6},{5,7},{6,4},{7,5},{8,10},{9,11},{10,... | collective-permute-start | bytes 3538952 | tf_op jit(solution)/shard_map/ppermute | solution.py:1142
  116.5 19.9 %collective-permute-start.6 = (bf16[96,3072]{1,0:T(8,128)(2,1)S(1)}, bf16[96,3072]{1,0:T(8,128)(2,1)S(1)}, u32[]{:S(2)}, u32[]{:S(2)}) collective-permute-start(bf16[96,3072]{1,0:T(8,128)(2,1)S(1)} %get-tuple-element.149), channel_id=1, source_target_pairs={{0,4},{1,5},{2,6},{3,7},{4,0},{5,1},{6,2},{7,3},{8,12},{9,13},{10,... | collective-permute-start | bytes 1769480 | tf_op jit(solution)/shard_map/ppermute | solution.py:1142
  136.4 4.7 %collective-permute-start.8 = (bf16[384,2048]{1,0:T(8,128)(2,1)}, bf16[384,2048]{1,0:T(8,128)(2,1)S(1)}, u32[]{:S(2)}, u32[]{:S(2)}) collective-permute-start(bf16[384,2048]{1,0:T(8,128)(2,1)} %get-tuple-element.155), channel_id=1, source_target_pairs={{0,1},{1,0},{2,3},{3,2},{4,5},{5,4},{6,7},{7,6},{8,9},{9,8},{10,11... | collective-permute-start | bytes 4718600 | tf_op jit(solution)/shard_map/ppermute | solution.py:1142
  136.5 9.0 %collective-permute-start.5 = (bf16[16,1792]{1,0:T(8,128)(2,1)}, bf16[16,1792]{1,0:T(8,128)(2,1)S(1)}, u32[]{:S(2)}, u32[]{:S(2)}) collective-permute-start(bf16[16,1792]{1,0:T(8,128)(2,1)} %get-tuple-element.144), channel_id=1, source_target_pairs={{16,0},{17,1},{18,2},{19,3},{20,4},{21,5},{22,6},{23,7},{24,8},{25... | collective-permute-start | bytes 172040 | tf_op jit(solution)/shard_map/ppermute | solution.py:1593
  137.8 3.3 %collective-permute-start.9 = (bf16[16,1024]{1,0:T(8,128)(2,1)}, bf16[16,1024]{1,0:T(8,128)(2,1)S(1)}, u32[]{:S(2)}, u32[]{:S(2)}) collective-permute-start(bf16[16,1024]{1,0:T(8,128)(2,1)} %get-tuple-element.156.small_ref), channel_id=1, source_target_pairs={{0,1},{1,0},{2,3},{3,2},{4,5},{5,4},{6,7},{7,6},{8,9},{9,8},{10,11... | collective-permute-start | bytes 98312 | tf_op jit(solution)/shard_map/ppermute | solution.py:1142
  138.3 2.8 %copy-start.8 = (bf16[16,1024]{1,0:T(8,128)(2,1)S(1)}, bf16[16,1024]{1,0:T(8,128)(2,1)}, u32[]{:S(2)}) copy-start(bf16[16,1024]{1,0:T(8,128)(2,1)} %get-tuple-element.156.small_ref) | copy-start | bytes 98308
  138.3 2.8 %copy-start.11 = (bf16[384,2048]{1,0:T(8,128)(2,1)S(1)}, bf16[384,2048]{1,0:T(8,128)(2,1)}, u32[]{:S(2)}) copy-start(bf16[384,2048]{1,0:T(8,128)(2,1)} %get-tuple-element.154.mine_ref) | copy-start | bytes 4718596
  138.4 23.2 %collective-permute-start.7 = (bf16[48,3072]{1,0:T(8,128)(2,1)S(1)}, bf16[48,3072]{1,0:T(8,128)(2,1)S(1)}, u32[]{:S(2)}, u32[]{:S(2)}) collective-permute-start(bf16[48,3072]{1,0:T(8,128)(2,1)S(1)} %get-tuple-element.153), channel_id=1, source_target_pairs={{0,8},{1,9},{2,10},{3,11},{4,12},{5,13},{6,14},{7,15},{8,0},{9,1},... | collective-permute-start | bytes 884744 | tf_op jit(solution)/shard_map/ppermute | solution.py:1142
  141.5 20.3 %collective-permute-start.10 = (bf16[208,1024]{1,0:T(8,128)(2,1)S(1)}, bf16[208,1024]{1,0:T(8,128)(2,1)S(1)}, u32[]{:S(2)}, u32[]{:S(2)}) collective-permute-start(bf16[208,1024]{1,0:T(8,128)(2,1)S(1)} %get-tuple-element.157), channel_id=1, source_target_pairs={{0,18},{1,19},{2,16},{3,17},{4,22},{5,23},{6,20},{7,21},{8,26},{9,... | collective-permute-start | bytes 1277960 | tf_op jit(solution)/shard_map/ppermute | solution.py:1661
  144.9 18.4 %collective-permute-start.11 = (bf16[208,1024]{1,0:T(8,128)(2,1)S(1)}, bf16[208,1024]{1,0:T(8,128)(2,1)S(1)}, u32[]{:S(2)}, u32[]{:S(2)}) collective-permute-start(bf16[208,1024]{1,0:T(8,128)(2,1)S(1)} %get-tuple-element.160), channel_id=1, source_target_pairs={{0,16},{16,0},{1,17},{17,1},{2,18},{18,2},{3,19},{19,3},{4,20},{20... | collective-permute-start | bytes 1277960 | tf_op jit(solution)/shard_map/ppermute | solution.py:1142
  144.9 19.1 %collective-permute-start.12 = (bf16[208,1024]{1,0:T(8,128)(2,1)S(1)}, bf16[208,1024]{1,0:T(8,128)(2,1)S(1)}, u32[]{:S(2)}, u32[]{:S(2)}) collective-permute-start(bf16[208,1024]{1,0:T(8,128)(2,1)S(1)} %get-tuple-element.161), channel_id=1, source_target_pairs={{0,2},{1,3},{2,0},{3,1},{4,6},{5,7},{6,4},{7,5},{8,10},{9,11},{10,... | collective-permute-start | bytes 1277960 | tf_op jit(solution)/shard_map/ppermute | solution.py:1142
  145.5 0.6 copy-start.17
  164.2 7.6 %collective-permute-start.13 = (bf16[64,1024]{1,0:T(8,128)(2,1)S(1)}, bf16[64,1024]{1,0:T(8,128)(2,1)S(1)}, u32[]{:S(2)}, u32[]{:S(2)}) collective-permute-start(bf16[64,1024]{1,0:T(8,128)(2,1)S(1)} %get-tuple-element.164), channel_id=1, source_target_pairs={{0,4},{1,5},{2,6},{3,7},{4,0},{5,1},{6,2},{7,3},{8,12},{9,13},{10,... | collective-permute-start | bytes 393224 | tf_op jit(solution)/shard_map/ppermute | solution.py:1142
  164.7 12.9 %collective-permute-start.14 = (bf16[64,1024]{1,0:T(8,128)(2,1)S(1)}, bf16[64,1024]{1,0:T(8,128)(2,1)S(1)}, u32[]{:S(2)}, u32[]{:S(2)}) collective-permute-start(bf16[64,1024]{1,0:T(8,128)(2,1)S(1)} %get-tuple-element.165), channel_id=1, source_target_pairs={{0,8},{1,9},{2,10},{3,11},{4,12},{5,13},{6,14},{7,15},{8,0},{9,1},... | collective-permute-start | bytes 393224 | tf_op jit(solution)/shard_map/ppermute | solution.py:1142
  166.2 11.4 %collective-permute-start.15 = (bf16[64,1024]{1,0:T(8,128)(2,1)S(1)}, bf16[64,1024]{1,0:T(8,128)(2,1)S(1)}, u32[]{:S(2)}, u32[]{:S(2)}) collective-permute-start(bf16[64,1024]{1,0:T(8,128)(2,1)S(1)} %get-tuple-element.166), channel_id=1, source_target_pairs={{0,12},{1,13},{2,14},{3,15},{4,8},{5,9},{6,10},{7,11},{8,4},{9,5},... | collective-permute-start | bytes 393224 | tf_op jit(solution)/shard_map/ppermute | solution.py:1142
  168.7 13.7 %collective-permute-start.17 = (bf16[48,3072]{1,0:T(8,128)(2,1)S(1)}, bf16[48,3072]{1,0:T(8,128)(2,1)S(1)}, u32[]{:S(2)}, u32[]{:S(2)}) collective-permute-start(bf16[48,3072]{1,0:T(8,128)(2,1)S(1)} %early_sum.1.early_ref), channel_id=1, source_target_pairs={{0,16},{16,0},{1,17},{17,1},{2,18},{18,2},{3,19},{19,3},{4,20},{20... | collective-permute-start | bytes 884744 | tf_op jit(solution)/shard_map/ppermute | solution.py:1142
  177.7 4.7 %collective-permute-start.16 = (bf16[48,1024]{1,0:T(8,128)(2,1)S(1)}, bf16[48,1024]{1,0:T(8,128)(2,1)S(1)}, u32[]{:S(2)}, u32[]{:S(2)}) collective-permute-start(bf16[48,1024]{1,0:T(8,128)(2,1)S(1)} %get-tuple-element.167.late_ref), channel_id=1, source_target_pairs={{0,16},{16,0},{1,17},{17,1},{2,18},{18,2},{3,19},{19,3},{4,20},{20... | collective-permute-start | bytes 294920 | tf_op jit(solution)/shard_map/ppermute | solution.py:1142

commit v6 on v5

--- a/solution.py
+++ b/solution.py
@@ -629,11 +629,12 @@
                 dweight = dweights[at : at + SUB] * decay
                 scored[place] = scored[place] + dweight
                 change = dweight * scores
-                low = change * early_f
-                low_parts.append(low.astype(BF16))
-                all_parts.append(change.astype(BF16))
-                sum0 = sum0 + fold(low)
-                sum1 = sum1 + fold(change)
+                low = (change * early_f).astype(BF16)
+                change = change.astype(BF16)
+                low_parts.append(low)
+                all_parts.append(change)
+                sum0 = sum0 + fold(low.astype(F32))
+                sum1 = sum1 + fold(change.astype(F32))
             weights.append(jnp.concatenate(parts, axis=0))
             lows.append(jnp.concatenate(low_parts, axis=0))
             alls.append(jnp.concatenate(all_parts, axis=0))
@@ -659,12 +660,12 @@
             dpre_ref[rows, cols] = (dconv * slope_ref[rows, cols].astype(F32)).astype(BF16)
             out0[rows, cols] = (xf * leave0[rows]).astype(BF16)
             out1[rows, cols] = (xf * leave1[rows]).astype(BF16)
-            came0 = xf * came0
-            came1 = xf * came1
-            sum0 = sum0 + fold(came0)
-            sum1 = sum1 + fold(came1)
-            firsts.append(came0.astype(BF16))
-            totals.append(came1.astype(BF16))
+            came0 = (xf * came0).astype(BF16)
+            came1 = (xf * came1).astype(BF16)
+            sum0 = sum0 + fold(came0.astype(F32))
+            sum1 = sum1 + fold(came1.astype(F32))
+            firsts.append(came0)
+            totals.append(came1)
         kept[0:8, cols] = sum0
         kept[8:16, cols] = sum1
         return lows + [jnp.concatenate(firsts, axis=0), jnp.concatenate(totals, axis=0)]

time: 184 us -> 184 us (level)
  no operation moved by 1% of the time
where the time goes in v6:
time: 184 us; the launch traced here: 183 us
  Pallas kernels  136 us (74%)
  starting transfers between devices  27.3 us (15%)
  waiting for transfers between devices  16.6 us (9%)
  local copies, waits for them, and re-layouts  2.63 us (1%)
    pallas_call x8, Pallas kernels, call(): pl.pallas_call(kernel, name=name, grid=(grid,), in_specs=in_specs, out_sp...  133 us
    ppermute x13, starting transfers between devices, traded(): return lax.ppermute(values, axis, [(i, i ^ bit) for i in range(size)])  15.3 us
    ppermute x13, waiting for transfers between devices, traded(): return lax.ppermute(values, axis, [(i, i ^ bit) for i in range(size)])  15.1 us
    ppermute x1, starting transfers between devices, local(): halo = lax.ppermute(x[count - 16:], 'dir', [(0, 1)])  4.83 us
  transfers between devices with their start and end apart: 18, of which 7 were waited for; matrix products, arithmetic and copies ran while one was open for 0% of the time, Pallas kernels for 46%

profile of v6, /device:TPU:0, one launch (start us, length us, event | category | flops | bytes accessed | tf_op | source)
XLA Modules:
  0.0 183.5 jit_solution(1655755444819560573)
XLA Ops:
  0.6 0.7 slice_bitcast_fusion
  1.4 4.8 %collective-permute-start = (bf16[16,768]{1,0:T(8,128)(2,1)S(1)}, bf16[16,768]{1,0:T(8,128)(2,1)S(1)}, u32[]{:S(2)}, u32[]{:S(2)}) collective-permute-start(bf16[16,768]{1,0:T(8,128)(2,1)S(1)} %slice_bitcast_fusion), channel_id=1, source_target_pairs={{0,16},{1,17},{2,18},{3,19},{4,20},{5,21},{6,22},{7,23},{8,24},{9,... | collective-permute-start | bytes 73736 | tf_op jit(solution)/shard_map/ppermute | solution.py:1201
  6.2 1.5 collective-permute-done.halo_ref
  7.7 0.6 copy-done.18
  8.3 20.8 %proj.1 = (bf16[1024,768]{1,0:T(8,128)(2,1)}, f32[48,1024]{1,0:T(8,128)}, f32[48,1024]{1,0:T(8,128)}, f32[48,128]{1,0:T(8,128)}, f32[48,1024]{1,0:T(8,128)}, /*i...) custom-call(s32[1,8]{1,0:T(1,128)} %lengths_ref.9, ...), custom_call_target="tpu_custom_call" | custom-call | flops 23000000512 | tf_op jit(solution)/shard_map/proj/pallas_call | solution.py:1126
  29.2 2.4 %collective-permute-start.1 = (bf16[64,1536]{1,0:T(8,128)(2,1)}, bf16[64,1536]{1,0:T(8,128)(2,1)S(1)}, u32[]{:S(2)}, u32[]{:S(2)}) collective-permute-start(bf16[64,1536]{1,0:T(8,128)(2,1)} %get-tuple-element.106), channel_id=1, source_target_pairs={{0,16},{16,0},{1,17},{17,1},{2,18},{18,2},{3,19},{19,3},{4,20},{20... | collective-permute-start | bytes 589832 | tf_op jit(solution)/shard_map/ppermute | solution.py:1292
  31.6 0.0 copy-start.6
  31.6 0.0 copy-start.7
  31.6 0.0 copy-start.9
  31.6 9.4 %gates.1 = (bf16[1024,1536]{1,0:T(8,128)(2,1)}, bf16[1024,1536]{1,0:T(8,128)(2,1)}, bf16[768,1024]{1,0:T(8,128)(2,1)S(1)}) custom-call(bf16[1024,768]{1,0:T(8,128)(2,1)} %get-tuple-element.96.normed_ref, bf16[1024,768]{1,0:T(8,128)(2,1)} %bitcast.9, bf16[768,1536]{1,0:T(8,128)(2,1)} %wz_ref.5, bf16[1536,768]{1,0:T(8,128)(2,1)} %wo_ref.3), custom_call_target="tpu_custom_call" | custom-call | flops 11500000256 | tf_op jit(solution)/shard_map/gates/pallas_call | solution.py:1126
  41.0 28.5 %mix.1 = (bf16[1024,1536]{1,0:T(8,128)(2,1)}, bf16[1024,1536]{1,0:T(8,128)(2,1)}, bf16[1024,1536]{1,0:T(8,128)(2,1)}, f32[48,1024]{1,0:T(8,128)S(1)}, f32[1024,1...) custom-call(s32[1,8]{1,0:T(1,128)S(1)} %copy-done.7, ...), custom_call_target="tpu_custom_call" | custom-call | flops 34500001792 | tf_op jit(solution)/shard_map/mix/pallas_call | solution.py:1126
  69.6 0.1 collective-permute-start.2
  69.7 11.6 %weights.1 = (bf16[384,3072]{1,0:T(8,128)(2,1)}, bf16[384,3072]{1,0:T(8,128)(2,1)}, f32[4,1,192]{2,1,0:T(1,128)S(1)}) custom-call(bf16[768,1024]{1,0:T(8,128)(2,1)S(1)} %get-tuple-element.97.turned_ref, bf16[1024,1536]{1,0:T(8,128)(2,1)} %get-tuple-element.109.dz_ref, bf16[1024,1536]{1,0:T(8,128)(2,1)} %get-tuple-element.110.mixed_ref, ...), custom_call_target="tpu_custom_call" | custom-call | flops 11500000256 | tf_op jit(solution)/shard_map/weights/pallas_call | solution.py:1126
  81.4 0.1 collective-permute-start.3
  81.5 0.5 copy-done.15
  82.0 0.1 copy-done.16
  82.1 5.8 %back0.1 = (bf16[1024,1792]{1,0:T(8,128)(2,1)}, f32[144,1024]{1,0:T(8,128)}, f32[64,1536]{1,0:T(8,128)}) custom-call(s32[1,8]{1,0:T(1,128)} %lengths_ref.9, f32[24]{0:T(128)} %skip_ref.5, bf16[1024,1792]{1,0:T(8,128)(2,1)} %get-tuple-element.99.act_ref, bf16[1024,1792]{1,0:T(8,128)(2,1)} %get-tuple-element.118.slope_ref, ...), custom_call_target="tpu_custom_call" | custom-call | flops 3449999872 | tf_op jit(solution)/shard_map/back0/pallas_call | solution.py:1126
  87.8 0.6 halve_y.1
  88.5 1.6 collective-permute-start.4
  90.1 23.5 %back1.1 = (bf16[1024,1792]{1,0:T(8,128)(2,1)}, f32[144,1024]{1,0:T(8,128)}, f32[64,1536]{1,0:T(8,128)}) custom-call(s32[1,8]{1,0:T(1,128)} %lengths_ref.9, f32[24]{0:T(128)} %skip_ref.5, bf16[1024,1792]{1,0:T(8,128)(2,1)} %get-tuple-element.99.act_ref, ...), custom_call_target="tpu_custom_call", output_to_operand_aliasing={{0}: (19, {}), {1}: (20, {})} | custom-call | flops 29899999232 | tf_op jit(solution)/shard_map/back1/pallas_call | solution.py:1126
  113.6 2.8 %collective-permute-done.4.got_ref = bf16[192,3072]{1,0:T(8,128)(2,1)S(1)} collective-permute-done((bf16[192,3072]{1,0:T(8,128)(2,1)S(1)}, bf16[192,3072]{1,0:T(8,128)(2,1)S(1)}, u32[]{:S(2)}, u32[]{:S(2)}) %collective-permute-start.4) | collective-permute-done | bytes 1179680 | tf_op jit(solution)/shard_map/ppermute | solution.py:1143
  116.3 0.2 halve_z.1
  116.6 1.6 collective-permute-start.6
  118.2 18.2 %conv_back.1 = (bf16[1024,1792]{1,0:T(8,128)(2,1)}, bf16[16,1792]{1,0:T(8,128)(2,1)}, bf16[384,2048]{1,0:T(8,128)(2,1)}, bf16[384,2048]{1,0:T(8,128)(2,1)}, bf16...) custom-call(s32[1,8]{1,0:T(1,128)} %lengths_ref.9, bf16[768,1024]{1,0:T(8,128)(2,1)} %copy-done.12, ...), custom_call_target="tpu_custom_call" | custom-call | flops 19549999104 | tf_op jit(solution)/shard_map/conv_back/pallas_call | solution.py:1126
  136.5 0.1 collective-permute-start.8
  136.6 1.3 collective-permute-start.5
  137.9 0.6 collective-permute-start.9
  138.4 0.1 halve_z2.1
  138.5 2.6 %collective-permute-start.7 = (bf16[48,3072]{1,0:T(8,128)(2,1)S(1)}, bf16[48,3072]{1,0:T(8,128)(2,1)S(1)}, u32[]{:S(2)}, u32[]{:S(2)}) collective-permute-start(bf16[48,3072]{1,0:T(8,128)(2,1)S(1)} %get-tuple-element.153), channel_id=1, source_target_pairs={{0,8},{1,9},{2,10},{3,11},{4,12},{5,13},{6,14},{7,15},{8,0},{9,1},... | collective-permute-start | bytes 884744 | tf_op jit(solution)/shard_map/ppermute | solution.py:1143
  141.2 0.4 quarters.1
  141.6 3.4 %collective-permute-start.10 = (bf16[208,1024]{1,0:T(8,128)(2,1)S(1)}, bf16[208,1024]{1,0:T(8,128)(2,1)S(1)}, u32[]{:S(2)}, u32[]{:S(2)}) collective-permute-start(bf16[208,1024]{1,0:T(8,128)(2,1)S(1)} %get-tuple-element.157), channel_id=1, source_target_pairs={{0,18},{1,19},{2,16},{3,17},{4,22},{5,23},{6,20},{7,21},{8,26},{9,... | collective-permute-start | bytes 1277960 | tf_op jit(solution)/shard_map/ppermute | solution.py:1662
  145.0 0.6 collective-permute-start.12
  145.6 0.6 copy-done.17
  146.2 15.5 %inputs.1 = (bf16[1024,768]{1,0:T(8,128)(2,1)}, bf16[1024,768]{1,0:T(8,128)(2,1)}) custom-call(bf16[1024,768]{1,0:T(8,128)(2,1)} %bitcast.8, bf16[1024,768]{1,0:T(8,128)(2,1)} %bitcast.11, f32[768]{0:T(1024)} %gain_ref.7, bf16[1024,1792]{1,0:T(8,128)(2,1)} %get-tuple-element.143.dproj_ref, bf16[16,1792]{1,0:T(8,128)(2,1)} %copy-done.17, ...), custom_call_target="tpu_custom_call" | custom-call | flops 18400000000 | tf_op jit(solution)/shard_map/inputs/pallas_call | solution.py:1126
  161.8 0.1 early_sum.1.early_ref
  161.8 1.5 collective-permute-done.11.a_ref
  163.4 0.7 collective-permute-done.12.b_ref
  164.1 0.2 levels.1
  164.3 0.5 collective-permute-start.13
  164.8 1.5 collective-permute-start.14
  166.3 2.4 %collective-permute-start.15 = (bf16[64,1024]{1,0:T(8,128)(2,1)S(1)}, bf16[64,1024]{1,0:T(8,128)(2,1)S(1)}, u32[]{:S(2)}, u32[]{:S(2)}) collective-permute-start(bf16[64,1024]{1,0:T(8,128)(2,1)S(1)} %get-tuple-element.166), channel_id=1, source_target_pairs={{0,12},{1,13},{2,14},{3,15},{4,8},{5,9},{6,10},{7,11},{8,4},{9,5},... | collective-permute-start | bytes 393224 | tf_op jit(solution)/shard_map/ppermute | solution.py:1143
  168.7 1.8 collective-permute-start.17
  170.5 1.4 collective-permute-done.13.a_ref
  171.9 5.8 %collective-permute-done.14.b_ref = bf16[64,1024]{1,0:T(8,128)(2,1)S(1)} collective-permute-done((bf16[64,1024]{1,0:T(8,128)(2,1)S(1)}, bf16[64,1024]{1,0:T(8,128)(2,1)S(1)}, u32[]{:S(2)}, u32[]{:S(2)}) %collective-permute-start.14) | collective-permute-done | bytes 131104 | tf_op jit(solution)/shard_map/ppermute | solution.py:1143
  177.7 0.1 last.1
  177.8 1.9 %collective-permute-start.16 = (bf16[48,1024]{1,0:T(8,128)(2,1)S(1)}, bf16[48,1024]{1,0:T(8,128)(2,1)S(1)}, u32[]{:S(2)}, u32[]{:S(2)}) collective-permute-start(bf16[48,1024]{1,0:T(8,128)(2,1)S(1)} %get-tuple-element.167.late_ref), channel_id=1, source_target_pairs={{0,16},{16,0},{1,17},{17,1},{2,18},{18,2},{3,19},{19,3},{4,20},{20... | collective-permute-start | bytes 294920 | tf_op jit(solution)/shard_map/ppermute | solution.py:1143
  179.7 2.8 %collective-permute-done.16.lategot_ref = bf16[48,1024]{1,0:T(8,128)(2,1)S(1)} collective-permute-done((bf16[48,1024]{1,0:T(8,128)(2,1)S(1)}, bf16[48,1024]{1,0:T(8,128)(2,1)S(1)}, u32[]{:S(2)}, u32[]{:S(2)}) %collective-permute-start.16) | collective-permute-done | bytes 98336 | tf_op jit(solution)/shard_map/ppermute | solution.py:1143
  182.5 1.0 finish.1
  (43 shorter events, 0.1 us)
Async XLA Ops:
  1.4 6.3 %collective-permute-start = (bf16[16,768]{1,0:T(8,128)(2,1)S(1)}, bf16[16,768]{1,0:T(8,128)(2,1)S(1)}, u32[]{:S(2)}, u32[]{:S(2)}) collective-permute-start(bf16[16,768]{1,0:T(8,128)(2,1)S(1)} %slice_bitcast_fusion), channel_id=1, source_target_pairs={{0,16},{1,17},{2,18},{3,19},{4,20},{5,21},{6,22},{7,23},{8,24},{9,... | collective-permute-start | bytes 73736 | tf_op jit(solution)/shard_map/ppermute | solution.py:1201
  7.7 0.6 copy-start.18
  29.2 11.8 %collective-permute-start.1 = (bf16[64,1536]{1,0:T(8,128)(2,1)}, bf16[64,1536]{1,0:T(8,128)(2,1)S(1)}, u32[]{:S(2)}, u32[]{:S(2)}) collective-permute-start(bf16[64,1536]{1,0:T(8,128)(2,1)} %get-tuple-element.106), channel_id=1, source_target_pairs={{0,16},{16,0},{1,17},{17,1},{2,18},{18,2},{3,19},{19,3},{4,20},{20... | collective-permute-start | bytes 589832 | tf_op jit(solution)/shard_map/ppermute | solution.py:1292
  31.5 9.4 %copy-start.1 = (bf16[96,1536]{1,0:T(8,128)(2,1)S(1)}, bf16[96,1536]{1,0:T(8,128)(2,1)}, u32[]{:S(2)}) copy-start(bf16[96,1536]{1,0:T(8,128)(2,1)} %constant.6.clone.e0_ref) | copy-start | bytes 884740
  31.5 9.4 %copy-start.2 = (bf16[96,1536]{1,0:T(8,128)(2,1)S(1)}, bf16[96,1536]{1,0:T(8,128)(2,1)}, u32[]{:S(2)}) copy-start(bf16[96,1536]{1,0:T(8,128)(2,1)} %constant.7.clone.e1_ref) | copy-start | bytes 884740
  31.5 9.4 %copy-start.3 = (f32[6,8,1536]{2,1,0:T(8,128)S(1)}, f32[6,8,1536]{2,1,0:T(8,128)}, u32[]{:S(2)}) copy-start(f32[6,8,1536]{2,1,0:T(8,128)} %get-tuple-element.105.keeps_ref) | copy-start | bytes 884740
  31.5 9.5 %copy-start.4 = (f32[48,1024]{1,0:T(8,128)S(1)}, f32[48,1024]{1,0:T(8,128)}, u32[]{:S(2)}) copy-start(f32[48,1024]{1,0:T(8,128)} %get-tuple-element.100.target_ref) | copy-start | bytes 589828
  31.6 9.5 %copy-start.5 = (f32[48,1024]{1,0:T(8,128)S(1)}, f32[48,1024]{1,0:T(8,128)}, u32[]{:S(2)}) copy-start(f32[48,1024]{1,0:T(8,128)} %get-tuple-element.101.source_ref) | copy-start | bytes 589828
  31.6 9.5 %copy-start.6 = (f32[24]{0:T(128)S(1)}, f32[24]{0:T(128)}, u32[]{:S(2)}) copy-start(f32[24]{0:T(128)} %skip_ref.5) | copy-start | bytes 292
  31.6 9.5 %copy-start.7 = (s32[1,8]{1,0:T(1,128)S(1)}, s32[1,8]{1,0:T(1,128)}, u32[]{:S(2)}) copy-start(s32[1,8]{1,0:T(1,128)} %lengths_ref.9) | copy-start | bytes 100
  31.6 9.5 %copy-start.9 = (f32[1536]{0:T(1024)S(1)}, f32[1536]{0:T(1024)}, u32[]{:S(2)}) copy-start(f32[1536]{0:T(1024)} %gain_ref.5) | copy-start | bytes 18436
  41.0 28.8 %copy-start.12 = (bf16[768,1024]{1,0:T(8,128)(2,1)}, bf16[768,1024]{1,0:T(8,128)(2,1)S(1)}, u32[]{:S(2)}) copy-start(bf16[768,1024]{1,0:T(8,128)(2,1)S(1)} %get-tuple-element.97.turned_ref) | copy-start | bytes 4718596
  41.0 28.6 %copy-start = (bf16[64,1536]{1,0:T(8,128)(2,1)}, bf16[64,1536]{1,0:T(8,128)(2,1)S(1)}, u32[]{:S(2)}) copy-start(bf16[64,1536]{1,0:T(8,128)(2,1)S(1)} %collective-permute-done.1.recv_ref._dpre_ref._moves_ref) | copy-start | bytes 589828
  69.6 11.8 %copy-start.13 = (f32[48,1024]{1,0:T(8,128)}, f32[48,1024]{1,0:T(8,128)S(1)}, u32[]{:S(2)}) copy-start(f32[48,1024]{1,0:T(8,128)S(1)} %get-tuple-element.140.r_ref) | copy-start | bytes 589828
  69.6 11.8 %copy-start.14 = (f32[16,1536]{1,0:T(8,128)}, f32[16,1536]{1,0:T(8,128)S(1)}, u32[]{:S(2)}) copy-start(f32[16,1536]{1,0:T(8,128)S(1)} %get-tuple-element.142.mix_sums_ref) | copy-start | bytes 294916
  69.6 11.8 %collective-permute-start.2 = (bf16[64,1536]{1,0:T(8,128)(2,1)S(1)}, bf16[64,1536]{1,0:T(8,128)(2,1)S(1)}, u32[]{:S(2)}, u32[]{:S(2)}) collective-permute-start(bf16[64,1536]{1,0:T(8,128)(2,1)S(1)} %get-tuple-element.113), channel_id=1, source_target_pairs={{0,16},{16,0},{1,17},{17,1},{2,18},{18,2},{3,19},{19,3},{4,20},{20... | collective-permute-start | bytes 589832 | tf_op jit(solution)/shard_map/ppermute | solution.py:1380
  81.4 0.6 copy-start.15
  81.4 0.7 copy-start.16
  81.4 6.4 %collective-permute-start.3 = (bf16[384,3072]{1,0:T(8,128)(2,1)}, bf16[384,3072]{1,0:T(8,128)(2,1)S(1)}, u32[]{:S(2)}, u32[]{:S(2)}) collective-permute-start(bf16[384,3072]{1,0:T(8,128)(2,1)} %get-tuple-element.115), channel_id=1, source_target_pairs={{0,1},{1,0},{2,3},{3,2},{4,5},{5,4},{6,7},{7,6},{8,9},{9,8},{10,11... | collective-permute-start | bytes 7077896 | tf_op jit(solution)/shard_map/ppermute | solution.py:1143
  82.0 5.8 %copy-start.10 = (bf16[384,3072]{1,0:T(8,128)(2,1)S(1)}, bf16[384,3072]{1,0:T(8,128)(2,1)}, u32[]{:S(2)}) copy-start(bf16[384,3072]{1,0:T(8,128)(2,1)} %get-tuple-element.114.kept_ref) | copy-start | bytes 7077892
  88.5 27.9 %collective-permute-start.4 = (bf16[192,3072]{1,0:T(8,128)(2,1)S(1)}, bf16[192,3072]{1,0:T(8,128)(2,1)S(1)}, u32[]{:S(2)}, u32[]{:S(2)}) collective-permute-start(bf16[192,3072]{1,0:T(8,128)(2,1)S(1)} %get-tuple-element.127), channel_id=1, source_target_pairs={{0,2},{1,3},{2,0},{3,1},{4,6},{5,7},{6,4},{7,5},{8,10},{9,11},{10,... | collective-permute-start | bytes 3538952 | tf_op jit(solution)/shard_map/ppermute | solution.py:1143
  116.6 19.9 %collective-permute-start.6 = (bf16[96,3072]{1,0:T(8,128)(2,1)S(1)}, bf16[96,3072]{1,0:T(8,128)(2,1)S(1)}, u32[]{:S(2)}, u32[]{:S(2)}) collective-permute-start(bf16[96,3072]{1,0:T(8,128)(2,1)S(1)} %get-tuple-element.149), channel_id=1, source_target_pairs={{0,4},{1,5},{2,6},{3,7},{4,0},{5,1},{6,2},{7,3},{8,12},{9,13},{10,... | collective-permute-start | bytes 1769480 | tf_op jit(solution)/shard_map/ppermute | solution.py:1143
  136.5 4.7 %collective-permute-start.8 = (bf16[384,2048]{1,0:T(8,128)(2,1)}, bf16[384,2048]{1,0:T(8,128)(2,1)S(1)}, u32[]{:S(2)}, u32[]{:S(2)}) collective-permute-start(bf16[384,2048]{1,0:T(8,128)(2,1)} %get-tuple-element.155), channel_id=1, source_target_pairs={{0,1},{1,0},{2,3},{3,2},{4,5},{5,4},{6,7},{7,6},{8,9},{9,8},{10,11... | collective-permute-start | bytes 4718600 | tf_op jit(solution)/shard_map/ppermute | solution.py:1143
  136.6 9.0 %collective-permute-start.5 = (bf16[16,1792]{1,0:T(8,128)(2,1)}, bf16[16,1792]{1,0:T(8,128)(2,1)S(1)}, u32[]{:S(2)}, u32[]{:S(2)}) collective-permute-start(bf16[16,1792]{1,0:T(8,128)(2,1)} %get-tuple-element.144), channel_id=1, source_target_pairs={{16,0},{17,1},{18,2},{19,3},{20,4},{21,5},{22,6},{23,7},{24,8},{25... | collective-permute-start | bytes 172040 | tf_op jit(solution)/shard_map/ppermute | solution.py:1594
  137.9 3.3 %collective-permute-start.9 = (bf16[16,1024]{1,0:T(8,128)(2,1)}, bf16[16,1024]{1,0:T(8,128)(2,1)S(1)}, u32[]{:S(2)}, u32[]{:S(2)}) collective-permute-start(bf16[16,1024]{1,0:T(8,128)(2,1)} %get-tuple-element.156.small_ref), channel_id=1, source_target_pairs={{0,1},{1,0},{2,3},{3,2},{4,5},{5,4},{6,7},{7,6},{8,9},{9,8},{10,11... | collective-permute-start | bytes 98312 | tf_op jit(solution)/shard_map/ppermute | solution.py:1143
  138.4 2.8 %copy-start.8 = (bf16[16,1024]{1,0:T(8,128)(2,1)S(1)}, bf16[16,1024]{1,0:T(8,128)(2,1)}, u32[]{:S(2)}) copy-start(bf16[16,1024]{1,0:T(8,128)(2,1)} %get-tuple-element.156.small_ref) | copy-start | bytes 98308
  138.4 2.8 %copy-start.11 = (bf16[384,2048]{1,0:T(8,128)(2,1)S(1)}, bf16[384,2048]{1,0:T(8,128)(2,1)}, u32[]{:S(2)}) copy-start(bf16[384,2048]{1,0:T(8,128)(2,1)} %get-tuple-element.154.mine_ref) | copy-start | bytes 4718596
  138.5 23.2 %collective-permute-start.7 = (bf16[48,3072]{1,0:T(8,128)(2,1)S(1)}, bf16[48,3072]{1,0:T(8,128)(2,1)S(1)}, u32[]{:S(2)}, u32[]{:S(2)}) collective-permute-start(bf16[48,3072]{1,0:T(8,128)(2,1)S(1)} %get-tuple-element.153), channel_id=1, source_target_pairs={{0,8},{1,9},{2,10},{3,11},{4,12},{5,13},{6,14},{7,15},{8,0},{9,1},... | collective-permute-start | bytes 884744 | tf_op jit(solution)/shard_map/ppermute | solution.py:1143
  141.6 20.3 %collective-permute-start.10 = (bf16[208,1024]{1,0:T(8,128)(2,1)S(1)}, bf16[208,1024]{1,0:T(8,128)(2,1)S(1)}, u32[]{:S(2)}, u32[]{:S(2)}) collective-permute-start(bf16[208,1024]{1,0:T(8,128)(2,1)S(1)} %get-tuple-element.157), channel_id=1, source_target_pairs={{0,18},{1,19},{2,16},{3,17},{4,22},{5,23},{6,20},{7,21},{8,26},{9,... | collective-permute-start | bytes 1277960 | tf_op jit(solution)/shard_map/ppermute | solution.py:1662
  145.0 18.4 %collective-permute-start.11 = (bf16[208,1024]{1,0:T(8,128)(2,1)S(1)}, bf16[208,1024]{1,0:T(8,128)(2,1)S(1)}, u32[]{:S(2)}, u32[]{:S(2)}) collective-permute-start(bf16[208,1024]{1,0:T(8,128)(2,1)S(1)} %get-tuple-element.160), channel_id=1, source_target_pairs={{0,16},{16,0},{1,17},{17,1},{2,18},{18,2},{3,19},{19,3},{4,20},{20... | collective-permute-start | bytes 1277960 | tf_op jit(solution)/shard_map/ppermute | solution.py:1143
  145.0 19.1 %collective-permute-start.12 = (bf16[208,1024]{1,0:T(8,128)(2,1)S(1)}, bf16[208,1024]{1,0:T(8,128)(2,1)S(1)}, u32[]{:S(2)}, u32[]{:S(2)}) collective-permute-start(bf16[208,1024]{1,0:T(8,128)(2,1)S(1)} %get-tuple-element.161), channel_id=1, source_target_pairs={{0,2},{1,3},{2,0},{3,1},{4,6},{5,7},{6,4},{7,5},{8,10},{9,11},{10,... | collective-permute-start | bytes 1277960 | tf_op jit(solution)/shard_map/ppermute | solution.py:1143
  145.6 0.6 copy-start.17
  164.3 7.6 %collective-permute-start.13 = (bf16[64,1024]{1,0:T(8,128)(2,1)S(1)}, bf16[64,1024]{1,0:T(8,128)(2,1)S(1)}, u32[]{:S(2)}, u32[]{:S(2)}) collective-permute-start(bf16[64,1024]{1,0:T(8,128)(2,1)S(1)} %get-tuple-element.164), channel_id=1, source_target_pairs={{0,4},{1,5},{2,6},{3,7},{4,0},{5,1},{6,2},{7,3},{8,12},{9,13},{10,... | collective-permute-start | bytes 393224 | tf_op jit(solution)/shard_map/ppermute | solution.py:1143
  164.8 12.9 %collective-permute-start.14 = (bf16[64,1024]{1,0:T(8,128)(2,1)S(1)}, bf16[64,1024]{1,0:T(8,128)(2,1)S(1)}, u32[]{:S(2)}, u32[]{:S(2)}) collective-permute-start(bf16[64,1024]{1,0:T(8,128)(2,1)S(1)} %get-tuple-element.165), channel_id=1, source_target_pairs={{0,8},{1,9},{2,10},{3,11},{4,12},{5,13},{6,14},{7,15},{8,0},{9,1},... | collective-permute-start | bytes 393224 | tf_op jit(solution)/shard_map/ppermute | solution.py:1143
  166.3 11.4 %collective-permute-start.15 = (bf16[64,1024]{1,0:T(8,128)(2,1)S(1)}, bf16[64,1024]{1,0:T(8,128)(2,1)S(1)}, u32[]{:S(2)}, u32[]{:S(2)}) collective-permute-start(bf16[64,1024]{1,0:T(8,128)(2,1)S(1)} %get-tuple-element.166), channel_id=1, source_target_pairs={{0,12},{1,13},{2,14},{3,15},{4,8},{5,9},{6,10},{7,11},{8,4},{9,5},... | collective-permute-start | bytes 393224 | tf_op jit(solution)/shard_map/ppermute | solution.py:1143
  168.7 13.7 %collective-permute-start.17 = (bf16[48,3072]{1,0:T(8,128)(2,1)S(1)}, bf16[48,3072]{1,0:T(8,128)(2,1)S(1)}, u32[]{:S(2)}, u32[]{:S(2)}) collective-permute-start(bf16[48,3072]{1,0:T(8,128)(2,1)S(1)} %early_sum.1.early_ref), channel_id=1, source_target_pairs={{0,16},{16,0},{1,17},{17,1},{2,18},{18,2},{3,19},{19,3},{4,20},{20... | collective-permute-start | bytes 884744 | tf_op jit(solution)/shard_map/ppermute | solution.py:1143
  177.8 4.7 %collective-permute-start.16 = (bf16[48,1024]{1,0:T(8,128)(2,1)S(1)}, bf16[48,1024]{1,0:T(8,128)(2,1)S(1)}, u32[]{:S(2)}, u32[]{:S(2)}) collective-permute-start(bf16[48,1024]{1,0:T(8,128)(2,1)S(1)} %get-tuple-element.167.late_ref), channel_id=1, source_target_pairs={{0,16},{16,0},{1,17},{17,1},{2,18},{18,2},{3,19},{19,3},{4,20},{20... | collective-permute-start | bytes 294920 | tf_op jit(solution)/shard_map/ppermute | solution.py:1143
